TPU v7x, 32 devices: a whole 2x2x4 slice. The times are simulated.
32 devices in a mesh: row: 8 (over z, core), col: 4 (over y, x).
Axes of the slice: x: 2, y: 2, z: 4, core: 2. Of those that a mesh axis runs over, the one named last changes fastest.
Arguments:
- queries: bfloat16 [1536, 3072], P('row', 'col'), may hold values from -24 to 24
- keys_tile: bfloat16 [1536, 3072], P('row', 'col'), may hold values from -4.5 to 4.5
- values_tile: bfloat16 [1536, 3072], P('row', 'col'), may hold values from -6 to 6
- out_weight: bfloat16 [3072, 6144], P('row', 'col'), may hold values from -0.75 to 0.75
- out_grad: bfloat16 [1536, 6144], P('row', 'col'), may hold values from -1.5 to 1.5
Outputs:
- mixed: bfloat16 [1536, 6144], P('row', 'col')
- query_grad: bfloat16 [1536, 3072], P('row', 'col')
- key_grad: bfloat16 [1536, 3072], P('row', 'col')
- value_grad: bfloat16 [1536, 3072], P('row', 'col')
- weight_grad: bfloat16 [3072, 6144], P('row', 'col')
All inputs are finite; a program needn't handle non-finite values.
Results may differ from a plain program's by a relative error of at most 0.019.
Values may be sent and summed in bfloat16 or wider, within the bound.
No kernel may reach another device: no remote copies, remote signals or barrier semaphores. Data moves between devices by JAX's collectives and lax.ppermute only.
A program may use at most 128 MiB of HBM per device.

v0:
```python
import jax
import jax.numpy as jnp
from jax import lax
from jax.sharding import PartitionSpec as P

HD = 128


def head_forward(args):
    query_head, key_head, value_head = args
    scores = jnp.einsum(
        "qd,kd->qk", query_head, key_head, preferred_element_type=jnp.float32
    ) * HD ** (-0.5)
    top = jnp.max(scores, axis=1, keepdims=True)
    lse = top[:, 0] + jnp.log(jnp.sum(jnp.exp(scores - top), axis=1))
    probs = jnp.exp(scores - lse[:, None]).astype(jnp.bfloat16)
    attn = jnp.dot(probs, value_head, preferred_element_type=jnp.float32).astype(jnp.bfloat16)
    return (attn, lse)


def score_grads(query_head, key_head, value_head, grad_head, lse, delta):
    scores = jnp.einsum(
        "qd,kd->qk", query_head, key_head, preferred_element_type=jnp.float32
    ) * HD ** (-0.5)
    probs = jnp.exp(scores - lse[:, None]).astype(jnp.bfloat16)
    dprob = jnp.einsum("qd,kd->qk", grad_head, value_head, preferred_element_type=jnp.float32)
    dscore = (probs.astype(jnp.float32) * (dprob - delta[:, None]) * HD ** (-0.5)).astype(
        jnp.bfloat16
    )
    return (probs, dscore)


def split_heads(block):
    return block.reshape(block.shape[0], block.shape[1] // HD, HD).transpose(1, 0, 2)


def merge_heads(block):
    return block.transpose(1, 0, 2).reshape(block.shape[1], block.shape[0] * HD)


def per_device(queries, keys_tile, values_tile, out_weight, out_grad):
    query3 = split_heads(queries)
    key_local = split_heads(keys_tile)
    value_local = split_heads(values_tile)
    key_every, value_every = (
        lax.all_gather(key_local, "row", axis=1, tiled=True),
        lax.all_gather(value_local, "row", axis=1, tiled=True),
    )
    attn3, lse = lax.map(head_forward, (query3, key_every, value_every))
    attn = merge_heads(attn3)
    attn_row = lax.all_gather(attn, "col", axis=1, tiled=True)
    weight_col = lax.all_gather(out_weight, "row", axis=0, tiled=True)
    mixed = jnp.dot(attn_row, weight_col, preferred_element_type=jnp.float32).astype(jnp.bfloat16)
    partial_grad = jnp.einsum("rc,fc->rf", out_grad, weight_col, preferred_element_type=jnp.float32)
    d_attn = lax.psum_scatter(partial_grad, "col", scatter_dimension=1, tiled=True).astype(
        jnp.bfloat16
    )
    weight_grad = lax.psum_scatter(
        jnp.einsum("rf,rc->fc", attn_row, out_grad, preferred_element_type=jnp.float32).astype(
            jnp.bfloat16
        ),
        "row",
        scatter_dimension=0,
        tiled=True,
    )
    grad3 = split_heads(d_attn)
    delta = jnp.sum(grad3.astype(jnp.float32) * attn3.astype(jnp.float32), axis=2)

    def head_backward(args):
        query_head, key_head, value_head, grad_head, lse_head, delta_head = args
        probs, dscore = score_grads(
            query_head, key_head, value_head, grad_head, lse_head, delta_head
        )
        query_g = jnp.dot(dscore, key_head, preferred_element_type=jnp.float32).astype(jnp.bfloat16)
        key_term = jnp.einsum("qk,qd->kd", dscore, query_head, preferred_element_type=jnp.float32)
        value_term = jnp.einsum("qk,qd->kd", probs, grad_head, preferred_element_type=jnp.float32)
        return (query_g, key_term, value_term)

    query_g3, key_terms, value_terms = lax.map(
        head_backward, (query3, key_every, value_every, grad3, lse, delta)
    )
    key_g3, value_g3 = (
        lax.psum_scatter(key_terms, "row", scatter_dimension=1, tiled=True),
        lax.psum_scatter(value_terms, "row", scatter_dimension=1, tiled=True),
    )
    key_g3 = key_g3.astype(jnp.bfloat16)
    value_g3 = value_g3.astype(jnp.bfloat16)
    return (mixed, merge_heads(query_g3), merge_heads(key_g3), merge_heads(value_g3), weight_grad)


def solution(mesh):
    in_specs = (P("row", "col"), P("row", "col"), P("row", "col"), P("row", "col"), P("row", "col"))
    out_specs = (
        P("row", "col"),
        P("row", "col"),
        P("row", "col"),
        P("row", "col"),
        P("row", "col"),
    )
    return jax.shard_map(
        per_device, mesh=mesh, in_specs=in_specs, out_specs=out_specs, check_vma=False
    )
```

profile of v0, /device:TPU:0, one launch (start us, length us, event | category | flops | bytes accessed | tf_op | source)
XLA Modules:
  0.0 468.4 jit_solution(2326513487862883330)
XLA Ops:
  11.8 91.4 %all-gather.11.cloned.1.call-done = bf16[3072,1536]{1,0:T(8,128)(2,1)} async-done(((bf16[384,1536]{1,0:T(8,128)(2,1)}), bf16[3072,1536]{1,0:T(8,128)(2,1)}) %all-gather.11.cloned.1.call-update) | async-done | bytes 9437200 | tf_op jit(solution)/shard_map/all_gather | solution.py:52
  103.1 8.3 %fusion.41 = f32[192,3072]{1,0:T(8,128)} fusion(bf16[192,1536]{1,0:T(8,128)(2,1)S(1)} %copy-done, bf16[3072,1536]{1,0:T(8,128)(2,1)} %all-gather.11.cloned.1.call-done), kind=kOutput, calls=%fused_computation.62 | convolution fusion | flops 1811939328 | bytes 12386304 | tf_op jit(solution)/shard_map/rc,fc->rf/dot_general | solution.py:54
  111.5 23.9 %all-gather.5.cloned.1.call-done = bf16[6,1536,128]{2,1,0:T(8,128)(2,1)} async-done(((bf16[6,192,128]{2,1,0:T(8,128)(2,1)}), bf16[6,1536,128]{2,1,0:T(8,128)(2,1)}) %all-gather.5.cloned.1.call-update) | async-done | bytes 2359312 | tf_op jit(solution)/shard_map/all_gather | solution.py:46
  135.4 33.0 %all-gather.7.cloned.1.call-done = bf16[6,1536,128]{2,1,0:T(8,128)(2,1)} async-done(((bf16[6,192,128]{2,1,0:T(8,128)(2,1)}), bf16[6,1536,128]{2,1,0:T(8,128)(2,1)}) %all-gather.7.cloned.1.call-update) | async-done | bytes 2359312 | tf_op jit(solution)/shard_map/all_gather | solution.py:47
  168.4 19.4 %while.26 = (s32[]{:T(128)}, bf16[6,192,128]{2,1,0:T(8,128)(2,1)S(1)}, f32[6,192]{1,0:T(8,128)S(1)}, bf16[6,192,128]{2,1,0:T(8,128)(2,1)S(1)}, bf16[6,1536,128]{...) while((s32[]{:T(128)}, bf16[6,192,128]{2,1,0:T(8,128)(2,1)S(1)}, ...), condition=%wide.region_3.4_spmd, body=%wide.region_0.3_spmd.sunk | while | flops 152788800 | bytes 4432993 | solution.py:49
  168.4 1.4 fusion.72
  170.2 1.4 fusion.73
  171.6 1.4 fusion.72
  173.4 1.4 fusion.73
  174.8 1.4 fusion.72
  176.6 1.4 fusion.73
  178.1 1.4 fusion.72
  179.8 1.4 fusion.73
  181.3 1.4 fusion.72
  183.1 1.4 fusion.73
  184.6 1.4 fusion.72
  186.3 1.4 fusion.73
  188.6 19.2 %reduce-scatter.5.cloned.1.call-done = f32[192,768]{1,0:T(8,128)} async-done(((f32[192,3072]{1,0:T(8,128)}), f32[192,768]{1,0:T(8,128)}) %reduce-scatter.5.cloned.1.call-update) | async-done | bytes 589840 | tf_op jit(solution)/shard_map/reduce_scatter | solution.py:55
  209.8 40.1 %while.27 = (s32[]{:T(128)}, bf16[6,192,128]{2,1,0:T(8,128)(2,1)S(1)}, f32[6,1536,128]{2,1,0:T(8,128)}, f32[6,1536,128]{2,1,0:T(8,128)}, bf16[6,192,128]{2,1,0:T...) while((s32[]{:T(128)}, ...), condition=%wide.region_7.8_spmd, body=%wide.region_6.7_spmd.sunk | while | flops 379871232 | bytes 6547577 | solution.py:79
  209.8 1.3 fusion.84
  216.5 1.4 fusion.84
  217.9 1.4 fusion.85
  221.9 1.4 fusion.88
  223.2 1.3 fusion.84
  228.6 1.4 fusion.88
  250.8 6.7 %convolution_convert_fusion.2 = bf16[3072,1536]{1,0:T(8,128)(2,1)} fusion(bf16[192,3072]{1,0:T(8,128)(2,1)} %all-gather.9.cloned.1.call-done, bf16[192,1536]{1,0:T(8,128)(2,1)S(1)} %copy-done), kind=kOutput, calls=%fused_computation.52 | convolution fusion | flops 1816657920 | bytes 11206656 | tf_op jit(solution)/shard_map/rf,rc->fc/dot_general | solution.py:59
  258.8 6.5 %convolution_convert_fusion.3 = bf16[192,1536]{1,0:T(8,128)(2,1)} fusion(bf16[192,3072]{1,0:T(8,128)(2,1)S(1)} %copy-done.1, bf16[3072,1536]{1,0:T(8,128)(2,1)} %all-gather.11.cloned.1.call-done), kind=kOutput, calls=%fused_computation.53 | convolution fusion | flops 1812234240 | bytes 11206656 | tf_op jit(solution)/shard_map/dot_general | solution.py:53
  266.0 39.1 %reduce-scatter.9.cloned.1.call-done = f32[6,192,128]{2,1,0:T(8,128)} async-done(((f32[6,1536,128]{2,1,0:T(8,128)}), f32[6,192,128]{2,1,0:T(8,128)}) %reduce-scatter.9.cloned.1.call-update) | async-done | bytes 589840 | tf_op jit(solution)/shard_map/reduce_scatter | solution.py:84
  305.1 1.8 copy_bitcast_fusion
  306.9 53.8 %reduce-scatter.7.cloned.1.call-done = f32[6,192,128]{2,1,0:T(8,128)} async-done(((f32[6,1536,128]{2,1,0:T(8,128)}), f32[6,192,128]{2,1,0:T(8,128)}) %reduce-scatter.7.cloned.1.call-update) | async-done | bytes 589840 | tf_op jit(solution)/shard_map/reduce_scatter | solution.py:83
  360.8 1.8 copy_bitcast_fusion.1
  362.6 99.0 %reduce-scatter.11.cloned.1.call-done = bf16[384,1536]{1,0:T(8,128)(2,1)} async-done(((bf16[3072,1536]{1,0:T(8,128)(2,1)}), bf16[384,1536]{1,0:T(8,128)(2,1)}) %reduce-scatter.11.cloned.1.call-update) | async-done | bytes 1179664 | tf_op jit(solution)/shard_map/reduce_scatter | solution.py:58
  (91 shorter events, 44.2 us)
Async XLA Ops:
  7.2 96.0 %copy-start = (bf16[192,1536]{1,0:T(8,128)(2,1)S(1)}, bf16[192,1536]{1,0:T(8,128)(2,1)}, u32[]{:S(2)}) copy-start(bf16[192,1536]{1,0:T(8,128)(2,1)} %param.13) | copy-start | bytes 1769476
  7.2 2.9 copy-start.2
  7.2 4.2 copy-start.3
  7.2 95.9 %all-gather.11.cloned.1.call-start = ((), (), s32[]{:S(2)}) async-start(), calls=%async_computation.7 | async-start | bytes 10616832 | tf_op jit(solution)/shard_map/all_gather | solution.py:52
  7.9 127.5 %all-gather.5.cloned.1.call-start = ((), (), s32[]{:S(2)}) async-start(), calls=%async_computation.4 | async-start | bytes 2654208 | tf_op jit(solution)/shard_map/all_gather | solution.py:46
  10.1 158.3 %all-gather.7.cloned.1.call-start = ((), (), s32[]{:S(2)}) async-start(), calls=%async_computation.5 | async-start | bytes 2654208 | tf_op jit(solution)/shard_map/all_gather | solution.py:47
  11.3 196.6 %reduce-scatter.5.cloned.1.call-start = ((), (), s32[]{:S(2)}) async-start(), calls=%async_computation.8 | async-start | bytes 2949120 | tf_op jit(solution)/shard_map/reduce_scatter | solution.py:55
  111.4 139.4 %all-gather.9.cloned.1.call-start = ((), (), s32[]{:S(2)}) async-start(), calls=%async_computation.6 | async-start | bytes 1474560 | tf_op jit(solution)/shard_map/all_gather | solution.py:51
  188.6 116.5 %reduce-scatter.9.cloned.1.call-start = ((), (), s32[]{:S(2)}) async-start(), calls=%async_computation.10 | async-start | bytes 5308416 | tf_op jit(solution)/shard_map/reduce_scatter | solution.py:84
  250.0 110.8 %reduce-scatter.7.cloned.1.call-start = ((), (), s32[]{:S(2)}) async-start(), calls=%async_computation.9 | async-start | bytes 5308416 | tf_op jit(solution)/shard_map/reduce_scatter | solution.py:83
  250.7 210.8 %reduce-scatter.11.cloned.1.call-start = ((), (), s32[]{:S(2)}) async-start(), calls=%async_computation.11 | async-start | bytes 10616832 | tf_op jit(solution)/shard_map/reduce_scatter | solution.py:58
  257.5 1.3 copy-start.1
Sparse Core Ops, SparseCore 0:
  9.7 93.4 all-gather.10
  105.3 30.0 all-gather.4
  137.6 30.7 all-gather.6
  171.3 36.5 reduce-scatter.4
  210.1 27.8 all-gather.8
  250.1 54.9 reduce-scatter.8
  307.4 53.3 reduce-scatter.6
  363.6 97.8 reduce-scatter.10
where the time goes:
time: 470 us; the launch traced here: 468 us
  waiting for transfers between devices  361 us (77%)
  matrix products  78.5 us (17%)
  between operations  14.3 us (3%)
  local copies, waits for them, and re-layouts  7.14 us (2%)
  other arithmetic  7.01 us (1%)
    reduce_scatter x1, waiting for transfers between devices, per_device(): lax.psum_scatter(jnp.einsum('rf,rc->fc', attn_row, out_grad, preferred_el...  99 us
    all_gather x1, waiting for transfers between devices, per_device(): weight_col = lax.all_gather(out_weight, 'row', axis=0, tiled=True)  91.4 us
    reduce_scatter x1, waiting for transfers between devices, per_device(): lax.psum_scatter(key_terms, 'row', scatter_dimension=1, tiled=True)  53.8 us
    reduce_scatter x1, waiting for transfers between devices, per_device(): lax.psum_scatter(value_terms, 'row', scatter_dimension=1, tiled=True)  39.1 us
    all_gather x1, waiting for transfers between devices, per_device(): lax.all_gather(value_local, 'row', axis=1, tiled=True)  33 us
    all_gather x1, waiting for transfers between devices, per_device(): lax.all_gather(key_local, 'row', axis=1, tiled=True)  23.9 us
    reduce_scatter x1, waiting for transfers between devices, per_device(): lax.psum_scatter(partial_grad, 'col', scatter_dimension=1, tiled=True)  19.2 us
  transfers between devices with their start and end apart: 8, of which 7 were waited for; matrix products, arithmetic and copies ran while one was open for 20% of the time, Pallas kernels for 0%

commit v1 on v0

--- a/solution.py
+++ b/solution.py
@@ -1,9 +1,17 @@
+import functools
+
 import jax
 import jax.numpy as jnp
 from jax import lax
+from jax.experimental import pallas as pl
+from jax.experimental.pallas import tpu as pltpu
 from jax.sharding import PartitionSpec as P
 
 HD = 128
+SCALE = HD ** (-0.5)
+LOG2E = 1.4426950408889634
+F32 = jnp.float32
+BF16 = jnp.bfloat16
 
 
 def head_forward(args):
@@ -88,15 +96,269 @@
     return (mixed, merge_heads(query_g3), merge_heads(key_g3), merge_heads(value_g3), weight_grad)
 
 
+PLANES, CORES, COLS = 4, 2, 4
+
+
+def row_shift(s):
+    return [
+        (CORES * z + k, CORES * ((z + s) % PLANES) + k)
+        for z in range(PLANES)
+        for k in range(CORES)
+    ]
+
+
+SWAP = [(CORES * z + k, CORES * z + 1 - k) for z in range(PLANES) for k in range(CORES)]
+
+
+def col_xor(j):
+    return [(c, c ^ j) for c in range(COLS)]
+
+
+def pick(stack, index):
+    return lax.dynamic_index_in_dim(stack, index, 0, keepdims=False)
+
+
+def nt(a, b):
+    return lax.dot_general(a, b, (((1,), (1,)), ((), ())), preferred_element_type=F32)
+
+
+def tn(a, b):
+    return lax.dot_general(a, b, (((0,), (0,)), ((), ())), preferred_element_type=F32)
+
+
+def forward_kernel(q_ref, k_ref, v_ref, p_ref, attn_ref):
+    raw = nt(k_ref[0], q_ref[...])
+    top = jnp.max(raw, axis=0, keepdims=True)
+    e = jnp.exp2((raw - top) * (SCALE * LOG2E))
+    total = jnp.sum(e, axis=0, keepdims=True)
+    probs = (e * (1.0 / total)).astype(BF16)
+    p_ref[0] = probs
+    attn_ref[...] = tn(v_ref[0], probs).T.astype(BF16)
+
+
+def attention_forward(q, k, v):
+    rows, keys = q.shape[0] // 3, k.shape[1]
+    return pl.pallas_call(
+        forward_kernel,
+        grid=(3,),
+        in_specs=[
+            pl.BlockSpec((rows, HD), lambda i: (i, 0)),
+            pl.BlockSpec((1, keys, HD), lambda i: (i // 2, 0, 0)),
+            pl.BlockSpec((1, keys, HD), lambda i: (i // 2, 0, 0)),
+        ],
+        out_specs=[
+            pl.BlockSpec((1, keys, rows), lambda i: (i, 0, 0)),
+            pl.BlockSpec((rows, HD), lambda i: (i, 0)),
+        ],
+        out_shape=[
+            jax.ShapeDtypeStruct((3, keys, rows), BF16),
+            jax.ShapeDtypeStruct((3 * rows, HD), BF16),
+        ],
+        compiler_params=pltpu.CompilerParams(vmem_limit_bytes=40 * 2**20),
+        cost_estimate=pl.CostEstimate(
+            flops=3 * 4 * rows * keys * HD,
+            bytes_accessed=3 * rows * keys * 2,
+            transcendentals=3 * rows * keys,
+        ),
+        name="attention_forward",
+    )(q, k, v)
+
+
+def backward_kernel(q_ref, k_ref, v_ref, p_ref, attn_ref, grad_ref, dq_ref, dk_ref, dv_ref):
+    step = pl.program_id(0)
+    grad = grad_ref[...]
+    product = grad.astype(F32) * attn_ref[...].astype(F32)
+    delta = jnp.sum(product.T, axis=0, keepdims=True)
+    probs = p_ref[0]
+    dprob = nt(v_ref[0], grad)
+    dscore = (probs.astype(F32) * (dprob - delta) * SCALE).astype(BF16)
+    dq_ref[...] = tn(k_ref[0], dscore).T.astype(BF16)
+    dk = jnp.dot(dscore, q_ref[...], preferred_element_type=F32)
+    dv = jnp.dot(probs, grad, preferred_element_type=F32)
+
+    @pl.when(step != 1)
+    def _():
+        dk_ref[0] = dk
+        dv_ref[0] = dv
+
+    @pl.when(step == 1)
+    def _():
+        dk_ref[0] += dk
+        dv_ref[0] += dv
+
+
+def attention_backward(q, k, v, probs, attn, grad):
+    rows, keys = q.shape[0] // 3, k.shape[1]
+    by_query = pl.BlockSpec((rows, HD), lambda i: (i, 0))
+    by_head = pl.BlockSpec((1, keys, HD), lambda i: (i // 2, 0, 0))
+    return pl.pallas_call(
+        backward_kernel,
+        grid=(3,),
+        in_specs=[
+            by_query,
+            by_head,
+            by_head,
+            pl.BlockSpec((1, keys, rows), lambda i: (i, 0, 0)),
+            by_query,
+            by_query,
+        ],
+        out_specs=[by_query, by_head, by_head],
+        out_shape=[
+            jax.ShapeDtypeStruct(q.shape, BF16),
+            jax.ShapeDtypeStruct(k.shape, F32),
+            jax.ShapeDtypeStruct(k.shape, F32),
+        ],
+        compiler_params=pltpu.CompilerParams(vmem_limit_bytes=48 * 2**20),
+        cost_estimate=pl.CostEstimate(
+            flops=3 * 8 * rows * keys * HD,
+            bytes_accessed=3 * rows * keys * 2,
+            transcendentals=0,
+        ),
+        name="attention_backward",
+    )(q, k, v, probs, attn, grad)
+
+
+def per_device_fast(queries, keys_tile, values_tile, out_weight, out_grad):
+    tokens = queries.shape[0]
+    half = tokens // 2
+    row, col = lax.axis_index("row"), lax.axis_index("col")
+    plane, core = row // CORES, row % CORES
+
+    def head(block, g):
+        return block[:, g * HD : (g + 1) * HD]
+
+    def spread(pieces):
+        return [pick(pieces, col)] + [
+            lax.ppermute(pick(pieces, col ^ j), "col", col_xor(j)) for j in range(1, COLS)
+        ]
+
+    def input_piece(d):
+        y, x = divmod(d, 2)
+        a, b = 3 * y + x, 3 * y + 2
+        return jnp.concatenate(
+            [
+                head(queries, a),
+                head(queries, b)[x * half : (x + 1) * half],
+                head(keys_tile, a),
+                head(keys_tile, b),
+                head(values_tile, a),
+                head(values_tile, b),
+            ]
+        )
+
+    over_col = jnp.stack(spread(jnp.stack([input_piece(d) for d in range(COLS)])))
+    arrived = [pick(over_col, col ^ plane)]
+    for s in range(1, PLANES):
+        arrived.append(
+            lax.ppermute(pick(over_col, col ^ ((plane + s) % PLANES)), "row", row_shift(s))
+        )
+    arrived = jnp.stack(arrived)
+
+    grads = [out_grad]
+    for s in range(1, PLANES):
+        grads.append(lax.ppermute(grads[-1], "row", row_shift(1)))
+    grads_own = jnp.concatenate(grads)
+    grads_other = jnp.concatenate([lax.ppermute(g, "row", SWAP) for g in grads])
+    weight_other = lax.ppermute(out_weight, "row", SWAP)
+    weight = jnp.where(
+        core == 0,
+        jnp.concatenate([out_weight, weight_other]),
+        jnp.concatenate([weight_other, out_weight]),
+    )
+
+    q = jnp.concatenate(
+        [
+            arrived[:, :tokens].reshape(PLANES * tokens, HD),
+            arrived[:, tokens : tokens + half].reshape(PLANES * half, HD),
+        ]
+    )
+    kv_own = arrived[:, tokens + half :].reshape(PLANES, 4, tokens, HD).transpose(1, 0, 2, 3)
+    kv_own = kv_own.reshape(4, PLANES * tokens, HD)
+    kv = jnp.concatenate([kv_own, lax.ppermute(kv_own, "row", SWAP)], axis=1)
+    k, v = kv[:2], kv[2:]
+    probs, attn = attention_forward(q, k, v)
+
+    attn_col = jnp.stack([attn] + [lax.ppermute(attn, "col", col_xor(j)) for j in range(1, COLS)])
+    by_col = [pick(attn_col, col ^ d) for d in range(COLS)]
+    columns = []
+    for y in range(2):
+        columns += [by_col[2 * y][: PLANES * tokens], by_col[2 * y + 1][: PLANES * tokens]]
+        halves = [by_col[2 * y + x][PLANES * tokens :].reshape(PLANES, half, HD) for x in range(2)]
+        columns.append(jnp.concatenate(halves, axis=1).reshape(PLANES * tokens, HD))
+    attn_plane = jnp.concatenate(columns, axis=1)
+
+    def term(s):
+        block = attn_plane[s * tokens : (s + 1) * tokens]
+        return jnp.dot(block, weight, preferred_element_type=F32)
+
+    moving = term(1).astype(BF16)
+    for s in range(2, PLANES + 1):
+        moving = lax.ppermute(moving, "row", row_shift(1)).astype(F32) + term(s % PLANES)
+        moving = moving.astype(BF16)
+    mixed = moving
+
+    d_part = nt(grads_own, weight).astype(BF16)
+
+    def grad_piece(d):
+        y, x = divmod(d, 2)
+        b = head(d_part, 3 * y + 2).reshape(PLANES, 2, half, HD)[:, x]
+        return jnp.concatenate([head(d_part, 3 * y + x), b.reshape(PLANES * half, HD)])
+
+    d_terms = spread(jnp.stack([grad_piece(d) for d in range(COLS)]))
+    d_attn = sum(t.astype(F32) for t in d_terms).astype(BF16)
+
+    width = out_weight.shape[0]
+    attn_own = lax.dynamic_slice_in_dim(attn_plane, core * width, width, 1)
+    attn_sent = lax.dynamic_slice_in_dim(attn_plane, (1 - core) * width, width, 1)
+    attn_other = lax.ppermute(attn_sent, "row", SWAP)
+    weight_grad = (tn(attn_own, grads_own) + tn(attn_other, grads_other)).astype(BF16)
+
+    dq, dk, dv = attention_backward(q, k, v, probs, attn, d_attn)
+    dkv = jnp.concatenate([dk, dv])
+    own = PLANES * tokens
+    dkv = dkv[:, :own] + lax.ppermute(dkv[:, own:].astype(BF16), "row", SWAP).astype(F32)
+    dkv = dkv.astype(BF16).reshape(4, PLANES, tokens, HD)
+    dq_a = dq[:own].reshape(PLANES, tokens, HD)
+    dq_b = dq[own:].reshape(PLANES, half, HD)
+    home = [jnp.concatenate([dq_a[s], dq_b[s]] + [dkv[i, s] for i in range(4)]) for s in range(PLANES)]
+    home = jnp.stack(
+        home[:1] + [lax.ppermute(home[s], "row", row_shift(-s)) for s in range(1, PLANES)]
+    )
+    back = [pick(home, (col - plane) % PLANES)] + [
+        lax.ppermute(pick(home, ((col ^ j) - plane) % PLANES), "col", col_xor(j))
+        for j in range(1, COLS)
+    ]
+    back = jnp.stack(back)
+    back = [pick(back, col ^ d) for d in range(COLS)]
+    outs = [[], [], []]
+    for y in range(2):
+        left, right = back[2 * y], back[2 * y + 1]
+        outs[0] += [
+            left[:tokens],
+            right[:tokens],
+            jnp.concatenate([left[tokens : tokens + half], right[tokens : tokens + half]]),
+        ]
+        for i in range(2):
+            at = tokens + half + 2 * i * tokens
+            b = left[at + tokens : at + 2 * tokens].astype(F32) + right[at + tokens : at + 2 * tokens].astype(F32)
+            outs[1 + i] += [left[at : at + tokens], right[at : at + tokens], b.astype(BF16)]
+    query_g, key_g, value_g = [jnp.concatenate(o, axis=1) for o in outs]
+    return (mixed, query_g, key_g, value_g, weight_grad)
+
+
 def solution(mesh):
-    in_specs = (P("row", "col"), P("row", "col"), P("row", "col"), P("row", "col"), P("row", "col"))
-    out_specs = (
-        P("row", "col"),
-        P("row", "col"),
-        P("row", "col"),
-        P("row", "col"),
-        P("row", "col"),
-    )
-    return jax.shard_map(
-        per_device, mesh=mesh, in_specs=in_specs, out_specs=out_specs, check_vma=False
-    )
+    spec = P("row", "col")
+    fast = mesh.shape["row"] == PLANES * CORES and mesh.shape["col"] == COLS
+
+    def run(queries, keys_tile, values_tile, out_weight, out_grad):
+        heads = queries.shape[1] // HD
+        fits = fast and heads == 6 * COLS and queries.shape[0] % (32 * mesh.shape["row"]) == 0
+        return jax.shard_map(
+            per_device_fast if fits else per_device,
+            mesh=mesh,
+            in_specs=(spec,) * 5,
+            out_specs=(spec,) * 5,
+            check_vma=False,
+        )(queries, keys_tile, values_tile, out_weight, out_grad)
+
+    return run

time: 470 us -> 202 us (0.43)
  waiting for transfers between devices: 361 us -> 131 us
  matrix products: 78.5 us -> 12.6 us
  starting transfers between devices: 0.32 us -> 34.3 us
  between operations: 14.3 us -> 1.3 us
  Pallas kernels: 0 us -> 10.9 us
  other arithmetic: 7.01 us -> 1.63 us
    reduce_scatter x4 -> x0, waiting for transfers between devices: 211 us -> none  [the longest x1 99 us: per_device(): lax.psum_scatter(jnp.einsum('rf,rc->fc', attn_row, out_grad, preferred_el...]
    all_gather x4 -> x0, waiting for transfers between devices: 148 us -> none  [the longest x1 91.4 us: per_device(): weight_col = lax.all_gather(out_weight, 'row', axis=0, tiled=True)]
    ppermute x0 -> x32, waiting for transfers between devices: none -> 131 us  [the longest x3 36.4 us: per_device_fast(): grads.append(lax.ppermute(grads[-1], 'row', row_shift(1)))]
    dot_general x45 -> x7, matrix products: 78.5 us -> 12.6 us  [the longest x4 6.11 us: term(): return jnp.dot(block, weight, preferred_element_type=F32)]
    ppermute x0 -> x32, starting transfers between devices: none -> 34.3 us  [the longest x6 8.16 us: spread(): lax.ppermute(pick(pieces, col ^ j), 'col', col_xor(j))]
    pallas_call x0 -> x2, Pallas kernels: none -> 10.9 us  [the longest x1 6.11 us: attention_backward(): pl.pallas_call(backward_kernel, grid=(3,), in_specs=[by_query, by_head, b...]
    unnamed x8 -> x43, local copies, waits for them, and re-layouts: 1.26 us -> 8 us
  transfers between devices with their start and end apart: 8 -> 32, of which waited for: 7 -> 18; matrix products, arithmetic and copies ran while one was open for 20% -> 8% of each run, Pallas kernels for 0% -> 5%
where the time goes in v1:
time: 202 us; the launch traced here: 201 us
  waiting for transfers between devices  131 us (65%)
  starting transfers between devices  34.3 us (17%)
  matrix products  12.6 us (6%)
  Pallas kernels  10.9 us (5%)
  local copies, waits for them, and re-layouts  9.12 us (5%)
    ppermute x3, waiting for transfers between devices, per_device_fast(): grads.append(lax.ppermute(grads[-1], 'row', row_shift(1)))  36.4 us
    ppermute x3, waiting for transfers between devices, per_device_fast(): lax.ppermute(home[s], 'row', row_shift(-s))  25.8 us
    ppermute x6, waiting for transfers between devices, spread(): lax.ppermute(pick(pieces, col ^ j), 'col', col_xor(j))  22.2 us
    ppermute x3, waiting for transfers between devices, per_device_fast(): lax.ppermute(pick(over_col, col ^ (plane + s) % PLANES), 'row', row_shift...  22.1 us
    ppermute x3, waiting for transfers between devices, per_device_fast(): lax.ppermute(moving, 'row', row_shift(1)).astype(F32) + term(s % PLANES)  16.9 us
    ppermute x6, starting transfers between devices, spread(): lax.ppermute(pick(pieces, col ^ j), 'col', col_xor(j))  8.16 us
    unnamed x43, local copies, waits for them, and re-layouts  8 us
    ppermute x3, starting transfers between devices, per_device_fast(): lax.ppermute(moving, 'row', row_shift(1)).astype(F32) + term(s % PLANES)  6.6 us
  transfers between devices with their start and end apart: 32, of which 18 were waited for; matrix products, arithmetic and copies ran while one was open for 8% of the time, Pallas kernels for 5%

profile of v1, /device:TPU:0, one launch (start us, length us, event | category | flops | bytes accessed | tf_op | source)
XLA Modules:
  0.0 201.0 jit_solution(1998882843891957785)
XLA Ops:
  5.4 4.0 %collective-permute-start.2 = (bf16[1056,128]{1,0:T(8,128)(2,1)S(1)}, bf16[1056,128]{1,0:T(8,128)(2,1)S(1)}, u32[]{:S(2)}, u32[]{:S(2)}) collective-permute-start(bf16[1056,128]{1,0:T(8,128)(2,1)S(1)} %get-tuple-element.59), channel_id=1, source_target_pairs={{0,3},{1,2},{2,1},{3,0},{4,7},{5,6},{6,5},{7,4},{8,11},{9,10},{10,... | collective-permute-start | bytes 811016 | tf_op jit(solution)/shard_map/ppermute | solution.py:232
  10.0 6.7 %collective-permute-done.2 = bf16[1056,128]{1,0:T(8,128)(2,1)S(1)} collective-permute-done((bf16[1056,128]{1,0:T(8,128)(2,1)S(1)}, bf16[1056,128]{1,0:T(8,128)(2,1)S(1)}, u32[]{:S(2)}, u32[]{:S(2)}) %collective-permute-start.2) | collective-permute-done | bytes 270368 | tf_op jit(solution)/shard_map/ppermute | solution.py:232
  16.7 4.9 %collective-permute-done.1 = bf16[1056,128]{1,0:T(8,128)(2,1)S(1)} collective-permute-done((bf16[1056,128]{1,0:T(8,128)(2,1)S(1)}, bf16[1056,128]{1,0:T(8,128)(2,1)S(1)}, u32[]{:S(2)}, u32[]{:S(2)}) %collective-permute-start.1) | collective-permute-done | bytes 270368 | tf_op jit(solution)/shard_map/ppermute | solution.py:232
  22.2 3.7 %collective-permute-start.5 = (bf16[1056,128]{1,0:T(8,128)(2,1)S(1)}, bf16[1056,128]{1,0:T(8,128)(2,1)S(1)}, u32[]{:S(2)}, u32[]{:S(2)}) collective-permute-start(bf16[1056,128]{1,0:T(8,128)(2,1)S(1)} %get-tuple-element.55), channel_id=1, source_target_pairs={{0,24},{4,28},{8,0},{12,4},{16,8},{20,12},{24,16},{28,20},{1,25},{... | collective-permute-start | bytes 811016 | tf_op jit(solution)/shard_map/ppermute | solution.py:253
  26.9 5.9 %collective-permute-done.5 = bf16[1056,128]{1,0:T(8,128)(2,1)S(1)} collective-permute-done((bf16[1056,128]{1,0:T(8,128)(2,1)S(1)}, bf16[1056,128]{1,0:T(8,128)(2,1)S(1)}, u32[]{:S(2)}, u32[]{:S(2)}) %collective-permute-start.5) | collective-permute-done | bytes 270368 | tf_op jit(solution)/shard_map/ppermute | solution.py:253
  32.8 16.2 %collective-permute-done.4 = bf16[1056,128]{1,0:T(8,128)(2,1)S(1)} collective-permute-done((bf16[1056,128]{1,0:T(8,128)(2,1)S(1)}, bf16[1056,128]{1,0:T(8,128)(2,1)S(1)}, u32[]{:S(2)}, u32[]{:S(2)}) %collective-permute-start.4) | collective-permute-done | bytes 270368 | tf_op jit(solution)/shard_map/ppermute | solution.py:253
  51.8 15.0 %collective-permute-done.14 = bf16[192,1536]{1,0:T(8,128)(2,1)} collective-permute-done((bf16[192,1536]{1,0:T(8,128)(2,1)S(1)}, bf16[192,1536]{1,0:T(8,128)(2,1)}, u32[]{:S(2)}, u32[]{:S(2)}) %collective-permute-start.14) | collective-permute-done | bytes 589856 | tf_op jit(solution)/shard_map/ppermute | solution.py:259
  66.9 4.8 %attention_forward.1 = (bf16[3,1536,384]{2,1,0:T(8,128)(2,1)S(1)}, bf16[1152,128]{1,0:T(8,128)(2,1)S(1)}) custom-call(bf16[1152,128]{1,0:T(8,128)(2,1)S(1)} %pad_maximum_fusion.10.q_ref, bf16[2,1536,128]{2,1,0:T(8,128)(2,1)S(1)} %get-tuple-element.16.k_ref, bf16[2,1536,128]{2,1,0:T(8,128)(2,1)S(1)} %get-tuple-element.15.v_ref), custom_call_target="tpu_custom_call" | custom-call | flops 905969664 | bytes 3538944 | tf_op jit(solution)/shard_map/attention_forward/pallas_call | solution.py:141
  72.8 2.0 collective-permute-start.8
  75.3 1.1 constant_dynamic-update-slice_fusion.28
  76.4 6.3 %collective-permute-done.15 = bf16[192,1536]{1,0:T(8,128)(2,1)S(1)} collective-permute-done((bf16[192,1536]{1,0:T(8,128)(2,1)}, bf16[192,1536]{1,0:T(8,128)(2,1)S(1)}, u32[]{:S(2)}, u32[]{:S(2)}) %collective-permute-start.15) | collective-permute-done | bytes 589856 | tf_op jit(solution)/shard_map/ppermute | solution.py:259
  83.4 3.3 %collective-permute-done.8 = bf16[1152,128]{1,0:T(8,128)(2,1)S(1)} collective-permute-done((bf16[1152,128]{1,0:T(8,128)(2,1)S(1)}, bf16[1152,128]{1,0:T(8,128)(2,1)S(1)}, u32[]{:S(2)}, u32[]{:S(2)}) %collective-permute-start.8) | collective-permute-done | bytes 294944 | tf_op jit(solution)/shard_map/ppermute | solution.py:281
  86.7 1.3 collective-permute-start.16
  88.6 15.1 %collective-permute-done.16 = bf16[192,1536]{1,0:T(8,128)(2,1)S(1)} collective-permute-done((bf16[192,1536]{1,0:T(8,128)(2,1)S(1)}, bf16[192,1536]{1,0:T(8,128)(2,1)S(1)}, u32[]{:S(2)}, u32[]{:S(2)}) %collective-permute-start.16) | collective-permute-done | bytes 589856 | tf_op jit(solution)/shard_map/ppermute | solution.py:259
  103.8 2.0 %convolution_convert_fusion.1 = bf16[768,768]{1,0:T(8,128)(2,1)S(1)} fusion(bf16[768,1536]{1,0:T(8,128)(2,1)S(1)} %constant_dynamic-update-slice_fusion.26, bf16[384,1536]{1,0:T(8,128)(2,1)S(1)} %collective-permute-done.10, bf16[384,1536]{1,0:T(8,128)(2,1)S(1)} %copy-done.7, pred[]{:T(512)S(6)} %eq.12), kind=kOutput, calls=%fused_computation.17 | convolution fusion | flops 1823145984 | bytes 5898241 | tf_op jit(solution)/shard_map/dot_general | solution.py:122
  107.5 2.0 collective-permute-start.18
  110.0 1.6 convolution_convert_fusion
  111.6 5.7 %collective-permute-done.19 = bf16[1152,128]{1,0:T(8,128)(2,1)S(1)} collective-permute-done((bf16[1152,128]{1,0:T(8,128)(2,1)S(1)}, bf16[1152,128]{1,0:T(8,128)(2,1)S(1)}, u32[]{:S(2)}, u32[]{:S(2)}) %collective-permute-start.19) | collective-permute-done | bytes 294944 | tf_op jit(solution)/shard_map/ppermute | solution.py:232
  117.3 4.4 %collective-permute-done.18 = bf16[1152,128]{1,0:T(8,128)(2,1)S(1)} collective-permute-done((bf16[1152,128]{1,0:T(8,128)(2,1)S(1)}, bf16[1152,128]{1,0:T(8,128)(2,1)S(1)}, u32[]{:S(2)}, u32[]{:S(2)}) %collective-permute-start.18) | collective-permute-done | bytes 294944 | tf_op jit(solution)/shard_map/ppermute | solution.py:232
  122.0 6.1 %attention_backward.1 = (bf16[1152,128]{1,0:T(8,128)(2,1)S(1)}, f32[2,1536,128]{2,1,0:T(8,128)S(1)}, f32[2,1536,128]{2,1,0:T(8,128)S(1)}) custom-call(bf16[1152,128]{1,0:T(8,128)(2,1)S(1)} %pad_maximum_fusion.10.q_ref, bf16[2,1536,128]{2,1,0:T(8,128)(2,1)S(1)} %get-tuple-element.16.k_ref, bf16[2,1536,128]{2,1,0:T(8,128)(2,1)S(1)} %get-tuple-element.15.v_ref, ...), custom_call_target="tpu_custom_call" | custom-call | flops 1811939328 | bytes 3538944 | tf_op jit(solution)/shard_map/attention_backward/pallas_call | solution.py:194
  129.1 10.0 %collective-permute-done.11 = bf16[192,1536]{1,0:T(8,128)(2,1)} collective-permute-done((bf16[192,1536]{1,0:T(8,128)(2,1)}, bf16[192,1536]{1,0:T(8,128)(2,1)}, u32[]{:S(2)}, u32[]{:S(2)}) %collective-permute-start.11) | collective-permute-done | bytes 589856 | tf_op jit(solution)/shard_map/ppermute | solution.py:296
  139.1 1.9 add_convert_fusion.2
  141.4 2.3 %fusion.1 = f32[384,1536]{1,0:T(8,128)S(1)} fusion(bf16[768,384]{1,0:T(8,128)(2,1)} %collective-permute-done.27, bf16[192,1536]{1,0:T(8,128)(2,1)S(1)} %collective-permute-done.31, bf16[192,1536]{1,0:T(8,128)(2,1)S(1)} %collective-permute-done.30, bf16[192,1536]{1,0:T(8,128)(2,1)S(1)} %collective-permute-done.29, bf16[192,1536]{1,0:T(8,128)(2,1)} %collective-permute-done.28), kind=kOutput, calls=%fused_computation.4 | convolution fusion | flops 915406848 | bytes 5308416 | tf_op jit(solution)/shard_map/dot_general | solution.py:126
  144.1 4.3 %collective-permute-start.22 = (bf16[1056,128]{1,0:T(8,128)(2,1)S(1)}, bf16[1056,128]{1,0:T(8,128)(2,1)S(1)}, u32[]{:S(2)}, u32[]{:S(2)}) collective-permute-start(bf16[1056,128]{1,0:T(8,128)(2,1)S(1)} %get-tuple-element.64), channel_id=1, source_target_pairs={{0,16},{4,20},{8,24},{12,28},{16,0},{20,4},{24,8},{28,12},{1,17},{... | collective-permute-start | bytes 811016 | tf_op jit(solution)/shard_map/ppermute | solution.py:325
  148.5 2.1 %fusion = bf16[384,1536]{1,0:T(8,128)(2,1)} fusion(f32[384,1536]{1,0:T(8,128)S(1)} %fusion.1, bf16[768,1536]{1,0:T(8,128)(2,1)S(1)} %constant_dynamic-update-slice_fusion.26, bf16[768,768]{1,0:T(8,128)(2,1)S(1)} %constant_dynamic-update-slice_fusion.24, s32[]{:T(128)S(6)} %select_n.126), kind=kOutput, calls=%fused_computation.1 | convolution fusion | flops 907149312 | bytes 6488068 | tf_op jit(solution)/shard_map/dot_general | solution.py:126
  150.6 14.6 %collective-permute-done.23 = bf16[1056,128]{1,0:T(8,128)(2,1)S(1)} collective-permute-done((bf16[1056,128]{1,0:T(8,128)(2,1)S(1)}, bf16[1056,128]{1,0:T(8,128)(2,1)S(1)}, u32[]{:S(2)}, u32[]{:S(2)}) %collective-permute-start.23) | collective-permute-done | bytes 270368 | tf_op jit(solution)/shard_map/ppermute | solution.py:325
  165.2 11.2 %collective-permute-done.22 = bf16[1056,128]{1,0:T(8,128)(2,1)S(1)} collective-permute-done((bf16[1056,128]{1,0:T(8,128)(2,1)S(1)}, bf16[1056,128]{1,0:T(8,128)(2,1)S(1)}, u32[]{:S(2)}, u32[]{:S(2)}) %collective-permute-start.22) | collective-permute-done | bytes 270368 | tf_op jit(solution)/shard_map/ppermute | solution.py:325
  177.6 2.0 collective-permute-start.25
  181.0 6.4 %collective-permute-start.13 = (bf16[192,1536]{1,0:T(8,128)(2,1)S(1)}, bf16[192,1536]{1,0:T(8,128)(2,1)S(1)}, u32[]{:S(2)}, u32[]{:S(2)}) collective-permute-start(bf16[192,1536]{1,0:T(8,128)(2,1)S(1)} %add_convert_fusion.1), channel_id=1, source_target_pairs={{0,8},{4,12},{8,16},{12,20},{16,24},{20,28},{24,0},{28,4},{1,9},{5... | collective-permute-start | bytes 1769480 | tf_op jit(solution)/shard_map/ppermute | solution.py:296
  187.4 4.3 %collective-permute-done.25 = bf16[1056,128]{1,0:T(8,128)(2,1)S(1)} collective-permute-done((bf16[1056,128]{1,0:T(8,128)(2,1)S(1)}, bf16[1056,128]{1,0:T(8,128)(2,1)S(1)}, u32[]{:S(2)}, u32[]{:S(2)}) %collective-permute-start.25) | collective-permute-done | bytes 270368 | tf_op jit(solution)/shard_map/ppermute | solution.py:328
  192.4 6.9 %collective-permute-done.13 = bf16[192,1536]{1,0:T(8,128)(2,1)S(1)} collective-permute-done((bf16[192,1536]{1,0:T(8,128)(2,1)S(1)}, bf16[192,1536]{1,0:T(8,128)(2,1)S(1)}, u32[]{:S(2)}, u32[]{:S(2)}) %collective-permute-start.13) | collective-permute-done | bytes 589856 | tf_op jit(solution)/shard_map/ppermute | solution.py:296
  199.3 1.7 add_convert_fusion
  (123 shorter events, 19.9 us)
Async XLA Ops:
  5.4 11.3 %collective-permute-start.2 = (bf16[1056,128]{1,0:T(8,128)(2,1)S(1)}, bf16[1056,128]{1,0:T(8,128)(2,1)S(1)}, u32[]{:S(2)}, u32[]{:S(2)}) collective-permute-start(bf16[1056,128]{1,0:T(8,128)(2,1)S(1)} %get-tuple-element.59), channel_id=1, source_target_pairs={{0,3},{1,2},{2,1},{3,0},{4,7},{5,6},{6,5},{7,4},{8,11},{9,10},{10,... | collective-permute-start | bytes 811016 | tf_op jit(solution)/shard_map/ppermute | solution.py:232
  9.4 12.3 %collective-permute-start.1 = (bf16[1056,128]{1,0:T(8,128)(2,1)S(1)}, bf16[1056,128]{1,0:T(8,128)(2,1)S(1)}, u32[]{:S(2)}, u32[]{:S(2)}) collective-permute-start(bf16[1056,128]{1,0:T(8,128)(2,1)S(1)} %get-tuple-element.60), channel_id=1, source_target_pairs={{0,2},{1,3},{2,0},{3,1},{4,6},{5,7},{6,4},{7,5},{8,10},{9,11},{10,... | collective-permute-start | bytes 811016 | tf_op jit(solution)/shard_map/ppermute | solution.py:232
  9.9 12.1 %collective-permute-start = (bf16[1056,128]{1,0:T(8,128)(2,1)S(1)}, bf16[1056,128]{1,0:T(8,128)(2,1)S(1)}, u32[]{:S(2)}, u32[]{:S(2)}) collective-permute-start(bf16[1056,128]{1,0:T(8,128)(2,1)S(1)} %get-tuple-element.61), channel_id=1, source_target_pairs={{0,1},{1,0},{2,3},{3,2},{4,5},{5,4},{6,7},{7,6},{8,9},{9,8},{10,11... | collective-permute-start | bytes 811016 | tf_op jit(solution)/shard_map/ppermute | solution.py:232
  22.2 10.6 %collective-permute-start.5 = (bf16[1056,128]{1,0:T(8,128)(2,1)S(1)}, bf16[1056,128]{1,0:T(8,128)(2,1)S(1)}, u32[]{:S(2)}, u32[]{:S(2)}) collective-permute-start(bf16[1056,128]{1,0:T(8,128)(2,1)S(1)} %get-tuple-element.55), channel_id=1, source_target_pairs={{0,24},{4,28},{8,0},{12,4},{16,8},{20,12},{24,16},{28,20},{1,25},{... | collective-permute-start | bytes 811016 | tf_op jit(solution)/shard_map/ppermute | solution.py:253
  25.8 23.1 %collective-permute-start.4 = (bf16[1056,128]{1,0:T(8,128)(2,1)S(1)}, bf16[1056,128]{1,0:T(8,128)(2,1)S(1)}, u32[]{:S(2)}, u32[]{:S(2)}) collective-permute-start(bf16[1056,128]{1,0:T(8,128)(2,1)S(1)} %get-tuple-element.56), channel_id=1, source_target_pairs={{0,16},{4,20},{8,24},{12,28},{16,0},{20,4},{24,8},{28,12},{1,17},{... | collective-permute-start | bytes 811016 | tf_op jit(solution)/shard_map/ppermute | solution.py:253
  25.8 23.1 %collective-permute-start.3 = (bf16[1056,128]{1,0:T(8,128)(2,1)S(1)}, bf16[1056,128]{1,0:T(8,128)(2,1)S(1)}, u32[]{:S(2)}, u32[]{:S(2)}) collective-permute-start(bf16[1056,128]{1,0:T(8,128)(2,1)S(1)} %get-tuple-element.57), channel_id=1, source_target_pairs={{0,8},{4,12},{8,16},{12,20},{16,24},{20,28},{24,0},{28,4},{1,9},{5... | collective-permute-start | bytes 811016 | tf_op jit(solution)/shard_map/ppermute | solution.py:253
  49.1 17.7 %collective-permute-start.6 = (bf16[4,768,128]{2,1,0:T(8,128)(2,1)S(1)}, bf16[4,768,128]{2,1,0:T(8,128)(2,1)S(1)}, u32[]{:S(2)}, u32[]{:S(2)}) collective-permute-start(bf16[4,768,128]{2,1,0:T(8,128)(2,1)S(1)} %bitcast.240), channel_id=1, source_target_pairs={{0,4},{4,0},{8,12},{12,8},{16,20},{20,16},{24,28},{28,24},{1,5},{5... | collective-permute-start | bytes 2359304 | tf_op jit(solution)/shard_map/ppermute | solution.py:277
  50.0 16.8 %collective-permute-start.14 = (bf16[192,1536]{1,0:T(8,128)(2,1)S(1)}, bf16[192,1536]{1,0:T(8,128)(2,1)}, u32[]{:S(2)}, u32[]{:S(2)}) collective-permute-start(bf16[192,1536]{1,0:T(8,128)(2,1)S(1)} %copy-done.1), channel_id=1, source_target_pairs={{0,8},{4,12},{8,16},{12,20},{16,24},{20,28},{24,0},{28,4},{1,9},{5... | collective-permute-start | bytes 1769480 | tf_op jit(solution)/shard_map/ppermute | solution.py:259
  50.9 77.6 %collective-permute-start.28 = (bf16[192,1536]{1,0:T(8,128)(2,1)S(1)}, bf16[192,1536]{1,0:T(8,128)(2,1)}, u32[]{:S(2)}, u32[]{:S(2)}) collective-permute-start(bf16[192,1536]{1,0:T(8,128)(2,1)S(1)} %copy-done.1), channel_id=1, source_target_pairs={{0,4},{4,0},{8,12},{12,8},{16,20},{20,16},{24,28},{28,24},{1,5},{5... | collective-permute-start | bytes 1769480 | tf_op jit(solution)/shard_map/ppermute | solution.py:261
  66.8 16.0 %collective-permute-start.15 = (bf16[192,1536]{1,0:T(8,128)(2,1)}, bf16[192,1536]{1,0:T(8,128)(2,1)S(1)}, u32[]{:S(2)}, u32[]{:S(2)}) collective-permute-start(bf16[192,1536]{1,0:T(8,128)(2,1)} %collective-permute-done.14), channel_id=1, source_target_pairs={{0,8},{4,12},{8,16},{12,20},{16,24},{20,28},{24,0},{28,4},{1,9},{5... | collective-permute-start | bytes 1769480 | tf_op jit(solution)/shard_map/ppermute | solution.py:259
  71.7 11.1 %collective-permute-start.9 = (bf16[1152,128]{1,0:T(8,128)(2,1)S(1)}, bf16[1152,128]{1,0:T(8,128)(2,1)S(1)}, u32[]{:S(2)}, u32[]{:S(2)}) collective-permute-start(bf16[1152,128]{1,0:T(8,128)(2,1)S(1)} %get-tuple-element.10.attn_ref), channel_id=1, source_target_pairs={{0,3},{1,2},{2,1},{3,0},{4,7},{5,6},{6,5},{7,4},{8,11},{9,10},{10,... | collective-permute-start | bytes 884744 | tf_op jit(solution)/shard_map/ppermute | solution.py:281
  72.8 13.9 %collective-permute-start.8 = (bf16[1152,128]{1,0:T(8,128)(2,1)S(1)}, bf16[1152,128]{1,0:T(8,128)(2,1)S(1)}, u32[]{:S(2)}, u32[]{:S(2)}) collective-permute-start(bf16[1152,128]{1,0:T(8,128)(2,1)S(1)} %get-tuple-element.10.attn_ref), channel_id=1, source_target_pairs={{0,2},{1,3},{2,0},{3,1},{4,6},{5,7},{6,4},{7,5},{8,10},{9,11},{10,... | collective-permute-start | bytes 884744 | tf_op jit(solution)/shard_map/ppermute | solution.py:281
  74.8 13.2 %collective-permute-start.7 = (bf16[1152,128]{1,0:T(8,128)(2,1)S(1)}, bf16[1152,128]{1,0:T(8,128)(2,1)S(1)}, u32[]{:S(2)}, u32[]{:S(2)}) collective-permute-start(bf16[1152,128]{1,0:T(8,128)(2,1)S(1)} %get-tuple-element.10.attn_ref), channel_id=1, source_target_pairs={{0,1},{1,0},{2,3},{3,2},{4,5},{5,4},{6,7},{7,6},{8,9},{9,8},{10,11... | collective-permute-start | bytes 884744 | tf_op jit(solution)/shard_map/ppermute | solution.py:281
  82.7 21.0 %collective-permute-start.10 = (bf16[384,1536]{1,0:T(8,128)(2,1)S(1)}, bf16[384,1536]{1,0:T(8,128)(2,1)S(1)}, u32[]{:S(2)}, u32[]{:S(2)}) collective-permute-start(bf16[384,1536]{1,0:T(8,128)(2,1)S(1)} %copy-done.7), channel_id=1, source_target_pairs={{0,4},{4,0},{8,12},{12,8},{16,20},{20,16},{24,28},{28,24},{1,5},{5... | collective-permute-start | bytes 3538952 | tf_op jit(solution)/shard_map/ppermute | solution.py:262
  82.8 58.3 %collective-permute-start.29 = (bf16[192,1536]{1,0:T(8,128)(2,1)}, bf16[192,1536]{1,0:T(8,128)(2,1)S(1)}, u32[]{:S(2)}, u32[]{:S(2)}) collective-permute-start(bf16[192,1536]{1,0:T(8,128)(2,1)} %collective-permute-done.14), channel_id=1, source_target_pairs={{0,4},{4,0},{8,12},{12,8},{16,20},{20,16},{24,28},{28,24},{1,5},{5... | collective-permute-start | bytes 1769480 | tf_op jit(solution)/shard_map/ppermute | solution.py:261
  86.7 17.0 %collective-permute-start.16 = (bf16[192,1536]{1,0:T(8,128)(2,1)S(1)}, bf16[192,1536]{1,0:T(8,128)(2,1)S(1)}, u32[]{:S(2)}, u32[]{:S(2)}) collective-permute-start(bf16[192,1536]{1,0:T(8,128)(2,1)S(1)} %collective-permute-done.15), channel_id=1, source_target_pairs={{0,8},{4,12},{8,16},{12,20},{16,24},{20,28},{24,0},{28,4},{1,9},{5... | collective-permute-start | bytes 1769480 | tf_op jit(solution)/shard_map/ppermute | solution.py:259
  106.4 10.9 %collective-permute-start.19 = (bf16[1152,128]{1,0:T(8,128)(2,1)S(1)}, bf16[1152,128]{1,0:T(8,128)(2,1)S(1)}, u32[]{:S(2)}, u32[]{:S(2)}) collective-permute-start(bf16[1152,128]{1,0:T(8,128)(2,1)S(1)} %get-tuple-element.18), channel_id=1, source_target_pairs={{0,3},{1,2},{2,1},{3,0},{4,7},{5,6},{6,5},{7,4},{8,11},{9,10},{10,... | collective-permute-start | bytes 884744 | tf_op jit(solution)/shard_map/ppermute | solution.py:232
  107.5 14.3 %collective-permute-start.18 = (bf16[1152,128]{1,0:T(8,128)(2,1)S(1)}, bf16[1152,128]{1,0:T(8,128)(2,1)S(1)}, u32[]{:S(2)}, u32[]{:S(2)}) collective-permute-start(bf16[1152,128]{1,0:T(8,128)(2,1)S(1)} %get-tuple-element.19), channel_id=1, source_target_pairs={{0,2},{1,3},{2,0},{3,1},{4,6},{5,7},{6,4},{7,5},{8,10},{9,11},{10,... | collective-permute-start | bytes 884744 | tf_op jit(solution)/shard_map/ppermute | solution.py:232
  109.4 12.4 %collective-permute-start.17 = (bf16[1152,128]{1,0:T(8,128)(2,1)S(1)}, bf16[1152,128]{1,0:T(8,128)(2,1)S(1)}, u32[]{:S(2)}, u32[]{:S(2)}) collective-permute-start(bf16[1152,128]{1,0:T(8,128)(2,1)S(1)} %get-tuple-element.17), channel_id=1, source_target_pairs={{0,1},{1,0},{2,3},{3,2},{4,5},{5,4},{6,7},{7,6},{8,9},{9,8},{10,11... | collective-permute-start | bytes 884744 | tf_op jit(solution)/shard_map/ppermute | solution.py:232
  117.3 24.0 %collective-permute-start.30 = (bf16[192,1536]{1,0:T(8,128)(2,1)S(1)}, bf16[192,1536]{1,0:T(8,128)(2,1)S(1)}, u32[]{:S(2)}, u32[]{:S(2)}) collective-permute-start(bf16[192,1536]{1,0:T(8,128)(2,1)S(1)} %collective-permute-done.15), channel_id=1, source_target_pairs={{0,4},{4,0},{8,12},{12,8},{16,20},{20,16},{24,28},{28,24},{1,5},{5... | collective-permute-start | bytes 1769480 | tf_op jit(solution)/shard_map/ppermute | solution.py:261
  121.8 17.4 %collective-permute-start.11 = (bf16[192,1536]{1,0:T(8,128)(2,1)}, bf16[192,1536]{1,0:T(8,128)(2,1)}, u32[]{:S(2)}, u32[]{:S(2)}) collective-permute-start(bf16[192,1536]{1,0:T(8,128)(2,1)} %convolution_convert_fusion), channel_id=1, source_target_pairs={{0,8},{4,12},{8,16},{12,20},{16,24},{20,28},{24,0},{28,4},{1,9},{5... | collective-permute-start | bytes 1769480 | tf_op jit(solution)/shard_map/ppermute | solution.py:296
  121.9 19.5 %collective-permute-start.27 = (bf16[768,384]{1,0:T(8,128)(2,1)S(1)}, bf16[768,384]{1,0:T(8,128)(2,1)}, u32[]{:S(2)}, u32[]{:S(2)}) collective-permute-start(bf16[768,384]{1,0:T(8,128)(2,1)S(1)} %constant_dynamic-slice_fusion), channel_id=1, source_target_pairs={{0,4},{4,0},{8,12},{12,8},{16,20},{20,16},{24,28},{28,24},{1,5},{5... | collective-permute-start | bytes 1769480 | tf_op jit(solution)/shard_map/ppermute | solution.py:313
  128.5 12.8 %collective-permute-start.31 = (bf16[192,1536]{1,0:T(8,128)(2,1)S(1)}, bf16[192,1536]{1,0:T(8,128)(2,1)S(1)}, u32[]{:S(2)}, u32[]{:S(2)}) collective-permute-start(bf16[192,1536]{1,0:T(8,128)(2,1)S(1)} %collective-permute-done.16), channel_id=1, source_target_pairs={{0,4},{4,0},{8,12},{12,8},{16,20},{20,16},{24,28},{28,24},{1,5},{5... | collective-permute-start | bytes 1769480 | tf_op jit(solution)/shard_map/ppermute | solution.py:261
  139.1 4.6 %collective-permute-start.20 = (bf16[4,768,128]{2,1,0:T(8,128)(2,1)S(1)}, bf16[4,768,128]{2,1,0:T(8,128)(2,1)S(1)}, u32[]{:S(2)}, u32[]{:S(2)}) collective-permute-start(bf16[4,768,128]{2,1,0:T(8,128)(2,1)S(1)} %slice.651), channel_id=1, source_target_pairs={{0,4},{4,0},{8,12},{12,8},{16,20},{20,16},{24,28},{28,24},{1,5},{5... | collective-permute-start | bytes 2359304 | tf_op jit(solution)/shard_map/ppermute | solution.py:319
  141.1 39.1 %collective-permute-start.12 = (bf16[192,1536]{1,0:T(8,128)(2,1)S(1)}, bf16[192,1536]{1,0:T(8,128)(2,1)S(1)}, u32[]{:S(2)}, u32[]{:S(2)}) collective-permute-start(bf16[192,1536]{1,0:T(8,128)(2,1)S(1)} %add_convert_fusion.2), channel_id=1, source_target_pairs={{0,8},{4,12},{8,16},{12,20},{16,24},{20,28},{24,0},{28,4},{1,9},{5... | collective-permute-start | bytes 1769480 | tf_op jit(solution)/shard_map/ppermute | solution.py:296
  144.0 21.1 %collective-permute-start.23 = (bf16[1056,128]{1,0:T(8,128)(2,1)S(1)}, bf16[1056,128]{1,0:T(8,128)(2,1)S(1)}, u32[]{:S(2)}, u32[]{:S(2)}) collective-permute-start(bf16[1056,128]{1,0:T(8,128)(2,1)S(1)} %get-tuple-element.63), channel_id=1, source_target_pairs={{0,8},{4,12},{8,16},{12,20},{16,24},{20,28},{24,0},{28,4},{1,9},{5... | collective-permute-start | bytes 811016 | tf_op jit(solution)/shard_map/ppermute | solution.py:325
  144.1 32.2 %collective-permute-start.22 = (bf16[1056,128]{1,0:T(8,128)(2,1)S(1)}, bf16[1056,128]{1,0:T(8,128)(2,1)S(1)}, u32[]{:S(2)}, u32[]{:S(2)}) collective-permute-start(bf16[1056,128]{1,0:T(8,128)(2,1)S(1)} %get-tuple-element.64), channel_id=1, source_target_pairs={{0,16},{4,20},{8,24},{12,28},{16,0},{20,4},{24,8},{28,12},{1,17},{... | collective-permute-start | bytes 811016 | tf_op jit(solution)/shard_map/ppermute | solution.py:325
  148.5 27.9 %collective-permute-start.21 = (bf16[1056,128]{1,0:T(8,128)(2,1)S(1)}, bf16[1056,128]{1,0:T(8,128)(2,1)S(1)}, u32[]{:S(2)}, u32[]{:S(2)}) collective-permute-start(bf16[1056,128]{1,0:T(8,128)(2,1)S(1)} %get-tuple-element.65), channel_id=1, source_target_pairs={{0,24},{4,28},{8,0},{12,4},{16,8},{20,12},{24,16},{28,20},{1,25},{... | collective-permute-start | bytes 811016 | tf_op jit(solution)/shard_map/ppermute | solution.py:325
  176.6 10.8 %collective-permute-start.26 = (bf16[1056,128]{1,0:T(8,128)(2,1)S(1)}, bf16[1056,128]{1,0:T(8,128)(2,1)S(1)}, u32[]{:S(2)}, u32[]{:S(2)}) collective-permute-start(bf16[1056,128]{1,0:T(8,128)(2,1)S(1)} %get-tuple-element.51), channel_id=1, source_target_pairs={{0,3},{1,2},{2,1},{3,0},{4,7},{5,6},{6,5},{7,4},{8,11},{9,10},{10,... | collective-permute-start | bytes 811016 | tf_op jit(solution)/shard_map/ppermute | solution.py:328
  177.6 14.1 %collective-permute-start.25 = (bf16[1056,128]{1,0:T(8,128)(2,1)S(1)}, bf16[1056,128]{1,0:T(8,128)(2,1)S(1)}, u32[]{:S(2)}, u32[]{:S(2)}) collective-permute-start(bf16[1056,128]{1,0:T(8,128)(2,1)S(1)} %get-tuple-element.52), channel_id=1, source_target_pairs={{0,2},{1,3},{2,0},{3,1},{4,6},{5,7},{6,4},{7,5},{8,10},{9,11},{10,... | collective-permute-start | bytes 811016 | tf_op jit(solution)/shard_map/ppermute | solution.py:328
  179.6 12.2 %collective-permute-start.24 = (bf16[1056,128]{1,0:T(8,128)(2,1)S(1)}, bf16[1056,128]{1,0:T(8,128)(2,1)S(1)}, u32[]{:S(2)}, u32[]{:S(2)}) collective-permute-start(bf16[1056,128]{1,0:T(8,128)(2,1)S(1)} %get-tuple-element.53), channel_id=1, source_target_pairs={{0,1},{1,0},{2,3},{3,2},{4,5},{5,4},{6,7},{7,6},{8,9},{9,8},{10,11... | collective-permute-start | bytes 811016 | tf_op jit(solution)/shard_map/ppermute | solution.py:328
  181.0 18.3 %collective-permute-start.13 = (bf16[192,1536]{1,0:T(8,128)(2,1)S(1)}, bf16[192,1536]{1,0:T(8,128)(2,1)S(1)}, u32[]{:S(2)}, u32[]{:S(2)}) collective-permute-start(bf16[192,1536]{1,0:T(8,128)(2,1)S(1)} %add_convert_fusion.1), channel_id=1, source_target_pairs={{0,8},{4,12},{8,16},{12,20},{16,24},{20,28},{24,0},{28,4},{1,9},{5... | collective-permute-start | bytes 1769480 | tf_op jit(solution)/shard_map/ppermute | solution.py:296
  (10 other events, 89.0 us)

commit v2 on v1

--- a/solution.py
+++ b/solution.py
@@ -97,6 +97,7 @@
 
 
 PLANES, CORES, COLS = 4, 2, 4
+ORDER = (0, 1, 3, 2)
 
 
 def row_shift(s):
@@ -154,17 +155,14 @@
             jax.ShapeDtypeStruct((3, keys, rows), BF16),
             jax.ShapeDtypeStruct((3 * rows, HD), BF16),
         ],
-        compiler_params=pltpu.CompilerParams(vmem_limit_bytes=40 * 2**20),
-        cost_estimate=pl.CostEstimate(
-            flops=3 * 4 * rows * keys * HD,
-            bytes_accessed=3 * rows * keys * 2,
-            transcendentals=3 * rows * keys,
-        ),
+        compiler_params=pltpu.CompilerParams(vmem_limit_bytes=16 * 2**20),
         name="attention_forward",
     )(q, k, v)
 
 
-def backward_kernel(q_ref, k_ref, v_ref, p_ref, attn_ref, grad_ref, dq_ref, dk_ref, dv_ref):
+def backward_kernel(
+    q_ref, k_ref, v_ref, p_ref, attn_ref, grad_ref, dq_ref, own_ref, other_ref, sums_ref
+):
     step = pl.program_id(0)
     grad = grad_ref[...]
     product = grad.astype(F32) * attn_ref[...].astype(F32)
@@ -176,21 +174,25 @@
     dk = jnp.dot(dscore, q_ref[...], preferred_element_type=F32)
     dv = jnp.dot(probs, grad, preferred_element_type=F32)
 
-    @pl.when(step != 1)
+    @pl.when(step == 0)
     def _():
-        dk_ref[0] = dk
-        dv_ref[0] = dv
-
-    @pl.when(step == 1)
+        sums_ref[0] = dk
+        sums_ref[1] = dv
+
+    @pl.when(step != 0)
     def _():
-        dk_ref[0] += dk
-        dv_ref[0] += dv
+        half = dk.shape[0] // 2
+        for i, new in enumerate((dk, dv)):
+            new = jnp.where(step == 1, sums_ref[i], 0.0) + new
+            own_ref[i, 0] = new[:half]
+            other_ref[i, 0] = new[half:].astype(BF16)
 
 
 def attention_backward(q, k, v, probs, attn, grad):
     rows, keys = q.shape[0] // 3, k.shape[1]
     by_query = pl.BlockSpec((rows, HD), lambda i: (i, 0))
     by_head = pl.BlockSpec((1, keys, HD), lambda i: (i // 2, 0, 0))
+    by_half = pl.BlockSpec((2, 1, keys // 2, HD), lambda i: (0, i // 2, 0, 0))
     return pl.pallas_call(
         backward_kernel,
         grid=(3,),
@@ -202,131 +204,186 @@
             by_query,
             by_query,
         ],
-        out_specs=[by_query, by_head, by_head],
+        out_specs=[by_query, by_half, by_half],
         out_shape=[
             jax.ShapeDtypeStruct(q.shape, BF16),
-            jax.ShapeDtypeStruct(k.shape, F32),
-            jax.ShapeDtypeStruct(k.shape, F32),
+            jax.ShapeDtypeStruct((2, 2, keys // 2, HD), F32),
+            jax.ShapeDtypeStruct((2, 2, keys // 2, HD), BF16),
         ],
-        compiler_params=pltpu.CompilerParams(vmem_limit_bytes=48 * 2**20),
-        cost_estimate=pl.CostEstimate(
-            flops=3 * 8 * rows * keys * HD,
-            bytes_accessed=3 * rows * keys * 2,
-            transcendentals=0,
-        ),
+        scratch_shapes=[pltpu.VMEM((2, keys, HD), F32)],
+        compiler_params=pltpu.CompilerParams(vmem_limit_bytes=20 * 2**20),
         name="attention_backward",
     )(q, k, v, probs, attn, grad)
+
+
+def pack_kernel(q_ref, k_ref, v_ref, *out_refs):
+    tokens = q_ref.shape[0]
+    half = tokens // 2
+    col = lax.axis_index("col")
+    for j, out_ref in enumerate(out_refs):
+        to = lax.bitwise_xor(col, j)
+        y, x = lax.div(to, 2), lax.rem(to, 2)
+        a = pl.ds(pl.multiple_of((3 * y + x) * HD, HD), HD)
+        b = pl.ds(pl.multiple_of((3 * y + 2) * HD, HD), HD)
+        at = tokens + half
+        out_ref[:tokens] = q_ref[:, a]
+        out_ref[tokens:at] = q_ref[pl.ds(pl.multiple_of(x * half, half), half), b]
+        for i, block in enumerate((k_ref[:, a], k_ref[:, b], v_ref[:, a], v_ref[:, b])):
+            out_ref[at + i * tokens : at + (i + 1) * tokens] = block
+
+
+def pack(queries, keys, values):
+    tokens = queries.shape[0]
+    piece = jax.ShapeDtypeStruct((tokens // 2 + 5 * tokens, HD), BF16)
+    return pl.pallas_call(
+        pack_kernel,
+        out_shape=[piece] * COLS,
+        cost_estimate=pl.CostEstimate(flops=0, bytes_accessed=6 * queries.size, transcendentals=0),
+        name="pack_inputs",
+    )(queries, keys, values)
+
+
+def after(value, *earlier):
+    return lax.optimization_barrier((value, earlier))[0]
 
 
 def per_device_fast(queries, keys_tile, values_tile, out_weight, out_grad):
     tokens = queries.shape[0]
     half = tokens // 2
+    own = PLANES * tokens
+    width = out_weight.shape[0]
     row, col = lax.axis_index("row"), lax.axis_index("col")
     plane, core = row // CORES, row % CORES
 
     def head(block, g):
         return block[:, g * HD : (g + 1) * HD]
 
-    def spread(pieces):
-        return [pick(pieces, col)] + [
-            lax.ppermute(pick(pieces, col ^ j), "col", col_xor(j)) for j in range(1, COLS)
-        ]
-
-    def input_piece(d):
-        y, x = divmod(d, 2)
-        a, b = 3 * y + x, 3 * y + 2
-        return jnp.concatenate(
-            [
-                head(queries, a),
-                head(queries, b)[x * half : (x + 1) * half],
-                head(keys_tile, a),
-                head(keys_tile, b),
-                head(values_tile, a),
-                head(values_tile, b),
-            ]
-        )
-
-    over_col = jnp.stack(spread(jnp.stack([input_piece(d) for d in range(COLS)])))
+    def to_col(block, j):
+        return lax.ppermute(block, "col", col_xor(j))
+
+    def to_plane(block, s):
+        return lax.ppermute(block, "row", row_shift(s))
+
+    def swap(block):
+        return lax.ppermute(block, "row", SWAP)
+
+    grad_1 = to_plane(out_grad, 1)
+    grad_3 = to_plane(out_grad, -1)
+    weight_other = swap(out_weight)
+
+    pieces = pack(queries, keys_tile, values_tile)
+    over_col = jnp.stack([pieces[0]] + [to_col(pieces[j], j) for j in (1, 2, 3)])
+    over_col = after(over_col, grad_1, grad_3)
     arrived = [pick(over_col, col ^ plane)]
-    for s in range(1, PLANES):
-        arrived.append(
-            lax.ppermute(pick(over_col, col ^ ((plane + s) % PLANES)), "row", row_shift(s))
-        )
+    for s in ORDER[1:]:
+        arrived.append(to_plane(pick(over_col, col ^ ((plane + s) % PLANES)), s))
     arrived = jnp.stack(arrived)
-
-    grads = [out_grad]
-    for s in range(1, PLANES):
-        grads.append(lax.ppermute(grads[-1], "row", row_shift(1)))
-    grads_own = jnp.concatenate(grads)
-    grads_other = jnp.concatenate([lax.ppermute(g, "row", SWAP) for g in grads])
-    weight_other = lax.ppermute(out_weight, "row", SWAP)
     weight = jnp.where(
         core == 0,
         jnp.concatenate([out_weight, weight_other]),
         jnp.concatenate([weight_other, out_weight]),
     )
 
+    def grad_pieces(*blocks):
+        part = jnp.concatenate([nt(g, weight).astype(BF16) for g in blocks])
+        rows = part.shape[0]
+
+        def piece(d):
+            y, x = divmod(d, 2)
+            b = head(part, 3 * y + 2).reshape(rows // tokens, 2, half, HD)[:, x]
+            return jnp.concatenate([head(part, 3 * y + x), b.reshape(rows // 2, HD)])
+
+        every = jnp.stack([piece(d) for d in range(COLS)])
+        return [pick(every, col ^ j) for j in range(COLS)]
+
+    def sum_over_col(sent):
+        terms = sent[:1] + [to_col(sent[j], j) for j in (1, 2, 3)]
+        return sum(t.astype(F32) for t in terms).astype(BF16)
+
+    early = grad_pieces(out_grad, grad_1, grad_3)
+    d_attn_early = sum_over_col(early)
+    arrived = after(arrived, early)
+
     q = jnp.concatenate(
         [
-            arrived[:, :tokens].reshape(PLANES * tokens, HD),
+            arrived[:, :tokens].reshape(own, HD),
             arrived[:, tokens : tokens + half].reshape(PLANES * half, HD),
         ]
     )
     kv_own = arrived[:, tokens + half :].reshape(PLANES, 4, tokens, HD).transpose(1, 0, 2, 3)
-    kv_own = kv_own.reshape(4, PLANES * tokens, HD)
-    kv = jnp.concatenate([kv_own, lax.ppermute(kv_own, "row", SWAP)], axis=1)
-    k, v = kv[:2], kv[2:]
+    kv_own = kv_own.reshape(4, own, HD)
+    kv = [jnp.concatenate([kv_own[i], swap(kv_own[i])]) for i in range(4)]
+    k, v = jnp.stack(kv[:2]), jnp.stack(kv[2:])
+
+    grad_2 = to_plane(after(grad_1, arrived), 1)
+    grads = [out_grad, grad_1, grad_3, grad_2]
+
     probs, attn = attention_forward(q, k, v)
 
-    attn_col = jnp.stack([attn] + [lax.ppermute(attn, "col", col_xor(j)) for j in range(1, COLS)])
-    by_col = [pick(attn_col, col ^ d) for d in range(COLS)]
-    columns = []
-    for y in range(2):
-        columns += [by_col[2 * y][: PLANES * tokens], by_col[2 * y + 1][: PLANES * tokens]]
-        halves = [by_col[2 * y + x][PLANES * tokens :].reshape(PLANES, half, HD) for x in range(2)]
-        columns.append(jnp.concatenate(halves, axis=1).reshape(PLANES * tokens, HD))
-    attn_plane = jnp.concatenate(columns, axis=1)
+    def plane_heads(a, b):
+        sent = jnp.concatenate([a, b])
+        every = jnp.stack([sent] + [to_col(sent, j) for j in (1, 2, 3)])
+        by_col = [pick(every, col ^ d) for d in range(COLS)]
+        rows = a.shape[0]
+        columns = []
+        for y in range(2):
+            columns += [by_col[2 * y][:rows], by_col[2 * y + 1][:rows]]
+            halves = [by_col[2 * y + x][rows:].reshape(-1, half, HD) for x in range(2)]
+            columns.append(jnp.concatenate(halves, axis=1).reshape(rows, HD))
+        return jnp.concatenate(columns, axis=1)
+
+    attn_a, attn_b = attn[:own], attn[own:]
+    heads_2 = plane_heads(attn_a[3 * tokens :], attn_b[3 * half :])
+    heads_rest = plane_heads(attn_a[: 3 * tokens], attn_b[: 3 * half])
+    attn_plane = jnp.concatenate([heads_rest, heads_2])
 
     def term(s):
-        block = attn_plane[s * tokens : (s + 1) * tokens]
+        block = heads_2 if s == 2 else heads_rest[ORDER.index(s) * tokens :][:tokens]
         return jnp.dot(block, weight, preferred_element_type=F32)
 
-    moving = term(1).astype(BF16)
-    for s in range(2, PLANES + 1):
-        moving = lax.ppermute(moving, "row", row_shift(1)).astype(F32) + term(s % PLANES)
-        moving = moving.astype(BF16)
-    mixed = moving
-
-    d_part = nt(grads_own, weight).astype(BF16)
-
-    def grad_piece(d):
-        y, x = divmod(d, 2)
-        b = head(d_part, 3 * y + 2).reshape(PLANES, 2, half, HD)[:, x]
-        return jnp.concatenate([head(d_part, 3 * y + x), b.reshape(PLANES * half, HD)])
-
-    d_terms = spread(jnp.stack([grad_piece(d) for d in range(COLS)]))
-    d_attn = sum(t.astype(F32) for t in d_terms).astype(BF16)
-
-    width = out_weight.shape[0]
-    attn_own = lax.dynamic_slice_in_dim(attn_plane, core * width, width, 1)
-    attn_sent = lax.dynamic_slice_in_dim(attn_plane, (1 - core) * width, width, 1)
-    attn_other = lax.ppermute(attn_sent, "row", SWAP)
-    weight_grad = (tn(attn_own, grads_own) + tn(attn_other, grads_other)).astype(BF16)
-
-    dq, dk, dv = attention_backward(q, k, v, probs, attn, d_attn)
-    dkv = jnp.concatenate([dk, dv])
-    own = PLANES * tokens
-    dkv = dkv[:, :own] + lax.ppermute(dkv[:, own:].astype(BF16), "row", SWAP).astype(F32)
+    late = grad_pieces(after(grad_2, attn))
+    d_attn_late = sum_over_col(late)
+    mixed_2 = to_plane(term(2).astype(BF16), 1)
+    mixed_1 = to_plane(after(term(1).astype(BF16), mixed_2), -1)
+
+    d_attn = jnp.concatenate(
+        [
+            d_attn_early[: 3 * tokens],
+            d_attn_late[:tokens],
+            d_attn_early[3 * tokens :],
+            d_attn_late[tokens:],
+        ]
+    )
+    dq, dkv, dkv_other = attention_backward(q, k, v, probs, attn, d_attn)
+    dkv_other = jnp.stack([jnp.stack([swap(dkv_other[i, h]) for h in range(2)]) for i in range(2)])
+    dkv = dkv + dkv_other.astype(F32)
     dkv = dkv.astype(BF16).reshape(4, PLANES, tokens, HD)
     dq_a = dq[:own].reshape(PLANES, tokens, HD)
     dq_b = dq[own:].reshape(PLANES, half, HD)
-    home = [jnp.concatenate([dq_a[s], dq_b[s]] + [dkv[i, s] for i in range(4)]) for s in range(PLANES)]
-    home = jnp.stack(
-        home[:1] + [lax.ppermute(home[s], "row", row_shift(-s)) for s in range(1, PLANES)]
-    )
+    home = [
+        jnp.concatenate([dq_a[p], dq_b[p]] + [dkv[i, p] for i in range(4)])
+        for p in (ORDER.index(s) for s in range(PLANES))
+    ]
+    home, mixed_2, mixed_1 = after((home, mixed_2, mixed_1))
+
+    attn_own = lax.dynamic_slice_in_dim(attn_plane, core * width, width, 1)
+    attn_sent = lax.dynamic_slice_in_dim(attn_plane, (1 - core) * width, width, 1)
+    attn_other = swap(attn_sent)
+    grads_own = jnp.concatenate(grads)
+    grads_other = jnp.concatenate([swap(g) for g in grads])
+    weight_grad = (
+        tn(after(attn_own, home), grads_own) + tn(attn_other, grads_other)
+    ).astype(BF16)
+
+    home = jnp.stack(home[:1] + [to_plane(home[s], -s) for s in range(1, PLANES)])
+
+    term_3 = (mixed_2.astype(F32) + term(3)).astype(BF16)
+    base = term(0) + mixed_1.astype(F32)
+    term_3, base = after((term_3, base), home)
+    mixed_3 = to_plane(term_3, 1)
+
     back = [pick(home, (col - plane) % PLANES)] + [
-        lax.ppermute(pick(home, ((col ^ j) - plane) % PLANES), "col", col_xor(j))
-        for j in range(1, COLS)
+        to_col(pick(home, ((col ^ j) - plane) % PLANES), j) for j in (1, 2, 3)
     ]
     back = jnp.stack(back)
     back = [pick(back, col ^ d) for d in range(COLS)]
@@ -340,9 +397,11 @@
         ]
         for i in range(2):
             at = tokens + half + 2 * i * tokens
-            b = left[at + tokens : at + 2 * tokens].astype(F32) + right[at + tokens : at + 2 * tokens].astype(F32)
-            outs[1 + i] += [left[at : at + tokens], right[at : at + tokens], b.astype(BF16)]
+            to = at + tokens
+            b = left[to : to + tokens].astype(F32) + right[to : to + tokens].astype(F32)
+            outs[1 + i] += [left[at:to], right[at:to], b.astype(BF16)]
     query_g, key_g, value_g = [jnp.concatenate(o, axis=1) for o in outs]
+    mixed = (base + mixed_3.astype(F32)).astype(BF16)
     return (mixed, query_g, key_g, value_g, weight_grad)
 
 

time: 202 us -> 168 us (0.83)
  waiting for transfers between devices: 131 us -> 88 us
  starting transfers between devices: 34.3 us -> 45.7 us
  local copies, waits for them, and re-layouts: 9.12 us -> 1.99 us
  other arithmetic: 1.63 us -> 4.05 us
    ppermute x32 -> x44, waiting for transfers between devices: 131 us -> 88 us  [the longest x12 53.8 us: to_plane(): return lax.ppermute(block, 'row', row_shift(s))]
    ppermute x32 -> x44, starting transfers between devices: 34.3 us -> 45.7 us  [the longest x18 21.1 us: to_col(): return lax.ppermute(block, 'col', col_xor(j))]
    unnamed x43 -> x30, local copies, waits for them, and re-layouts: 8 us -> 1.07 us
    dot_general x1 -> x4, matrix products: 2.03 us -> 5.95 us  [nt(): lax.dot_general(a, b, (((1,), (1,)), ((), ())), preferred_element_type=F32)]
    dot_general x4, matrix products: 6.11 us -> 3.39 us  [term(): return jnp.dot(block, weight, preferred_element_type=F32)]
    pallas_call x0 -> x1, Pallas kernels: none -> 2.31 us  [pack(): pl.pallas_call(pack_kernel, out_shape=[piece] * COLS, cost_estimate=pl.Co...]
  transfers between devices with their start and end apart: 32 -> 44, of which waited for: 18 -> 28; matrix products, arithmetic and copies ran while one was open for 8% -> 11% of each run, Pallas kernels for 5% -> 7%
where the time goes in v2:
time: 168 us
  waiting for transfers between devices  88 us (52%)
  starting transfers between devices  45.7 us (27%)
  matrix products  14.1 us (8%)
  Pallas kernels  12.2 us (7%)
  other arithmetic  4.05 us (2%)
  local copies, waits for them, and re-layouts  1.99 us (1%)
    ppermute x12, waiting for transfers between devices, to_plane(): return lax.ppermute(block, 'row', row_shift(s))  53.8 us
    ppermute x18, waiting for transfers between devices, to_col(): return lax.ppermute(block, 'col', col_xor(j))  31.6 us
    ppermute x18, starting transfers between devices, to_col(): return lax.ppermute(block, 'col', col_xor(j))  21.1 us
    ppermute x12, starting transfers between devices, to_plane(): return lax.ppermute(block, 'row', row_shift(s))  20.9 us
    dot_general x4, matrix products, nt(): lax.dot_general(a, b, (((1,), (1,)), ((), ())), preferred_element_type=F32)  5.95 us
    pallas_call x1, Pallas kernels, attention_backward(): pl.pallas_call(backward_kernel, grid=(3,), in_specs=[by_query, by_head, b...  5.12 us
    pallas_call x1, Pallas kernels, attention_forward(): pl.pallas_call(forward_kernel, grid=(3,), in_specs=[pl.BlockSpec((rows, H...  4.8 us
    dot_general x2, matrix products, tn(): lax.dot_general(a, b, (((0,), (0,)), ((), ())), preferred_element_type=F32)  4.75 us
  transfers between devices with their start and end apart: 44, of which 28 were waited for; matrix products, arithmetic and copies ran while one was open for 11% of the time, Pallas kernels for 7%

profile of v2, /device:TPU:0, one launch (start us, length us, event | category | flops | bytes accessed | tf_op | source)
XLA Modules:
  0.0 167.5 jit_solution(3175507553120687037)
XLA Ops:
  1.1 2.3 %pack_inputs.1 = (bf16[1056,128]{1,0:T(8,128)(2,1)}, bf16[1056,128]{1,0:T(8,128)(2,1)}, bf16[1056,128]{1,0:T(8,128)(2,1)}, bf16[1056,128]{1,0:T(8,128)(2,1)}) custom-call(bf16[192,768]{1,0:T(8,128)(2,1)} %q_ref.1, bf16[192,768]{1,0:T(8,128)(2,1)} %k_ref.1, bf16[192,768]{1,0:T(8,128)(2,1)} %v_ref.1), custom_call_target="tpu_custom_call" | custom-call | bytes 884736 | tf_op jit(solution)/shard_map/pack_inputs/pallas_call | solution.py:238
  3.5 3.5 %collective-permute-start.2 = (bf16[1056,128]{1,0:T(8,128)(2,1)}, bf16[1056,128]{1,0:T(8,128)(2,1)S(1)}, u32[]{:S(2)}, u32[]{:S(2)}) collective-permute-start(bf16[1056,128]{1,0:T(8,128)(2,1)} %get-tuple-element.31), channel_id=1, source_target_pairs={{0,3},{1,2},{2,1},{3,0},{4,7},{5,6},{6,5},{7,4},{8,11},{9,10},{10,... | collective-permute-start | bytes 811016 | tf_op jit(solution)/shard_map/ppermute | solution.py:262
  6.9 1.6 collective-permute-start.3
  8.5 2.2 %collective-permute-start.4 = (bf16[192,1536]{1,0:T(8,128)(2,1)}, bf16[192,1536]{1,0:T(8,128)(2,1)}, u32[]{:S(2)}, u32[]{:S(2)}) collective-permute-start(bf16[192,1536]{1,0:T(8,128)(2,1)} %param.9), channel_id=1, source_target_pairs={{0,24},{4,28},{8,0},{12,4},{16,8},{20,12},{24,16},{28,20},{1,25},{... | collective-permute-start | bytes 1769480 | tf_op jit(solution)/shard_map/ppermute | solution.py:265
  11.3 3.1 %collective-permute-done.2 = bf16[1056,128]{1,0:T(8,128)(2,1)S(1)} collective-permute-done((bf16[1056,128]{1,0:T(8,128)(2,1)}, bf16[1056,128]{1,0:T(8,128)(2,1)S(1)}, u32[]{:S(2)}, u32[]{:S(2)}) %collective-permute-start.2) | collective-permute-done | bytes 270368 | tf_op jit(solution)/shard_map/ppermute | solution.py:262
  14.4 1.7 %collective-permute-start = (bf16[1056,128]{1,0:T(8,128)(2,1)}, bf16[1056,128]{1,0:T(8,128)(2,1)S(1)}, u32[]{:S(2)}, u32[]{:S(2)}) collective-permute-start(bf16[1056,128]{1,0:T(8,128)(2,1)} %get-tuple-element.29), channel_id=1, source_target_pairs={{0,1},{1,0},{2,3},{3,2},{4,5},{5,4},{6,7},{7,6},{8,9},{9,8},{10,11... | collective-permute-start | bytes 811016 | tf_op jit(solution)/shard_map/ppermute | solution.py:262
  16.1 4.0 %collective-permute-done.1 = bf16[1056,128]{1,0:T(8,128)(2,1)S(1)} collective-permute-done((bf16[1056,128]{1,0:T(8,128)(2,1)}, bf16[1056,128]{1,0:T(8,128)(2,1)S(1)}, u32[]{:S(2)}, u32[]{:S(2)}) %collective-permute-start.1) | collective-permute-done | bytes 270368 | tf_op jit(solution)/shard_map/ppermute | solution.py:262
  20.1 2.8 %collective-permute-done = bf16[1056,128]{1,0:T(8,128)(2,1)S(1)} collective-permute-done((bf16[1056,128]{1,0:T(8,128)(2,1)}, bf16[1056,128]{1,0:T(8,128)(2,1)S(1)}, u32[]{:S(2)}, u32[]{:S(2)}) %collective-permute-start) | collective-permute-done | bytes 270368 | tf_op jit(solution)/shard_map/ppermute | solution.py:262
  25.2 11.4 %collective-permute-done.4 = bf16[192,1536]{1,0:T(8,128)(2,1)} collective-permute-done((bf16[192,1536]{1,0:T(8,128)(2,1)}, bf16[192,1536]{1,0:T(8,128)(2,1)}, u32[]{:S(2)}, u32[]{:S(2)}) %collective-permute-start.4) | collective-permute-done | bytes 589856 | tf_op jit(solution)/shard_map/ppermute | solution.py:265
  38.1 2.2 %collective-permute-start.6 = (bf16[1056,128]{1,0:T(8,128)(2,1)S(1)}, bf16[1056,128]{1,0:T(8,128)(2,1)S(1)}, u32[]{:S(2)}, u32[]{:S(2)}) collective-permute-start(bf16[1056,128]{1,0:T(8,128)(2,1)S(1)} %get-tuple-element.81), channel_id=1, source_target_pairs={{0,24},{4,28},{8,0},{12,4},{16,8},{20,12},{24,16},{28,20},{1,25},{... | collective-permute-start | bytes 811016 | tf_op jit(solution)/shard_map/ppermute | solution.py:265
  40.3 2.0 %fusion.18 = bf16[192,768]{1,0:T(8,128)(2,1)S(1)} fusion(bf16[192,1536]{1,0:T(8,128)(2,1)} %collective-permute-done.4, bf16[384,1536]{1,0:T(8,128)(2,1)S(1)} %collective-permute-done.8, bf16[384,1536]{1,0:T(8,128)(2,1)S(1)} %copy-done.4, pred[]{:T(512)S(6)} %eq.12), kind=kOutput, calls=%fused_computation.34 | convolution fusion | flops 463749120 | bytes 3244033 | tf_op jit(solution)/shard_map/dot_general | solution.py:123
  42.3 2.1 %fusion.17 = bf16[192,768]{1,0:T(8,128)(2,1)S(1)} fusion(bf16[192,1536]{1,0:T(8,128)(2,1)} %collective-permute-done.3, bf16[384,1536]{1,0:T(8,128)(2,1)S(1)} %collective-permute-done.8, bf16[384,1536]{1,0:T(8,128)(2,1)S(1)} %copy-done.4, pred[]{:T(512)S(6)} %eq.12), kind=kOutput, calls=%fused_computation.33 | convolution fusion | flops 463749120 | bytes 3244033 | tf_op jit(solution)/shard_map/dot_general | solution.py:123
  47.9 10.5 %collective-permute-done.7 = bf16[1056,128]{1,0:T(8,128)(2,1)S(1)} collective-permute-done((bf16[1056,128]{1,0:T(8,128)(2,1)S(1)}, bf16[1056,128]{1,0:T(8,128)(2,1)S(1)}, u32[]{:S(2)}, u32[]{:S(2)}) %collective-permute-start.7) | collective-permute-done | bytes 270368 | tf_op jit(solution)/shard_map/ppermute | solution.py:265
  59.1 5.2 %collective-permute-done.13 = bf16[864,128]{1,0:T(8,128)(2,1)S(1)} collective-permute-done((bf16[864,128]{1,0:T(8,128)(2,1)S(1)}, bf16[864,128]{1,0:T(8,128)(2,1)S(1)}, u32[]{:S(2)}, u32[]{:S(2)}) %collective-permute-start.13) | collective-permute-done | bytes 221216 | tf_op jit(solution)/shard_map/ppermute | solution.py:262
  67.5 4.8 %attention_forward.1 = (bf16[3,1536,384]{2,1,0:T(8,128)(2,1)S(1)}, bf16[1152,128]{1,0:T(8,128)(2,1)S(1)}) custom-call(bf16[1152,128]{1,0:T(8,128)(2,1)S(1)} %pad_maximum_fusion.9.q_ref, bf16[2,1536,128]{2,1,0:T(8,128)(2,1)S(1)} %pad_maximum_fusion.7.k_ref, bf16[2,1536,128]{2,1,0:T(8,128)(2,1)S(1)} %pad_maximum_fusion.8.v_ref), custom_call_target="tpu_custom_call" | custom-call | tf_op jit(solution)/shard_map/attention_forward/pallas_call | solution.py:142
  72.9 1.5 collective-permute-start.25
  76.5 1.9 %collective-permute-done.26 = bf16[288,128]{1,0:T(8,128)(2,1)S(1)} collective-permute-done((bf16[288,128]{1,0:T(8,128)(2,1)S(1)}, bf16[288,128]{1,0:T(8,128)(2,1)S(1)}, u32[]{:S(2)}, u32[]{:S(2)}) %collective-permute-start.26) | collective-permute-done | bytes 73760 | tf_op jit(solution)/shard_map/ppermute | solution.py:262
  78.6 1.6 collective-permute-start.28
  81.6 3.8 %collective-permute-done.30 = bf16[864,128]{1,0:T(8,128)(2,1)S(1)} collective-permute-done((bf16[864,128]{1,0:T(8,128)(2,1)S(1)}, bf16[864,128]{1,0:T(8,128)(2,1)S(1)}, u32[]{:S(2)}, u32[]{:S(2)}) %collective-permute-start.30) | collective-permute-done | bytes 221216 | tf_op jit(solution)/shard_map/ppermute | solution.py:262
  85.4 3.4 %collective-permute-done.29 = bf16[864,128]{1,0:T(8,128)(2,1)S(1)} collective-permute-done((bf16[864,128]{1,0:T(8,128)(2,1)S(1)}, bf16[864,128]{1,0:T(8,128)(2,1)S(1)}, u32[]{:S(2)}, u32[]{:S(2)}) %collective-permute-start.29) | collective-permute-done | bytes 221216 | tf_op jit(solution)/shard_map/ppermute | solution.py:262
  95.0 2.4 %collective-permute-done.19 = bf16[288,128]{1,0:T(8,128)(2,1)S(1)} collective-permute-done((bf16[288,128]{1,0:T(8,128)(2,1)S(1)}, bf16[288,128]{1,0:T(8,128)(2,1)S(1)}, u32[]{:S(2)}, u32[]{:S(2)}) %collective-permute-start.19) | collective-permute-done | bytes 73760 | tf_op jit(solution)/shard_map/ppermute | solution.py:262
  97.9 5.1 %attention_backward.1 = (bf16[1152,128]{1,0:T(8,128)(2,1)S(1)}, f32[2,2,768,128]{3,2,1,0:T(8,128)S(1)}, bf16[2,2,768,128]{3,2,1,0:T(8,128)(2,1)S(1)}) custom-call(bf16[1152,128]{1,0:T(8,128)(2,1)S(1)} %pad_maximum_fusion.9.q_ref, bf16[2,1536,128]{2,1,0:T(8,128)(2,1)S(1)} %pad_maximum_fusion.7.k_ref, bf16[2,1536,128]{2,1,0:T(8,128)(2,1)S(1)} %pad_maximum_fusion.8.v_ref, ...), custom_call_target="tpu_custom_call" | custom-call | tf_op jit(solution)/shard_map/attention_backward/pallas_call | solution.py:196
  106.3 2.3 %collective-permute-start.31 = (bf16[192,1536]{1,0:T(8,128)(2,1)S(1)}, bf16[192,1536]{1,0:T(8,128)(2,1)S(1)}, u32[]{:S(2)}, u32[]{:S(2)}) collective-permute-start(bf16[192,1536]{1,0:T(8,128)(2,1)S(1)} %convolution_convert_fusion), channel_id=1, source_target_pairs={{0,24},{4,28},{8,0},{12,4},{16,8},{20,12},{24,16},{28,20},{1,25},{... | collective-permute-start | bytes 1769480 | tf_op jit(solution)/shard_map/ppermute | solution.py:265
  111.0 10.7 %collective-permute-done.31 = bf16[192,1536]{1,0:T(8,128)(2,1)S(1)} collective-permute-done((bf16[192,1536]{1,0:T(8,128)(2,1)S(1)}, bf16[192,1536]{1,0:T(8,128)(2,1)S(1)}, u32[]{:S(2)}, u32[]{:S(2)}) %collective-permute-start.31) | collective-permute-done | bytes 589856 | tf_op jit(solution)/shard_map/ppermute | solution.py:265
  121.8 4.6 %collective-permute-start.33 = (bf16[1056,128]{1,0:T(8,128)(2,1)S(1)}, bf16[1056,128]{1,0:T(8,128)(2,1)S(1)}, u32[]{:S(2)}, u32[]{:S(2)}) collective-permute-start(bf16[1056,128]{1,0:T(8,128)(2,1)S(1)} %get-tuple-element.46), channel_id=1, source_target_pairs={{0,16},{4,20},{8,24},{12,28},{16,0},{20,4},{24,8},{28,12},{1,17},{... | collective-permute-start | bytes 811016 | tf_op jit(solution)/shard_map/ppermute | solution.py:265
  126.4 3.4 %fusion = bf16[384,1536]{1,0:T(8,128)(2,1)} fusion(f32[384,1536]{1,0:T(8,128)S(1)} %fusion.8, bf16[768,384]{1,0:T(8,128)(2,1)S(1)} %get-tuple-element.50, bf16[192,1536]{1,0:T(8,128)(2,1)S(1)} %collective-permute-done.16, bf16[192,1536]{1,0:T(8,128)(2,1)} %collective-permute-done.4, bf16[192,1536]{1,0:T(8,128)(2,1)} %collective-permute-done.3, ...), kind=kOutput, calls=%fused_computation.1 | convolution fusion | flops 916586496 | bytes 6488064 | tf_op jit(solution)/shard_map/dot_general | solution.py:127
  130.7 2.7 %collective-permute-done.34 = bf16[1056,128]{1,0:T(8,128)(2,1)S(1)} collective-permute-done((bf16[1056,128]{1,0:T(8,128)(2,1)S(1)}, bf16[1056,128]{1,0:T(8,128)(2,1)S(1)}, u32[]{:S(2)}, u32[]{:S(2)}) %collective-permute-start.34) | collective-permute-done | bytes 270368 | tf_op jit(solution)/shard_map/ppermute | solution.py:265
  133.4 10.3 %collective-permute-done.33 = bf16[1056,128]{1,0:T(8,128)(2,1)S(1)} collective-permute-done((bf16[1056,128]{1,0:T(8,128)(2,1)S(1)}, bf16[1056,128]{1,0:T(8,128)(2,1)S(1)}, u32[]{:S(2)}, u32[]{:S(2)}) %collective-permute-start.33) | collective-permute-done | bytes 270368 | tf_op jit(solution)/shard_map/ppermute | solution.py:265
  143.8 1.5 collective-permute-start.38
  148.3 6.3 %collective-permute-start.35 = (bf16[192,1536]{1,0:T(8,128)(2,1)S(1)}, bf16[192,1536]{1,0:T(8,128)(2,1)S(1)}, u32[]{:S(2)}, u32[]{:S(2)}) collective-permute-start(bf16[192,1536]{1,0:T(8,128)(2,1)S(1)} %add_convert_fusion.2), channel_id=1, source_target_pairs={{0,8},{4,12},{8,16},{12,20},{16,24},{20,28},{24,0},{28,4},{1,9},{5... | collective-permute-start | bytes 1769480 | tf_op jit(solution)/shard_map/ppermute | solution.py:265
  154.6 4.3 %collective-permute-done.37 = bf16[1056,128]{1,0:T(8,128)(2,1)S(1)} collective-permute-done((bf16[1056,128]{1,0:T(8,128)(2,1)S(1)}, bf16[1056,128]{1,0:T(8,128)(2,1)S(1)}, u32[]{:S(2)}, u32[]{:S(2)}) %collective-permute-start.37) | collective-permute-done | bytes 270368 | tf_op jit(solution)/shard_map/ppermute | solution.py:262
  159.5 7.0 %collective-permute-done.35 = bf16[192,1536]{1,0:T(8,128)(2,1)S(1)} collective-permute-done((bf16[192,1536]{1,0:T(8,128)(2,1)S(1)}, bf16[192,1536]{1,0:T(8,128)(2,1)S(1)}, u32[]{:S(2)}, u32[]{:S(2)}) %collective-permute-start.35) | collective-permute-done | bytes 589856 | tf_op jit(solution)/shard_map/ppermute | solution.py:265
  (170 shorter events, 33.8 us)
Async XLA Ops:
  0.6 39.6 %collective-permute-start.8 = (bf16[384,1536]{1,0:T(8,128)(2,1)}, bf16[384,1536]{1,0:T(8,128)(2,1)S(1)}, u32[]{:S(2)}, u32[]{:S(2)}) collective-permute-start(bf16[384,1536]{1,0:T(8,128)(2,1)} %param.8), channel_id=1, source_target_pairs={{0,4},{4,0},{8,12},{12,8},{16,20},{20,16},{24,28},{28,24},{1,5},{5... | collective-permute-start | bytes 3538952 | tf_op jit(solution)/shard_map/ppermute | solution.py:268
  3.5 10.9 %collective-permute-start.2 = (bf16[1056,128]{1,0:T(8,128)(2,1)}, bf16[1056,128]{1,0:T(8,128)(2,1)S(1)}, u32[]{:S(2)}, u32[]{:S(2)}) collective-permute-start(bf16[1056,128]{1,0:T(8,128)(2,1)} %get-tuple-element.31), channel_id=1, source_target_pairs={{0,3},{1,2},{2,1},{3,0},{4,7},{5,6},{6,5},{7,4},{8,11},{9,10},{10,... | collective-permute-start | bytes 811016 | tf_op jit(solution)/shard_map/ppermute | solution.py:262
  6.9 18.3 %collective-permute-start.3 = (bf16[192,1536]{1,0:T(8,128)(2,1)}, bf16[192,1536]{1,0:T(8,128)(2,1)}, u32[]{:S(2)}, u32[]{:S(2)}) collective-permute-start(bf16[192,1536]{1,0:T(8,128)(2,1)} %param.9), channel_id=1, source_target_pairs={{0,8},{4,12},{8,16},{12,20},{16,24},{20,28},{24,0},{28,4},{1,9},{5... | collective-permute-start | bytes 1769480 | tf_op jit(solution)/shard_map/ppermute | solution.py:265
  8.5 28.1 %collective-permute-start.4 = (bf16[192,1536]{1,0:T(8,128)(2,1)}, bf16[192,1536]{1,0:T(8,128)(2,1)}, u32[]{:S(2)}, u32[]{:S(2)}) collective-permute-start(bf16[192,1536]{1,0:T(8,128)(2,1)} %param.9), channel_id=1, source_target_pairs={{0,24},{4,28},{8,0},{12,4},{16,8},{20,12},{24,16},{28,20},{1,25},{... | collective-permute-start | bytes 1769480 | tf_op jit(solution)/shard_map/ppermute | solution.py:265
  10.7 9.3 %collective-permute-start.1 = (bf16[1056,128]{1,0:T(8,128)(2,1)}, bf16[1056,128]{1,0:T(8,128)(2,1)S(1)}, u32[]{:S(2)}, u32[]{:S(2)}) collective-permute-start(bf16[1056,128]{1,0:T(8,128)(2,1)} %get-tuple-element.30), channel_id=1, source_target_pairs={{0,2},{1,3},{2,0},{3,1},{4,6},{5,7},{6,4},{7,5},{8,10},{9,11},{10,... | collective-permute-start | bytes 811016 | tf_op jit(solution)/shard_map/ppermute | solution.py:262
  14.4 8.5 %collective-permute-start = (bf16[1056,128]{1,0:T(8,128)(2,1)}, bf16[1056,128]{1,0:T(8,128)(2,1)S(1)}, u32[]{:S(2)}, u32[]{:S(2)}) collective-permute-start(bf16[1056,128]{1,0:T(8,128)(2,1)} %get-tuple-element.29), channel_id=1, source_target_pairs={{0,1},{1,0},{2,3},{3,2},{4,5},{5,4},{6,7},{7,6},{8,9},{9,8},{10,11... | collective-permute-start | bytes 811016 | tf_op jit(solution)/shard_map/ppermute | solution.py:262
  36.7 21.7 %collective-permute-start.7 = (bf16[1056,128]{1,0:T(8,128)(2,1)S(1)}, bf16[1056,128]{1,0:T(8,128)(2,1)S(1)}, u32[]{:S(2)}, u32[]{:S(2)}) collective-permute-start(bf16[1056,128]{1,0:T(8,128)(2,1)S(1)} %get-tuple-element.80), channel_id=1, source_target_pairs={{0,16},{4,20},{8,24},{12,28},{16,0},{20,4},{24,8},{28,12},{1,17},{... | collective-permute-start | bytes 811016 | tf_op jit(solution)/shard_map/ppermute | solution.py:265
  38.1 20.9 %collective-permute-start.6 = (bf16[1056,128]{1,0:T(8,128)(2,1)S(1)}, bf16[1056,128]{1,0:T(8,128)(2,1)S(1)}, u32[]{:S(2)}, u32[]{:S(2)}) collective-permute-start(bf16[1056,128]{1,0:T(8,128)(2,1)S(1)} %get-tuple-element.81), channel_id=1, source_target_pairs={{0,24},{4,28},{8,0},{12,4},{16,8},{20,12},{24,16},{28,20},{1,25},{... | collective-permute-start | bytes 811016 | tf_op jit(solution)/shard_map/ppermute | solution.py:265
  40.2 18.7 %collective-permute-start.5 = (bf16[1056,128]{1,0:T(8,128)(2,1)S(1)}, bf16[1056,128]{1,0:T(8,128)(2,1)S(1)}, u32[]{:S(2)}, u32[]{:S(2)}) collective-permute-start(bf16[1056,128]{1,0:T(8,128)(2,1)S(1)} %get-tuple-element.82), channel_id=1, source_target_pairs={{0,8},{4,12},{8,16},{12,20},{16,24},{20,28},{24,0},{28,4},{1,9},{5... | collective-permute-start | bytes 811016 | tf_op jit(solution)/shard_map/ppermute | solution.py:265
  45.8 13.2 %collective-permute-start.15 = (bf16[864,128]{1,0:T(8,128)(2,1)S(1)}, bf16[864,128]{1,0:T(8,128)(2,1)S(1)}, u32[]{:S(2)}, u32[]{:S(2)}) collective-permute-start(bf16[864,128]{1,0:T(8,128)(2,1)S(1)} %get-tuple-element.88), channel_id=1, source_target_pairs={{0,3},{1,2},{2,1},{3,0},{4,7},{5,6},{6,5},{7,4},{8,11},{9,10},{10,... | collective-permute-start | bytes 663560 | tf_op jit(solution)/shard_map/ppermute | solution.py:262
  46.4 12.7 %collective-permute-start.14 = (bf16[864,128]{1,0:T(8,128)(2,1)S(1)}, bf16[864,128]{1,0:T(8,128)(2,1)S(1)}, u32[]{:S(2)}, u32[]{:S(2)}) collective-permute-start(bf16[864,128]{1,0:T(8,128)(2,1)S(1)} %get-tuple-element.89), channel_id=1, source_target_pairs={{0,2},{1,3},{2,0},{3,1},{4,6},{5,7},{6,4},{7,5},{8,10},{9,11},{10,... | collective-permute-start | bytes 663560 | tf_op jit(solution)/shard_map/ppermute | solution.py:262
  58.4 5.9 %collective-permute-start.13 = (bf16[864,128]{1,0:T(8,128)(2,1)S(1)}, bf16[864,128]{1,0:T(8,128)(2,1)S(1)}, u32[]{:S(2)}, u32[]{:S(2)}) collective-permute-start(bf16[864,128]{1,0:T(8,128)(2,1)S(1)} %get-tuple-element.87), channel_id=1, source_target_pairs={{0,1},{1,0},{2,3},{3,2},{4,5},{5,4},{6,7},{7,6},{8,9},{9,8},{10,11... | collective-permute-start | bytes 663560 | tf_op jit(solution)/shard_map/ppermute | solution.py:262
  66.2 24.0 %collective-permute-start.16 = (bf16[192,1536]{1,0:T(8,128)(2,1)}, bf16[192,1536]{1,0:T(8,128)(2,1)S(1)}, u32[]{:S(2)}, u32[]{:S(2)}) collective-permute-start(bf16[192,1536]{1,0:T(8,128)(2,1)} %collective-permute-done.3), channel_id=1, source_target_pairs={{0,8},{4,12},{8,16},{12,20},{16,24},{20,28},{24,0},{28,4},{1,9},{5... | collective-permute-start | bytes 1769480 | tf_op jit(solution)/shard_map/ppermute | solution.py:265
  72.4 6.1 %collective-permute-start.26 = (bf16[288,128]{1,0:T(8,128)(2,1)S(1)}, bf16[288,128]{1,0:T(8,128)(2,1)S(1)}, u32[]{:S(2)}, u32[]{:S(2)}) collective-permute-start(bf16[288,128]{1,0:T(8,128)(2,1)S(1)} %get-tuple-element.148), channel_id=1, source_target_pairs={{0,3},{1,2},{2,1},{3,0},{4,7},{5,6},{6,5},{7,4},{8,11},{9,10},{10,... | collective-permute-start | bytes 221192 | tf_op jit(solution)/shard_map/ppermute | solution.py:262
  72.9 5.7 %collective-permute-start.25 = (bf16[288,128]{1,0:T(8,128)(2,1)S(1)}, bf16[288,128]{1,0:T(8,128)(2,1)S(1)}, u32[]{:S(2)}, u32[]{:S(2)}) collective-permute-start(bf16[288,128]{1,0:T(8,128)(2,1)S(1)} %get-tuple-element.148), channel_id=1, source_target_pairs={{0,2},{1,3},{2,0},{3,1},{4,6},{5,7},{6,4},{7,5},{8,10},{9,11},{10,... | collective-permute-start | bytes 221192 | tf_op jit(solution)/shard_map/ppermute | solution.py:262
  74.4 5.8 %collective-permute-start.24 = (bf16[288,128]{1,0:T(8,128)(2,1)S(1)}, bf16[288,128]{1,0:T(8,128)(2,1)S(1)}, u32[]{:S(2)}, u32[]{:S(2)}) collective-permute-start(bf16[288,128]{1,0:T(8,128)(2,1)S(1)} %get-tuple-element.148), channel_id=1, source_target_pairs={{0,1},{1,0},{2,3},{3,2},{4,5},{5,4},{6,7},{7,6},{8,9},{9,8},{10,11... | collective-permute-start | bytes 221192 | tf_op jit(solution)/shard_map/ppermute | solution.py:262
  76.0 9.4 %collective-permute-start.30 = (bf16[864,128]{1,0:T(8,128)(2,1)S(1)}, bf16[864,128]{1,0:T(8,128)(2,1)S(1)}, u32[]{:S(2)}, u32[]{:S(2)}) collective-permute-start(bf16[864,128]{1,0:T(8,128)(2,1)S(1)} %get-tuple-element.142), channel_id=1, source_target_pairs={{0,3},{1,2},{2,1},{3,0},{4,7},{5,6},{6,5},{7,4},{8,11},{9,10},{10,... | collective-permute-start | bytes 663560 | tf_op jit(solution)/shard_map/ppermute | solution.py:262
  78.5 10.4 %collective-permute-start.29 = (bf16[864,128]{1,0:T(8,128)(2,1)S(1)}, bf16[864,128]{1,0:T(8,128)(2,1)S(1)}, u32[]{:S(2)}, u32[]{:S(2)}) collective-permute-start(bf16[864,128]{1,0:T(8,128)(2,1)S(1)} %get-tuple-element.142), channel_id=1, source_target_pairs={{0,2},{1,3},{2,0},{3,1},{4,6},{5,7},{6,4},{7,5},{8,10},{9,11},{10,... | collective-permute-start | bytes 663560 | tf_op jit(solution)/shard_map/ppermute | solution.py:262
  78.6 10.2 %collective-permute-start.28 = (bf16[864,128]{1,0:T(8,128)(2,1)S(1)}, bf16[864,128]{1,0:T(8,128)(2,1)S(1)}, u32[]{:S(2)}, u32[]{:S(2)}) collective-permute-start(bf16[864,128]{1,0:T(8,128)(2,1)S(1)} %get-tuple-element.142), channel_id=1, source_target_pairs={{0,1},{1,0},{2,3},{3,2},{4,5},{5,4},{6,7},{7,6},{8,9},{9,8},{10,11... | collective-permute-start | bytes 663560 | tf_op jit(solution)/shard_map/ppermute | solution.py:262
  81.3 22.9 %collective-permute-start.27 = (bf16[192,1536]{1,0:T(8,128)(2,1)S(1)}, bf16[192,1536]{1,0:T(8,128)(2,1)S(1)}, u32[]{:S(2)}, u32[]{:S(2)}) collective-permute-start(bf16[192,1536]{1,0:T(8,128)(2,1)S(1)} %convolution_convert_fusion.1), channel_id=1, source_target_pairs={{0,8},{4,12},{8,16},{12,20},{16,24},{20,28},{24,0},{28,4},{1,9},{5... | collective-permute-start | bytes 1769480 | tf_op jit(solution)/shard_map/ppermute | solution.py:265
  91.4 6.1 %collective-permute-start.19 = (bf16[288,128]{1,0:T(8,128)(2,1)S(1)}, bf16[288,128]{1,0:T(8,128)(2,1)S(1)}, u32[]{:S(2)}, u32[]{:S(2)}) collective-permute-start(bf16[288,128]{1,0:T(8,128)(2,1)S(1)} %get-tuple-element.133), channel_id=1, source_target_pairs={{0,3},{1,2},{2,1},{3,0},{4,7},{5,6},{6,5},{7,4},{8,11},{9,10},{10,... | collective-permute-start | bytes 221192 | tf_op jit(solution)/shard_map/ppermute | solution.py:262
  92.4 5.1 %collective-permute-start.18 = (bf16[288,128]{1,0:T(8,128)(2,1)S(1)}, bf16[288,128]{1,0:T(8,128)(2,1)S(1)}, u32[]{:S(2)}, u32[]{:S(2)}) collective-permute-start(bf16[288,128]{1,0:T(8,128)(2,1)S(1)} %get-tuple-element.134), channel_id=1, source_target_pairs={{0,2},{1,3},{2,0},{3,1},{4,6},{5,7},{6,4},{7,5},{8,10},{9,11},{10,... | collective-permute-start | bytes 221192 | tf_op jit(solution)/shard_map/ppermute | solution.py:262
  93.4 4.4 %collective-permute-start.17 = (bf16[288,128]{1,0:T(8,128)(2,1)S(1)}, bf16[288,128]{1,0:T(8,128)(2,1)S(1)}, u32[]{:S(2)}, u32[]{:S(2)}) collective-permute-start(bf16[288,128]{1,0:T(8,128)(2,1)S(1)} %get-tuple-element.132), channel_id=1, source_target_pairs={{0,1},{1,0},{2,3},{3,2},{4,5},{5,4},{6,7},{7,6},{8,9},{9,8},{10,11... | collective-permute-start | bytes 221192 | tf_op jit(solution)/shard_map/ppermute | solution.py:262
  105.5 4.2 %collective-permute-start.43 = (bf16[192,1536]{1,0:T(8,128)(2,1)S(1)}, bf16[192,1536]{1,0:T(8,128)(2,1)S(1)}, u32[]{:S(2)}, u32[]{:S(2)}) collective-permute-start(bf16[192,1536]{1,0:T(8,128)(2,1)S(1)} %collective-permute-done.16), channel_id=1, source_target_pairs={{0,4},{4,0},{8,12},{12,8},{16,20},{20,16},{24,28},{28,24},{1,5},{5... | collective-permute-start | bytes 1769480 | tf_op jit(solution)/shard_map/ppermute | solution.py:268
  106.3 15.4 %collective-permute-start.31 = (bf16[192,1536]{1,0:T(8,128)(2,1)S(1)}, bf16[192,1536]{1,0:T(8,128)(2,1)S(1)}, u32[]{:S(2)}, u32[]{:S(2)}) collective-permute-start(bf16[192,1536]{1,0:T(8,128)(2,1)S(1)} %convolution_convert_fusion), channel_id=1, source_target_pairs={{0,24},{4,28},{8,0},{12,4},{16,8},{20,12},{24,16},{28,20},{1,25},{... | collective-permute-start | bytes 1769480 | tf_op jit(solution)/shard_map/ppermute | solution.py:265
  121.8 11.6 %collective-permute-start.34 = (bf16[1056,128]{1,0:T(8,128)(2,1)S(1)}, bf16[1056,128]{1,0:T(8,128)(2,1)S(1)}, u32[]{:S(2)}, u32[]{:S(2)}) collective-permute-start(bf16[1056,128]{1,0:T(8,128)(2,1)S(1)} %get-tuple-element.47), channel_id=1, source_target_pairs={{0,8},{4,12},{8,16},{12,20},{16,24},{20,28},{24,0},{28,4},{1,9},{5... | collective-permute-start | bytes 811016 | tf_op jit(solution)/shard_map/ppermute | solution.py:265
  121.8 21.8 %collective-permute-start.33 = (bf16[1056,128]{1,0:T(8,128)(2,1)S(1)}, bf16[1056,128]{1,0:T(8,128)(2,1)S(1)}, u32[]{:S(2)}, u32[]{:S(2)}) collective-permute-start(bf16[1056,128]{1,0:T(8,128)(2,1)S(1)} %get-tuple-element.46), channel_id=1, source_target_pairs={{0,16},{4,20},{8,24},{12,28},{16,0},{20,4},{24,8},{28,12},{1,17},{... | collective-permute-start | bytes 811016 | tf_op jit(solution)/shard_map/ppermute | solution.py:265
  126.4 17.2 %collective-permute-start.32 = (bf16[1056,128]{1,0:T(8,128)(2,1)S(1)}, bf16[1056,128]{1,0:T(8,128)(2,1)S(1)}, u32[]{:S(2)}, u32[]{:S(2)}) collective-permute-start(bf16[1056,128]{1,0:T(8,128)(2,1)S(1)} %get-tuple-element.45), channel_id=1, source_target_pairs={{0,24},{4,28},{8,0},{12,4},{16,8},{20,12},{24,16},{28,20},{1,25},{... | collective-permute-start | bytes 811016 | tf_op jit(solution)/shard_map/ppermute | solution.py:265
  143.8 10.8 %collective-permute-start.38 = (bf16[1056,128]{1,0:T(8,128)(2,1)S(1)}, bf16[1056,128]{1,0:T(8,128)(2,1)S(1)}, u32[]{:S(2)}, u32[]{:S(2)}) collective-permute-start(bf16[1056,128]{1,0:T(8,128)(2,1)S(1)} %get-tuple-element.76), channel_id=1, source_target_pairs={{0,3},{1,2},{2,1},{3,0},{4,7},{5,6},{6,5},{7,4},{8,11},{9,10},{10,... | collective-permute-start | bytes 811016 | tf_op jit(solution)/shard_map/ppermute | solution.py:262
  145.4 13.5 %collective-permute-start.37 = (bf16[1056,128]{1,0:T(8,128)(2,1)S(1)}, bf16[1056,128]{1,0:T(8,128)(2,1)S(1)}, u32[]{:S(2)}, u32[]{:S(2)}) collective-permute-start(bf16[1056,128]{1,0:T(8,128)(2,1)S(1)} %get-tuple-element.77), channel_id=1, source_target_pairs={{0,2},{1,3},{2,0},{3,1},{4,6},{5,7},{6,4},{7,5},{8,10},{9,11},{10,... | collective-permute-start | bytes 811016 | tf_op jit(solution)/shard_map/ppermute | solution.py:262
  146.8 12.1 %collective-permute-start.36 = (bf16[1056,128]{1,0:T(8,128)(2,1)S(1)}, bf16[1056,128]{1,0:T(8,128)(2,1)S(1)}, u32[]{:S(2)}, u32[]{:S(2)}) collective-permute-start(bf16[1056,128]{1,0:T(8,128)(2,1)S(1)} %get-tuple-element.78), channel_id=1, source_target_pairs={{0,1},{1,0},{2,3},{3,2},{4,5},{5,4},{6,7},{7,6},{8,9},{9,8},{10,11... | collective-permute-start | bytes 811016 | tf_op jit(solution)/shard_map/ppermute | solution.py:262
  148.3 18.3 %collective-permute-start.35 = (bf16[192,1536]{1,0:T(8,128)(2,1)S(1)}, bf16[192,1536]{1,0:T(8,128)(2,1)S(1)}, u32[]{:S(2)}, u32[]{:S(2)}) collective-permute-start(bf16[192,1536]{1,0:T(8,128)(2,1)S(1)} %add_convert_fusion.2), channel_id=1, source_target_pairs={{0,8},{4,12},{8,16},{12,20},{16,24},{20,28},{24,0},{28,4},{1,9},{5... | collective-permute-start | bytes 1769480 | tf_op jit(solution)/shard_map/ppermute | solution.py:265
  (20 other events, 104.2 us)

commit v3 on v2

--- a/solution.py
+++ b/solution.py
@@ -98,6 +98,8 @@
 
 PLANES, CORES, COLS = 4, 2, 4
 ORDER = (0, 1, 3, 2)
+WINDOW = pl.CostEstimate(flops=4 * 10**10, bytes_accessed=0, transcendentals=0)
+SMALL = pl.CostEstimate(flops=10**6, bytes_accessed=10**3, transcendentals=0)
 
 
 def row_shift(s):
@@ -152,19 +154,33 @@
             pl.BlockSpec((rows, HD), lambda i: (i, 0)),
         ],
         out_shape=[
-            jax.ShapeDtypeStruct((3, keys, rows), BF16),
+            pltpu.HBM((3, keys, rows), BF16),
             jax.ShapeDtypeStruct((3 * rows, HD), BF16),
         ],
         compiler_params=pltpu.CompilerParams(vmem_limit_bytes=16 * 2**20),
+        cost_estimate=WINDOW,
         name="attention_forward",
     )(q, k, v)
 
 
 def backward_kernel(
-    q_ref, k_ref, v_ref, p_ref, attn_ref, grad_ref, dq_ref, own_ref, other_ref, sums_ref
+    q_ref, k_ref, v_ref, p_ref, attn_ref, early_ref, *refs
 ):
+    late_refs, (dq_ref, own_ref, other_ref, grad_ref, sums_ref) = refs[:COLS], refs[COLS:]
     step = pl.program_id(0)
-    grad = grad_ref[...]
+    rows = q_ref.shape[0]
+
+    @pl.when(step == 0)
+    def _():
+        early_a, late_a = early_ref.shape[0] * 2 // 3, late_refs[0].shape[0] * 2 // 3
+        late = sum(ref[...].astype(F32) for ref in late_refs).astype(BF16)
+        own = early_a + late_a
+        grad_ref[:early_a] = early_ref[:early_a]
+        grad_ref[early_a:own] = late[:late_a]
+        grad_ref[own : own + early_a // 2] = early_ref[early_a:]
+        grad_ref[own + early_a // 2 :] = late[late_a:]
+
+    grad = grad_ref[pl.ds(pl.multiple_of(step * rows, rows), rows)]
     product = grad.astype(F32) * attn_ref[...].astype(F32)
     delta = jnp.sum(product.T, axis=0, keepdims=True)
     probs = p_ref[0]
@@ -188,7 +204,7 @@
             other_ref[i, 0] = new[half:].astype(BF16)
 
 
-def attention_backward(q, k, v, probs, attn, grad):
+def attention_backward(q, k, v, probs, attn, early, late):
     rows, keys = q.shape[0] // 3, k.shape[1]
     by_query = pl.BlockSpec((rows, HD), lambda i: (i, 0))
     by_head = pl.BlockSpec((1, keys, HD), lambda i: (i // 2, 0, 0))
@@ -202,7 +218,7 @@
             by_head,
             pl.BlockSpec((1, keys, rows), lambda i: (i, 0, 0)),
             by_query,
-            by_query,
+            *[pl.BlockSpec(block.shape, lambda i: (0, 0)) for block in (early, *late)],
         ],
         out_specs=[by_query, by_half, by_half],
         out_shape=[
@@ -210,10 +226,11 @@
             jax.ShapeDtypeStruct((2, 2, keys // 2, HD), F32),
             jax.ShapeDtypeStruct((2, 2, keys // 2, HD), BF16),
         ],
-        scratch_shapes=[pltpu.VMEM((2, keys, HD), F32)],
+        scratch_shapes=[pltpu.VMEM(q.shape, BF16), pltpu.VMEM((2, keys, HD), F32)],
         compiler_params=pltpu.CompilerParams(vmem_limit_bytes=20 * 2**20),
+        cost_estimate=WINDOW,
         name="attention_backward",
-    )(q, k, v, probs, attn, grad)
+    )(q, k, v, probs, attn, early, *late)
 
 
 def pack_kernel(q_ref, k_ref, v_ref, *out_refs):
@@ -238,9 +255,129 @@
     return pl.pallas_call(
         pack_kernel,
         out_shape=[piece] * COLS,
-        cost_estimate=pl.CostEstimate(flops=0, bytes_accessed=6 * queries.size, transcendentals=0),
+        cost_estimate=WINDOW,
         name="pack_inputs",
     )(queries, keys, values)
+
+
+def grad_kernel(*refs):
+    n = len(refs) - 2 - COLS - 1
+    own_ref, other_ref = refs[n : n + 2]
+    out_refs, part_ref = refs[n + 2 : -1], refs[-1]
+    tokens = refs[0].shape[0]
+    half = tokens // 2
+    core, col = lax.rem(lax.axis_index("row"), CORES), lax.axis_index("col")
+    for i in range(n):
+        rows = pl.ds(i * tokens, tokens)
+        block = refs[i][...]
+        part_ref[core, rows] = nt(block, own_ref[...]).astype(BF16)
+        part_ref[1 - core, rows] = nt(block, other_ref[...]).astype(BF16)
+    for j, out_ref in enumerate(out_refs):
+        to = lax.bitwise_xor(col, j)
+        y, x = lax.div(to, 2), lax.rem(to, 2)
+        out_ref[: n * tokens] = part_ref[y, :, pl.ds(pl.multiple_of(x * HD, HD), HD)]
+        for i in range(n):
+            rows = pl.ds(pl.multiple_of(i * tokens + x * half, half), half)
+            out_ref[pl.ds(n * tokens + i * half, half)] = part_ref[y, rows, 2 * HD : 3 * HD]
+
+
+def grad_pieces(blocks, own, other, cost=WINDOW):
+    rows = len(blocks) * blocks[0].shape[0]
+    piece = jax.ShapeDtypeStruct((rows + rows // 2, HD), BF16)
+    return pl.pallas_call(
+        grad_kernel,
+        out_shape=[piece] * COLS,
+        scratch_shapes=[pltpu.VMEM((CORES, rows, own.shape[0]), BF16)],
+        compiler_params=pltpu.CompilerParams(vmem_limit_bytes=20 * 2**20),
+        cost_estimate=cost,
+        name="grad_pieces",
+    )(*blocks, own, other)
+
+
+def group(ref, index):
+    width = ref.shape[1] // CORES
+    return ref[:, pl.ds(pl.multiple_of(index * width, width), width)]
+
+
+def term_kernel(block_ref, own_ref, other_ref, out_ref):
+    core = lax.rem(lax.axis_index("row"), CORES)
+    out = jnp.dot(group(block_ref, core), own_ref[...], preferred_element_type=F32)
+    out += jnp.dot(group(block_ref, 1 - core), other_ref[...], preferred_element_type=F32)
+    out_ref[...] = out.astype(out_ref.dtype)
+
+
+def mixed_term(block, own, other, dtype, cost=SMALL):
+    return pl.pallas_call(
+        term_kernel,
+        out_shape=jax.ShapeDtypeStruct((block.shape[0], own.shape[1]), dtype),
+        compiler_params=pltpu.CompilerParams(vmem_limit_bytes=20 * 2**20),
+        cost_estimate=cost,
+        name="mixed_term",
+    )(block, own, other)
+
+
+def weight_grad_kernel(n, *refs):
+    head_refs, grad_refs, total_refs, out_ref = refs[:n], refs[n : 2 * n], refs[2 * n : -1], refs[-1]
+    width = out_ref.shape[1] // 4
+    for i in range(4):
+        columns = pl.ds(i * width, width)
+        total = sum(tn(h[...], g[:, columns]) for h, g in zip(head_refs, grad_refs))
+        for total_ref in total_refs:
+            total = total + total_ref[:, columns].astype(F32)
+        out_ref[:, columns] = total.astype(BF16)
+
+
+def weight_grad_part(heads, grads, *total):
+    return pl.pallas_call(
+        functools.partial(weight_grad_kernel, len(heads)),
+        out_shape=jax.ShapeDtypeStruct((heads[0].shape[1], grads[0].shape[1]), BF16),
+        compiler_params=pltpu.CompilerParams(vmem_limit_bytes=28 * 2**20),
+        cost_estimate=WINDOW,
+        name="weight_grad",
+    )(*heads, *grads, *total)
+
+
+def join_kernel(*refs):
+    in_refs, (q_ref, kv_ref) = refs[:PLANES], refs[PLANES:]
+    tokens = kv_ref.shape[1] // PLANES
+    half = tokens // 2
+    for p, in_ref in enumerate(in_refs):
+        q_ref[p * tokens : (p + 1) * tokens] = in_ref[:tokens]
+        at = PLANES * tokens + p * half
+        q_ref[at : at + half] = in_ref[tokens : tokens + half]
+        for i in range(4):
+            at = tokens + half + i * tokens
+            kv_ref[i, p * tokens : (p + 1) * tokens] = in_ref[at : at + tokens]
+
+
+def join(blocks, tokens):
+    return pl.pallas_call(
+        join_kernel,
+        out_shape=[
+            jax.ShapeDtypeStruct((PLANES * (tokens + tokens // 2), HD), BF16),
+            jax.ShapeDtypeStruct((4, PLANES * tokens, HD), BF16),
+        ],
+        cost_estimate=SMALL,
+        name="join",
+    )(*blocks)
+
+
+def fence_kernel(in_ref, out_ref):
+    del in_ref, out_ref
+
+
+def fence(*earlier):
+    mark = lax.optimization_barrier((jnp.zeros((8, 128), F32), earlier))[0]
+    return pl.pallas_call(
+        fence_kernel,
+        in_specs=[pl.BlockSpec(memory_space=pl.ANY)],
+        out_specs=pl.BlockSpec(memory_space=pl.ANY),
+        out_shape=jax.ShapeDtypeStruct(mark.shape, mark.dtype),
+        input_output_aliases={0: 0},
+        compiler_params=pltpu.CompilerParams(has_side_effects=True),
+        cost_estimate=WINDOW,
+        name="fence",
+    )(mark)
 
 
 def after(value, *earlier):
@@ -269,62 +406,37 @@
 
     grad_1 = to_plane(out_grad, 1)
     grad_3 = to_plane(out_grad, -1)
-    weight_other = swap(out_weight)
-
-    pieces = pack(queries, keys_tile, values_tile)
-    over_col = jnp.stack([pieces[0]] + [to_col(pieces[j], j) for j in (1, 2, 3)])
-    over_col = after(over_col, grad_1, grad_3)
+    weights = (out_weight, swap(out_weight))
+
+    pieces = pack(*after((queries, keys_tile, values_tile), fence()))
+    pieces = after(pieces, weights[1])
+    moved = after([to_col(pieces[j], j) for j in (1, 2, 3)], fence(pieces))
+    over_col = jnp.stack([pieces[0], *moved])
+
+    def add_up(*terms):
+        return sum(t.astype(F32) for t in terms).astype(BF16)
+
     arrived = [pick(over_col, col ^ plane)]
     for s in ORDER[1:]:
         arrived.append(to_plane(pick(over_col, col ^ ((plane + s) % PLANES)), s))
-    arrived = jnp.stack(arrived)
-    weight = jnp.where(
-        core == 0,
-        jnp.concatenate([out_weight, weight_other]),
-        jnp.concatenate([weight_other, out_weight]),
-    )
-
-    def grad_pieces(*blocks):
-        part = jnp.concatenate([nt(g, weight).astype(BF16) for g in blocks])
-        rows = part.shape[0]
-
-        def piece(d):
-            y, x = divmod(d, 2)
-            b = head(part, 3 * y + 2).reshape(rows // tokens, 2, half, HD)[:, x]
-            return jnp.concatenate([head(part, 3 * y + x), b.reshape(rows // 2, HD)])
-
-        every = jnp.stack([piece(d) for d in range(COLS)])
-        return [pick(every, col ^ j) for j in range(COLS)]
-
-    def sum_over_col(sent):
-        terms = sent[:1] + [to_col(sent[j], j) for j in (1, 2, 3)]
-        return sum(t.astype(F32) for t in terms).astype(BF16)
-
-    early = grad_pieces(out_grad, grad_1, grad_3)
-    d_attn_early = sum_over_col(early)
+    early = grad_pieces((out_grad, grad_1, grad_3), *weights)
+    early_sent = [to_col(early[j], j) for j in (1, 2)]
+    early_sent.append(to_col(after(early[3], arrived[1]), 3))
+
     arrived = after(arrived, early)
-
-    q = jnp.concatenate(
-        [
-            arrived[:, :tokens].reshape(own, HD),
-            arrived[:, tokens : tokens + half].reshape(PLANES * half, HD),
-        ]
-    )
-    kv_own = arrived[:, tokens + half :].reshape(PLANES, 4, tokens, HD).transpose(1, 0, 2, 3)
-    kv_own = kv_own.reshape(4, own, HD)
-    kv = [jnp.concatenate([kv_own[i], swap(kv_own[i])]) for i in range(4)]
-    k, v = jnp.stack(kv[:2]), jnp.stack(kv[2:])
+    q, kv = join(arrived, tokens)
+    kv = jnp.concatenate([kv, swap(kv)], axis=1)
+    k, v = kv[:2], kv[2:]
 
     grad_2 = to_plane(after(grad_1, arrived), 1)
     grads = [out_grad, grad_1, grad_3, grad_2]
 
     probs, attn = attention_forward(q, k, v)
-
-    def plane_heads(a, b):
-        sent = jnp.concatenate([a, b])
-        every = jnp.stack([sent] + [to_col(sent, j) for j in (1, 2, 3)])
+    grad_2 = after(grad_2, attn)
+    d_attn_early = add_up(early[0], *after(early_sent, attn))
+
+    def plane_heads(rows, every):
         by_col = [pick(every, col ^ d) for d in range(COLS)]
-        rows = a.shape[0]
         columns = []
         for y in range(2):
             columns += [by_col[2 * y][:rows], by_col[2 * y + 1][:rows]]
@@ -333,28 +445,20 @@
         return jnp.concatenate(columns, axis=1)
 
     attn_a, attn_b = attn[:own], attn[own:]
-    heads_2 = plane_heads(attn_a[3 * tokens :], attn_b[3 * half :])
-    heads_rest = plane_heads(attn_a[: 3 * tokens], attn_b[: 3 * half])
-    attn_plane = jnp.concatenate([heads_rest, heads_2])
-
-    def term(s):
-        block = heads_2 if s == 2 else heads_rest[ORDER.index(s) * tokens :][:tokens]
-        return jnp.dot(block, weight, preferred_element_type=F32)
-
-    late = grad_pieces(after(grad_2, attn))
-    d_attn_late = sum_over_col(late)
-    mixed_2 = to_plane(term(2).astype(BF16), 1)
-    mixed_1 = to_plane(after(term(1).astype(BF16), mixed_2), -1)
-
-    d_attn = jnp.concatenate(
-        [
-            d_attn_early[: 3 * tokens],
-            d_attn_late[:tokens],
-            d_attn_early[3 * tokens :],
-            d_attn_late[tokens:],
-        ]
-    )
-    dq, dkv, dkv_other = attention_backward(q, k, v, probs, attn, d_attn)
+    sent = jnp.concatenate([attn_a[3 * tokens :], attn_b[3 * half :]])
+    got = after([to_col(sent, j) for j in (1, 2, 3)], grad_2)
+    heads_2 = plane_heads(tokens, jnp.stack([sent, *got]))
+    term_2 = mixed_term(heads_2, *weights, BF16)
+    mixed_2 = to_plane(term_2, 1)
+    late = grad_pieces((after(grad_2, term_2),), *weights)
+    late = [late[0]] + [to_col(late[j], j) for j in (1, 2, 3)]
+    sent = jnp.concatenate([attn_a[: 3 * tokens], attn_b[: 3 * half]])
+    pair = jnp.stack([sent, to_col(sent, 1)])
+    rest = [pair, to_col(pair, 2)]
+
+    dq, dkv, dkv_other = attention_backward(q, k, v, probs, attn, d_attn_early, late)
+    rest, mixed_2 = after((rest, mixed_2), dq)
+
     dkv_other = jnp.stack([jnp.stack([swap(dkv_other[i, h]) for h in range(2)]) for i in range(2)])
     dkv = dkv + dkv_other.astype(F32)
     dkv = dkv.astype(BF16).reshape(4, PLANES, tokens, HD)
@@ -364,27 +468,34 @@
         jnp.concatenate([dq_a[p], dq_b[p]] + [dkv[i, p] for i in range(4)])
         for p in (ORDER.index(s) for s in range(PLANES))
     ]
-    home, mixed_2, mixed_1 = after((home, mixed_2, mixed_1))
-
-    attn_own = lax.dynamic_slice_in_dim(attn_plane, core * width, width, 1)
-    attn_sent = lax.dynamic_slice_in_dim(attn_plane, (1 - core) * width, width, 1)
-    attn_other = swap(attn_sent)
-    grads_own = jnp.concatenate(grads)
-    grads_other = jnp.concatenate([swap(g) for g in grads])
-    weight_grad = (
-        tn(after(attn_own, home), grads_own) + tn(attn_other, grads_other)
-    ).astype(BF16)
-
-    home = jnp.stack(home[:1] + [to_plane(home[s], -s) for s in range(1, PLANES)])
-
-    term_3 = (mixed_2.astype(F32) + term(3)).astype(BF16)
-    base = term(0) + mixed_1.astype(F32)
-    term_3, base = after((term_3, base), home)
-    mixed_3 = to_plane(term_3, 1)
-
+
+    away = [to_plane(home[s], -s) for s in range(1, PLANES)]
+
+    heads_rest = plane_heads(3 * tokens, jnp.concatenate(rest))
+    heads = [heads_rest[p * tokens : (p + 1) * tokens] for p in range(3)] + [heads_2]
+    ours, theirs = [
+        [lax.dynamic_slice_in_dim(h, g * width, width, 1) for h in heads] for g in (core, 1 - core)
+    ]
+    total = weight_grad_part(after(theirs, home), grads)
+
+    head_0, head_1, head_3 = after(heads[:3], total)
+    term_1 = mixed_term(head_1, *weights, BF16)
+    mixed_1 = to_plane(term_1, -1)
+    term_3 = (mixed_2.astype(F32) + mixed_term(head_3, *weights, F32)).astype(BF16)
+    total = swap(total)
+    term_0 = mixed_term(after(head_0, term_1, term_3), *weights, F32, WINDOW)
+
+    away, mixed_1, total = after((away, mixed_1, total), term_0)
+    home = [home[0], *away]
+    weight_grad = weight_grad_part(after(ours, home), grads, total)
+
+    mixed_3 = to_plane(after(term_3, home), 1)
+
+    home = jnp.stack(home)
     back = [pick(home, (col - plane) % PLANES)] + [
         to_col(pick(home, ((col ^ j) - plane) % PLANES), j) for j in (1, 2, 3)
     ]
+    back, mixed_3 = after((back, mixed_3), weight_grad)
     back = jnp.stack(back)
     back = [pick(back, col ^ d) for d in range(COLS)]
     outs = [[], [], []]
@@ -401,7 +512,7 @@
             b = left[to : to + tokens].astype(F32) + right[to : to + tokens].astype(F32)
             outs[1 + i] += [left[at:to], right[at:to], b.astype(BF16)]
     query_g, key_g, value_g = [jnp.concatenate(o, axis=1) for o in outs]
-    mixed = (base + mixed_3.astype(F32)).astype(BF16)
+    mixed = (term_0 + mixed_1.astype(F32) + mixed_3.astype(F32)).astype(BF16)
     return (mixed, query_g, key_g, value_g, weight_grad)
 
 

time: 168 us -> 161 us (0.958)
  Pallas kernels: 12.2 us -> 30.3 us
  matrix products: 14.1 us -> 0 us
  waiting for transfers between devices: 88 us -> 76.2 us
  local copies, waits for them, and re-layouts: 1.99 us -> 8.93 us
  starting transfers between devices: 45.7 us -> 41.3 us
  other arithmetic: 4.05 us -> 2.23 us
    pallas_call x1 -> x12, Pallas kernels: 2.31 us -> 19.6 us  [the longest x2 7.22 us: weight_grad_part(): pl.pallas_call(functools.partial(weight_grad_kernel, len(heads)), out_sha...]
    dot_general x10 -> x0, matrix products: 14.1 us -> none  [the longest x4 5.95 us: nt(): lax.dot_general(a, b, (((1,), (1,)), ((), ())), preferred_element_type=F32)]
    ppermute x12, waiting for transfers between devices: 53.8 us -> 46.7 us  [to_plane(): return lax.ppermute(block, 'row', row_shift(s))]
    unnamed x30 -> x49, local copies, waits for them, and re-layouts: 1.07 us -> 6.22 us
    ppermute x14 -> x7, starting transfers between devices: 3.78 us -> 1.23 us  [swap(): return lax.ppermute(block, 'row', SWAP)]
    ppermute x18 -> x17, waiting for transfers between devices: 31.6 us -> 29.1 us  [to_col(): return lax.ppermute(block, 'col', col_xor(j))]
    ppermute x14 -> x7, waiting for transfers between devices: 2.6 us -> 0.44 us  [swap(): return lax.ppermute(block, 'row', SWAP)]
    ppermute x18 -> x17, starting transfers between devices: 21.1 us -> 20 us  [to_col(): return lax.ppermute(block, 'col', col_xor(j))]
  transfers between devices with their start and end apart: 44 -> 36, of which waited for: 28 -> 19; matrix products, arithmetic and copies ran while one was open for 11% -> 4% of each run, Pallas kernels for 7% -> 18%
where the time goes in v3:
time: 161 us; the launch traced here: 160 us
  waiting for transfers between devices  76.2 us (47%)
  starting transfers between devices  41.3 us (26%)
  Pallas kernels  30.3 us (19%)
  local copies, waits for them, and re-layouts  8.93 us (6%)
  other arithmetic  2.23 us (1%)
    ppermute x12, waiting for transfers between devices, to_plane(): return lax.ppermute(block, 'row', row_shift(s))  46.7 us
    ppermute x17, waiting for transfers between devices, to_col(): return lax.ppermute(block, 'col', col_xor(j))  29.1 us
    ppermute x12, starting transfers between devices, to_plane(): return lax.ppermute(block, 'row', row_shift(s))  20.1 us
    ppermute x17, starting transfers between devices, to_col(): return lax.ppermute(block, 'col', col_xor(j))  20 us
    pallas_call x2, Pallas kernels, weight_grad_part(): pl.pallas_call(functools.partial(weight_grad_kernel, len(heads)), out_sha...  7.22 us
    unnamed x49, local copies, waits for them, and re-layouts  6.22 us
    pallas_call x1, Pallas kernels, attention_forward(): pl.pallas_call(forward_kernel, grid=(3,), in_specs=[pl.BlockSpec((rows, H...  5.46 us
    pallas_call x1, Pallas kernels, attention_backward(): pl.pallas_call(backward_kernel, grid=(3,), in_specs=[by_query, by_head, b...  5.26 us
  transfers between devices with their start and end apart: 36, of which 19 were waited for; matrix products, arithmetic and copies ran while one was open for 4% of the time, Pallas kernels for 18%

profile of v3, /device:TPU:0, one launch (start us, length us, event | category | flops | bytes accessed | tf_op | source)
XLA Modules:
  0.0 160.2 jit_solution(6140247519640434929)
XLA Ops:
  0.6 3.1 %collective-permute-start.7 = (bf16[192,1536]{1,0:T(8,128)(2,1)}, bf16[192,1536]{1,0:T(8,128)(2,1)}, u32[]{:S(2)}, u32[]{:S(2)}) collective-permute-start(bf16[192,1536]{1,0:T(8,128)(2,1)} %refs_4_.3), channel_id=1, source_target_pairs={{0,8},{4,12},{8,16},{12,20},{16,24},{20,28},{24,0},{28,4},{1,9},{5... | collective-permute-start | bytes 1769480 | tf_op jit(solution)/shard_map/ppermute | solution.py:402
  3.7 2.1 %collective-permute-start.8 = (bf16[192,1536]{1,0:T(8,128)(2,1)}, bf16[192,1536]{1,0:T(8,128)(2,1)}, u32[]{:S(2)}, u32[]{:S(2)}) collective-permute-start(bf16[192,1536]{1,0:T(8,128)(2,1)} %refs_4_.3), channel_id=1, source_target_pairs={{0,24},{4,28},{8,0},{12,4},{16,8},{20,12},{24,16},{28,20},{1,25},{... | collective-permute-start | bytes 1769480 | tf_op jit(solution)/shard_map/ppermute | solution.py:402
  6.4 2.3 %pack_inputs.1 = (bf16[1056,128]{1,0:T(8,128)(2,1)}, bf16[1056,128]{1,0:T(8,128)(2,1)}, bf16[1056,128]{1,0:T(8,128)(2,1)}, bf16[1056,128]{1,0:T(8,128)(2,1)}) custom-call(bf16[192,768]{1,0:T(8,128)(2,1)} %q_ref, bf16[192,768]{1,0:T(8,128)(2,1)} %k_ref, bf16[192,768]{1,0:T(8,128)(2,1)} %v_ref), custom_call_target="tpu_custom_call" | custom-call | flops 40000000000 | tf_op jit(solution)/shard_map/pack_inputs/pallas_call | solution.py:255
  8.9 1.6 %collective-permute-start.1 = (bf16[1056,128]{1,0:T(8,128)(2,1)}, bf16[1056,128]{1,0:T(8,128)(2,1)S(1)}, u32[]{:S(2)}, u32[]{:S(2)}) collective-permute-start(bf16[1056,128]{1,0:T(8,128)(2,1)} %get-tuple-element.83), channel_id=1, source_target_pairs={{0,1},{1,0},{2,3},{3,2},{4,5},{5,4},{6,7},{7,6},{8,9},{9,8},{10,11... | collective-permute-start | bytes 811016 | tf_op jit(solution)/shard_map/ppermute | solution.py:399
  12.4 6.0 %collective-permute-done.1 = bf16[1056,128]{1,0:T(8,128)(2,1)S(1)} collective-permute-done((bf16[1056,128]{1,0:T(8,128)(2,1)}, bf16[1056,128]{1,0:T(8,128)(2,1)S(1)}, u32[]{:S(2)}, u32[]{:S(2)}) %collective-permute-start.1) | collective-permute-done | bytes 270368 | tf_op jit(solution)/shard_map/ppermute | solution.py:399
  18.4 6.7 %collective-permute-done.2 = bf16[1056,128]{1,0:T(8,128)(2,1)S(1)} collective-permute-done((bf16[1056,128]{1,0:T(8,128)(2,1)}, bf16[1056,128]{1,0:T(8,128)(2,1)S(1)}, u32[]{:S(2)}, u32[]{:S(2)}) %collective-permute-start.2) | collective-permute-done | bytes 270368 | tf_op jit(solution)/shard_map/ppermute | solution.py:399
  26.0 3.8 %collective-permute-start.5 = (bf16[1056,128]{1,0:T(8,128)(2,1)S(1)}, bf16[1056,128]{1,0:T(8,128)(2,1)S(1)}, u32[]{:S(2)}, u32[]{:S(2)}) collective-permute-start(bf16[1056,128]{1,0:T(8,128)(2,1)S(1)} %get-tuple-element.172), channel_id=1, source_target_pairs={{0,24},{4,28},{8,0},{12,4},{16,8},{20,12},{24,16},{28,20},{1,25},{... | collective-permute-start | bytes 811016 | tf_op jit(solution)/shard_map/ppermute | solution.py:402
  29.8 3.2 %collective-permute-done.8.refs_2_.refs_6_ = bf16[192,1536]{1,0:T(8,128)(2,1)} collective-permute-done((bf16[192,1536]{1,0:T(8,128)(2,1)}, bf16[192,1536]{1,0:T(8,128)(2,1)}, u32[]{:S(2)}, u32[]{:S(2)}) %collective-permute-start.8) | collective-permute-done | bytes 589856 | tf_op jit(solution)/shard_map/ppermute | solution.py:402
  33.1 3.8 %grad_pieces.2 = (bf16[864,128]{1,0:T(8,128)(2,1)S(1)}, bf16[864,128]{1,0:T(8,128)(2,1)S(1)}, bf16[864,128]{1,0:T(8,128)(2,1)S(1)}, bf16[864,128]{1,0:T(8,128)(2,1)S(1)}) custom-call(bf16[192,1536]{1,0:T(8,128)(2,1)S(1)} %copy-done.1, bf16[192,1536]{1,0:T(8,128)(2,1)} %collective-permute-done.7.refs_1_.refs_5_, ...), custom_call_target="tpu_custom_call" | custom-call | flops 40000000000 | tf_op jit(solution)/shard_map/grad_pieces/pallas_call | solution.py:287
  38.6 4.3 %collective-permute-done.5.refs_2_ = bf16[1056,128]{1,0:T(8,128)(2,1)S(1)} collective-permute-done((bf16[1056,128]{1,0:T(8,128)(2,1)S(1)}, bf16[1056,128]{1,0:T(8,128)(2,1)S(1)}, u32[]{:S(2)}, u32[]{:S(2)}) %collective-permute-start.5) | collective-permute-done | bytes 270368 | tf_op jit(solution)/shard_map/ppermute | solution.py:402
  42.9 12.2 %collective-permute-done.6.refs_3_ = bf16[1056,128]{1,0:T(8,128)(2,1)S(1)} collective-permute-done((bf16[1056,128]{1,0:T(8,128)(2,1)S(1)}, bf16[1056,128]{1,0:T(8,128)(2,1)S(1)}, u32[]{:S(2)}, u32[]{:S(2)}) %collective-permute-start.6) | collective-permute-done | bytes 270368 | tf_op jit(solution)/shard_map/ppermute | solution.py:402
  55.8 2.2 %join.1 = (bf16[1152,128]{1,0:T(8,128)(2,1)}, bf16[4,768,128]{2,1,0:T(8,128)(2,1)}) custom-call(bf16[1056,128]{1,0:T(8,128)(2,1)} %get-tuple-element.94.refs_0_, bf16[1056,128]{1,0:T(8,128)(2,1)} %copy-done.7, bf16[1056,128]{1,0:T(8,128)(2,1)} %copy-done.8, bf16[1056,128]{1,0:T(8,128)(2,1)} %copy-done.9), custom_call_target="tpu_custom_call" | custom-call | flops 1000000 | bytes 1000 | tf_op jit(solution)/shard_map/join/pallas_call | solution.py:354
  59.6 1.5 collective-permute-start.18
  65.0 5.5 %attention_forward.1 = (bf16[3,1536,384]{2,1,0:T(8,128)(2,1)}, bf16[1152,128]{1,0:T(8,128)(2,1)S(1)}) custom-call(bf16[1152,128]{1,0:T(8,128)(2,1)S(1)} %copy-done.2, bf16[2,1536,128]{2,1,0:T(8,128)(2,1)S(1)} %get-tuple-element.146.k_ref, bf16[2,1536,128]{2,1,0:T(8,128)(2,1)S(1)} %get-tuple-element.145.v_ref), custom_call_target="tpu_custom_call" | custom-call | flops 40000000000 | tf_op jit(solution)/shard_map/attention_forward/pallas_call | solution.py:144
  70.5 1.5 collective-permute-start.12
  72.0 1.5 collective-permute-start.13
  74.1 1.5 collective-permute-start.10
  75.7 2.7 %collective-permute-done.15.refs_0_.refs_7_ = bf16[192,1536]{1,0:T(8,128)(2,1)S(1)} collective-permute-done((bf16[192,1536]{1,0:T(8,128)(2,1)}, bf16[192,1536]{1,0:T(8,128)(2,1)S(1)}, u32[]{:S(2)}, u32[]{:S(2)}) %collective-permute-start.15) | collective-permute-done | bytes 589856 | tf_op jit(solution)/shard_map/ppermute | solution.py:402
  83.6 1.8 %collective-permute-start.22 = (bf16[288,128]{1,0:T(8,128)(2,1)S(1)}, bf16[288,128]{1,0:T(8,128)(2,1)S(1)}, u32[]{:S(2)}, u32[]{:S(2)}) collective-permute-start(bf16[288,128]{1,0:T(8,128)(2,1)S(1)} %get-tuple-element.115), channel_id=1, source_target_pairs={{0,3},{1,2},{2,1},{3,0},{4,7},{5,6},{6,5},{7,4},{8,11},{9,10},{10,... | collective-permute-start | bytes 221192 | tf_op jit(solution)/shard_map/ppermute | solution.py:399
  87.1 1.7 %collective-permute-done.22.refs_3_ = bf16[288,128]{1,0:T(8,128)(2,1)S(1)} collective-permute-done((bf16[288,128]{1,0:T(8,128)(2,1)S(1)}, bf16[288,128]{1,0:T(8,128)(2,1)S(1)}, u32[]{:S(2)}, u32[]{:S(2)}) %collective-permute-start.22) | collective-permute-done | bytes 73760 | tf_op jit(solution)/shard_map/ppermute | solution.py:399
  88.8 5.3 %attention_backward.1 = (bf16[1152,128]{1,0:T(8,128)(2,1)S(1)}, f32[2,2,768,128]{3,2,1,0:T(8,128)S(1)}, bf16[2,2,768,128]{3,2,1,0:T(8,128)(2,1)S(1)}) custom-call(bf16[1152,128]{1,0:T(8,128)(2,1)S(1)} %copy-done.2, bf16[2,1536,128]{2,1,0:T(8,128)(2,1)S(1)} %get-tuple-element.146.k_ref, bf16[2,1536,128]{2,1,0:T(8,128)(2,1)S(1)} %get-tuple-element.145.v_ref, ...), custom_call_target="tpu_custom_call" | custom-call | flops 40000000000 | tf_op jit(solution)/shard_map/attention_backward/pallas_call | solution.py:212
  97.0 3.8 %collective-permute-start.27 = (bf16[1056,128]{1,0:T(8,128)(2,1)S(1)}, bf16[1056,128]{1,0:T(8,128)(2,1)S(1)}, u32[]{:S(2)}, u32[]{:S(2)}) collective-permute-start(bf16[1056,128]{1,0:T(8,128)(2,1)S(1)} %get-tuple-element.185), channel_id=1, source_target_pairs={{0,24},{4,28},{8,0},{12,4},{16,8},{20,12},{24,16},{28,20},{1,25},{... | collective-permute-start | bytes 811016 | tf_op jit(solution)/shard_map/ppermute | solution.py:402
  101.4 1.9 %collective-permute-start.29 = (bf16[1056,128]{1,0:T(8,128)(2,1)S(1)}, bf16[1056,128]{1,0:T(8,128)(2,1)S(1)}, u32[]{:S(2)}, u32[]{:S(2)}) collective-permute-start(bf16[1056,128]{1,0:T(8,128)(2,1)S(1)} %get-tuple-element.183), channel_id=1, source_target_pairs={{0,8},{4,12},{8,16},{12,20},{16,24},{20,28},{24,0},{28,4},{1,9},{5... | collective-permute-start | bytes 811016 | tf_op jit(solution)/shard_map/ppermute | solution.py:402
  103.4 4.6 %collective-permute-done.11 = bf16[2,864,128]{2,1,0:T(8,128)(2,1)S(1)} collective-permute-done((bf16[2,864,128]{2,1,0:T(8,128)(2,1)S(1)}, bf16[2,864,128]{2,1,0:T(8,128)(2,1)S(1)}, u32[]{:S(2)}, u32[]{:S(2)}) %collective-permute-start.11) | collective-permute-done | bytes 442400 | tf_op jit(solution)/shard_map/ppermute | solution.py:399
  108.6 3.1 %weight_grad.2 = bf16[384,1536]{1,0:T(8,128)(2,1)S(1)} custom-call(bf16[192,384]{1,0:T(8,128)(2,1)S(1)} %get-tuple-element.121.refs_0_, bf16[192,384]{1,0:T(8,128)(2,1)S(1)} %get-tuple-element.122.refs_1_, bf16[192,384]{1,0:T(8,128)(2,1)S(1)} %get-tuple-element.123.refs_2_, bf16[192,384]{1,0:T(8,128)(2,1)S(1)} %get-tuple-element.124.refs_3_, ...), custom_call_target="tpu_custom_call" | custom-call | flops 40000000000 | tf_op jit(solution)/shard_map/weight_grad/pallas_call | solution.py:331
  112.5 3.9 %collective-permute-start.30 = (bf16[192,1536]{1,0:T(8,128)(2,1)S(1)}, bf16[192,1536]{1,0:T(8,128)(2,1)S(1)}, u32[]{:S(2)}, u32[]{:S(2)}) collective-permute-start(bf16[192,1536]{1,0:T(8,128)(2,1)S(1)} %mixed_term.5), channel_id=1, source_target_pairs={{0,24},{4,28},{8,0},{12,4},{16,8},{20,12},{24,16},{28,20},{1,25},{... | collective-permute-start | bytes 1769480 | tf_op jit(solution)/shard_map/ppermute | solution.py:402
  118.1 8.0 %collective-permute-done.28 = bf16[1056,128]{1,0:T(8,128)(2,1)S(1)} collective-permute-done((bf16[1056,128]{1,0:T(8,128)(2,1)S(1)}, bf16[1056,128]{1,0:T(8,128)(2,1)S(1)}, u32[]{:S(2)}, u32[]{:S(2)}) %collective-permute-start.28) | collective-permute-done | bytes 270368 | tf_op jit(solution)/shard_map/ppermute | solution.py:402
  126.1 11.7 %collective-permute-done.30 = bf16[192,1536]{1,0:T(8,128)(2,1)S(1)} collective-permute-done((bf16[192,1536]{1,0:T(8,128)(2,1)S(1)}, bf16[192,1536]{1,0:T(8,128)(2,1)S(1)}, u32[]{:S(2)}, u32[]{:S(2)}) %collective-permute-start.30) | collective-permute-done | bytes 589856 | tf_op jit(solution)/shard_map/ppermute | solution.py:402
  138.0 1.6 collective-permute-start.32
  142.3 4.1 %weight_grad.3 = bf16[384,1536]{1,0:T(8,128)(2,1)} custom-call(bf16[192,384]{1,0:T(8,128)(2,1)S(1)} %get-tuple-element.135.refs_0_, bf16[192,384]{1,0:T(8,128)(2,1)S(1)} %get-tuple-element.136.refs_1_, bf16[192,384]{1,0:T(8,128)(2,1)S(1)} %get-tuple-element.137.refs_2_, bf16[192,384]{1,0:T(8,128)(2,1)S(1)} %get-tuple-element.138.refs_3_, ...), custom_call_target="tpu_custom_call" | custom-call | flops 40000000000 | tf_op jit(solution)/shard_map/weight_grad/pallas_call | solution.py:331
  147.5 6.1 %collective-permute-done.33 = bf16[1056,128]{1,0:T(8,128)(2,1)S(1)} collective-permute-done((bf16[1056,128]{1,0:T(8,128)(2,1)S(1)}, bf16[1056,128]{1,0:T(8,128)(2,1)S(1)}, u32[]{:S(2)}, u32[]{:S(2)}) %collective-permute-start.33) | collective-permute-done | bytes 270368 | tf_op jit(solution)/shard_map/ppermute | solution.py:399
  153.5 4.2 %collective-permute-done.35 = bf16[192,1536]{1,0:T(8,128)(2,1)S(1)} collective-permute-done((bf16[192,1536]{1,0:T(8,128)(2,1)S(1)}, bf16[192,1536]{1,0:T(8,128)(2,1)S(1)}, u32[]{:S(2)}, u32[]{:S(2)}) %collective-permute-start.35) | collective-permute-done | bytes 589856 | tf_op jit(solution)/shard_map/ppermute | solution.py:402
  (144 shorter events, 31.7 us)
Async XLA Ops:
  0.6 29.2 %collective-permute-start.7 = (bf16[192,1536]{1,0:T(8,128)(2,1)}, bf16[192,1536]{1,0:T(8,128)(2,1)}, u32[]{:S(2)}, u32[]{:S(2)}) collective-permute-start(bf16[192,1536]{1,0:T(8,128)(2,1)} %refs_4_.3), channel_id=1, source_target_pairs={{0,8},{4,12},{8,16},{12,20},{16,24},{20,28},{24,0},{28,4},{1,9},{5... | collective-permute-start | bytes 1769480 | tf_op jit(solution)/shard_map/ppermute | solution.py:402
  3.7 29.3 %collective-permute-start.8 = (bf16[192,1536]{1,0:T(8,128)(2,1)}, bf16[192,1536]{1,0:T(8,128)(2,1)}, u32[]{:S(2)}, u32[]{:S(2)}) collective-permute-start(bf16[192,1536]{1,0:T(8,128)(2,1)} %refs_4_.3), channel_id=1, source_target_pairs={{0,24},{4,28},{8,0},{12,4},{16,8},{20,12},{24,16},{28,20},{1,25},{... | collective-permute-start | bytes 1769480 | tf_op jit(solution)/shard_map/ppermute | solution.py:402
  5.8 3.1 %collective-permute-start = (bf16[384,1536]{1,0:T(8,128)(2,1)}, bf16[384,1536]{1,0:T(8,128)(2,1)S(1)}, u32[]{:S(2)}, u32[]{:S(2)}) collective-permute-start(bf16[384,1536]{1,0:T(8,128)(2,1)} %own_ref.7), channel_id=1, source_target_pairs={{0,4},{4,0},{8,12},{12,8},{16,20},{20,16},{24,28},{28,24},{1,5},{5... | collective-permute-start | bytes 3538952 | tf_op jit(solution)/shard_map/ppermute | solution.py:405
  8.9 9.5 %collective-permute-start.1 = (bf16[1056,128]{1,0:T(8,128)(2,1)}, bf16[1056,128]{1,0:T(8,128)(2,1)S(1)}, u32[]{:S(2)}, u32[]{:S(2)}) collective-permute-start(bf16[1056,128]{1,0:T(8,128)(2,1)} %get-tuple-element.83), channel_id=1, source_target_pairs={{0,1},{1,0},{2,3},{3,2},{4,5},{5,4},{6,7},{7,6},{8,9},{9,8},{10,11... | collective-permute-start | bytes 811016 | tf_op jit(solution)/shard_map/ppermute | solution.py:399
  10.5 14.5 %collective-permute-start.2 = (bf16[1056,128]{1,0:T(8,128)(2,1)}, bf16[1056,128]{1,0:T(8,128)(2,1)S(1)}, u32[]{:S(2)}, u32[]{:S(2)}) collective-permute-start(bf16[1056,128]{1,0:T(8,128)(2,1)} %get-tuple-element.84), channel_id=1, source_target_pairs={{0,2},{1,3},{2,0},{3,1},{4,6},{5,7},{6,4},{7,5},{8,10},{9,11},{10,... | collective-permute-start | bytes 811016 | tf_op jit(solution)/shard_map/ppermute | solution.py:399
  12.0 13.0 %collective-permute-start.3 = (bf16[1056,128]{1,0:T(8,128)(2,1)}, bf16[1056,128]{1,0:T(8,128)(2,1)S(1)}, u32[]{:S(2)}, u32[]{:S(2)}) collective-permute-start(bf16[1056,128]{1,0:T(8,128)(2,1)} %get-tuple-element.85), channel_id=1, source_target_pairs={{0,3},{1,2},{2,1},{3,0},{4,7},{5,6},{6,5},{7,4},{8,11},{9,10},{10,... | collective-permute-start | bytes 811016 | tf_op jit(solution)/shard_map/ppermute | solution.py:399
  26.0 12.6 %collective-permute-start.4 = (bf16[1056,128]{1,0:T(8,128)(2,1)S(1)}, bf16[1056,128]{1,0:T(8,128)(2,1)S(1)}, u32[]{:S(2)}, u32[]{:S(2)}) collective-permute-start(bf16[1056,128]{1,0:T(8,128)(2,1)S(1)} %get-tuple-element.173), channel_id=1, source_target_pairs={{0,8},{4,12},{8,16},{12,20},{16,24},{20,28},{24,0},{28,4},{1,9},{5... | collective-permute-start | bytes 811016 | tf_op jit(solution)/shard_map/ppermute | solution.py:402
  26.0 16.9 %collective-permute-start.5 = (bf16[1056,128]{1,0:T(8,128)(2,1)S(1)}, bf16[1056,128]{1,0:T(8,128)(2,1)S(1)}, u32[]{:S(2)}, u32[]{:S(2)}) collective-permute-start(bf16[1056,128]{1,0:T(8,128)(2,1)S(1)} %get-tuple-element.172), channel_id=1, source_target_pairs={{0,24},{4,28},{8,0},{12,4},{16,8},{20,12},{24,16},{28,20},{1,25},{... | collective-permute-start | bytes 811016 | tf_op jit(solution)/shard_map/ppermute | solution.py:402
  29.8 25.3 %collective-permute-start.6 = (bf16[1056,128]{1,0:T(8,128)(2,1)S(1)}, bf16[1056,128]{1,0:T(8,128)(2,1)S(1)}, u32[]{:S(2)}, u32[]{:S(2)}) collective-permute-start(bf16[1056,128]{1,0:T(8,128)(2,1)S(1)} %get-tuple-element.171), channel_id=1, source_target_pairs={{0,16},{4,20},{8,24},{12,28},{16,0},{20,4},{24,8},{28,12},{1,17},{... | collective-permute-start | bytes 811016 | tf_op jit(solution)/shard_map/ppermute | solution.py:402
  58.0 4.7 %collective-permute-start.9 = (bf16[4,768,128]{2,1,0:T(8,128)(2,1)}, bf16[4,768,128]{2,1,0:T(8,128)(2,1)}, u32[]{:S(2)}, u32[]{:S(2)}) collective-permute-start(bf16[4,768,128]{2,1,0:T(8,128)(2,1)} %get-tuple-element.99), channel_id=1, source_target_pairs={{0,4},{4,0},{8,12},{12,8},{16,20},{20,16},{24,28},{28,24},{1,5},{5... | collective-permute-start | bytes 2359304 | tf_op jit(solution)/shard_map/ppermute | solution.py:405
  58.1 14.0 %collective-permute-start.17 = (bf16[864,128]{1,0:T(8,128)(2,1)}, bf16[864,128]{1,0:T(8,128)(2,1)S(1)}, u32[]{:S(2)}, u32[]{:S(2)}) collective-permute-start(bf16[864,128]{1,0:T(8,128)(2,1)} %copy-done.4), channel_id=1, source_target_pairs={{0,1},{1,0},{2,3},{3,2},{4,5},{5,4},{6,7},{7,6},{8,9},{9,8},{10,11... | collective-permute-start | bytes 663560 | tf_op jit(solution)/shard_map/ppermute | solution.py:399
  59.6 14.0 %collective-permute-start.18 = (bf16[864,128]{1,0:T(8,128)(2,1)}, bf16[864,128]{1,0:T(8,128)(2,1)S(1)}, u32[]{:S(2)}, u32[]{:S(2)}) collective-permute-start(bf16[864,128]{1,0:T(8,128)(2,1)} %copy-done.3), channel_id=1, source_target_pairs={{0,2},{1,3},{2,0},{3,1},{4,6},{5,7},{6,4},{7,5},{8,10},{9,11},{10,... | collective-permute-start | bytes 663560 | tf_op jit(solution)/shard_map/ppermute | solution.py:399
  61.1 13.0 %collective-permute-start.19 = (bf16[864,128]{1,0:T(8,128)(2,1)S(1)}, bf16[864,128]{1,0:T(8,128)(2,1)S(1)}, u32[]{:S(2)}, u32[]{:S(2)}) collective-permute-start(bf16[864,128]{1,0:T(8,128)(2,1)S(1)} %get-tuple-element.107), channel_id=1, source_target_pairs={{0,3},{1,2},{2,1},{3,0},{4,7},{5,6},{6,5},{7,4},{8,11},{9,10},{10,... | collective-permute-start | bytes 663560 | tf_op jit(solution)/shard_map/ppermute | solution.py:399
  61.6 16.9 %collective-permute-start.15 = (bf16[192,1536]{1,0:T(8,128)(2,1)}, bf16[192,1536]{1,0:T(8,128)(2,1)S(1)}, u32[]{:S(2)}, u32[]{:S(2)}) collective-permute-start(bf16[192,1536]{1,0:T(8,128)(2,1)} %collective-permute-done.7.refs_1_.refs_5_), channel_id=1, source_target_pairs={{0,8},{4,12},{8,16},{12,20},{16,24},{20,28},{24,0},{28,4},{1,9},{5... | collective-permute-start | bytes 1769480 | tf_op jit(solution)/shard_map/ppermute | solution.py:402
  70.5 8.0 %collective-permute-start.12 = (bf16[288,128]{1,0:T(8,128)(2,1)S(1)}, bf16[288,128]{1,0:T(8,128)(2,1)S(1)}, u32[]{:S(2)}, u32[]{:S(2)}) collective-permute-start(bf16[288,128]{1,0:T(8,128)(2,1)S(1)} %get-tuple-element.225), channel_id=1, source_target_pairs={{0,1},{1,0},{2,3},{3,2},{4,5},{5,4},{6,7},{7,6},{8,9},{9,8},{10,11... | collective-permute-start | bytes 221192 | tf_op jit(solution)/shard_map/ppermute | solution.py:399
  72.0 6.4 %collective-permute-start.13 = (bf16[288,128]{1,0:T(8,128)(2,1)S(1)}, bf16[288,128]{1,0:T(8,128)(2,1)S(1)}, u32[]{:S(2)}, u32[]{:S(2)}) collective-permute-start(bf16[288,128]{1,0:T(8,128)(2,1)S(1)} %get-tuple-element.225), channel_id=1, source_target_pairs={{0,2},{1,3},{2,0},{3,1},{4,6},{5,7},{6,4},{7,5},{8,10},{9,11},{10,... | collective-permute-start | bytes 221192 | tf_op jit(solution)/shard_map/ppermute | solution.py:399
  73.5 6.1 %collective-permute-start.14 = (bf16[288,128]{1,0:T(8,128)(2,1)S(1)}, bf16[288,128]{1,0:T(8,128)(2,1)S(1)}, u32[]{:S(2)}, u32[]{:S(2)}) collective-permute-start(bf16[288,128]{1,0:T(8,128)(2,1)S(1)} %get-tuple-element.225), channel_id=1, source_target_pairs={{0,3},{1,2},{2,1},{3,0},{4,7},{5,6},{6,5},{7,4},{8,11},{9,10},{10,... | collective-permute-start | bytes 221192 | tf_op jit(solution)/shard_map/ppermute | solution.py:399
  74.1 20.8 %collective-permute-start.10 = (bf16[864,128]{1,0:T(8,128)(2,1)S(1)}, bf16[864,128]{1,0:T(8,128)(2,1)S(1)}, u32[]{:S(2)}, u32[]{:S(2)}) collective-permute-start(bf16[864,128]{1,0:T(8,128)(2,1)S(1)} %get-tuple-element.223), channel_id=1, source_target_pairs={{0,1},{1,0},{2,3},{3,2},{4,5},{5,4},{6,7},{7,6},{8,9},{9,8},{10,11... | collective-permute-start | bytes 663560 | tf_op jit(solution)/shard_map/ppermute | solution.py:399
  80.7 27.2 %collective-permute-start.16 = (bf16[192,1536]{1,0:T(8,128)(2,1)S(1)}, bf16[192,1536]{1,0:T(8,128)(2,1)S(1)}, u32[]{:S(2)}, u32[]{:S(2)}) collective-permute-start(bf16[192,1536]{1,0:T(8,128)(2,1)S(1)} %mixed_term.4), channel_id=1, source_target_pairs={{0,8},{4,12},{8,16},{12,20},{16,24},{20,28},{24,0},{28,4},{1,9},{5... | collective-permute-start | bytes 1769480 | tf_op jit(solution)/shard_map/ppermute | solution.py:402
  81.8 4.4 %collective-permute-start.20 = (bf16[288,128]{1,0:T(8,128)(2,1)S(1)}, bf16[288,128]{1,0:T(8,128)(2,1)S(1)}, u32[]{:S(2)}, u32[]{:S(2)}) collective-permute-start(bf16[288,128]{1,0:T(8,128)(2,1)S(1)} %get-tuple-element.113), channel_id=1, source_target_pairs={{0,1},{1,0},{2,3},{3,2},{4,5},{5,4},{6,7},{7,6},{8,9},{9,8},{10,11... | collective-permute-start | bytes 221192 | tf_op jit(solution)/shard_map/ppermute | solution.py:399
  82.4 4.8 %collective-permute-start.21 = (bf16[288,128]{1,0:T(8,128)(2,1)S(1)}, bf16[288,128]{1,0:T(8,128)(2,1)S(1)}, u32[]{:S(2)}, u32[]{:S(2)}) collective-permute-start(bf16[288,128]{1,0:T(8,128)(2,1)S(1)} %get-tuple-element.114), channel_id=1, source_target_pairs={{0,2},{1,3},{2,0},{3,1},{4,6},{5,7},{6,4},{7,5},{8,10},{9,11},{10,... | collective-permute-start | bytes 221192 | tf_op jit(solution)/shard_map/ppermute | solution.py:399
  83.6 5.3 %collective-permute-start.22 = (bf16[288,128]{1,0:T(8,128)(2,1)S(1)}, bf16[288,128]{1,0:T(8,128)(2,1)S(1)}, u32[]{:S(2)}, u32[]{:S(2)}) collective-permute-start(bf16[288,128]{1,0:T(8,128)(2,1)S(1)} %get-tuple-element.115), channel_id=1, source_target_pairs={{0,3},{1,2},{2,1},{3,0},{4,7},{5,6},{6,5},{7,4},{8,11},{9,10},{10,... | collective-permute-start | bytes 221192 | tf_op jit(solution)/shard_map/ppermute | solution.py:399
  95.7 12.2 %collective-permute-start.11 = (bf16[2,864,128]{2,1,0:T(8,128)(2,1)S(1)}, bf16[2,864,128]{2,1,0:T(8,128)(2,1)S(1)}, u32[]{:S(2)}, u32[]{:S(2)}) collective-permute-start(bf16[2,864,128]{2,1,0:T(8,128)(2,1)S(1)} %pad_maximum_fusion.3), channel_id=1, source_target_pairs={{0,2},{1,3},{2,0},{3,1},{4,6},{5,7},{6,4},{7,5},{8,10},{9,11},{10,... | collective-permute-start | bytes 1327112 | tf_op jit(solution)/shard_map/ppermute | solution.py:399
  97.0 21.1 %collective-permute-start.27 = (bf16[1056,128]{1,0:T(8,128)(2,1)S(1)}, bf16[1056,128]{1,0:T(8,128)(2,1)S(1)}, u32[]{:S(2)}, u32[]{:S(2)}) collective-permute-start(bf16[1056,128]{1,0:T(8,128)(2,1)S(1)} %get-tuple-element.185), channel_id=1, source_target_pairs={{0,24},{4,28},{8,0},{12,4},{16,8},{20,12},{24,16},{28,20},{1,25},{... | collective-permute-start | bytes 811016 | tf_op jit(solution)/shard_map/ppermute | solution.py:402
  100.8 25.3 %collective-permute-start.28 = (bf16[1056,128]{1,0:T(8,128)(2,1)S(1)}, bf16[1056,128]{1,0:T(8,128)(2,1)S(1)}, u32[]{:S(2)}, u32[]{:S(2)}) collective-permute-start(bf16[1056,128]{1,0:T(8,128)(2,1)S(1)} %get-tuple-element.184), channel_id=1, source_target_pairs={{0,16},{4,20},{8,24},{12,28},{16,0},{20,4},{24,8},{28,12},{1,17},{... | collective-permute-start | bytes 811016 | tf_op jit(solution)/shard_map/ppermute | solution.py:402
  101.4 24.7 %collective-permute-start.29 = (bf16[1056,128]{1,0:T(8,128)(2,1)S(1)}, bf16[1056,128]{1,0:T(8,128)(2,1)S(1)}, u32[]{:S(2)}, u32[]{:S(2)}) collective-permute-start(bf16[1056,128]{1,0:T(8,128)(2,1)S(1)} %get-tuple-element.183), channel_id=1, source_target_pairs={{0,8},{4,12},{8,16},{12,20},{16,24},{20,28},{24,0},{28,4},{1,9},{5... | collective-permute-start | bytes 811016 | tf_op jit(solution)/shard_map/ppermute | solution.py:402
  111.7 26.1 %collective-permute-start.31 = (bf16[384,1536]{1,0:T(8,128)(2,1)S(1)}, bf16[384,1536]{1,0:T(8,128)(2,1)S(1)}, u32[]{:S(2)}, u32[]{:S(2)}) collective-permute-start(bf16[384,1536]{1,0:T(8,128)(2,1)S(1)} %weight_grad.2), channel_id=1, source_target_pairs={{0,4},{4,0},{8,12},{12,8},{16,20},{20,16},{24,28},{28,24},{1,5},{5... | collective-permute-start | bytes 3538952 | tf_op jit(solution)/shard_map/ppermute | solution.py:405
  112.5 25.3 %collective-permute-start.30 = (bf16[192,1536]{1,0:T(8,128)(2,1)S(1)}, bf16[192,1536]{1,0:T(8,128)(2,1)S(1)}, u32[]{:S(2)}, u32[]{:S(2)}) collective-permute-start(bf16[192,1536]{1,0:T(8,128)(2,1)S(1)} %mixed_term.5), channel_id=1, source_target_pairs={{0,24},{4,28},{8,0},{12,4},{16,8},{20,12},{24,16},{28,20},{1,25},{... | collective-permute-start | bytes 1769480 | tf_op jit(solution)/shard_map/ppermute | solution.py:402
  138.0 9.4 %collective-permute-start.32 = (bf16[1056,128]{1,0:T(8,128)(2,1)S(1)}, bf16[1056,128]{1,0:T(8,128)(2,1)S(1)}, u32[]{:S(2)}, u32[]{:S(2)}) collective-permute-start(bf16[1056,128]{1,0:T(8,128)(2,1)S(1)} %get-tuple-element.169), channel_id=1, source_target_pairs={{0,1},{1,0},{2,3},{3,2},{4,5},{5,4},{6,7},{7,6},{8,9},{9,8},{10,11... | collective-permute-start | bytes 811016 | tf_op jit(solution)/shard_map/ppermute | solution.py:399
  139.6 13.9 %collective-permute-start.33 = (bf16[1056,128]{1,0:T(8,128)(2,1)S(1)}, bf16[1056,128]{1,0:T(8,128)(2,1)S(1)}, u32[]{:S(2)}, u32[]{:S(2)}) collective-permute-start(bf16[1056,128]{1,0:T(8,128)(2,1)S(1)} %get-tuple-element.168), channel_id=1, source_target_pairs={{0,2},{1,3},{2,0},{3,1},{4,6},{5,7},{6,4},{7,5},{8,10},{9,11},{10,... | collective-permute-start | bytes 811016 | tf_op jit(solution)/shard_map/ppermute | solution.py:399
  140.8 12.7 %collective-permute-start.34 = (bf16[1056,128]{1,0:T(8,128)(2,1)S(1)}, bf16[1056,128]{1,0:T(8,128)(2,1)S(1)}, u32[]{:S(2)}, u32[]{:S(2)}) collective-permute-start(bf16[1056,128]{1,0:T(8,128)(2,1)S(1)} %get-tuple-element.167), channel_id=1, source_target_pairs={{0,3},{1,2},{2,1},{3,0},{4,7},{5,6},{6,5},{7,4},{8,11},{9,10},{10,... | collective-permute-start | bytes 811016 | tf_op jit(solution)/shard_map/ppermute | solution.py:399
  141.6 16.2 %collective-permute-start.35 = (bf16[192,1536]{1,0:T(8,128)(2,1)S(1)}, bf16[192,1536]{1,0:T(8,128)(2,1)S(1)}, u32[]{:S(2)}, u32[]{:S(2)}) collective-permute-start(bf16[192,1536]{1,0:T(8,128)(2,1)S(1)} %add_convert_fusion.2), channel_id=1, source_target_pairs={{0,8},{4,12},{8,16},{12,20},{16,24},{20,28},{24,0},{28,4},{1,9},{5... | collective-permute-start | bytes 1769480 | tf_op jit(solution)/shard_map/ppermute | solution.py:402
  (18 other events, 82.0 us)

commit v4 on v3

--- a/solution.py
+++ b/solution.py
@@ -129,55 +129,82 @@
     return lax.dot_general(a, b, (((0,), (0,)), ((), ())), preferred_element_type=F32)
 
 
-def forward_kernel(q_ref, k_ref, v_ref, p_ref, attn_ref):
-    raw = nt(k_ref[0], q_ref[...])
+def forward_kernel(*refs):
+    own_refs, other_refs, (p_ref, attn_ref, q_ref, k_ref, v_ref) = refs[:PLANES], refs[PLANES:-5], refs[-5:]
+    step = pl.program_id(0)
+    rows = attn_ref.shape[0]
+
+    @pl.when(step == 0)
+    def _():
+        tokens = k_ref.shape[1] // (2 * PLANES)
+        half = tokens // 2
+        for p, own_ref in enumerate(own_refs):
+            q_ref[p * tokens : (p + 1) * tokens] = own_ref[:tokens]
+            at = PLANES * tokens + p * half
+            q_ref[at : at + half] = own_ref[tokens : tokens + half]
+        for p, in_ref in enumerate(own_refs + other_refs):
+            for i in range(4):
+                at = tokens + half + i * tokens
+                out_ref = (k_ref, v_ref)[i // 2]
+                out_ref[i % 2, p * tokens : (p + 1) * tokens] = in_ref[at : at + tokens]
+
+    head = lax.div(step, 2)
+    raw = nt(k_ref[head], q_ref[pl.ds(pl.multiple_of(step * rows, rows), rows)])
     top = jnp.max(raw, axis=0, keepdims=True)
     e = jnp.exp2((raw - top) * (SCALE * LOG2E))
     total = jnp.sum(e, axis=0, keepdims=True)
     probs = (e * (1.0 / total)).astype(BF16)
     p_ref[0] = probs
-    attn_ref[...] = tn(v_ref[0], probs).T.astype(BF16)
-
-
-def attention_forward(q, k, v):
-    rows, keys = q.shape[0] // 3, k.shape[1]
+    attn_ref[...] = tn(v_ref[head], probs).T.astype(BF16)
+
+
+def attention_forward(own, other, tokens):
+    rows, keys = 2 * tokens, 2 * PLANES * tokens
+
+    def whole(*shape):
+        return pl.BlockSpec(shape, lambda i: (0,) * len(shape))
+
     return pl.pallas_call(
         forward_kernel,
         grid=(3,),
-        in_specs=[
-            pl.BlockSpec((rows, HD), lambda i: (i, 0)),
-            pl.BlockSpec((1, keys, HD), lambda i: (i // 2, 0, 0)),
-            pl.BlockSpec((1, keys, HD), lambda i: (i // 2, 0, 0)),
-        ],
+        in_specs=[whole(*own[0].shape)] * (2 * PLANES),
         out_specs=[
             pl.BlockSpec((1, keys, rows), lambda i: (i, 0, 0)),
             pl.BlockSpec((rows, HD), lambda i: (i, 0)),
+            whole(3 * rows, HD),
+            whole(2, keys, HD),
+            whole(2, keys, HD),
         ],
         out_shape=[
             pltpu.HBM((3, keys, rows), BF16),
             jax.ShapeDtypeStruct((3 * rows, HD), BF16),
+            jax.ShapeDtypeStruct((3 * rows, HD), BF16),
+            jax.ShapeDtypeStruct((2, keys, HD), BF16),
+            jax.ShapeDtypeStruct((2, keys, HD), BF16),
         ],
-        compiler_params=pltpu.CompilerParams(vmem_limit_bytes=16 * 2**20),
+        compiler_params=pltpu.CompilerParams(vmem_limit_bytes=24 * 2**20),
         cost_estimate=WINDOW,
         name="attention_forward",
-    )(q, k, v)
+    )(*own, *other)
 
 
 def backward_kernel(
-    q_ref, k_ref, v_ref, p_ref, attn_ref, early_ref, *refs
+    q_ref, k_ref, v_ref, p_ref, attn_ref, *refs
 ):
-    late_refs, (dq_ref, own_ref, other_ref, grad_ref, sums_ref) = refs[:COLS], refs[COLS:]
+    early_refs, late_refs, refs = refs[:COLS], refs[COLS : 2 * COLS], refs[2 * COLS :]
+    dq_ref, own_ref, other_ref, grad_ref, sums_ref = refs
     step = pl.program_id(0)
     rows = q_ref.shape[0]
 
     @pl.when(step == 0)
     def _():
-        early_a, late_a = early_ref.shape[0] * 2 // 3, late_refs[0].shape[0] * 2 // 3
+        early_a, late_a = early_refs[0].shape[0] * 2 // 3, late_refs[0].shape[0] * 2 // 3
+        early = sum(ref[...].astype(F32) for ref in early_refs).astype(BF16)
         late = sum(ref[...].astype(F32) for ref in late_refs).astype(BF16)
         own = early_a + late_a
-        grad_ref[:early_a] = early_ref[:early_a]
+        grad_ref[:early_a] = early[:early_a]
         grad_ref[early_a:own] = late[:late_a]
-        grad_ref[own : own + early_a // 2] = early_ref[early_a:]
+        grad_ref[own : own + early_a // 2] = early[early_a:]
         grad_ref[own + early_a // 2 :] = late[late_a:]
 
     grad = grad_ref[pl.ds(pl.multiple_of(step * rows, rows), rows)]
@@ -218,7 +245,7 @@
             by_head,
             pl.BlockSpec((1, keys, rows), lambda i: (i, 0, 0)),
             by_query,
-            *[pl.BlockSpec(block.shape, lambda i: (0, 0)) for block in (early, *late)],
+            *[pl.BlockSpec(block.shape, lambda i: (0, 0)) for block in (*early, *late)],
         ],
         out_specs=[by_query, by_half, by_half],
         out_shape=[
@@ -230,7 +257,7 @@
         compiler_params=pltpu.CompilerParams(vmem_limit_bytes=20 * 2**20),
         cost_estimate=WINDOW,
         name="attention_backward",
-    )(q, k, v, probs, attn, early, *late)
+    )(q, k, v, probs, attn, *early, *late)
 
 
 def pack_kernel(q_ref, k_ref, v_ref, *out_refs):
@@ -337,28 +364,42 @@
     )(*heads, *grads, *total)
 
 
-def join_kernel(*refs):
-    in_refs, (q_ref, kv_ref) = refs[:PLANES], refs[PLANES:]
-    tokens = kv_ref.shape[1] // PLANES
+def unpack_kernel(*refs):
+    in_refs, out_refs = refs[:COLS], refs[COLS:]
+    tokens = out_refs[0].shape[0]
     half = tokens // 2
-    for p, in_ref in enumerate(in_refs):
-        q_ref[p * tokens : (p + 1) * tokens] = in_ref[:tokens]
-        at = PLANES * tokens + p * half
-        q_ref[at : at + half] = in_ref[tokens : tokens + half]
-        for i in range(4):
-            at = tokens + half + i * tokens
-            kv_ref[i, p * tokens : (p + 1) * tokens] = in_ref[at : at + tokens]
-
-
-def join(blocks, tokens):
-    return pl.pallas_call(
-        join_kernel,
-        out_shape=[
-            jax.ShapeDtypeStruct((PLANES * (tokens + tokens // 2), HD), BF16),
-            jax.ShapeDtypeStruct((4, PLANES * tokens, HD), BF16),
-        ],
+    col = lax.axis_index("col")
+    for j, in_ref in enumerate(in_refs):
+        of = lax.bitwise_xor(col, j)
+        y, x = lax.div(of, 2), lax.rem(of, 2)
+        a = pl.ds(pl.multiple_of((3 * y + x) * HD, HD), HD)
+        b = pl.ds(pl.multiple_of((3 * y + 2) * HD, HD), HD)
+        out_refs[0][:, a] = in_ref[:tokens]
+        out_refs[0][pl.ds(pl.multiple_of(x * half, half), half), b] = in_ref[tokens : tokens + half]
+        for i in range(2):
+            at = tokens + half + 2 * i * tokens
+            out_refs[1 + i][:, a] = in_ref[at : at + tokens]
+    for y in range(2):
+        b = pl.ds((3 * y + 2) * HD, HD)
+        for i in range(2):
+            at = tokens + half + (2 * i + 1) * tokens
+
+            def load(x):
+                entry = lax.bitwise_xor(col, 2 * y + x)
+                block = in_refs[0][at : at + tokens].astype(F32)
+                for j in range(1, COLS):
+                    block = jnp.where(entry == j, in_refs[j][at : at + tokens].astype(F32), block)
+                return block
+
+            out_refs[1 + i][:, b] = (load(0) + load(1)).astype(BF16)
+
+
+def unpack(blocks, tokens, width):
+    return pl.pallas_call(
+        unpack_kernel,
+        out_shape=[jax.ShapeDtypeStruct((tokens, width), BF16)] * 3,
         cost_estimate=SMALL,
-        name="join",
+        name="unpack_outputs",
     )(*blocks)
 
 
@@ -373,7 +414,6 @@
         in_specs=[pl.BlockSpec(memory_space=pl.ANY)],
         out_specs=pl.BlockSpec(memory_space=pl.ANY),
         out_shape=jax.ShapeDtypeStruct(mark.shape, mark.dtype),
-        input_output_aliases={0: 0},
         compiler_params=pltpu.CompilerParams(has_side_effects=True),
         cost_estimate=WINDOW,
         name="fence",
@@ -413,27 +453,23 @@
     moved = after([to_col(pieces[j], j) for j in (1, 2, 3)], fence(pieces))
     over_col = jnp.stack([pieces[0], *moved])
 
-    def add_up(*terms):
-        return sum(t.astype(F32) for t in terms).astype(BF16)
-
     arrived = [pick(over_col, col ^ plane)]
     for s in ORDER[1:]:
         arrived.append(to_plane(pick(over_col, col ^ ((plane + s) % PLANES)), s))
+
     early = grad_pieces((out_grad, grad_1, grad_3), *weights)
-    early_sent = [to_col(early[j], j) for j in (1, 2)]
-    early_sent.append(to_col(after(early[3], arrived[1]), 3))
-
-    arrived = after(arrived, early)
-    q, kv = join(arrived, tokens)
-    kv = jnp.concatenate([kv, swap(kv)], axis=1)
-    k, v = kv[:2], kv[2:]
+    early = list(early)
+    early[1:] = [to_col(block, j) for j, block in enumerate(after(early[1:], arrived[1:3]), 1)]
+
+    own_part = after(arrived, early)
+    other_part = [swap(block) for block in own_part]
+    other_part = after(other_part, fence(own_part))
 
     grad_2 = to_plane(after(grad_1, arrived), 1)
     grads = [out_grad, grad_1, grad_3, grad_2]
 
-    probs, attn = attention_forward(q, k, v)
+    probs, attn, q, k, v = attention_forward(own_part, other_part, tokens)
     grad_2 = after(grad_2, attn)
-    d_attn_early = add_up(early[0], *after(early_sent, attn))
 
     def plane_heads(rows, every):
         by_col = [pick(every, col ^ d) for d in range(COLS)]
@@ -456,7 +492,7 @@
     pair = jnp.stack([sent, to_col(sent, 1)])
     rest = [pair, to_col(pair, 2)]
 
-    dq, dkv, dkv_other = attention_backward(q, k, v, probs, attn, d_attn_early, late)
+    dq, dkv, dkv_other = attention_backward(q, k, v, probs, attn, early, late)
     rest, mixed_2 = after((rest, mixed_2), dq)
 
     dkv_other = jnp.stack([jnp.stack([swap(dkv_other[i, h]) for h in range(2)]) for i in range(2)])
@@ -485,7 +521,7 @@
     total = swap(total)
     term_0 = mixed_term(after(head_0, term_1, term_3), *weights, F32, WINDOW)
 
-    away, mixed_1, total = after((away, mixed_1, total), term_0)
+    away, total = after((away, total), term_0)
     home = [home[0], *away]
     weight_grad = weight_grad_part(after(ours, home), grads, total)
 
@@ -495,23 +531,9 @@
     back = [pick(home, (col - plane) % PLANES)] + [
         to_col(pick(home, ((col ^ j) - plane) % PLANES), j) for j in (1, 2, 3)
     ]
-    back, mixed_3 = after((back, mixed_3), weight_grad)
-    back = jnp.stack(back)
-    back = [pick(back, col ^ d) for d in range(COLS)]
-    outs = [[], [], []]
-    for y in range(2):
-        left, right = back[2 * y], back[2 * y + 1]
-        outs[0] += [
-            left[:tokens],
-            right[:tokens],
-            jnp.concatenate([left[tokens : tokens + half], right[tokens : tokens + half]]),
-        ]
-        for i in range(2):
-            at = tokens + half + 2 * i * tokens
-            to = at + tokens
-            b = left[to : to + tokens].astype(F32) + right[to : to + tokens].astype(F32)
-            outs[1 + i] += [left[at:to], right[at:to], b.astype(BF16)]
-    query_g, key_g, value_g = [jnp.concatenate(o, axis=1) for o in outs]
+    query_g, key_g, value_g = unpack(after(back, weight_grad), tokens, queries.shape[1])
+    mixed_3 = after(mixed_3, query_g)
+    mixed_1 = after(mixed_1, weight_grad)
     mixed = (term_0 + mixed_1.astype(F32) + mixed_3.astype(F32)).astype(BF16)
     return (mixed, query_g, key_g, value_g, weight_grad)
 

time: 161 us -> 155 us (0.963)
  waiting for transfers between devices: 76.2 us -> 57.8 us
  starting transfers between devices: 41.3 us -> 51 us
  Pallas kernels: 30.3 us -> 34.6 us
  local copies, waits for them, and re-layouts: 8.93 us -> 6.99 us
    ppermute x12, waiting for transfers between devices: 46.7 us -> 29.9 us  [to_plane(): return lax.ppermute(block, 'row', row_shift(s))]
    ppermute x12, starting transfers between devices: 20.1 us -> 27.7 us  [to_plane(): return lax.ppermute(block, 'row', row_shift(s))]
    ppermute x17, waiting for transfers between devices: 29.1 us -> 25.5 us  [to_col(): return lax.ppermute(block, 'col', col_xor(j))]
    ppermute x7 -> x10, waiting for transfers between devices: 0.44 us -> 2.44 us  [swap(): return lax.ppermute(block, 'row', SWAP)]
    unnamed x49 -> x43, local copies, waits for them, and re-layouts: 6.22 us -> 4.34 us
    pallas_call x2, Pallas kernels: 4.72 us -> 6.36 us  [grad_pieces(): pl.pallas_call(grad_kernel, out_shape=[piece] * COLS, scratch_shapes=[plt...]
  transfers between devices with their start and end apart: 36 -> 39, of which waited for: 19 -> 21; matrix products, arithmetic and copies ran while one was open for 4% -> 3% of each run, Pallas kernels for 18% -> 22%
where the time goes in v4:
time: 155 us; the launch traced here: 154 us
  waiting for transfers between devices  57.8 us (37%)
  starting transfers between devices  51 us (33%)
  Pallas kernels  34.6 us (22%)
  local copies, waits for them, and re-layouts  6.99 us (5%)
  other arithmetic  2.63 us (2%)
    ppermute x12, waiting for transfers between devices, to_plane(): return lax.ppermute(block, 'row', row_shift(s))  29.9 us
    ppermute x12, starting transfers between devices, to_plane(): return lax.ppermute(block, 'row', row_shift(s))  27.7 us
    ppermute x17, waiting for transfers between devices, to_col(): return lax.ppermute(block, 'col', col_xor(j))  25.5 us
    ppermute x17, starting transfers between devices, to_col(): return lax.ppermute(block, 'col', col_xor(j))  21 us
    pallas_call x2, Pallas kernels, weight_grad_part(): pl.pallas_call(functools.partial(weight_grad_kernel, len(heads)), out_sha...  7.21 us
    pallas_call x1, Pallas kernels, attention_forward(): pl.pallas_call(forward_kernel, grid=(3,), in_specs=[whole(*own[0].shape)]...  6.91 us
    pallas_call x1, Pallas kernels, attention_backward(): pl.pallas_call(backward_kernel, grid=(3,), in_specs=[by_query, by_head, b...  6.46 us
    pallas_call x2, Pallas kernels, grad_pieces(): pl.pallas_call(grad_kernel, out_shape=[piece] * COLS, scratch_shapes=[plt...  6.36 us
  transfers between devices with their start and end apart: 39, of which 21 were waited for; matrix products, arithmetic and copies ran while one was open for 3% of the time, Pallas kernels for 22%

profile of v4, /device:TPU:0, one launch (start us, length us, event | category | flops | bytes accessed | tf_op | source)
XLA Modules:
  0.0 154.1 jit_solution(7582455417609076279)
XLA Ops:
  0.6 3.1 %collective-permute-start.7 = (bf16[192,1536]{1,0:T(8,128)(2,1)}, bf16[192,1536]{1,0:T(8,128)(2,1)S(1)}, u32[]{:S(2)}, u32[]{:S(2)}) collective-permute-start(bf16[192,1536]{1,0:T(8,128)(2,1)} %refs_4_.3), channel_id=1, source_target_pairs={{0,8},{4,12},{8,16},{12,20},{16,24},{20,28},{24,0},{28,4},{1,9},{5... | collective-permute-start | bytes 1769480 | tf_op jit(solution)/shard_map/ppermute | solution.py:442
  3.7 2.1 %collective-permute-start.8 = (bf16[192,1536]{1,0:T(8,128)(2,1)}, bf16[192,1536]{1,0:T(8,128)(2,1)}, u32[]{:S(2)}, u32[]{:S(2)}) collective-permute-start(bf16[192,1536]{1,0:T(8,128)(2,1)} %refs_4_.3), channel_id=1, source_target_pairs={{0,24},{4,28},{8,0},{12,4},{16,8},{20,12},{24,16},{28,20},{1,25},{... | collective-permute-start | bytes 1769480 | tf_op jit(solution)/shard_map/ppermute | solution.py:442
  6.4 2.3 %pack_inputs.1 = (bf16[1056,128]{1,0:T(8,128)(2,1)}, bf16[1056,128]{1,0:T(8,128)(2,1)}, bf16[1056,128]{1,0:T(8,128)(2,1)}, bf16[1056,128]{1,0:T(8,128)(2,1)}) custom-call(bf16[192,768]{1,0:T(8,128)(2,1)} %q_ref, bf16[192,768]{1,0:T(8,128)(2,1)} %k_ref, bf16[192,768]{1,0:T(8,128)(2,1)} %v_ref), custom_call_target="tpu_custom_call" | custom-call | flops 40000000000 | tf_op jit(solution)/shard_map/pack_inputs/pallas_call | solution.py:282
  8.9 1.6 %collective-permute-start.1 = (bf16[1056,128]{1,0:T(8,128)(2,1)}, bf16[1056,128]{1,0:T(8,128)(2,1)S(1)}, u32[]{:S(2)}, u32[]{:S(2)}) collective-permute-start(bf16[1056,128]{1,0:T(8,128)(2,1)} %get-tuple-element.91), channel_id=1, source_target_pairs={{0,1},{1,0},{2,3},{3,2},{4,5},{5,4},{6,7},{7,6},{8,9},{9,8},{10,11... | collective-permute-start | bytes 811016 | tf_op jit(solution)/shard_map/ppermute | solution.py:439
  10.5 1.5 collective-permute-start.2
  12.4 6.0 %collective-permute-done.1 = bf16[1056,128]{1,0:T(8,128)(2,1)S(1)} collective-permute-done((bf16[1056,128]{1,0:T(8,128)(2,1)}, bf16[1056,128]{1,0:T(8,128)(2,1)S(1)}, u32[]{:S(2)}, u32[]{:S(2)}) %collective-permute-start.1) | collective-permute-done | bytes 270368 | tf_op jit(solution)/shard_map/ppermute | solution.py:439
  18.4 6.7 %collective-permute-done.2 = bf16[1056,128]{1,0:T(8,128)(2,1)S(1)} collective-permute-done((bf16[1056,128]{1,0:T(8,128)(2,1)}, bf16[1056,128]{1,0:T(8,128)(2,1)S(1)}, u32[]{:S(2)}, u32[]{:S(2)}) %collective-permute-start.2) | collective-permute-done | bytes 270368 | tf_op jit(solution)/shard_map/ppermute | solution.py:439
  26.0 3.8 %collective-permute-start.5 = (bf16[1056,128]{1,0:T(8,128)(2,1)S(1)}, bf16[1056,128]{1,0:T(8,128)(2,1)}, u32[]{:S(2)}, u32[]{:S(2)}) collective-permute-start(bf16[1056,128]{1,0:T(8,128)(2,1)S(1)} %get-tuple-element.166), channel_id=1, source_target_pairs={{0,24},{4,28},{8,0},{12,4},{16,8},{20,12},{24,16},{28,20},{1,25},{... | collective-permute-start | bytes 811016 | tf_op jit(solution)/shard_map/ppermute | solution.py:442
  29.8 3.2 %collective-permute-done.8.refs_2_.refs_6_ = bf16[192,1536]{1,0:T(8,128)(2,1)} collective-permute-done((bf16[192,1536]{1,0:T(8,128)(2,1)}, bf16[192,1536]{1,0:T(8,128)(2,1)}, u32[]{:S(2)}, u32[]{:S(2)}) %collective-permute-start.8) | collective-permute-done | bytes 589856 | tf_op jit(solution)/shard_map/ppermute | solution.py:442
  33.1 4.4 %grad_pieces.2 = (bf16[864,128]{1,0:T(8,128)(2,1)S(1)}, bf16[864,128]{1,0:T(8,128)(2,1)}, bf16[864,128]{1,0:T(8,128)(2,1)}, bf16[864,128]{1,0:T(8,128)(2,1)}) custom-call(bf16[192,1536]{1,0:T(8,128)(2,1)S(1)} %copy-done.1, bf16[192,1536]{1,0:T(8,128)(2,1)S(1)} %collective-permute-done.7.refs_1_.refs_5_, ...), custom_call_target="tpu_custom_call" | custom-call | flops 40000000000 | tf_op jit(solution)/shard_map/grad_pieces/pallas_call | solution.py:314
  38.6 4.4 %collective-permute-done.5.refs_2_ = bf16[1056,128]{1,0:T(8,128)(2,1)} collective-permute-done((bf16[1056,128]{1,0:T(8,128)(2,1)S(1)}, bf16[1056,128]{1,0:T(8,128)(2,1)}, u32[]{:S(2)}, u32[]{:S(2)}) %collective-permute-start.5) | collective-permute-done | bytes 270368 | tf_op jit(solution)/shard_map/ppermute | solution.py:442
  46.5 8.7 %collective-permute-done.6.refs_3_ = bf16[1056,128]{1,0:T(8,128)(2,1)} collective-permute-done((bf16[1056,128]{1,0:T(8,128)(2,1)}, bf16[1056,128]{1,0:T(8,128)(2,1)}, u32[]{:S(2)}, u32[]{:S(2)}) %collective-permute-start.6) | collective-permute-done | bytes 270368 | tf_op jit(solution)/shard_map/ppermute | solution.py:442
  59.1 6.9 %attention_forward.1 = (bf16[3,1536,384]{2,1,0:T(8,128)(2,1)}, bf16[1152,128]{1,0:T(8,128)(2,1)S(1)}, bf16[1152,128]{1,0:T(8,128)(2,1)S(1)}, bf16[2,1536,128]{2,1,0:T(8,128)(2,1)S(1)}, bf16[2,1536,128]{2,1,0:T(8,128)(2,1)S(1)}) custom-call(bf16[1056,128]{1,0:T(8,128)(2,1)S(1)} %get-tuple-element.105.refs_0_, ...), custom_call_target="tpu_custom_call" | custom-call | flops 40000000000 | tf_op jit(solution)/shard_map/attention_forward/pallas_call | solution.py:167
  66.0 1.5 %collective-permute-start.18 = (bf16[288,128]{1,0:T(8,128)(2,1)S(1)}, bf16[288,128]{1,0:T(8,128)(2,1)S(1)}, u32[]{:S(2)}, u32[]{:S(2)}) collective-permute-start(bf16[288,128]{1,0:T(8,128)(2,1)S(1)} %get-tuple-element.219), channel_id=1, source_target_pairs={{0,1},{1,0},{2,3},{3,2},{4,5},{5,4},{6,7},{7,6},{8,9},{9,8},{10,11... | collective-permute-start | bytes 221192 | tf_op jit(solution)/shard_map/ppermute | solution.py:439
  69.7 1.6 %collective-permute-start.16 = (bf16[864,128]{1,0:T(8,128)(2,1)S(1)}, bf16[864,128]{1,0:T(8,128)(2,1)S(1)}, u32[]{:S(2)}, u32[]{:S(2)}) collective-permute-start(bf16[864,128]{1,0:T(8,128)(2,1)S(1)} %get-tuple-element.217), channel_id=1, source_target_pairs={{0,1},{1,0},{2,3},{3,2},{4,5},{5,4},{6,7},{7,6},{8,9},{9,8},{10,11... | collective-permute-start | bytes 663560 | tf_op jit(solution)/shard_map/ppermute | solution.py:439
  72.4 2.8 %collective-permute-done.20 = bf16[288,128]{1,0:T(8,128)(2,1)S(1)} collective-permute-done((bf16[288,128]{1,0:T(8,128)(2,1)S(1)}, bf16[288,128]{1,0:T(8,128)(2,1)S(1)}, u32[]{:S(2)}, u32[]{:S(2)}) %collective-permute-start.20) | collective-permute-done | bytes 73760 | tf_op jit(solution)/shard_map/ppermute | solution.py:439
  76.2 2.7 %collective-permute-start.22 = (bf16[192,1536]{1,0:T(8,128)(2,1)S(1)}, bf16[192,1536]{1,0:T(8,128)(2,1)S(1)}, u32[]{:S(2)}, u32[]{:S(2)}) collective-permute-start(bf16[192,1536]{1,0:T(8,128)(2,1)S(1)} %mixed_term.4), channel_id=1, source_target_pairs={{0,8},{4,12},{8,16},{12,20},{16,24},{20,28},{24,0},{28,4},{1,9},{5... | collective-permute-start | bytes 1769480 | tf_op jit(solution)/shard_map/ppermute | solution.py:442
  78.9 2.0 %grad_pieces.3 = (bf16[288,128]{1,0:T(8,128)(2,1)S(1)}, bf16[288,128]{1,0:T(8,128)(2,1)S(1)}, bf16[288,128]{1,0:T(8,128)(2,1)S(1)}, bf16[288,128]{1,0:T(8,128)(2,1)S(1)}) custom-call(bf16[192,1536]{1,0:T(8,128)(2,1)} %collective-permute-done.21.refs_0_.refs_7_, bf16[384,1536]{1,0:T(8,128)(2,1)S(1)} %copy-done, ...), custom_call_target="tpu_custom_call" | custom-call | flops 40000000000 | tf_op jit(solution)/shard_map/grad_pieces/pallas_call | solution.py:314
  81.6 2.9 %collective-permute-start.25 = (bf16[288,128]{1,0:T(8,128)(2,1)S(1)}, bf16[288,128]{1,0:T(8,128)(2,1)S(1)}, u32[]{:S(2)}, u32[]{:S(2)}) collective-permute-start(bf16[288,128]{1,0:T(8,128)(2,1)S(1)} %get-tuple-element.128), channel_id=1, source_target_pairs={{0,3},{1,2},{2,1},{3,0},{4,7},{5,6},{6,5},{7,4},{8,11},{9,10},{10,... | collective-permute-start | bytes 221192 | tf_op jit(solution)/shard_map/ppermute | solution.py:439
  86.9 6.5 %attention_backward.1 = (bf16[1152,128]{1,0:T(8,128)(2,1)S(1)}, f32[2,2,768,128]{3,2,1,0:T(8,128)S(1)}, bf16[2,2,768,128]{3,2,1,0:T(8,128)(2,1)S(1)}) custom-call(bf16[1152,128]{1,0:T(8,128)(2,1)S(1)} %get-tuple-element.120.q_ref, bf16[2,1536,128]{2,1,0:T(8,128)(2,1)S(1)} %get-tuple-element.121.k_ref, bf16[2,1536,128]{2,1,0:T(8,128)(2,1)S(1)} %get-tuple-element.122.v_ref, ...), custom_call_target="tpu_custom_call" | custom-call | flops 40000000000 | tf_op jit(solution)/shard_map/attention_backward/pallas_call | solution.py:239
  94.9 1.9 %collective-permute-start.17 = (bf16[2,864,128]{2,1,0:T(8,128)(2,1)S(1)}, bf16[2,864,128]{2,1,0:T(8,128)(2,1)S(1)}, u32[]{:S(2)}, u32[]{:S(2)}) collective-permute-start(bf16[2,864,128]{2,1,0:T(8,128)(2,1)S(1)} %pad_maximum_fusion.2), channel_id=1, source_target_pairs={{0,2},{1,3},{2,0},{3,1},{4,6},{5,7},{6,4},{7,5},{8,10},{9,11},{10,... | collective-permute-start | bytes 1327112 | tf_op jit(solution)/shard_map/ppermute | solution.py:439
  97.3 1.5 collective-permute-start.31
  98.8 1.6 %collective-permute-start.32 = (bf16[1056,128]{1,0:T(8,128)(2,1)S(1)}, bf16[1056,128]{1,0:T(8,128)(2,1)S(1)}, u32[]{:S(2)}, u32[]{:S(2)}) collective-permute-start(bf16[1056,128]{1,0:T(8,128)(2,1)S(1)} %get-tuple-element.177), channel_id=1, source_target_pairs={{0,16},{4,20},{8,24},{12,28},{16,0},{20,4},{24,8},{28,12},{1,17},{... | collective-permute-start | bytes 811016 | tf_op jit(solution)/shard_map/ppermute | solution.py:442
  100.6 6.7 %collective-permute-done.17 = bf16[2,864,128]{2,1,0:T(8,128)(2,1)S(1)} collective-permute-done((bf16[2,864,128]{2,1,0:T(8,128)(2,1)S(1)}, bf16[2,864,128]{2,1,0:T(8,128)(2,1)S(1)}, u32[]{:S(2)}, u32[]{:S(2)}) %collective-permute-start.17) | collective-permute-done | bytes 442400 | tf_op jit(solution)/shard_map/ppermute | solution.py:439
  108.9 3.1 %weight_grad.2 = bf16[384,1536]{1,0:T(8,128)(2,1)S(1)} custom-call(bf16[192,384]{1,0:T(8,128)(2,1)S(1)} %get-tuple-element.134.refs_0_, bf16[192,384]{1,0:T(8,128)(2,1)S(1)} %get-tuple-element.135.refs_1_, bf16[192,384]{1,0:T(8,128)(2,1)S(1)} %get-tuple-element.136.refs_2_, bf16[192,384]{1,0:T(8,128)(2,1)S(1)} %get-tuple-element.137.refs_3_, ...), custom_call_target="tpu_custom_call" | custom-call | flops 40000000000 | tf_op jit(solution)/shard_map/weight_grad/pallas_call | solution.py:358
  112.9 1.7 %collective-permute-start.30 = (bf16[192,1536]{1,0:T(8,128)(2,1)S(1)}, bf16[192,1536]{1,0:T(8,128)(2,1)S(1)}, u32[]{:S(2)}, u32[]{:S(2)}) collective-permute-start(bf16[192,1536]{1,0:T(8,128)(2,1)S(1)} %mixed_term.5), channel_id=1, source_target_pairs={{0,24},{4,28},{8,0},{12,4},{16,8},{20,12},{24,16},{28,20},{1,25},{... | collective-permute-start | bytes 1769480 | tf_op jit(solution)/shard_map/ppermute | solution.py:442
  117.1 8.0 %collective-permute-done.32 = bf16[1056,128]{1,0:T(8,128)(2,1)S(1)} collective-permute-done((bf16[1056,128]{1,0:T(8,128)(2,1)S(1)}, bf16[1056,128]{1,0:T(8,128)(2,1)S(1)}, u32[]{:S(2)}, u32[]{:S(2)}) %collective-permute-start.32) | collective-permute-done | bytes 270368 | tf_op jit(solution)/shard_map/ppermute | solution.py:442
  126.1 1.7 %collective-permute-start.36 = (bf16[1056,128]{1,0:T(8,128)(2,1)S(1)}, bf16[1056,128]{1,0:T(8,128)(2,1)S(1)}, u32[]{:S(2)}, u32[]{:S(2)}) collective-permute-start(bf16[1056,128]{1,0:T(8,128)(2,1)S(1)} %get-tuple-element.163), channel_id=1, source_target_pairs={{0,1},{1,0},{2,3},{3,2},{4,5},{5,4},{6,7},{7,6},{8,9},{9,8},{10,11... | collective-permute-start | bytes 811016 | tf_op jit(solution)/shard_map/ppermute | solution.py:439
  129.6 11.0 %collective-permute-start.35 = (bf16[192,1536]{1,0:T(8,128)(2,1)}, bf16[192,1536]{1,0:T(8,128)(2,1)S(1)}, u32[]{:S(2)}, u32[]{:S(2)}) collective-permute-start(bf16[192,1536]{1,0:T(8,128)(2,1)} %add_convert_fusion.2), channel_id=1, source_target_pairs={{0,8},{4,12},{8,16},{12,20},{16,24},{20,28},{24,0},{28,4},{1,9},{5... | collective-permute-start | bytes 1769480 | tf_op jit(solution)/shard_map/ppermute | solution.py:442
  140.5 4.1 %weight_grad.3 = bf16[384,1536]{1,0:T(8,128)(2,1)} custom-call(bf16[192,384]{1,0:T(8,128)(2,1)S(1)} %get-tuple-element.146.refs_0_, bf16[192,384]{1,0:T(8,128)(2,1)S(1)} %get-tuple-element.147.refs_1_, bf16[192,384]{1,0:T(8,128)(2,1)S(1)} %get-tuple-element.148.refs_2_, bf16[192,384]{1,0:T(8,128)(2,1)S(1)} %get-tuple-element.149.refs_3_, ...), custom_call_target="tpu_custom_call" | custom-call | flops 40000000000 | tf_op jit(solution)/shard_map/weight_grad/pallas_call | solution.py:358
  144.6 3.9 %collective-permute-done.30 = bf16[192,1536]{1,0:T(8,128)(2,1)S(1)} collective-permute-done((bf16[192,1536]{1,0:T(8,128)(2,1)S(1)}, bf16[192,1536]{1,0:T(8,128)(2,1)S(1)}, u32[]{:S(2)}, u32[]{:S(2)}) %collective-permute-start.30) | collective-permute-done | bytes 589856 | tf_op jit(solution)/shard_map/ppermute | solution.py:442
  150.9 2.3 %unpack_outputs.1 = (bf16[192,768]{1,0:T(8,128)(2,1)}, bf16[192,768]{1,0:T(8,128)(2,1)}, bf16[192,768]{1,0:T(8,128)(2,1)}) custom-call(bf16[1056,128]{1,0:T(8,128)(2,1)} %get-tuple-element.153.refs_0_, bf16[1056,128]{1,0:T(8,128)(2,1)} %copy-done.11, bf16[1056,128]{1,0:T(8,128)(2,1)} %copy-done.12, bf16[1056,128]{1,0:T(8,128)(2,1)} %copy-done.13), custom_call_target="tpu_custom_call" | custom-call | flops 1000000 | bytes 1000 | tf_op jit(solution)/shard_map/unpack_outputs/pallas_call | solution.py:398
  (136 shorter events, 30.8 us)
Async XLA Ops:
  0.6 29.2 %collective-permute-start.7 = (bf16[192,1536]{1,0:T(8,128)(2,1)}, bf16[192,1536]{1,0:T(8,128)(2,1)S(1)}, u32[]{:S(2)}, u32[]{:S(2)}) collective-permute-start(bf16[192,1536]{1,0:T(8,128)(2,1)} %refs_4_.3), channel_id=1, source_target_pairs={{0,8},{4,12},{8,16},{12,20},{16,24},{20,28},{24,0},{28,4},{1,9},{5... | collective-permute-start | bytes 1769480 | tf_op jit(solution)/shard_map/ppermute | solution.py:442
  3.7 29.3 %collective-permute-start.8 = (bf16[192,1536]{1,0:T(8,128)(2,1)}, bf16[192,1536]{1,0:T(8,128)(2,1)}, u32[]{:S(2)}, u32[]{:S(2)}) collective-permute-start(bf16[192,1536]{1,0:T(8,128)(2,1)} %refs_4_.3), channel_id=1, source_target_pairs={{0,24},{4,28},{8,0},{12,4},{16,8},{20,12},{24,16},{28,20},{1,25},{... | collective-permute-start | bytes 1769480 | tf_op jit(solution)/shard_map/ppermute | solution.py:442
  5.8 3.1 %collective-permute-start = (bf16[384,1536]{1,0:T(8,128)(2,1)}, bf16[384,1536]{1,0:T(8,128)(2,1)S(1)}, u32[]{:S(2)}, u32[]{:S(2)}) collective-permute-start(bf16[384,1536]{1,0:T(8,128)(2,1)} %own_ref.7), channel_id=1, source_target_pairs={{0,4},{4,0},{8,12},{12,8},{16,20},{20,16},{24,28},{28,24},{1,5},{5... | collective-permute-start | bytes 3538952 | tf_op jit(solution)/shard_map/ppermute | solution.py:445
  8.9 9.5 %collective-permute-start.1 = (bf16[1056,128]{1,0:T(8,128)(2,1)}, bf16[1056,128]{1,0:T(8,128)(2,1)S(1)}, u32[]{:S(2)}, u32[]{:S(2)}) collective-permute-start(bf16[1056,128]{1,0:T(8,128)(2,1)} %get-tuple-element.91), channel_id=1, source_target_pairs={{0,1},{1,0},{2,3},{3,2},{4,5},{5,4},{6,7},{7,6},{8,9},{9,8},{10,11... | collective-permute-start | bytes 811016 | tf_op jit(solution)/shard_map/ppermute | solution.py:439
  10.5 14.5 %collective-permute-start.2 = (bf16[1056,128]{1,0:T(8,128)(2,1)}, bf16[1056,128]{1,0:T(8,128)(2,1)S(1)}, u32[]{:S(2)}, u32[]{:S(2)}) collective-permute-start(bf16[1056,128]{1,0:T(8,128)(2,1)} %get-tuple-element.92), channel_id=1, source_target_pairs={{0,2},{1,3},{2,0},{3,1},{4,6},{5,7},{6,4},{7,5},{8,10},{9,11},{10,... | collective-permute-start | bytes 811016 | tf_op jit(solution)/shard_map/ppermute | solution.py:439
  12.0 13.0 %collective-permute-start.3 = (bf16[1056,128]{1,0:T(8,128)(2,1)}, bf16[1056,128]{1,0:T(8,128)(2,1)S(1)}, u32[]{:S(2)}, u32[]{:S(2)}) collective-permute-start(bf16[1056,128]{1,0:T(8,128)(2,1)} %get-tuple-element.93), channel_id=1, source_target_pairs={{0,3},{1,2},{2,1},{3,0},{4,7},{5,6},{6,5},{7,4},{8,11},{9,10},{10,... | collective-permute-start | bytes 811016 | tf_op jit(solution)/shard_map/ppermute | solution.py:439
  26.0 12.6 %collective-permute-start.4 = (bf16[1056,128]{1,0:T(8,128)(2,1)S(1)}, bf16[1056,128]{1,0:T(8,128)(2,1)S(1)}, u32[]{:S(2)}, u32[]{:S(2)}) collective-permute-start(bf16[1056,128]{1,0:T(8,128)(2,1)S(1)} %get-tuple-element.167), channel_id=1, source_target_pairs={{0,8},{4,12},{8,16},{12,20},{16,24},{20,28},{24,0},{28,4},{1,9},{5... | collective-permute-start | bytes 811016 | tf_op jit(solution)/shard_map/ppermute | solution.py:442
  26.0 17.0 %collective-permute-start.5 = (bf16[1056,128]{1,0:T(8,128)(2,1)S(1)}, bf16[1056,128]{1,0:T(8,128)(2,1)}, u32[]{:S(2)}, u32[]{:S(2)}) collective-permute-start(bf16[1056,128]{1,0:T(8,128)(2,1)S(1)} %get-tuple-element.166), channel_id=1, source_target_pairs={{0,24},{4,28},{8,0},{12,4},{16,8},{20,12},{24,16},{28,20},{1,25},{... | collective-permute-start | bytes 811016 | tf_op jit(solution)/shard_map/ppermute | solution.py:442
  29.8 25.4 %collective-permute-start.6 = (bf16[1056,128]{1,0:T(8,128)(2,1)}, bf16[1056,128]{1,0:T(8,128)(2,1)}, u32[]{:S(2)}, u32[]{:S(2)}) collective-permute-start(bf16[1056,128]{1,0:T(8,128)(2,1)} %get-tuple-element.165), channel_id=1, source_target_pairs={{0,16},{4,20},{8,24},{12,28},{16,0},{20,4},{24,8},{28,12},{1,17},{... | collective-permute-start | bytes 811016 | tf_op jit(solution)/shard_map/ppermute | solution.py:442
  43.0 12.2 %collective-permute-start.10 = (bf16[864,128]{1,0:T(8,128)(2,1)}, bf16[864,128]{1,0:T(8,128)(2,1)}, u32[]{:S(2)}, u32[]{:S(2)}) collective-permute-start(bf16[864,128]{1,0:T(8,128)(2,1)} %get-tuple-element.103), channel_id=1, source_target_pairs={{0,2},{1,3},{2,0},{3,1},{4,6},{5,7},{6,4},{7,5},{8,10},{9,11},{10,... | collective-permute-start | bytes 663560 | tf_op jit(solution)/shard_map/ppermute | solution.py:439
  44.6 10.6 %collective-permute-start.11 = (bf16[864,128]{1,0:T(8,128)(2,1)}, bf16[864,128]{1,0:T(8,128)(2,1)}, u32[]{:S(2)}, u32[]{:S(2)}) collective-permute-start(bf16[864,128]{1,0:T(8,128)(2,1)} %get-tuple-element.104), channel_id=1, source_target_pairs={{0,3},{1,2},{2,1},{3,0},{4,7},{5,6},{6,5},{7,4},{8,11},{9,10},{10,... | collective-permute-start | bytes 663560 | tf_op jit(solution)/shard_map/ppermute | solution.py:439
  46.0 10.1 %collective-permute-start.9 = (bf16[864,128]{1,0:T(8,128)(2,1)}, bf16[864,128]{1,0:T(8,128)(2,1)}, u32[]{:S(2)}, u32[]{:S(2)}) collective-permute-start(bf16[864,128]{1,0:T(8,128)(2,1)} %get-tuple-element.102), channel_id=1, source_target_pairs={{0,1},{1,0},{2,3},{3,2},{4,5},{5,4},{6,7},{7,6},{8,9},{9,8},{10,11... | collective-permute-start | bytes 663560 | tf_op jit(solution)/shard_map/ppermute | solution.py:439
  55.2 17.2 %collective-permute-start.21 = (bf16[192,1536]{1,0:T(8,128)(2,1)S(1)}, bf16[192,1536]{1,0:T(8,128)(2,1)}, u32[]{:S(2)}, u32[]{:S(2)}) collective-permute-start(bf16[192,1536]{1,0:T(8,128)(2,1)S(1)} %collective-permute-done.7.refs_1_.refs_5_), channel_id=1, source_target_pairs={{0,8},{4,12},{8,16},{12,20},{16,24},{20,28},{24,0},{28,4},{1,9},{5... | collective-permute-start | bytes 1769480 | tf_op jit(solution)/shard_map/ppermute | solution.py:442
  66.0 6.3 %collective-permute-start.18 = (bf16[288,128]{1,0:T(8,128)(2,1)S(1)}, bf16[288,128]{1,0:T(8,128)(2,1)S(1)}, u32[]{:S(2)}, u32[]{:S(2)}) collective-permute-start(bf16[288,128]{1,0:T(8,128)(2,1)S(1)} %get-tuple-element.219), channel_id=1, source_target_pairs={{0,1},{1,0},{2,3},{3,2},{4,5},{5,4},{6,7},{7,6},{8,9},{9,8},{10,11... | collective-permute-start | bytes 221192 | tf_op jit(solution)/shard_map/ppermute | solution.py:439
  67.6 4.8 %collective-permute-start.19 = (bf16[288,128]{1,0:T(8,128)(2,1)S(1)}, bf16[288,128]{1,0:T(8,128)(2,1)S(1)}, u32[]{:S(2)}, u32[]{:S(2)}) collective-permute-start(bf16[288,128]{1,0:T(8,128)(2,1)S(1)} %get-tuple-element.219), channel_id=1, source_target_pairs={{0,2},{1,3},{2,0},{3,1},{4,6},{5,7},{6,4},{7,5},{8,10},{9,11},{10,... | collective-permute-start | bytes 221192 | tf_op jit(solution)/shard_map/ppermute | solution.py:439
  69.1 6.1 %collective-permute-start.20 = (bf16[288,128]{1,0:T(8,128)(2,1)S(1)}, bf16[288,128]{1,0:T(8,128)(2,1)S(1)}, u32[]{:S(2)}, u32[]{:S(2)}) collective-permute-start(bf16[288,128]{1,0:T(8,128)(2,1)S(1)} %get-tuple-element.219), channel_id=1, source_target_pairs={{0,3},{1,2},{2,1},{3,0},{4,7},{5,6},{6,5},{7,4},{8,11},{9,10},{10,... | collective-permute-start | bytes 221192 | tf_op jit(solution)/shard_map/ppermute | solution.py:439
  69.7 24.5 %collective-permute-start.16 = (bf16[864,128]{1,0:T(8,128)(2,1)S(1)}, bf16[864,128]{1,0:T(8,128)(2,1)S(1)}, u32[]{:S(2)}, u32[]{:S(2)}) collective-permute-start(bf16[864,128]{1,0:T(8,128)(2,1)S(1)} %get-tuple-element.217), channel_id=1, source_target_pairs={{0,1},{1,0},{2,3},{3,2},{4,5},{5,4},{6,7},{7,6},{8,9},{9,8},{10,11... | collective-permute-start | bytes 663560 | tf_op jit(solution)/shard_map/ppermute | solution.py:439
  76.2 31.1 %collective-permute-start.22 = (bf16[192,1536]{1,0:T(8,128)(2,1)S(1)}, bf16[192,1536]{1,0:T(8,128)(2,1)S(1)}, u32[]{:S(2)}, u32[]{:S(2)}) collective-permute-start(bf16[192,1536]{1,0:T(8,128)(2,1)S(1)} %mixed_term.4), channel_id=1, source_target_pairs={{0,8},{4,12},{8,16},{12,20},{16,24},{20,28},{24,0},{28,4},{1,9},{5... | collective-permute-start | bytes 1769480 | tf_op jit(solution)/shard_map/ppermute | solution.py:442
  81.0 4.4 %collective-permute-start.23 = (bf16[288,128]{1,0:T(8,128)(2,1)S(1)}, bf16[288,128]{1,0:T(8,128)(2,1)S(1)}, u32[]{:S(2)}, u32[]{:S(2)}) collective-permute-start(bf16[288,128]{1,0:T(8,128)(2,1)S(1)} %get-tuple-element.126), channel_id=1, source_target_pairs={{0,1},{1,0},{2,3},{3,2},{4,5},{5,4},{6,7},{7,6},{8,9},{9,8},{10,11... | collective-permute-start | bytes 221192 | tf_op jit(solution)/shard_map/ppermute | solution.py:439
  81.5 4.4 %collective-permute-start.24 = (bf16[288,128]{1,0:T(8,128)(2,1)S(1)}, bf16[288,128]{1,0:T(8,128)(2,1)S(1)}, u32[]{:S(2)}, u32[]{:S(2)}) collective-permute-start(bf16[288,128]{1,0:T(8,128)(2,1)S(1)} %get-tuple-element.127), channel_id=1, source_target_pairs={{0,2},{1,3},{2,0},{3,1},{4,6},{5,7},{6,4},{7,5},{8,10},{9,11},{10,... | collective-permute-start | bytes 221192 | tf_op jit(solution)/shard_map/ppermute | solution.py:439
  81.6 5.3 %collective-permute-start.25 = (bf16[288,128]{1,0:T(8,128)(2,1)S(1)}, bf16[288,128]{1,0:T(8,128)(2,1)S(1)}, u32[]{:S(2)}, u32[]{:S(2)}) collective-permute-start(bf16[288,128]{1,0:T(8,128)(2,1)S(1)} %get-tuple-element.128), channel_id=1, source_target_pairs={{0,3},{1,2},{2,1},{3,0},{4,7},{5,6},{6,5},{7,4},{8,11},{9,10},{10,... | collective-permute-start | bytes 221192 | tf_op jit(solution)/shard_map/ppermute | solution.py:439
  93.5 3.3 %collective-permute-start.27 = (bf16[768,128]{1,0:T(8,128)(2,1)S(1)}, bf16[768,128]{1,0:T(8,128)(2,1)S(1)}, u32[]{:S(2)}, u32[]{:S(2)}) collective-permute-start(bf16[768,128]{1,0:T(8,128)(2,1)S(1)} %get-tuple-element.195), channel_id=1, source_target_pairs={{0,4},{4,0},{8,12},{12,8},{16,20},{20,16},{24,28},{28,24},{1,5},{5... | collective-permute-start | bytes 589832 | tf_op jit(solution)/shard_map/ppermute | solution.py:445
  94.9 12.4 %collective-permute-start.17 = (bf16[2,864,128]{2,1,0:T(8,128)(2,1)S(1)}, bf16[2,864,128]{2,1,0:T(8,128)(2,1)S(1)}, u32[]{:S(2)}, u32[]{:S(2)}) collective-permute-start(bf16[2,864,128]{2,1,0:T(8,128)(2,1)S(1)} %pad_maximum_fusion.2), channel_id=1, source_target_pairs={{0,2},{1,3},{2,0},{3,1},{4,6},{5,7},{6,4},{7,5},{8,10},{9,11},{10,... | collective-permute-start | bytes 1327112 | tf_op jit(solution)/shard_map/ppermute | solution.py:439
  97.3 19.8 %collective-permute-start.31 = (bf16[1056,128]{1,0:T(8,128)(2,1)S(1)}, bf16[1056,128]{1,0:T(8,128)(2,1)S(1)}, u32[]{:S(2)}, u32[]{:S(2)}) collective-permute-start(bf16[1056,128]{1,0:T(8,128)(2,1)S(1)} %get-tuple-element.178), channel_id=1, source_target_pairs={{0,24},{4,28},{8,0},{12,4},{16,8},{20,12},{24,16},{28,20},{1,25},{... | collective-permute-start | bytes 811016 | tf_op jit(solution)/shard_map/ppermute | solution.py:442
  98.8 26.3 %collective-permute-start.32 = (bf16[1056,128]{1,0:T(8,128)(2,1)S(1)}, bf16[1056,128]{1,0:T(8,128)(2,1)S(1)}, u32[]{:S(2)}, u32[]{:S(2)}) collective-permute-start(bf16[1056,128]{1,0:T(8,128)(2,1)S(1)} %get-tuple-element.177), channel_id=1, source_target_pairs={{0,16},{4,20},{8,24},{12,28},{16,0},{20,4},{24,8},{28,12},{1,17},{... | collective-permute-start | bytes 811016 | tf_op jit(solution)/shard_map/ppermute | solution.py:442
  100.4 24.7 %collective-permute-start.33 = (bf16[1056,128]{1,0:T(8,128)(2,1)S(1)}, bf16[1056,128]{1,0:T(8,128)(2,1)S(1)}, u32[]{:S(2)}, u32[]{:S(2)}) collective-permute-start(bf16[1056,128]{1,0:T(8,128)(2,1)S(1)} %get-tuple-element.176), channel_id=1, source_target_pairs={{0,8},{4,12},{8,16},{12,20},{16,24},{20,28},{24,0},{28,4},{1,9},{5... | collective-permute-start | bytes 811016 | tf_op jit(solution)/shard_map/ppermute | solution.py:442
  112.0 13.1 %collective-permute-start.34 = (bf16[384,1536]{1,0:T(8,128)(2,1)S(1)}, bf16[384,1536]{1,0:T(8,128)(2,1)S(1)}, u32[]{:S(2)}, u32[]{:S(2)}) collective-permute-start(bf16[384,1536]{1,0:T(8,128)(2,1)S(1)} %weight_grad.2), channel_id=1, source_target_pairs={{0,4},{4,0},{8,12},{12,8},{16,20},{20,16},{24,28},{28,24},{1,5},{5... | collective-permute-start | bytes 3538952 | tf_op jit(solution)/shard_map/ppermute | solution.py:445
  112.9 35.7 %collective-permute-start.30 = (bf16[192,1536]{1,0:T(8,128)(2,1)S(1)}, bf16[192,1536]{1,0:T(8,128)(2,1)S(1)}, u32[]{:S(2)}, u32[]{:S(2)}) collective-permute-start(bf16[192,1536]{1,0:T(8,128)(2,1)S(1)} %mixed_term.5), channel_id=1, source_target_pairs={{0,24},{4,28},{8,0},{12,4},{16,8},{20,12},{24,16},{28,20},{1,25},{... | collective-permute-start | bytes 1769480 | tf_op jit(solution)/shard_map/ppermute | solution.py:442
  126.1 23.4 %collective-permute-start.36 = (bf16[1056,128]{1,0:T(8,128)(2,1)S(1)}, bf16[1056,128]{1,0:T(8,128)(2,1)S(1)}, u32[]{:S(2)}, u32[]{:S(2)}) collective-permute-start(bf16[1056,128]{1,0:T(8,128)(2,1)S(1)} %get-tuple-element.163), channel_id=1, source_target_pairs={{0,1},{1,0},{2,3},{3,2},{4,5},{5,4},{6,7},{7,6},{8,9},{9,8},{10,11... | collective-permute-start | bytes 811016 | tf_op jit(solution)/shard_map/ppermute | solution.py:439
  127.8 21.7 %collective-permute-start.37 = (bf16[1056,128]{1,0:T(8,128)(2,1)S(1)}, bf16[1056,128]{1,0:T(8,128)(2,1)S(1)}, u32[]{:S(2)}, u32[]{:S(2)}) collective-permute-start(bf16[1056,128]{1,0:T(8,128)(2,1)S(1)} %get-tuple-element.162), channel_id=1, source_target_pairs={{0,2},{1,3},{2,0},{3,1},{4,6},{5,7},{6,4},{7,5},{8,10},{9,11},{10,... | collective-permute-start | bytes 811016 | tf_op jit(solution)/shard_map/ppermute | solution.py:439
  128.5 21.0 %collective-permute-start.38 = (bf16[1056,128]{1,0:T(8,128)(2,1)S(1)}, bf16[1056,128]{1,0:T(8,128)(2,1)S(1)}, u32[]{:S(2)}, u32[]{:S(2)}) collective-permute-start(bf16[1056,128]{1,0:T(8,128)(2,1)S(1)} %get-tuple-element.161), channel_id=1, source_target_pairs={{0,3},{1,2},{2,1},{3,0},{4,7},{5,6},{6,5},{7,4},{8,11},{9,10},{10,... | collective-permute-start | bytes 811016 | tf_op jit(solution)/shard_map/ppermute | solution.py:439
  129.6 23.6 %collective-permute-start.35 = (bf16[192,1536]{1,0:T(8,128)(2,1)}, bf16[192,1536]{1,0:T(8,128)(2,1)S(1)}, u32[]{:S(2)}, u32[]{:S(2)}) collective-permute-start(bf16[192,1536]{1,0:T(8,128)(2,1)} %add_convert_fusion.2), channel_id=1, source_target_pairs={{0,8},{4,12},{8,16},{12,20},{16,24},{20,28},{24,0},{28,4},{1,9},{5... | collective-permute-start | bytes 1769480 | tf_op jit(solution)/shard_map/ppermute | solution.py:442
  (21 other events, 171.5 us)

commit v5 on v4

--- a/solution.py
+++ b/solution.py
@@ -191,7 +191,7 @@
 def backward_kernel(
     q_ref, k_ref, v_ref, p_ref, attn_ref, *refs
 ):
-    early_refs, late_refs, refs = refs[:COLS], refs[COLS : 2 * COLS], refs[2 * COLS :]
+    early_refs, late_refs, refs = refs[:1], refs[1 : 1 + COLS], refs[1 + COLS :]
     dq_ref, own_ref, other_ref, grad_ref, sums_ref = refs
     step = pl.program_id(0)
     rows = q_ref.shape[0]
@@ -199,7 +199,7 @@
     @pl.when(step == 0)
     def _():
         early_a, late_a = early_refs[0].shape[0] * 2 // 3, late_refs[0].shape[0] * 2 // 3
-        early = sum(ref[...].astype(F32) for ref in early_refs).astype(BF16)
+        early = early_refs[0][...]
         late = sum(ref[...].astype(F32) for ref in late_refs).astype(BF16)
         own = early_a + late_a
         grad_ref[:early_a] = early[:early_a]
@@ -420,6 +420,18 @@
     )(mark)
 
 
+def fence0(mark):
+    return pl.pallas_call(
+        fence_kernel,
+        in_specs=[pl.BlockSpec(memory_space=pl.ANY)],
+        out_specs=pl.BlockSpec(memory_space=pl.ANY),
+        out_shape=jax.ShapeDtypeStruct((8, 128), F32),
+        compiler_params=pltpu.CompilerParams(has_side_effects=True),
+        cost_estimate=WINDOW,
+        name="fence",
+    )(mark)
+
+
 def after(value, *earlier):
     return lax.optimization_barrier((value, earlier))[0]
 
@@ -448,7 +460,7 @@
     grad_3 = to_plane(out_grad, -1)
     weights = (out_weight, swap(out_weight))
 
-    pieces = pack(*after((queries, keys_tile, values_tile), fence()))
+    pieces = pack(*after((queries, keys_tile, values_tile), fence0(queries)))
     pieces = after(pieces, weights[1])
     moved = after([to_col(pieces[j], j) for j in (1, 2, 3)], fence(pieces))
     over_col = jnp.stack([pieces[0], *moved])
@@ -470,6 +482,7 @@
 
     probs, attn, q, k, v = attention_forward(own_part, other_part, tokens)
     grad_2 = after(grad_2, attn)
+    early = [sum(t.astype(F32) for t in after(early, attn)).astype(BF16)]
 
     def plane_heads(rows, every):
         by_col = [pick(every, col ^ d) for d in range(COLS)]
@@ -482,11 +495,11 @@
 
     attn_a, attn_b = attn[:own], attn[own:]
     sent = jnp.concatenate([attn_a[3 * tokens :], attn_b[3 * half :]])
-    got = after([to_col(sent, j) for j in (1, 2, 3)], grad_2)
+    late = grad_pieces((grad_2,), *weights)
+    got = after([to_col(sent, j) for j in (1, 2, 3)], late)
     heads_2 = plane_heads(tokens, jnp.stack([sent, *got]))
     term_2 = mixed_term(heads_2, *weights, BF16)
     mixed_2 = to_plane(term_2, 1)
-    late = grad_pieces((after(grad_2, term_2),), *weights)
     late = [late[0]] + [to_col(late[j], j) for j in (1, 2, 3)]
     sent = jnp.concatenate([attn_a[: 3 * tokens], attn_b[: 3 * half]])
     pair = jnp.stack([sent, to_col(sent, 1)])
@@ -516,7 +529,6 @@
 
     head_0, head_1, head_3 = after(heads[:3], total)
     term_1 = mixed_term(head_1, *weights, BF16)
-    mixed_1 = to_plane(term_1, -1)
     term_3 = (mixed_2.astype(F32) + mixed_term(head_3, *weights, F32)).astype(BF16)
     total = swap(total)
     term_0 = mixed_term(after(head_0, term_1, term_3), *weights, F32, WINDOW)
@@ -525,15 +537,15 @@
     home = [home[0], *away]
     weight_grad = weight_grad_part(after(ours, home), grads, total)
 
+    mixed_1 = to_plane(after(term_1, home), -1)
     mixed_3 = to_plane(after(term_3, home), 1)
 
-    home = jnp.stack(home)
+    home = after(jnp.stack(home), weight_grad)
     back = [pick(home, (col - plane) % PLANES)] + [
         to_col(pick(home, ((col ^ j) - plane) % PLANES), j) for j in (1, 2, 3)
     ]
-    query_g, key_g, value_g = unpack(after(back, weight_grad), tokens, queries.shape[1])
-    mixed_3 = after(mixed_3, query_g)
-    mixed_1 = after(mixed_1, weight_grad)
+    query_g, key_g, value_g = unpack(back, tokens, queries.shape[1])
+    mixed_1, mixed_3 = after((mixed_1, mixed_3), query_g)
     mixed = (term_0 + mixed_1.astype(F32) + mixed_3.astype(F32)).astype(BF16)
     return (mixed, query_g, key_g, value_g, weight_grad)
 

time: 155 us -> 148 us (0.955)
  starting transfers between devices: 51 us -> 42.8 us
  waiting for transfers between devices: 57.8 us -> 60.2 us
    ppermute x12, starting transfers between devices: 27.7 us -> 20.6 us  [to_plane(): return lax.ppermute(block, 'row', row_shift(s))]
    ppermute x17, waiting for transfers between devices: 25.5 us -> 30.3 us  [to_col(): return lax.ppermute(block, 'col', col_xor(j))]
    ppermute x12, waiting for transfers between devices: 29.9 us -> 26.9 us  [to_plane(): return lax.ppermute(block, 'row', row_shift(s))]
    unnamed x43 -> x35, local copies, waits for them, and re-layouts: 4.34 us -> 2.81 us
  transfers between devices with their start and end apart: 39 -> 39, of which waited for: 21 -> 19; matrix products, arithmetic and copies ran while one was open for 3% -> 4% of each run, Pallas kernels for 22% -> 23%
where the time goes in v5:
time: 148 us
  waiting for transfers between devices  60.2 us (41%)
  starting transfers between devices  42.8 us (29%)
  Pallas kernels  34.3 us (23%)
  local copies, waits for them, and re-layouts  5.46 us (4%)
  other arithmetic  3.9 us (3%)
    ppermute x17, waiting for transfers between devices, to_col(): return lax.ppermute(block, 'col', col_xor(j))  30.3 us
    ppermute x12, waiting for transfers between devices, to_plane(): return lax.ppermute(block, 'row', row_shift(s))  26.9 us
    ppermute x12, starting transfers between devices, to_plane(): return lax.ppermute(block, 'row', row_shift(s))  20.6 us
    ppermute x17, starting transfers between devices, to_col(): return lax.ppermute(block, 'col', col_xor(j))  19.9 us
    pallas_call x2, Pallas kernels, weight_grad_part(): pl.pallas_call(functools.partial(weight_grad_kernel, len(heads)), out_sha...  7.2 us
    pallas_call x1, Pallas kernels, attention_forward(): pl.pallas_call(forward_kernel, grid=(3,), in_specs=[whole(*own[0].shape)]...  6.95 us
    pallas_call x2, Pallas kernels, grad_pieces(): pl.pallas_call(grad_kernel, out_shape=[piece] * COLS, scratch_shapes=[plt...  6.36 us
    pallas_call x1, Pallas kernels, attention_backward(): pl.pallas_call(backward_kernel, grid=(3,), in_specs=[by_query, by_head, b...  5.23 us
  transfers between devices with their start and end apart: 39, of which 19 were waited for; matrix products, arithmetic and copies ran while one was open for 4% of the time, Pallas kernels for 23%

profile of v5, /device:TPU:0, one launch (start us, length us, event | category | flops | bytes accessed | tf_op | source)
XLA Modules:
  0.0 147.7 jit_solution(15348833639160209829)
XLA Ops:
  0.6 3.1 %collective-permute-start.7 = (bf16[192,1536]{1,0:T(8,128)(2,1)}, bf16[192,1536]{1,0:T(8,128)(2,1)S(1)}, u32[]{:S(2)}, u32[]{:S(2)}) collective-permute-start(bf16[192,1536]{1,0:T(8,128)(2,1)} %refs_4_.3), channel_id=1, source_target_pairs={{0,8},{4,12},{8,16},{12,20},{16,24},{20,28},{24,0},{28,4},{1,9},{5... | collective-permute-start | bytes 1769480 | tf_op jit(solution)/shard_map/ppermute | solution.py:454
  3.7 2.1 %collective-permute-start.8 = (bf16[192,1536]{1,0:T(8,128)(2,1)}, bf16[192,1536]{1,0:T(8,128)(2,1)}, u32[]{:S(2)}, u32[]{:S(2)}) collective-permute-start(bf16[192,1536]{1,0:T(8,128)(2,1)} %refs_4_.3), channel_id=1, source_target_pairs={{0,24},{4,28},{8,0},{12,4},{16,8},{20,12},{24,16},{28,20},{1,25},{... | collective-permute-start | bytes 1769480 | tf_op jit(solution)/shard_map/ppermute | solution.py:454
  5.8 2.3 %pack_inputs.1 = (bf16[1056,128]{1,0:T(8,128)(2,1)}, bf16[1056,128]{1,0:T(8,128)(2,1)}, bf16[1056,128]{1,0:T(8,128)(2,1)}, bf16[1056,128]{1,0:T(8,128)(2,1)}) custom-call(bf16[192,768]{1,0:T(8,128)(2,1)} %q_ref, bf16[192,768]{1,0:T(8,128)(2,1)} %k_ref, bf16[192,768]{1,0:T(8,128)(2,1)} %v_ref), custom_call_target="tpu_custom_call" | custom-call | flops 40000000000 | tf_op jit(solution)/shard_map/pack_inputs/pallas_call | solution.py:282
  8.9 1.6 %collective-permute-start.1 = (bf16[1056,128]{1,0:T(8,128)(2,1)}, bf16[1056,128]{1,0:T(8,128)(2,1)S(1)}, u32[]{:S(2)}, u32[]{:S(2)}) collective-permute-start(bf16[1056,128]{1,0:T(8,128)(2,1)} %get-tuple-element.92), channel_id=1, source_target_pairs={{0,1},{1,0},{2,3},{3,2},{4,5},{5,4},{6,7},{7,6},{8,9},{9,8},{10,11... | collective-permute-start | bytes 811016 | tf_op jit(solution)/shard_map/ppermute | solution.py:451
  12.9 5.5 %collective-permute-done.1 = bf16[1056,128]{1,0:T(8,128)(2,1)S(1)} collective-permute-done((bf16[1056,128]{1,0:T(8,128)(2,1)}, bf16[1056,128]{1,0:T(8,128)(2,1)S(1)}, u32[]{:S(2)}, u32[]{:S(2)}) %collective-permute-start.1) | collective-permute-done | bytes 270368 | tf_op jit(solution)/shard_map/ppermute | solution.py:451
  18.4 6.4 %collective-permute-done.2 = bf16[1056,128]{1,0:T(8,128)(2,1)S(1)} collective-permute-done((bf16[1056,128]{1,0:T(8,128)(2,1)}, bf16[1056,128]{1,0:T(8,128)(2,1)S(1)}, u32[]{:S(2)}, u32[]{:S(2)}) %collective-permute-start.2) | collective-permute-done | bytes 270368 | tf_op jit(solution)/shard_map/ppermute | solution.py:451
  25.7 3.8 %collective-permute-start.5 = (bf16[1056,128]{1,0:T(8,128)(2,1)S(1)}, bf16[1056,128]{1,0:T(8,128)(2,1)}, u32[]{:S(2)}, u32[]{:S(2)}) collective-permute-start(bf16[1056,128]{1,0:T(8,128)(2,1)S(1)} %get-tuple-element.168), channel_id=1, source_target_pairs={{0,24},{4,28},{8,0},{12,4},{16,8},{20,12},{24,16},{28,20},{1,25},{... | collective-permute-start | bytes 811016 | tf_op jit(solution)/shard_map/ppermute | solution.py:454
  29.5 3.5 %collective-permute-done.8.refs_2_.refs_6_ = bf16[192,1536]{1,0:T(8,128)(2,1)} collective-permute-done((bf16[192,1536]{1,0:T(8,128)(2,1)}, bf16[192,1536]{1,0:T(8,128)(2,1)}, u32[]{:S(2)}, u32[]{:S(2)}) %collective-permute-start.8) | collective-permute-done | bytes 589856 | tf_op jit(solution)/shard_map/ppermute | solution.py:454
  33.1 4.4 %grad_pieces.2 = (bf16[864,128]{1,0:T(8,128)(2,1)S(1)}, bf16[864,128]{1,0:T(8,128)(2,1)}, bf16[864,128]{1,0:T(8,128)(2,1)}, bf16[864,128]{1,0:T(8,128)(2,1)}) custom-call(bf16[192,1536]{1,0:T(8,128)(2,1)S(1)} %copy-done.1, bf16[192,1536]{1,0:T(8,128)(2,1)S(1)} %collective-permute-done.7.refs_1_.refs_5_, ...), custom_call_target="tpu_custom_call" | custom-call | flops 40000000000 | tf_op jit(solution)/shard_map/grad_pieces/pallas_call | solution.py:314
  38.7 4.3 %collective-permute-done.5.refs_2_ = bf16[1056,128]{1,0:T(8,128)(2,1)} collective-permute-done((bf16[1056,128]{1,0:T(8,128)(2,1)S(1)}, bf16[1056,128]{1,0:T(8,128)(2,1)}, u32[]{:S(2)}, u32[]{:S(2)}) %collective-permute-start.5) | collective-permute-done | bytes 270368 | tf_op jit(solution)/shard_map/ppermute | solution.py:454
  46.5 8.7 %collective-permute-done.6.refs_3_ = bf16[1056,128]{1,0:T(8,128)(2,1)} collective-permute-done((bf16[1056,128]{1,0:T(8,128)(2,1)}, bf16[1056,128]{1,0:T(8,128)(2,1)}, u32[]{:S(2)}, u32[]{:S(2)}) %collective-permute-start.6) | collective-permute-done | bytes 270368 | tf_op jit(solution)/shard_map/ppermute | solution.py:454
  59.1 6.9 %attention_forward.1 = (bf16[3,1536,384]{2,1,0:T(8,128)(2,1)}, bf16[1152,128]{1,0:T(8,128)(2,1)S(1)}, bf16[1152,128]{1,0:T(8,128)(2,1)S(1)}, bf16[2,1536,128]{2,1,0:T(8,128)(2,1)S(1)}, bf16[2,1536,128]{2,1,0:T(8,128)(2,1)S(1)}) custom-call(bf16[1056,128]{1,0:T(8,128)(2,1)S(1)} %get-tuple-element.106.refs_0_, ...), custom_call_target="tpu_custom_call" | custom-call | flops 40000000000 | tf_op jit(solution)/shard_map/attention_forward/pallas_call | solution.py:167
  66.1 1.6 %collective-permute-start.18 = (bf16[288,128]{1,0:T(8,128)(2,1)S(1)}, bf16[288,128]{1,0:T(8,128)(2,1)S(1)}, u32[]{:S(2)}, u32[]{:S(2)}) collective-permute-start(bf16[288,128]{1,0:T(8,128)(2,1)S(1)} %get-tuple-element.221), channel_id=1, source_target_pairs={{0,1},{1,0},{2,3},{3,2},{4,5},{5,4},{6,7},{7,6},{8,9},{9,8},{10,11... | collective-permute-start | bytes 221192 | tf_op jit(solution)/shard_map/ppermute | solution.py:451
  67.6 1.5 %collective-permute-start.19 = (bf16[288,128]{1,0:T(8,128)(2,1)S(1)}, bf16[288,128]{1,0:T(8,128)(2,1)S(1)}, u32[]{:S(2)}, u32[]{:S(2)}) collective-permute-start(bf16[288,128]{1,0:T(8,128)(2,1)S(1)} %get-tuple-element.221), channel_id=1, source_target_pairs={{0,2},{1,3},{2,0},{3,1},{4,6},{5,7},{6,4},{7,5},{8,10},{9,11},{10,... | collective-permute-start | bytes 221192 | tf_op jit(solution)/shard_map/ppermute | solution.py:451
  69.7 1.6 %collective-permute-start.16 = (bf16[864,128]{1,0:T(8,128)(2,1)S(1)}, bf16[864,128]{1,0:T(8,128)(2,1)S(1)}, u32[]{:S(2)}, u32[]{:S(2)}) collective-permute-start(bf16[864,128]{1,0:T(8,128)(2,1)S(1)} %get-tuple-element.219), channel_id=1, source_target_pairs={{0,1},{1,0},{2,3},{3,2},{4,5},{5,4},{6,7},{7,6},{8,9},{9,8},{10,11... | collective-permute-start | bytes 663560 | tf_op jit(solution)/shard_map/ppermute | solution.py:451
  72.6 2.0 %grad_pieces.3 = (bf16[288,128]{1,0:T(8,128)(2,1)S(1)}, bf16[288,128]{1,0:T(8,128)(2,1)S(1)}, bf16[288,128]{1,0:T(8,128)(2,1)S(1)}, bf16[288,128]{1,0:T(8,128)(2,1)S(1)}) custom-call(bf16[192,1536]{1,0:T(8,128)(2,1)} %collective-permute-done.21.refs_0_.refs_7_, bf16[384,1536]{1,0:T(8,128)(2,1)S(1)} %copy-done, ...), custom_call_target="tpu_custom_call" | custom-call | flops 40000000000 | tf_op jit(solution)/shard_map/grad_pieces/pallas_call | solution.py:314
  75.9 1.5 %collective-permute-start.24 = (bf16[288,128]{1,0:T(8,128)(2,1)S(1)}, bf16[288,128]{1,0:T(8,128)(2,1)S(1)}, u32[]{:S(2)}, u32[]{:S(2)}) collective-permute-start(bf16[288,128]{1,0:T(8,128)(2,1)S(1)} %get-tuple-element.120), channel_id=1, source_target_pairs={{0,2},{1,3},{2,0},{3,1},{4,6},{5,7},{6,4},{7,5},{8,10},{9,11},{10,... | collective-permute-start | bytes 221192 | tf_op jit(solution)/shard_map/ppermute | solution.py:451
  79.2 2.7 %collective-permute-start.22 = (bf16[192,1536]{1,0:T(8,128)(2,1)S(1)}, bf16[192,1536]{1,0:T(8,128)(2,1)S(1)}, u32[]{:S(2)}, u32[]{:S(2)}) collective-permute-start(bf16[192,1536]{1,0:T(8,128)(2,1)S(1)} %mixed_term.4), channel_id=1, source_target_pairs={{0,8},{4,12},{8,16},{12,20},{16,24},{20,28},{24,0},{28,4},{1,9},{5... | collective-permute-start | bytes 1769480 | tf_op jit(solution)/shard_map/ppermute | solution.py:454
  82.7 5.2 %attention_backward.1 = (bf16[1152,128]{1,0:T(8,128)(2,1)S(1)}, f32[2,2,768,128]{3,2,1,0:T(8,128)S(1)}, bf16[2,2,768,128]{3,2,1,0:T(8,128)(2,1)S(1)}) custom-call(bf16[1152,128]{1,0:T(8,128)(2,1)S(1)} %get-tuple-element.125.q_ref, bf16[2,1536,128]{2,1,0:T(8,128)(2,1)S(1)} %get-tuple-element.126.k_ref, bf16[2,1536,128]{2,1,0:T(8,128)(2,1)S(1)} %get-tuple-element.127.v_ref, ...), custom_call_target="tpu_custom_call" | custom-call | flops 40000000000 | tf_op jit(solution)/shard_map/attention_backward/pallas_call | solution.py:239
  90.7 2.3 %collective-permute-start.30 = (bf16[1056,128]{1,0:T(8,128)(2,1)S(1)}, bf16[1056,128]{1,0:T(8,128)(2,1)S(1)}, u32[]{:S(2)}, u32[]{:S(2)}) collective-permute-start(bf16[1056,128]{1,0:T(8,128)(2,1)S(1)} %get-tuple-element.180), channel_id=1, source_target_pairs={{0,24},{4,28},{8,0},{12,4},{16,8},{20,12},{24,16},{28,20},{1,25},{... | collective-permute-start | bytes 811016 | tf_op jit(solution)/shard_map/ppermute | solution.py:454
  94.1 1.8 %collective-permute-start.32 = (bf16[1056,128]{1,0:T(8,128)(2,1)S(1)}, bf16[1056,128]{1,0:T(8,128)(2,1)S(1)}, u32[]{:S(2)}, u32[]{:S(2)}) collective-permute-start(bf16[1056,128]{1,0:T(8,128)(2,1)S(1)} %get-tuple-element.178), channel_id=1, source_target_pairs={{0,8},{4,12},{8,16},{12,20},{16,24},{20,28},{24,0},{28,4},{1,9},{5... | collective-permute-start | bytes 811016 | tf_op jit(solution)/shard_map/ppermute | solution.py:454
  95.9 5.8 %collective-permute-done.17 = bf16[2,864,128]{2,1,0:T(8,128)(2,1)S(1)} collective-permute-done((bf16[2,864,128]{2,1,0:T(8,128)(2,1)S(1)}, bf16[2,864,128]{2,1,0:T(8,128)(2,1)S(1)}, u32[]{:S(2)}, u32[]{:S(2)}) %collective-permute-start.17) | collective-permute-done | bytes 442400 | tf_op jit(solution)/shard_map/ppermute | solution.py:451
  103.3 3.1 %weight_grad.2 = bf16[384,1536]{1,0:T(8,128)(2,1)S(1)} custom-call(bf16[192,384]{1,0:T(8,128)(2,1)S(1)} %get-tuple-element.138.refs_0_, bf16[192,384]{1,0:T(8,128)(2,1)S(1)} %get-tuple-element.139.refs_1_, bf16[192,384]{1,0:T(8,128)(2,1)S(1)} %get-tuple-element.140.refs_2_, bf16[192,384]{1,0:T(8,128)(2,1)S(1)} %get-tuple-element.141.refs_3_, ...), custom_call_target="tpu_custom_call" | custom-call | flops 40000000000 | tf_op jit(solution)/shard_map/weight_grad/pallas_call | solution.py:358
  108.2 1.6 %mixed_term.5 = bf16[192,1536]{1,0:T(8,128)(2,1)} custom-call(bf16[192,768]{1,0:T(8,128)(2,1)S(1)} %get-tuple-element.143.block_ref, bf16[384,1536]{1,0:T(8,128)(2,1)S(1)} %copy-done, bf16[384,1536]{1,0:T(8,128)(2,1)S(1)} %collective-permute-done.refs_4_.refs_2_.other_ref), custom_call_target="tpu_custom_call" | custom-call | flops 1000000 | bytes 1000 | tf_op jit(solution)/shard_map/mixed_term/pallas_call | solution.py:337
  110.6 7.5 %collective-permute-done.31 = bf16[1056,128]{1,0:T(8,128)(2,1)S(1)} collective-permute-done((bf16[1056,128]{1,0:T(8,128)(2,1)S(1)}, bf16[1056,128]{1,0:T(8,128)(2,1)S(1)}, u32[]{:S(2)}, u32[]{:S(2)}) %collective-permute-start.31) | collective-permute-done | bytes 270368 | tf_op jit(solution)/shard_map/ppermute | solution.py:454
  118.2 3.8 %collective-permute-start.34 = (bf16[192,1536]{1,0:T(8,128)(2,1)}, bf16[192,1536]{1,0:T(8,128)(2,1)S(1)}, u32[]{:S(2)}, u32[]{:S(2)}) collective-permute-start(bf16[192,1536]{1,0:T(8,128)(2,1)} %mixed_term.5), channel_id=1, source_target_pairs={{0,24},{4,28},{8,0},{12,4},{16,8},{20,12},{24,16},{28,20},{1,25},{... | collective-permute-start | bytes 1769480 | tf_op jit(solution)/shard_map/ppermute | solution.py:454
  122.0 4.1 %weight_grad.3 = bf16[384,1536]{1,0:T(8,128)(2,1)} custom-call(bf16[192,384]{1,0:T(8,128)(2,1)S(1)} %get-tuple-element.152.refs_0_, bf16[192,384]{1,0:T(8,128)(2,1)S(1)} %get-tuple-element.153.refs_1_, bf16[192,384]{1,0:T(8,128)(2,1)S(1)} %get-tuple-element.154.refs_2_, bf16[192,384]{1,0:T(8,128)(2,1)S(1)} %get-tuple-element.155.refs_3_, ...), custom_call_target="tpu_custom_call" | custom-call | flops 40000000000 | tf_op jit(solution)/shard_map/weight_grad/pallas_call | solution.py:358
  127.1 1.5 %collective-permute-start.36 = (bf16[1056,128]{1,0:T(8,128)(2,1)S(1)}, bf16[1056,128]{1,0:T(8,128)(2,1)S(1)}, u32[]{:S(2)}, u32[]{:S(2)}) collective-permute-start(bf16[1056,128]{1,0:T(8,128)(2,1)S(1)} %get-tuple-element.165), channel_id=1, source_target_pairs={{0,1},{1,0},{2,3},{3,2},{4,5},{5,4},{6,7},{7,6},{8,9},{9,8},{10,11... | collective-permute-start | bytes 811016 | tf_op jit(solution)/shard_map/ppermute | solution.py:451
  130.5 5.9 %collective-permute-done.36.refs_1_ = bf16[1056,128]{1,0:T(8,128)(2,1)S(1)} collective-permute-done((bf16[1056,128]{1,0:T(8,128)(2,1)S(1)}, bf16[1056,128]{1,0:T(8,128)(2,1)S(1)}, u32[]{:S(2)}, u32[]{:S(2)}) %collective-permute-start.36) | collective-permute-done | bytes 270368 | tf_op jit(solution)/shard_map/ppermute | solution.py:451
  136.5 5.0 %collective-permute-done.37.refs_2_ = bf16[1056,128]{1,0:T(8,128)(2,1)S(1)} collective-permute-done((bf16[1056,128]{1,0:T(8,128)(2,1)S(1)}, bf16[1056,128]{1,0:T(8,128)(2,1)S(1)}, u32[]{:S(2)}, u32[]{:S(2)}) %collective-permute-start.37) | collective-permute-done | bytes 270368 | tf_op jit(solution)/shard_map/ppermute | solution.py:451
  142.9 2.3 %unpack_outputs.1 = (bf16[192,768]{1,0:T(8,128)(2,1)}, bf16[192,768]{1,0:T(8,128)(2,1)}, bf16[192,768]{1,0:T(8,128)(2,1)}) custom-call(bf16[1056,128]{1,0:T(8,128)(2,1)} %get-tuple-element.166.refs_0_, bf16[1056,128]{1,0:T(8,128)(2,1)} %copy-done.7, bf16[1056,128]{1,0:T(8,128)(2,1)} %copy-done.8, bf16[1056,128]{1,0:T(8,128)(2,1)} %copy-done.9), custom_call_target="tpu_custom_call" | custom-call | flops 1000000 | bytes 1000 | tf_op jit(solution)/shard_map/unpack_outputs/pallas_call | solution.py:398
  145.2 1.5 %collective-permute-done.34 = bf16[192,1536]{1,0:T(8,128)(2,1)S(1)} collective-permute-done((bf16[192,1536]{1,0:T(8,128)(2,1)}, bf16[192,1536]{1,0:T(8,128)(2,1)S(1)}, u32[]{:S(2)}, u32[]{:S(2)}) %collective-permute-start.34) | collective-permute-done | bytes 589856 | tf_op jit(solution)/shard_map/ppermute | solution.py:454
  (129 shorter events, 31.6 us)
Async XLA Ops:
  0.6 28.9 %collective-permute-start.7 = (bf16[192,1536]{1,0:T(8,128)(2,1)}, bf16[192,1536]{1,0:T(8,128)(2,1)S(1)}, u32[]{:S(2)}, u32[]{:S(2)}) collective-permute-start(bf16[192,1536]{1,0:T(8,128)(2,1)} %refs_4_.3), channel_id=1, source_target_pairs={{0,8},{4,12},{8,16},{12,20},{16,24},{20,28},{24,0},{28,4},{1,9},{5... | collective-permute-start | bytes 1769480 | tf_op jit(solution)/shard_map/ppermute | solution.py:454
  3.7 29.3 %collective-permute-start.8 = (bf16[192,1536]{1,0:T(8,128)(2,1)}, bf16[192,1536]{1,0:T(8,128)(2,1)}, u32[]{:S(2)}, u32[]{:S(2)}) collective-permute-start(bf16[192,1536]{1,0:T(8,128)(2,1)} %refs_4_.3), channel_id=1, source_target_pairs={{0,24},{4,28},{8,0},{12,4},{16,8},{20,12},{24,16},{28,20},{1,25},{... | collective-permute-start | bytes 1769480 | tf_op jit(solution)/shard_map/ppermute | solution.py:454
  5.8 3.1 %collective-permute-start = (bf16[384,1536]{1,0:T(8,128)(2,1)}, bf16[384,1536]{1,0:T(8,128)(2,1)S(1)}, u32[]{:S(2)}, u32[]{:S(2)}) collective-permute-start(bf16[384,1536]{1,0:T(8,128)(2,1)} %own_ref.7), channel_id=1, source_target_pairs={{0,4},{4,0},{8,12},{12,8},{16,20},{20,16},{24,28},{28,24},{1,5},{5... | collective-permute-start | bytes 3538952 | tf_op jit(solution)/shard_map/ppermute | solution.py:457
  8.9 9.5 %collective-permute-start.1 = (bf16[1056,128]{1,0:T(8,128)(2,1)}, bf16[1056,128]{1,0:T(8,128)(2,1)S(1)}, u32[]{:S(2)}, u32[]{:S(2)}) collective-permute-start(bf16[1056,128]{1,0:T(8,128)(2,1)} %get-tuple-element.92), channel_id=1, source_target_pairs={{0,1},{1,0},{2,3},{3,2},{4,5},{5,4},{6,7},{7,6},{8,9},{9,8},{10,11... | collective-permute-start | bytes 811016 | tf_op jit(solution)/shard_map/ppermute | solution.py:451
  10.5 14.2 %collective-permute-start.2 = (bf16[1056,128]{1,0:T(8,128)(2,1)}, bf16[1056,128]{1,0:T(8,128)(2,1)S(1)}, u32[]{:S(2)}, u32[]{:S(2)}) collective-permute-start(bf16[1056,128]{1,0:T(8,128)(2,1)} %get-tuple-element.93), channel_id=1, source_target_pairs={{0,2},{1,3},{2,0},{3,1},{4,6},{5,7},{6,4},{7,5},{8,10},{9,11},{10,... | collective-permute-start | bytes 811016 | tf_op jit(solution)/shard_map/ppermute | solution.py:451
  12.0 12.7 %collective-permute-start.3 = (bf16[1056,128]{1,0:T(8,128)(2,1)}, bf16[1056,128]{1,0:T(8,128)(2,1)S(1)}, u32[]{:S(2)}, u32[]{:S(2)}) collective-permute-start(bf16[1056,128]{1,0:T(8,128)(2,1)} %get-tuple-element.94), channel_id=1, source_target_pairs={{0,3},{1,2},{2,1},{3,0},{4,7},{5,6},{6,5},{7,4},{8,11},{9,10},{10,... | collective-permute-start | bytes 811016 | tf_op jit(solution)/shard_map/ppermute | solution.py:451
  25.7 13.0 %collective-permute-start.4 = (bf16[1056,128]{1,0:T(8,128)(2,1)S(1)}, bf16[1056,128]{1,0:T(8,128)(2,1)}, u32[]{:S(2)}, u32[]{:S(2)}) collective-permute-start(bf16[1056,128]{1,0:T(8,128)(2,1)S(1)} %get-tuple-element.169), channel_id=1, source_target_pairs={{0,8},{4,12},{8,16},{12,20},{16,24},{20,28},{24,0},{28,4},{1,9},{5... | collective-permute-start | bytes 811016 | tf_op jit(solution)/shard_map/ppermute | solution.py:454
  25.7 17.3 %collective-permute-start.5 = (bf16[1056,128]{1,0:T(8,128)(2,1)S(1)}, bf16[1056,128]{1,0:T(8,128)(2,1)}, u32[]{:S(2)}, u32[]{:S(2)}) collective-permute-start(bf16[1056,128]{1,0:T(8,128)(2,1)S(1)} %get-tuple-element.168), channel_id=1, source_target_pairs={{0,24},{4,28},{8,0},{12,4},{16,8},{20,12},{24,16},{28,20},{1,25},{... | collective-permute-start | bytes 811016 | tf_op jit(solution)/shard_map/ppermute | solution.py:454
  29.5 25.7 %collective-permute-start.6 = (bf16[1056,128]{1,0:T(8,128)(2,1)}, bf16[1056,128]{1,0:T(8,128)(2,1)}, u32[]{:S(2)}, u32[]{:S(2)}) collective-permute-start(bf16[1056,128]{1,0:T(8,128)(2,1)} %get-tuple-element.167), channel_id=1, source_target_pairs={{0,16},{4,20},{8,24},{12,28},{16,0},{20,4},{24,8},{28,12},{1,17},{... | collective-permute-start | bytes 811016 | tf_op jit(solution)/shard_map/ppermute | solution.py:454
  43.0 12.2 %collective-permute-start.10 = (bf16[864,128]{1,0:T(8,128)(2,1)}, bf16[864,128]{1,0:T(8,128)(2,1)}, u32[]{:S(2)}, u32[]{:S(2)}) collective-permute-start(bf16[864,128]{1,0:T(8,128)(2,1)} %get-tuple-element.104), channel_id=1, source_target_pairs={{0,2},{1,3},{2,0},{3,1},{4,6},{5,7},{6,4},{7,5},{8,10},{9,11},{10,... | collective-permute-start | bytes 663560 | tf_op jit(solution)/shard_map/ppermute | solution.py:451
  44.6 10.6 %collective-permute-start.11 = (bf16[864,128]{1,0:T(8,128)(2,1)}, bf16[864,128]{1,0:T(8,128)(2,1)}, u32[]{:S(2)}, u32[]{:S(2)}) collective-permute-start(bf16[864,128]{1,0:T(8,128)(2,1)} %get-tuple-element.105), channel_id=1, source_target_pairs={{0,3},{1,2},{2,1},{3,0},{4,7},{5,6},{6,5},{7,4},{8,11},{9,10},{10,... | collective-permute-start | bytes 663560 | tf_op jit(solution)/shard_map/ppermute | solution.py:451
  46.0 10.1 %collective-permute-start.9 = (bf16[864,128]{1,0:T(8,128)(2,1)}, bf16[864,128]{1,0:T(8,128)(2,1)}, u32[]{:S(2)}, u32[]{:S(2)}) collective-permute-start(bf16[864,128]{1,0:T(8,128)(2,1)} %get-tuple-element.103), channel_id=1, source_target_pairs={{0,1},{1,0},{2,3},{3,2},{4,5},{5,4},{6,7},{7,6},{8,9},{9,8},{10,11... | collective-permute-start | bytes 663560 | tf_op jit(solution)/shard_map/ppermute | solution.py:451
  55.2 17.4 %collective-permute-start.21 = (bf16[192,1536]{1,0:T(8,128)(2,1)S(1)}, bf16[192,1536]{1,0:T(8,128)(2,1)}, u32[]{:S(2)}, u32[]{:S(2)}) collective-permute-start(bf16[192,1536]{1,0:T(8,128)(2,1)S(1)} %collective-permute-done.7.refs_1_.refs_5_), channel_id=1, source_target_pairs={{0,8},{4,12},{8,16},{12,20},{16,24},{20,28},{24,0},{28,4},{1,9},{5... | collective-permute-start | bytes 1769480 | tf_op jit(solution)/shard_map/ppermute | solution.py:454
  56.6 2.5 %collective-permute-start.15 = (bf16[1056,128]{1,0:T(8,128)(2,1)}, bf16[1056,128]{1,0:T(8,128)(2,1)}, u32[]{:S(2)}, u32[]{:S(2)}) collective-permute-start(bf16[1056,128]{1,0:T(8,128)(2,1)} %collective-permute-done.6.refs_3_), channel_id=1, source_target_pairs={{0,4},{4,0},{8,12},{12,8},{16,20},{20,16},{24,28},{28,24},{1,5},{5... | collective-permute-start | bytes 811016 | tf_op jit(solution)/shard_map/ppermute | solution.py:457
  66.1 9.8 %collective-permute-start.18 = (bf16[288,128]{1,0:T(8,128)(2,1)S(1)}, bf16[288,128]{1,0:T(8,128)(2,1)S(1)}, u32[]{:S(2)}, u32[]{:S(2)}) collective-permute-start(bf16[288,128]{1,0:T(8,128)(2,1)S(1)} %get-tuple-element.221), channel_id=1, source_target_pairs={{0,1},{1,0},{2,3},{3,2},{4,5},{5,4},{6,7},{7,6},{8,9},{9,8},{10,11... | collective-permute-start | bytes 221192 | tf_op jit(solution)/shard_map/ppermute | solution.py:451
  67.6 9.8 %collective-permute-start.19 = (bf16[288,128]{1,0:T(8,128)(2,1)S(1)}, bf16[288,128]{1,0:T(8,128)(2,1)S(1)}, u32[]{:S(2)}, u32[]{:S(2)}) collective-permute-start(bf16[288,128]{1,0:T(8,128)(2,1)S(1)} %get-tuple-element.221), channel_id=1, source_target_pairs={{0,2},{1,3},{2,0},{3,1},{4,6},{5,7},{6,4},{7,5},{8,10},{9,11},{10,... | collective-permute-start | bytes 221192 | tf_op jit(solution)/shard_map/ppermute | solution.py:451
  69.2 9.0 %collective-permute-start.20 = (bf16[288,128]{1,0:T(8,128)(2,1)S(1)}, bf16[288,128]{1,0:T(8,128)(2,1)S(1)}, u32[]{:S(2)}, u32[]{:S(2)}) collective-permute-start(bf16[288,128]{1,0:T(8,128)(2,1)S(1)} %get-tuple-element.221), channel_id=1, source_target_pairs={{0,3},{1,2},{2,1},{3,0},{4,7},{5,6},{6,5},{7,4},{8,11},{9,10},{10,... | collective-permute-start | bytes 221192 | tf_op jit(solution)/shard_map/ppermute | solution.py:451
  69.7 19.0 %collective-permute-start.16 = (bf16[864,128]{1,0:T(8,128)(2,1)S(1)}, bf16[864,128]{1,0:T(8,128)(2,1)S(1)}, u32[]{:S(2)}, u32[]{:S(2)}) collective-permute-start(bf16[864,128]{1,0:T(8,128)(2,1)S(1)} %get-tuple-element.219), channel_id=1, source_target_pairs={{0,1},{1,0},{2,3},{3,2},{4,5},{5,4},{6,7},{7,6},{8,9},{9,8},{10,11... | collective-permute-start | bytes 663560 | tf_op jit(solution)/shard_map/ppermute | solution.py:451
  74.6 7.3 %collective-permute-start.23 = (bf16[288,128]{1,0:T(8,128)(2,1)S(1)}, bf16[288,128]{1,0:T(8,128)(2,1)S(1)}, u32[]{:S(2)}, u32[]{:S(2)}) collective-permute-start(bf16[288,128]{1,0:T(8,128)(2,1)S(1)} %get-tuple-element.119), channel_id=1, source_target_pairs={{0,1},{1,0},{2,3},{3,2},{4,5},{5,4},{6,7},{7,6},{8,9},{9,8},{10,11... | collective-permute-start | bytes 221192 | tf_op jit(solution)/shard_map/ppermute | solution.py:451
  75.9 6.0 %collective-permute-start.24 = (bf16[288,128]{1,0:T(8,128)(2,1)S(1)}, bf16[288,128]{1,0:T(8,128)(2,1)S(1)}, u32[]{:S(2)}, u32[]{:S(2)}) collective-permute-start(bf16[288,128]{1,0:T(8,128)(2,1)S(1)} %get-tuple-element.120), channel_id=1, source_target_pairs={{0,2},{1,3},{2,0},{3,1},{4,6},{5,7},{6,4},{7,5},{8,10},{9,11},{10,... | collective-permute-start | bytes 221192 | tf_op jit(solution)/shard_map/ppermute | solution.py:451
  77.4 5.3 %collective-permute-start.25 = (bf16[288,128]{1,0:T(8,128)(2,1)S(1)}, bf16[288,128]{1,0:T(8,128)(2,1)S(1)}, u32[]{:S(2)}, u32[]{:S(2)}) collective-permute-start(bf16[288,128]{1,0:T(8,128)(2,1)S(1)} %get-tuple-element.121), channel_id=1, source_target_pairs={{0,3},{1,2},{2,1},{3,0},{4,7},{5,6},{6,5},{7,4},{8,11},{9,10},{10,... | collective-permute-start | bytes 221192 | tf_op jit(solution)/shard_map/ppermute | solution.py:451
  79.2 22.6 %collective-permute-start.22 = (bf16[192,1536]{1,0:T(8,128)(2,1)S(1)}, bf16[192,1536]{1,0:T(8,128)(2,1)S(1)}, u32[]{:S(2)}, u32[]{:S(2)}) collective-permute-start(bf16[192,1536]{1,0:T(8,128)(2,1)S(1)} %mixed_term.4), channel_id=1, source_target_pairs={{0,8},{4,12},{8,16},{12,20},{16,24},{20,28},{24,0},{28,4},{1,9},{5... | collective-permute-start | bytes 1769480 | tf_op jit(solution)/shard_map/ppermute | solution.py:454
  89.5 12.2 %collective-permute-start.17 = (bf16[2,864,128]{2,1,0:T(8,128)(2,1)S(1)}, bf16[2,864,128]{2,1,0:T(8,128)(2,1)S(1)}, u32[]{:S(2)}, u32[]{:S(2)}) collective-permute-start(bf16[2,864,128]{2,1,0:T(8,128)(2,1)S(1)} %pad_maximum_fusion.2), channel_id=1, source_target_pairs={{0,2},{1,3},{2,0},{3,1},{4,6},{5,7},{6,4},{7,5},{8,10},{9,11},{10,... | collective-permute-start | bytes 1327112 | tf_op jit(solution)/shard_map/ppermute | solution.py:451
  90.7 19.9 %collective-permute-start.30 = (bf16[1056,128]{1,0:T(8,128)(2,1)S(1)}, bf16[1056,128]{1,0:T(8,128)(2,1)S(1)}, u32[]{:S(2)}, u32[]{:S(2)}) collective-permute-start(bf16[1056,128]{1,0:T(8,128)(2,1)S(1)} %get-tuple-element.180), channel_id=1, source_target_pairs={{0,24},{4,28},{8,0},{12,4},{16,8},{20,12},{24,16},{28,20},{1,25},{... | collective-permute-start | bytes 811016 | tf_op jit(solution)/shard_map/ppermute | solution.py:454
  93.1 25.1 %collective-permute-start.31 = (bf16[1056,128]{1,0:T(8,128)(2,1)S(1)}, bf16[1056,128]{1,0:T(8,128)(2,1)S(1)}, u32[]{:S(2)}, u32[]{:S(2)}) collective-permute-start(bf16[1056,128]{1,0:T(8,128)(2,1)S(1)} %get-tuple-element.179), channel_id=1, source_target_pairs={{0,16},{4,20},{8,24},{12,28},{16,0},{20,4},{24,8},{28,12},{1,17},{... | collective-permute-start | bytes 811016 | tf_op jit(solution)/shard_map/ppermute | solution.py:454
  94.1 24.1 %collective-permute-start.32 = (bf16[1056,128]{1,0:T(8,128)(2,1)S(1)}, bf16[1056,128]{1,0:T(8,128)(2,1)S(1)}, u32[]{:S(2)}, u32[]{:S(2)}) collective-permute-start(bf16[1056,128]{1,0:T(8,128)(2,1)S(1)} %get-tuple-element.178), channel_id=1, source_target_pairs={{0,8},{4,12},{8,16},{12,20},{16,24},{20,28},{24,0},{28,4},{1,9},{5... | collective-permute-start | bytes 811016 | tf_op jit(solution)/shard_map/ppermute | solution.py:454
  106.4 11.7 %collective-permute-start.33 = (bf16[384,1536]{1,0:T(8,128)(2,1)S(1)}, bf16[384,1536]{1,0:T(8,128)(2,1)S(1)}, u32[]{:S(2)}, u32[]{:S(2)}) collective-permute-start(bf16[384,1536]{1,0:T(8,128)(2,1)S(1)} %weight_grad.2), channel_id=1, source_target_pairs={{0,4},{4,0},{8,12},{12,8},{16,20},{20,16},{24,28},{28,24},{1,5},{5... | collective-permute-start | bytes 3538952 | tf_op jit(solution)/shard_map/ppermute | solution.py:457
  118.2 27.0 %collective-permute-start.35 = (bf16[192,1536]{1,0:T(8,128)(2,1)}, bf16[192,1536]{1,0:T(8,128)(2,1)S(1)}, u32[]{:S(2)}, u32[]{:S(2)}) collective-permute-start(bf16[192,1536]{1,0:T(8,128)(2,1)} %add_convert_fusion.2), channel_id=1, source_target_pairs={{0,8},{4,12},{8,16},{12,20},{16,24},{20,28},{24,0},{28,4},{1,9},{5... | collective-permute-start | bytes 1769480 | tf_op jit(solution)/shard_map/ppermute | solution.py:454
  118.2 28.5 %collective-permute-start.34 = (bf16[192,1536]{1,0:T(8,128)(2,1)}, bf16[192,1536]{1,0:T(8,128)(2,1)S(1)}, u32[]{:S(2)}, u32[]{:S(2)}) collective-permute-start(bf16[192,1536]{1,0:T(8,128)(2,1)} %mixed_term.5), channel_id=1, source_target_pairs={{0,24},{4,28},{8,0},{12,4},{16,8},{20,12},{24,16},{28,20},{1,25},{... | collective-permute-start | bytes 1769480 | tf_op jit(solution)/shard_map/ppermute | solution.py:454
  127.1 9.4 %collective-permute-start.36 = (bf16[1056,128]{1,0:T(8,128)(2,1)S(1)}, bf16[1056,128]{1,0:T(8,128)(2,1)S(1)}, u32[]{:S(2)}, u32[]{:S(2)}) collective-permute-start(bf16[1056,128]{1,0:T(8,128)(2,1)S(1)} %get-tuple-element.165), channel_id=1, source_target_pairs={{0,1},{1,0},{2,3},{3,2},{4,5},{5,4},{6,7},{7,6},{8,9},{9,8},{10,11... | collective-permute-start | bytes 811016 | tf_op jit(solution)/shard_map/ppermute | solution.py:451
  128.6 12.9 %collective-permute-start.37 = (bf16[1056,128]{1,0:T(8,128)(2,1)S(1)}, bf16[1056,128]{1,0:T(8,128)(2,1)S(1)}, u32[]{:S(2)}, u32[]{:S(2)}) collective-permute-start(bf16[1056,128]{1,0:T(8,128)(2,1)S(1)} %get-tuple-element.164), channel_id=1, source_target_pairs={{0,2},{1,3},{2,0},{3,1},{4,6},{5,7},{6,4},{7,5},{8,10},{9,11},{10,... | collective-permute-start | bytes 811016 | tf_op jit(solution)/shard_map/ppermute | solution.py:451
  129.4 12.1 %collective-permute-start.38 = (bf16[1056,128]{1,0:T(8,128)(2,1)S(1)}, bf16[1056,128]{1,0:T(8,128)(2,1)S(1)}, u32[]{:S(2)}, u32[]{:S(2)}) collective-permute-start(bf16[1056,128]{1,0:T(8,128)(2,1)S(1)} %get-tuple-element.163), channel_id=1, source_target_pairs={{0,3},{1,2},{2,1},{3,0},{4,7},{5,6},{6,5},{7,4},{8,11},{9,10},{10,... | collective-permute-start | bytes 811016 | tf_op jit(solution)/shard_map/ppermute | solution.py:451
  (17 other events, 140.0 us)

commit v6 on v5

--- a/solution.py
+++ b/solution.py
@@ -471,10 +471,10 @@
 
     early = grad_pieces((out_grad, grad_1, grad_3), *weights)
     early = list(early)
-    early[1:] = [to_col(block, j) for j, block in enumerate(after(early[1:], arrived[1:3]), 1)]
+    early[1:] = [to_col(block, j) for j, block in enumerate(after(early[1:], arrived[1]), 1)]
 
     own_part = after(arrived, early)
-    other_part = [swap(block) for block in own_part]
+    other_part = [swap(block) for block in (*arrived[:3], own_part[3])]
     other_part = after(other_part, fence(own_part))
 
     grad_2 = to_plane(after(grad_1, arrived), 1)

time: 148 us -> 147 us (level)
  starting transfers between devices: 42.8 us -> 37.3 us
  waiting for transfers between devices: 60.2 us -> 64.7 us
    ppermute x12, starting transfers between devices: 20.6 us -> 15.8 us  [to_plane(): return lax.ppermute(block, 'row', row_shift(s))]
    ppermute x17, waiting for transfers between devices: 30.3 us -> 34.9 us  [to_col(): return lax.ppermute(block, 'col', col_xor(j))]
  transfers between devices with their start and end apart: 39 -> 39, of which waited for: 19 -> 20; matrix products, arithmetic and copies ran while one was open for 4% -> 4% of each run, Pallas kernels for 23% -> 23%
where the time goes in v6:
time: 147 us
  waiting for transfers between devices  64.7 us (44%)
  starting transfers between devices  37.3 us (25%)
  Pallas kernels  34.3 us (23%)
  local copies, waits for them, and re-layouts  5.56 us (4%)
  other arithmetic  3.9 us (3%)
    ppermute x17, waiting for transfers between devices, to_col(): return lax.ppermute(block, 'col', col_xor(j))  34.9 us
    ppermute x12, waiting for transfers between devices, to_plane(): return lax.ppermute(block, 'row', row_shift(s))  26.4 us
    ppermute x17, starting transfers between devices, to_col(): return lax.ppermute(block, 'col', col_xor(j))  19.6 us
    ppermute x12, starting transfers between devices, to_plane(): return lax.ppermute(block, 'row', row_shift(s))  15.8 us
    pallas_call x2, Pallas kernels, weight_grad_part(): pl.pallas_call(functools.partial(weight_grad_kernel, len(heads)), out_sha...  7.2 us
    pallas_call x1, Pallas kernels, attention_forward(): pl.pallas_call(forward_kernel, grid=(3,), in_specs=[whole(*own[0].shape)]...  6.95 us
    pallas_call x2, Pallas kernels, grad_pieces(): pl.pallas_call(grad_kernel, out_shape=[piece] * COLS, scratch_shapes=[plt...  6.37 us
    pallas_call x1, Pallas kernels, attention_backward(): pl.pallas_call(backward_kernel, grid=(3,), in_specs=[by_query, by_head, b...  5.23 us
  transfers between devices with their start and end apart: 39, of which 20 were waited for; matrix products, arithmetic and copies ran while one was open for 4% of the time, Pallas kernels for 23%

profile of v6, /device:TPU:0, one launch (start us, length us, event | category | flops | bytes accessed | tf_op | source)
XLA Modules:
  0.0 146.8 jit_solution(4752481015335789429)
XLA Ops:
  0.6 3.1 %collective-permute-start.7 = (bf16[192,1536]{1,0:T(8,128)(2,1)}, bf16[192,1536]{1,0:T(8,128)(2,1)S(1)}, u32[]{:S(2)}, u32[]{:S(2)}) collective-permute-start(bf16[192,1536]{1,0:T(8,128)(2,1)} %refs_4_.3), channel_id=1, source_target_pairs={{0,8},{4,12},{8,16},{12,20},{16,24},{20,28},{24,0},{28,4},{1,9},{5... | collective-permute-start | bytes 1769480 | tf_op jit(solution)/shard_map/ppermute | solution.py:454
  3.7 2.1 %collective-permute-start.8 = (bf16[192,1536]{1,0:T(8,128)(2,1)}, bf16[192,1536]{1,0:T(8,128)(2,1)}, u32[]{:S(2)}, u32[]{:S(2)}) collective-permute-start(bf16[192,1536]{1,0:T(8,128)(2,1)} %refs_4_.3), channel_id=1, source_target_pairs={{0,24},{4,28},{8,0},{12,4},{16,8},{20,12},{24,16},{28,20},{1,25},{... | collective-permute-start | bytes 1769480 | tf_op jit(solution)/shard_map/ppermute | solution.py:454
  5.8 2.3 %pack_inputs.1 = (bf16[1056,128]{1,0:T(8,128)(2,1)}, bf16[1056,128]{1,0:T(8,128)(2,1)}, bf16[1056,128]{1,0:T(8,128)(2,1)}, bf16[1056,128]{1,0:T(8,128)(2,1)}) custom-call(bf16[192,768]{1,0:T(8,128)(2,1)} %q_ref, bf16[192,768]{1,0:T(8,128)(2,1)} %k_ref, bf16[192,768]{1,0:T(8,128)(2,1)} %v_ref), custom_call_target="tpu_custom_call" | custom-call | flops 40000000000 | tf_op jit(solution)/shard_map/pack_inputs/pallas_call | solution.py:282
  8.9 1.6 %collective-permute-start.1 = (bf16[1056,128]{1,0:T(8,128)(2,1)}, bf16[1056,128]{1,0:T(8,128)(2,1)S(1)}, u32[]{:S(2)}, u32[]{:S(2)}) collective-permute-start(bf16[1056,128]{1,0:T(8,128)(2,1)} %get-tuple-element.92), channel_id=1, source_target_pairs={{0,1},{1,0},{2,3},{3,2},{4,5},{5,4},{6,7},{7,6},{8,9},{9,8},{10,11... | collective-permute-start | bytes 811016 | tf_op jit(solution)/shard_map/ppermute | solution.py:451
  10.5 1.5 %collective-permute-start.2 = (bf16[1056,128]{1,0:T(8,128)(2,1)}, bf16[1056,128]{1,0:T(8,128)(2,1)S(1)}, u32[]{:S(2)}, u32[]{:S(2)}) collective-permute-start(bf16[1056,128]{1,0:T(8,128)(2,1)} %get-tuple-element.93), channel_id=1, source_target_pairs={{0,2},{1,3},{2,0},{3,1},{4,6},{5,7},{6,4},{7,5},{8,10},{9,11},{10,... | collective-permute-start | bytes 811016 | tf_op jit(solution)/shard_map/ppermute | solution.py:451
  12.9 5.5 %collective-permute-done.1 = bf16[1056,128]{1,0:T(8,128)(2,1)S(1)} collective-permute-done((bf16[1056,128]{1,0:T(8,128)(2,1)}, bf16[1056,128]{1,0:T(8,128)(2,1)S(1)}, u32[]{:S(2)}, u32[]{:S(2)}) %collective-permute-start.1) | collective-permute-done | bytes 270368 | tf_op jit(solution)/shard_map/ppermute | solution.py:451
  18.4 6.4 %collective-permute-done.2 = bf16[1056,128]{1,0:T(8,128)(2,1)S(1)} collective-permute-done((bf16[1056,128]{1,0:T(8,128)(2,1)}, bf16[1056,128]{1,0:T(8,128)(2,1)S(1)}, u32[]{:S(2)}, u32[]{:S(2)}) %collective-permute-start.2) | collective-permute-done | bytes 270368 | tf_op jit(solution)/shard_map/ppermute | solution.py:451
  25.8 3.8 %collective-permute-start.5 = (bf16[1056,128]{1,0:T(8,128)(2,1)}, bf16[1056,128]{1,0:T(8,128)(2,1)}, u32[]{:S(2)}, u32[]{:S(2)}) collective-permute-start(bf16[1056,128]{1,0:T(8,128)(2,1)} %get-tuple-element.168), channel_id=1, source_target_pairs={{0,24},{4,28},{8,0},{12,4},{16,8},{20,12},{24,16},{28,20},{1,25},{... | collective-permute-start | bytes 811016 | tf_op jit(solution)/shard_map/ppermute | solution.py:454
  29.6 3.4 %collective-permute-done.8.refs_2_.refs_6_ = bf16[192,1536]{1,0:T(8,128)(2,1)} collective-permute-done((bf16[192,1536]{1,0:T(8,128)(2,1)}, bf16[192,1536]{1,0:T(8,128)(2,1)}, u32[]{:S(2)}, u32[]{:S(2)}) %collective-permute-start.8) | collective-permute-done | bytes 589856 | tf_op jit(solution)/shard_map/ppermute | solution.py:454
  33.1 4.4 %grad_pieces.2 = (bf16[864,128]{1,0:T(8,128)(2,1)S(1)}, bf16[864,128]{1,0:T(8,128)(2,1)}, bf16[864,128]{1,0:T(8,128)(2,1)}, bf16[864,128]{1,0:T(8,128)(2,1)}) custom-call(bf16[192,1536]{1,0:T(8,128)(2,1)S(1)} %copy-done.1, bf16[192,1536]{1,0:T(8,128)(2,1)S(1)} %collective-permute-done.7.refs_1_.refs_5_, ...), custom_call_target="tpu_custom_call" | custom-call | flops 40000000000 | tf_op jit(solution)/shard_map/grad_pieces/pallas_call | solution.py:314
  38.7 1.8 %collective-permute-start.10 = (bf16[864,128]{1,0:T(8,128)(2,1)}, bf16[864,128]{1,0:T(8,128)(2,1)}, u32[]{:S(2)}, u32[]{:S(2)}) collective-permute-start(bf16[864,128]{1,0:T(8,128)(2,1)} %get-tuple-element.104), channel_id=1, source_target_pairs={{0,2},{1,3},{2,0},{3,1},{4,6},{5,7},{6,4},{7,5},{8,10},{9,11},{10,... | collective-permute-start | bytes 663560 | tf_op jit(solution)/shard_map/ppermute | solution.py:451
  43.0 12.1 %collective-permute-done.6.refs_3_ = bf16[1056,128]{1,0:T(8,128)(2,1)} collective-permute-done((bf16[1056,128]{1,0:T(8,128)(2,1)}, bf16[1056,128]{1,0:T(8,128)(2,1)}, u32[]{:S(2)}, u32[]{:S(2)}) %collective-permute-start.6) | collective-permute-done | bytes 270368 | tf_op jit(solution)/shard_map/ppermute | solution.py:454
  57.9 7.0 %attention_forward.1 = (bf16[3,1536,384]{2,1,0:T(8,128)(2,1)}, bf16[1152,128]{1,0:T(8,128)(2,1)S(1)}, bf16[1152,128]{1,0:T(8,128)(2,1)S(1)}, bf16[2,1536,128]{2,1,0:T(8,128)(2,1)S(1)}, bf16[2,1536,128]{2,1,0:T(8,128)(2,1)S(1)}) custom-call(bf16[1056,128]{1,0:T(8,128)(2,1)S(1)} %get-tuple-element.106.refs_0_, ...), custom_call_target="tpu_custom_call" | custom-call | flops 40000000000 | tf_op jit(solution)/shard_map/attention_forward/pallas_call | solution.py:167
  64.8 1.6 %collective-permute-start.18 = (bf16[288,128]{1,0:T(8,128)(2,1)S(1)}, bf16[288,128]{1,0:T(8,128)(2,1)S(1)}, u32[]{:S(2)}, u32[]{:S(2)}) collective-permute-start(bf16[288,128]{1,0:T(8,128)(2,1)S(1)} %get-tuple-element.221), channel_id=1, source_target_pairs={{0,1},{1,0},{2,3},{3,2},{4,5},{5,4},{6,7},{7,6},{8,9},{9,8},{10,11... | collective-permute-start | bytes 221192 | tf_op jit(solution)/shard_map/ppermute | solution.py:451
  68.5 1.6 %collective-permute-start.16 = (bf16[864,128]{1,0:T(8,128)(2,1)S(1)}, bf16[864,128]{1,0:T(8,128)(2,1)S(1)}, u32[]{:S(2)}, u32[]{:S(2)}) collective-permute-start(bf16[864,128]{1,0:T(8,128)(2,1)S(1)} %get-tuple-element.219), channel_id=1, source_target_pairs={{0,1},{1,0},{2,3},{3,2},{4,5},{5,4},{6,7},{7,6},{8,9},{9,8},{10,11... | collective-permute-start | bytes 663560 | tf_op jit(solution)/shard_map/ppermute | solution.py:451
  72.3 2.0 %grad_pieces.3 = (bf16[288,128]{1,0:T(8,128)(2,1)S(1)}, bf16[288,128]{1,0:T(8,128)(2,1)S(1)}, bf16[288,128]{1,0:T(8,128)(2,1)S(1)}, bf16[288,128]{1,0:T(8,128)(2,1)S(1)}) custom-call(bf16[192,1536]{1,0:T(8,128)(2,1)} %collective-permute-done.21.refs_0_.refs_7_, bf16[384,1536]{1,0:T(8,128)(2,1)S(1)} %copy-done, ...), custom_call_target="tpu_custom_call" | custom-call | flops 40000000000 | tf_op jit(solution)/shard_map/grad_pieces/pallas_call | solution.py:314
  74.4 1.6 %collective-permute-start.23 = (bf16[288,128]{1,0:T(8,128)(2,1)S(1)}, bf16[288,128]{1,0:T(8,128)(2,1)S(1)}, u32[]{:S(2)}, u32[]{:S(2)}) collective-permute-start(bf16[288,128]{1,0:T(8,128)(2,1)S(1)} %get-tuple-element.119), channel_id=1, source_target_pairs={{0,1},{1,0},{2,3},{3,2},{4,5},{5,4},{6,7},{7,6},{8,9},{9,8},{10,11... | collective-permute-start | bytes 221192 | tf_op jit(solution)/shard_map/ppermute | solution.py:451
  75.9 1.5 %collective-permute-start.24 = (bf16[288,128]{1,0:T(8,128)(2,1)S(1)}, bf16[288,128]{1,0:T(8,128)(2,1)S(1)}, u32[]{:S(2)}, u32[]{:S(2)}) collective-permute-start(bf16[288,128]{1,0:T(8,128)(2,1)S(1)} %get-tuple-element.120), channel_id=1, source_target_pairs={{0,2},{1,3},{2,0},{3,1},{4,6},{5,7},{6,4},{7,5},{8,10},{9,11},{10,... | collective-permute-start | bytes 221192 | tf_op jit(solution)/shard_map/ppermute | solution.py:451
  79.1 2.0 %collective-permute-done.24.refs_3_ = bf16[288,128]{1,0:T(8,128)(2,1)S(1)} collective-permute-done((bf16[288,128]{1,0:T(8,128)(2,1)S(1)}, bf16[288,128]{1,0:T(8,128)(2,1)S(1)}, u32[]{:S(2)}, u32[]{:S(2)}) %collective-permute-start.24) | collective-permute-done | bytes 73760 | tf_op jit(solution)/shard_map/ppermute | solution.py:451
  81.1 1.6 %collective-permute-done.25.refs_4_ = bf16[288,128]{1,0:T(8,128)(2,1)S(1)} collective-permute-done((bf16[288,128]{1,0:T(8,128)(2,1)S(1)}, bf16[288,128]{1,0:T(8,128)(2,1)S(1)}, u32[]{:S(2)}, u32[]{:S(2)}) %collective-permute-start.25) | collective-permute-done | bytes 73760 | tf_op jit(solution)/shard_map/ppermute | solution.py:451
  82.7 5.2 %attention_backward.1 = (bf16[1152,128]{1,0:T(8,128)(2,1)S(1)}, f32[2,2,768,128]{3,2,1,0:T(8,128)S(1)}, bf16[2,2,768,128]{3,2,1,0:T(8,128)(2,1)S(1)}) custom-call(bf16[1152,128]{1,0:T(8,128)(2,1)S(1)} %get-tuple-element.125.q_ref, bf16[2,1536,128]{2,1,0:T(8,128)(2,1)S(1)} %get-tuple-element.126.k_ref, bf16[2,1536,128]{2,1,0:T(8,128)(2,1)S(1)} %get-tuple-element.127.v_ref, ...), custom_call_target="tpu_custom_call" | custom-call | flops 40000000000 | tf_op jit(solution)/shard_map/attention_backward/pallas_call | solution.py:239
  90.7 1.9 %collective-permute-start.30 = (bf16[1056,128]{1,0:T(8,128)(2,1)S(1)}, bf16[1056,128]{1,0:T(8,128)(2,1)S(1)}, u32[]{:S(2)}, u32[]{:S(2)}) collective-permute-start(bf16[1056,128]{1,0:T(8,128)(2,1)S(1)} %get-tuple-element.180), channel_id=1, source_target_pairs={{0,24},{4,28},{8,0},{12,4},{16,8},{20,12},{24,16},{28,20},{1,25},{... | collective-permute-start | bytes 811016 | tf_op jit(solution)/shard_map/ppermute | solution.py:454
  93.7 8.0 %collective-permute-done.17 = bf16[2,864,128]{2,1,0:T(8,128)(2,1)S(1)} collective-permute-done((bf16[2,864,128]{2,1,0:T(8,128)(2,1)S(1)}, bf16[2,864,128]{2,1,0:T(8,128)(2,1)S(1)}, u32[]{:S(2)}, u32[]{:S(2)}) %collective-permute-start.17) | collective-permute-done | bytes 442400 | tf_op jit(solution)/shard_map/ppermute | solution.py:451
  103.3 3.1 %weight_grad.2 = bf16[384,1536]{1,0:T(8,128)(2,1)S(1)} custom-call(bf16[192,384]{1,0:T(8,128)(2,1)S(1)} %get-tuple-element.138.refs_0_, bf16[192,384]{1,0:T(8,128)(2,1)S(1)} %get-tuple-element.139.refs_1_, bf16[192,384]{1,0:T(8,128)(2,1)S(1)} %get-tuple-element.140.refs_2_, bf16[192,384]{1,0:T(8,128)(2,1)S(1)} %get-tuple-element.141.refs_3_, ...), custom_call_target="tpu_custom_call" | custom-call | flops 40000000000 | tf_op jit(solution)/shard_map/weight_grad/pallas_call | solution.py:358
  108.2 1.6 %mixed_term.5 = bf16[192,1536]{1,0:T(8,128)(2,1)} custom-call(bf16[192,768]{1,0:T(8,128)(2,1)S(1)} %get-tuple-element.143.block_ref, bf16[384,1536]{1,0:T(8,128)(2,1)S(1)} %copy-done, bf16[384,1536]{1,0:T(8,128)(2,1)S(1)} %collective-permute-done.refs_4_.refs_2_.other_ref), custom_call_target="tpu_custom_call" | custom-call | flops 1000000 | bytes 1000 | tf_op jit(solution)/shard_map/mixed_term/pallas_call | solution.py:337
  110.6 6.9 %collective-permute-done.31 = bf16[1056,128]{1,0:T(8,128)(2,1)S(1)} collective-permute-done((bf16[1056,128]{1,0:T(8,128)(2,1)S(1)}, bf16[1056,128]{1,0:T(8,128)(2,1)S(1)}, u32[]{:S(2)}, u32[]{:S(2)}) %collective-permute-start.31) | collective-permute-done | bytes 270368 | tf_op jit(solution)/shard_map/ppermute | solution.py:454
  117.5 3.8 %collective-permute-start.34 = (bf16[192,1536]{1,0:T(8,128)(2,1)}, bf16[192,1536]{1,0:T(8,128)(2,1)S(1)}, u32[]{:S(2)}, u32[]{:S(2)}) collective-permute-start(bf16[192,1536]{1,0:T(8,128)(2,1)} %mixed_term.5), channel_id=1, source_target_pairs={{0,24},{4,28},{8,0},{12,4},{16,8},{20,12},{24,16},{28,20},{1,25},{... | collective-permute-start | bytes 1769480 | tf_op jit(solution)/shard_map/ppermute | solution.py:454
  121.4 4.1 %weight_grad.3 = bf16[384,1536]{1,0:T(8,128)(2,1)} custom-call(bf16[192,384]{1,0:T(8,128)(2,1)S(1)} %get-tuple-element.152.refs_0_, bf16[192,384]{1,0:T(8,128)(2,1)S(1)} %get-tuple-element.153.refs_1_, bf16[192,384]{1,0:T(8,128)(2,1)S(1)} %get-tuple-element.154.refs_2_, bf16[192,384]{1,0:T(8,128)(2,1)S(1)} %get-tuple-element.155.refs_3_, ...), custom_call_target="tpu_custom_call" | custom-call | flops 40000000000 | tf_op jit(solution)/shard_map/weight_grad/pallas_call | solution.py:358
  127.9 1.5 %collective-permute-start.37 = (bf16[1056,128]{1,0:T(8,128)(2,1)S(1)}, bf16[1056,128]{1,0:T(8,128)(2,1)S(1)}, u32[]{:S(2)}, u32[]{:S(2)}) collective-permute-start(bf16[1056,128]{1,0:T(8,128)(2,1)S(1)} %get-tuple-element.164), channel_id=1, source_target_pairs={{0,2},{1,3},{2,0},{3,1},{4,6},{5,7},{6,4},{7,5},{8,10},{9,11},{10,... | collective-permute-start | bytes 811016 | tf_op jit(solution)/shard_map/ppermute | solution.py:451
  129.9 5.9 %collective-permute-done.36.refs_1_ = bf16[1056,128]{1,0:T(8,128)(2,1)S(1)} collective-permute-done((bf16[1056,128]{1,0:T(8,128)(2,1)S(1)}, bf16[1056,128]{1,0:T(8,128)(2,1)S(1)}, u32[]{:S(2)}, u32[]{:S(2)}) %collective-permute-start.36) | collective-permute-done | bytes 270368 | tf_op jit(solution)/shard_map/ppermute | solution.py:451
  135.8 5.5 %collective-permute-done.37.refs_2_ = bf16[1056,128]{1,0:T(8,128)(2,1)S(1)} collective-permute-done((bf16[1056,128]{1,0:T(8,128)(2,1)S(1)}, bf16[1056,128]{1,0:T(8,128)(2,1)S(1)}, u32[]{:S(2)}, u32[]{:S(2)}) %collective-permute-start.37) | collective-permute-done | bytes 270368 | tf_op jit(solution)/shard_map/ppermute | solution.py:451
  142.8 2.3 %unpack_outputs.1 = (bf16[192,768]{1,0:T(8,128)(2,1)}, bf16[192,768]{1,0:T(8,128)(2,1)}, bf16[192,768]{1,0:T(8,128)(2,1)}) custom-call(bf16[1056,128]{1,0:T(8,128)(2,1)} %get-tuple-element.166.refs_0_, bf16[1056,128]{1,0:T(8,128)(2,1)} %copy-done.7, bf16[1056,128]{1,0:T(8,128)(2,1)} %copy-done.8, bf16[1056,128]{1,0:T(8,128)(2,1)} %copy-done.9), custom_call_target="tpu_custom_call" | custom-call | flops 1000000 | bytes 1000 | tf_op jit(solution)/shard_map/unpack_outputs/pallas_call | solution.py:398
  (129 shorter events, 29.0 us)
Async XLA Ops:
  0.6 29.0 %collective-permute-start.7 = (bf16[192,1536]{1,0:T(8,128)(2,1)}, bf16[192,1536]{1,0:T(8,128)(2,1)S(1)}, u32[]{:S(2)}, u32[]{:S(2)}) collective-permute-start(bf16[192,1536]{1,0:T(8,128)(2,1)} %refs_4_.3), channel_id=1, source_target_pairs={{0,8},{4,12},{8,16},{12,20},{16,24},{20,28},{24,0},{28,4},{1,9},{5... | collective-permute-start | bytes 1769480 | tf_op jit(solution)/shard_map/ppermute | solution.py:454
  3.7 29.3 %collective-permute-start.8 = (bf16[192,1536]{1,0:T(8,128)(2,1)}, bf16[192,1536]{1,0:T(8,128)(2,1)}, u32[]{:S(2)}, u32[]{:S(2)}) collective-permute-start(bf16[192,1536]{1,0:T(8,128)(2,1)} %refs_4_.3), channel_id=1, source_target_pairs={{0,24},{4,28},{8,0},{12,4},{16,8},{20,12},{24,16},{28,20},{1,25},{... | collective-permute-start | bytes 1769480 | tf_op jit(solution)/shard_map/ppermute | solution.py:454
  5.8 3.1 %collective-permute-start = (bf16[384,1536]{1,0:T(8,128)(2,1)}, bf16[384,1536]{1,0:T(8,128)(2,1)S(1)}, u32[]{:S(2)}, u32[]{:S(2)}) collective-permute-start(bf16[384,1536]{1,0:T(8,128)(2,1)} %own_ref.7), channel_id=1, source_target_pairs={{0,4},{4,0},{8,12},{12,8},{16,20},{20,16},{24,28},{28,24},{1,5},{5... | collective-permute-start | bytes 3538952 | tf_op jit(solution)/shard_map/ppermute | solution.py:457
  8.9 9.5 %collective-permute-start.1 = (bf16[1056,128]{1,0:T(8,128)(2,1)}, bf16[1056,128]{1,0:T(8,128)(2,1)S(1)}, u32[]{:S(2)}, u32[]{:S(2)}) collective-permute-start(bf16[1056,128]{1,0:T(8,128)(2,1)} %get-tuple-element.92), channel_id=1, source_target_pairs={{0,1},{1,0},{2,3},{3,2},{4,5},{5,4},{6,7},{7,6},{8,9},{9,8},{10,11... | collective-permute-start | bytes 811016 | tf_op jit(solution)/shard_map/ppermute | solution.py:451
  10.5 14.2 %collective-permute-start.2 = (bf16[1056,128]{1,0:T(8,128)(2,1)}, bf16[1056,128]{1,0:T(8,128)(2,1)S(1)}, u32[]{:S(2)}, u32[]{:S(2)}) collective-permute-start(bf16[1056,128]{1,0:T(8,128)(2,1)} %get-tuple-element.93), channel_id=1, source_target_pairs={{0,2},{1,3},{2,0},{3,1},{4,6},{5,7},{6,4},{7,5},{8,10},{9,11},{10,... | collective-permute-start | bytes 811016 | tf_op jit(solution)/shard_map/ppermute | solution.py:451
  12.0 12.7 %collective-permute-start.3 = (bf16[1056,128]{1,0:T(8,128)(2,1)}, bf16[1056,128]{1,0:T(8,128)(2,1)S(1)}, u32[]{:S(2)}, u32[]{:S(2)}) collective-permute-start(bf16[1056,128]{1,0:T(8,128)(2,1)} %get-tuple-element.94), channel_id=1, source_target_pairs={{0,3},{1,2},{2,1},{3,0},{4,7},{5,6},{6,5},{7,4},{8,11},{9,10},{10,... | collective-permute-start | bytes 811016 | tf_op jit(solution)/shard_map/ppermute | solution.py:451
  25.8 12.9 %collective-permute-start.4 = (bf16[1056,128]{1,0:T(8,128)(2,1)S(1)}, bf16[1056,128]{1,0:T(8,128)(2,1)}, u32[]{:S(2)}, u32[]{:S(2)}) collective-permute-start(bf16[1056,128]{1,0:T(8,128)(2,1)S(1)} %get-tuple-element.169), channel_id=1, source_target_pairs={{0,8},{4,12},{8,16},{12,20},{16,24},{20,28},{24,0},{28,4},{1,9},{5... | collective-permute-start | bytes 811016 | tf_op jit(solution)/shard_map/ppermute | solution.py:454
  25.8 17.2 %collective-permute-start.5 = (bf16[1056,128]{1,0:T(8,128)(2,1)}, bf16[1056,128]{1,0:T(8,128)(2,1)}, u32[]{:S(2)}, u32[]{:S(2)}) collective-permute-start(bf16[1056,128]{1,0:T(8,128)(2,1)} %get-tuple-element.168), channel_id=1, source_target_pairs={{0,24},{4,28},{8,0},{12,4},{16,8},{20,12},{24,16},{28,20},{1,25},{... | collective-permute-start | bytes 811016 | tf_op jit(solution)/shard_map/ppermute | solution.py:454
  29.6 25.6 %collective-permute-start.6 = (bf16[1056,128]{1,0:T(8,128)(2,1)}, bf16[1056,128]{1,0:T(8,128)(2,1)}, u32[]{:S(2)}, u32[]{:S(2)}) collective-permute-start(bf16[1056,128]{1,0:T(8,128)(2,1)} %get-tuple-element.167), channel_id=1, source_target_pairs={{0,16},{4,20},{8,24},{12,28},{16,0},{20,4},{24,8},{28,12},{1,17},{... | collective-permute-start | bytes 811016 | tf_op jit(solution)/shard_map/ppermute | solution.py:454
  38.7 16.5 %collective-permute-start.10 = (bf16[864,128]{1,0:T(8,128)(2,1)}, bf16[864,128]{1,0:T(8,128)(2,1)}, u32[]{:S(2)}, u32[]{:S(2)}) collective-permute-start(bf16[864,128]{1,0:T(8,128)(2,1)} %get-tuple-element.104), channel_id=1, source_target_pairs={{0,2},{1,3},{2,0},{3,1},{4,6},{5,7},{6,4},{7,5},{8,10},{9,11},{10,... | collective-permute-start | bytes 663560 | tf_op jit(solution)/shard_map/ppermute | solution.py:451
  40.5 14.7 %collective-permute-start.11 = (bf16[864,128]{1,0:T(8,128)(2,1)}, bf16[864,128]{1,0:T(8,128)(2,1)}, u32[]{:S(2)}, u32[]{:S(2)}) collective-permute-start(bf16[864,128]{1,0:T(8,128)(2,1)} %get-tuple-element.105), channel_id=1, source_target_pairs={{0,3},{1,2},{2,1},{3,0},{4,7},{5,6},{6,5},{7,4},{8,11},{9,10},{10,... | collective-permute-start | bytes 663560 | tf_op jit(solution)/shard_map/ppermute | solution.py:451
  41.9 13.8 %collective-permute-start.9 = (bf16[864,128]{1,0:T(8,128)(2,1)}, bf16[864,128]{1,0:T(8,128)(2,1)}, u32[]{:S(2)}, u32[]{:S(2)}) collective-permute-start(bf16[864,128]{1,0:T(8,128)(2,1)} %get-tuple-element.103), channel_id=1, source_target_pairs={{0,1},{1,0},{2,3},{3,2},{4,5},{5,4},{6,7},{7,6},{8,9},{9,8},{10,11... | collective-permute-start | bytes 663560 | tf_op jit(solution)/shard_map/ppermute | solution.py:451
  43.0 12.8 %collective-permute-start.12 = (bf16[1056,128]{1,0:T(8,128)(2,1)S(1)}, bf16[1056,128]{1,0:T(8,128)(2,1)}, u32[]{:S(2)}, u32[]{:S(2)}) collective-permute-start(bf16[1056,128]{1,0:T(8,128)(2,1)S(1)} %get-tuple-element.106.refs_0_), channel_id=1, source_target_pairs={{0,4},{4,0},{8,12},{12,8},{16,20},{20,16},{24,28},{28,24},{1,5},{5... | collective-permute-start | bytes 811016 | tf_op jit(solution)/shard_map/ppermute | solution.py:457
  55.2 17.2 %collective-permute-start.21 = (bf16[192,1536]{1,0:T(8,128)(2,1)S(1)}, bf16[192,1536]{1,0:T(8,128)(2,1)}, u32[]{:S(2)}, u32[]{:S(2)}) collective-permute-start(bf16[192,1536]{1,0:T(8,128)(2,1)S(1)} %collective-permute-done.7.refs_1_.refs_5_), channel_id=1, source_target_pairs={{0,8},{4,12},{8,16},{12,20},{16,24},{20,28},{24,0},{28,4},{1,9},{5... | collective-permute-start | bytes 1769480 | tf_op jit(solution)/shard_map/ppermute | solution.py:454
  64.8 11.1 %collective-permute-start.18 = (bf16[288,128]{1,0:T(8,128)(2,1)S(1)}, bf16[288,128]{1,0:T(8,128)(2,1)S(1)}, u32[]{:S(2)}, u32[]{:S(2)}) collective-permute-start(bf16[288,128]{1,0:T(8,128)(2,1)S(1)} %get-tuple-element.221), channel_id=1, source_target_pairs={{0,1},{1,0},{2,3},{3,2},{4,5},{5,4},{6,7},{7,6},{8,9},{9,8},{10,11... | collective-permute-start | bytes 221192 | tf_op jit(solution)/shard_map/ppermute | solution.py:451
  66.4 11.0 %collective-permute-start.19 = (bf16[288,128]{1,0:T(8,128)(2,1)S(1)}, bf16[288,128]{1,0:T(8,128)(2,1)S(1)}, u32[]{:S(2)}, u32[]{:S(2)}) collective-permute-start(bf16[288,128]{1,0:T(8,128)(2,1)S(1)} %get-tuple-element.221), channel_id=1, source_target_pairs={{0,2},{1,3},{2,0},{3,1},{4,6},{5,7},{6,4},{7,5},{8,10},{9,11},{10,... | collective-permute-start | bytes 221192 | tf_op jit(solution)/shard_map/ppermute | solution.py:451
  67.9 10.0 %collective-permute-start.20 = (bf16[288,128]{1,0:T(8,128)(2,1)S(1)}, bf16[288,128]{1,0:T(8,128)(2,1)S(1)}, u32[]{:S(2)}, u32[]{:S(2)}) collective-permute-start(bf16[288,128]{1,0:T(8,128)(2,1)S(1)} %get-tuple-element.221), channel_id=1, source_target_pairs={{0,3},{1,2},{2,1},{3,0},{4,7},{5,6},{6,5},{7,4},{8,11},{9,10},{10,... | collective-permute-start | bytes 221192 | tf_op jit(solution)/shard_map/ppermute | solution.py:451
  68.5 20.2 %collective-permute-start.16 = (bf16[864,128]{1,0:T(8,128)(2,1)S(1)}, bf16[864,128]{1,0:T(8,128)(2,1)S(1)}, u32[]{:S(2)}, u32[]{:S(2)}) collective-permute-start(bf16[864,128]{1,0:T(8,128)(2,1)S(1)} %get-tuple-element.219), channel_id=1, source_target_pairs={{0,1},{1,0},{2,3},{3,2},{4,5},{5,4},{6,7},{7,6},{8,9},{9,8},{10,11... | collective-permute-start | bytes 663560 | tf_op jit(solution)/shard_map/ppermute | solution.py:451
  74.4 4.7 %collective-permute-start.23 = (bf16[288,128]{1,0:T(8,128)(2,1)S(1)}, bf16[288,128]{1,0:T(8,128)(2,1)S(1)}, u32[]{:S(2)}, u32[]{:S(2)}) collective-permute-start(bf16[288,128]{1,0:T(8,128)(2,1)S(1)} %get-tuple-element.119), channel_id=1, source_target_pairs={{0,1},{1,0},{2,3},{3,2},{4,5},{5,4},{6,7},{7,6},{8,9},{9,8},{10,11... | collective-permute-start | bytes 221192 | tf_op jit(solution)/shard_map/ppermute | solution.py:451
  75.9 5.1 %collective-permute-start.24 = (bf16[288,128]{1,0:T(8,128)(2,1)S(1)}, bf16[288,128]{1,0:T(8,128)(2,1)S(1)}, u32[]{:S(2)}, u32[]{:S(2)}) collective-permute-start(bf16[288,128]{1,0:T(8,128)(2,1)S(1)} %get-tuple-element.120), channel_id=1, source_target_pairs={{0,2},{1,3},{2,0},{3,1},{4,6},{5,7},{6,4},{7,5},{8,10},{9,11},{10,... | collective-permute-start | bytes 221192 | tf_op jit(solution)/shard_map/ppermute | solution.py:451
  77.4 5.3 %collective-permute-start.25 = (bf16[288,128]{1,0:T(8,128)(2,1)S(1)}, bf16[288,128]{1,0:T(8,128)(2,1)S(1)}, u32[]{:S(2)}, u32[]{:S(2)}) collective-permute-start(bf16[288,128]{1,0:T(8,128)(2,1)S(1)} %get-tuple-element.121), channel_id=1, source_target_pairs={{0,3},{1,2},{2,1},{3,0},{4,7},{5,6},{6,5},{7,4},{8,11},{9,10},{10,... | collective-permute-start | bytes 221192 | tf_op jit(solution)/shard_map/ppermute | solution.py:451
  78.9 22.8 %collective-permute-start.22 = (bf16[192,1536]{1,0:T(8,128)(2,1)S(1)}, bf16[192,1536]{1,0:T(8,128)(2,1)S(1)}, u32[]{:S(2)}, u32[]{:S(2)}) collective-permute-start(bf16[192,1536]{1,0:T(8,128)(2,1)S(1)} %mixed_term.4), channel_id=1, source_target_pairs={{0,8},{4,12},{8,16},{12,20},{16,24},{20,28},{24,0},{28,4},{1,9},{5... | collective-permute-start | bytes 1769480 | tf_op jit(solution)/shard_map/ppermute | solution.py:454
  89.5 12.2 %collective-permute-start.17 = (bf16[2,864,128]{2,1,0:T(8,128)(2,1)S(1)}, bf16[2,864,128]{2,1,0:T(8,128)(2,1)S(1)}, u32[]{:S(2)}, u32[]{:S(2)}) collective-permute-start(bf16[2,864,128]{2,1,0:T(8,128)(2,1)S(1)} %pad_maximum_fusion.2), channel_id=1, source_target_pairs={{0,2},{1,3},{2,0},{3,1},{4,6},{5,7},{6,4},{7,5},{8,10},{9,11},{10,... | collective-permute-start | bytes 1327112 | tf_op jit(solution)/shard_map/ppermute | solution.py:451
  90.7 19.9 %collective-permute-start.30 = (bf16[1056,128]{1,0:T(8,128)(2,1)S(1)}, bf16[1056,128]{1,0:T(8,128)(2,1)S(1)}, u32[]{:S(2)}, u32[]{:S(2)}) collective-permute-start(bf16[1056,128]{1,0:T(8,128)(2,1)S(1)} %get-tuple-element.180), channel_id=1, source_target_pairs={{0,24},{4,28},{8,0},{12,4},{16,8},{20,12},{24,16},{28,20},{1,25},{... | collective-permute-start | bytes 811016 | tf_op jit(solution)/shard_map/ppermute | solution.py:454
  92.6 24.9 %collective-permute-start.31 = (bf16[1056,128]{1,0:T(8,128)(2,1)S(1)}, bf16[1056,128]{1,0:T(8,128)(2,1)S(1)}, u32[]{:S(2)}, u32[]{:S(2)}) collective-permute-start(bf16[1056,128]{1,0:T(8,128)(2,1)S(1)} %get-tuple-element.179), channel_id=1, source_target_pairs={{0,16},{4,20},{8,24},{12,28},{16,0},{20,4},{24,8},{28,12},{1,17},{... | collective-permute-start | bytes 811016 | tf_op jit(solution)/shard_map/ppermute | solution.py:454
  92.6 24.9 %collective-permute-start.32 = (bf16[1056,128]{1,0:T(8,128)(2,1)S(1)}, bf16[1056,128]{1,0:T(8,128)(2,1)S(1)}, u32[]{:S(2)}, u32[]{:S(2)}) collective-permute-start(bf16[1056,128]{1,0:T(8,128)(2,1)S(1)} %get-tuple-element.178), channel_id=1, source_target_pairs={{0,8},{4,12},{8,16},{12,20},{16,24},{20,28},{24,0},{28,4},{1,9},{5... | collective-permute-start | bytes 811016 | tf_op jit(solution)/shard_map/ppermute | solution.py:454
  106.4 11.1 %collective-permute-start.33 = (bf16[384,1536]{1,0:T(8,128)(2,1)S(1)}, bf16[384,1536]{1,0:T(8,128)(2,1)S(1)}, u32[]{:S(2)}, u32[]{:S(2)}) collective-permute-start(bf16[384,1536]{1,0:T(8,128)(2,1)S(1)} %weight_grad.2), channel_id=1, source_target_pairs={{0,4},{4,0},{8,12},{12,8},{16,20},{20,16},{24,28},{28,24},{1,5},{5... | collective-permute-start | bytes 3538952 | tf_op jit(solution)/shard_map/ppermute | solution.py:457
  117.5 27.5 %collective-permute-start.35 = (bf16[192,1536]{1,0:T(8,128)(2,1)}, bf16[192,1536]{1,0:T(8,128)(2,1)S(1)}, u32[]{:S(2)}, u32[]{:S(2)}) collective-permute-start(bf16[192,1536]{1,0:T(8,128)(2,1)} %add_convert_fusion.2), channel_id=1, source_target_pairs={{0,8},{4,12},{8,16},{12,20},{16,24},{20,28},{24,0},{28,4},{1,9},{5... | collective-permute-start | bytes 1769480 | tf_op jit(solution)/shard_map/ppermute | solution.py:454
  117.5 28.2 %collective-permute-start.34 = (bf16[192,1536]{1,0:T(8,128)(2,1)}, bf16[192,1536]{1,0:T(8,128)(2,1)S(1)}, u32[]{:S(2)}, u32[]{:S(2)}) collective-permute-start(bf16[192,1536]{1,0:T(8,128)(2,1)} %mixed_term.5), channel_id=1, source_target_pairs={{0,24},{4,28},{8,0},{12,4},{16,8},{20,12},{24,16},{28,20},{1,25},{... | collective-permute-start | bytes 1769480 | tf_op jit(solution)/shard_map/ppermute | solution.py:454
  126.4 9.4 %collective-permute-start.36 = (bf16[1056,128]{1,0:T(8,128)(2,1)S(1)}, bf16[1056,128]{1,0:T(8,128)(2,1)S(1)}, u32[]{:S(2)}, u32[]{:S(2)}) collective-permute-start(bf16[1056,128]{1,0:T(8,128)(2,1)S(1)} %get-tuple-element.165), channel_id=1, source_target_pairs={{0,1},{1,0},{2,3},{3,2},{4,5},{5,4},{6,7},{7,6},{8,9},{9,8},{10,11... | collective-permute-start | bytes 811016 | tf_op jit(solution)/shard_map/ppermute | solution.py:451
  127.9 13.4 %collective-permute-start.37 = (bf16[1056,128]{1,0:T(8,128)(2,1)S(1)}, bf16[1056,128]{1,0:T(8,128)(2,1)S(1)}, u32[]{:S(2)}, u32[]{:S(2)}) collective-permute-start(bf16[1056,128]{1,0:T(8,128)(2,1)S(1)} %get-tuple-element.164), channel_id=1, source_target_pairs={{0,2},{1,3},{2,0},{3,1},{4,6},{5,7},{6,4},{7,5},{8,10},{9,11},{10,... | collective-permute-start | bytes 811016 | tf_op jit(solution)/shard_map/ppermute | solution.py:451
  129.4 11.9 %collective-permute-start.38 = (bf16[1056,128]{1,0:T(8,128)(2,1)S(1)}, bf16[1056,128]{1,0:T(8,128)(2,1)S(1)}, u32[]{:S(2)}, u32[]{:S(2)}) collective-permute-start(bf16[1056,128]{1,0:T(8,128)(2,1)S(1)} %get-tuple-element.163), channel_id=1, source_target_pairs={{0,3},{1,2},{2,1},{3,0},{4,7},{5,6},{6,5},{7,4},{8,11},{9,10},{10,... | collective-permute-start | bytes 811016 | tf_op jit(solution)/shard_map/ppermute | solution.py:451
  (17 other events, 139.2 us)

commit v7 on v6

--- a/solution.py
+++ b/solution.py
@@ -528,19 +528,18 @@
     total = weight_grad_part(after(theirs, home), grads)
 
     head_0, head_1, head_3 = after(heads[:3], total)
-    term_1 = mixed_term(head_1, *weights, BF16)
+    term_1 = mixed_term(head_1, *weights, BF16, WINDOW)
     term_3 = (mixed_2.astype(F32) + mixed_term(head_3, *weights, F32)).astype(BF16)
     total = swap(total)
-    term_0 = mixed_term(after(head_0, term_1, term_3), *weights, F32, WINDOW)
-
-    away, total = after((away, total), term_0)
-    home = [home[0], *away]
-    weight_grad = weight_grad_part(after(ours, home), grads, total)
+
+    weight_grad = weight_grad_part(ours, grads, after(total, term_1, term_3))
+    home = [home[0], *after(away, weight_grad)]
+    term_0 = mixed_term(after(head_0, home), *weights, F32, WINDOW)
 
     mixed_1 = to_plane(after(term_1, home), -1)
     mixed_3 = to_plane(after(term_3, home), 1)
 
-    home = after(jnp.stack(home), weight_grad)
+    home = after(jnp.stack(home), term_0)
     back = [pick(home, (col - plane) % PLANES)] + [
         to_col(pick(home, ((col ^ j) - plane) % PLANES), j) for j in (1, 2, 3)
     ]

time: 147 us -> 148 us (level)
  no operation moved by 1% of the time
where the time goes in v7:
time: 148 us
  waiting for transfers between devices  65.3 us (44%)
  starting transfers between devices  37.3 us (25%)
  Pallas kernels  34.3 us (23%)
  other arithmetic  5.14 us (3%)
  local copies, waits for them, and re-layouts  4.96 us (3%)
    ppermute x17, waiting for transfers between devices, to_col(): return lax.ppermute(block, 'col', col_xor(j))  34.9 us
    ppermute x12, waiting for transfers between devices, to_plane(): return lax.ppermute(block, 'row', row_shift(s))  27 us
    ppermute x17, starting transfers between devices, to_col(): return lax.ppermute(block, 'col', col_xor(j))  19.6 us
    ppermute x12, starting transfers between devices, to_plane(): return lax.ppermute(block, 'row', row_shift(s))  15.8 us
    pallas_call x2, Pallas kernels, weight_grad_part(): pl.pallas_call(functools.partial(weight_grad_kernel, len(heads)), out_sha...  7.2 us
    pallas_call x1, Pallas kernels, attention_forward(): pl.pallas_call(forward_kernel, grid=(3,), in_specs=[whole(*own[0].shape)]...  6.95 us
    pallas_call x2, Pallas kernels, grad_pieces(): pl.pallas_call(grad_kernel, out_shape=[piece] * COLS, scratch_shapes=[plt...  6.36 us
    pallas_call x1, Pallas kernels, attention_backward(): pl.pallas_call(backward_kernel, grid=(3,), in_specs=[by_query, by_head, b...  5.23 us
  transfers between devices with their start and end apart: 39, of which 20 were waited for; matrix products, arithmetic and copies ran while one was open for 4% of the time, Pallas kernels for 23%

profile of v7, /device:TPU:0, one launch (start us, length us, event | category | flops | bytes accessed | tf_op | source)
XLA Modules:
  0.0 148.0 jit_solution(2773737936832285324)
XLA Ops:
  0.6 3.1 %collective-permute-start.7 = (bf16[192,1536]{1,0:T(8,128)(2,1)}, bf16[192,1536]{1,0:T(8,128)(2,1)S(1)}, u32[]{:S(2)}, u32[]{:S(2)}) collective-permute-start(bf16[192,1536]{1,0:T(8,128)(2,1)} %refs_4_.3), channel_id=1, source_target_pairs={{0,8},{4,12},{8,16},{12,20},{16,24},{20,28},{24,0},{28,4},{1,9},{5... | collective-permute-start | bytes 1769480 | tf_op jit(solution)/shard_map/ppermute | solution.py:454
  3.7 2.1 %collective-permute-start.8 = (bf16[192,1536]{1,0:T(8,128)(2,1)}, bf16[192,1536]{1,0:T(8,128)(2,1)}, u32[]{:S(2)}, u32[]{:S(2)}) collective-permute-start(bf16[192,1536]{1,0:T(8,128)(2,1)} %refs_4_.3), channel_id=1, source_target_pairs={{0,24},{4,28},{8,0},{12,4},{16,8},{20,12},{24,16},{28,20},{1,25},{... | collective-permute-start | bytes 1769480 | tf_op jit(solution)/shard_map/ppermute | solution.py:454
  5.8 2.3 %pack_inputs.1 = (bf16[1056,128]{1,0:T(8,128)(2,1)}, bf16[1056,128]{1,0:T(8,128)(2,1)}, bf16[1056,128]{1,0:T(8,128)(2,1)}, bf16[1056,128]{1,0:T(8,128)(2,1)}) custom-call(bf16[192,768]{1,0:T(8,128)(2,1)} %q_ref, bf16[192,768]{1,0:T(8,128)(2,1)} %k_ref, bf16[192,768]{1,0:T(8,128)(2,1)} %v_ref), custom_call_target="tpu_custom_call" | custom-call | flops 40000000000 | tf_op jit(solution)/shard_map/pack_inputs/pallas_call | solution.py:282
  8.9 1.6 %collective-permute-start.1 = (bf16[1056,128]{1,0:T(8,128)(2,1)}, bf16[1056,128]{1,0:T(8,128)(2,1)S(1)}, u32[]{:S(2)}, u32[]{:S(2)}) collective-permute-start(bf16[1056,128]{1,0:T(8,128)(2,1)} %get-tuple-element.88), channel_id=1, source_target_pairs={{0,1},{1,0},{2,3},{3,2},{4,5},{5,4},{6,7},{7,6},{8,9},{9,8},{10,11... | collective-permute-start | bytes 811016 | tf_op jit(solution)/shard_map/ppermute | solution.py:451
  12.9 5.5 %collective-permute-done.1 = bf16[1056,128]{1,0:T(8,128)(2,1)S(1)} collective-permute-done((bf16[1056,128]{1,0:T(8,128)(2,1)}, bf16[1056,128]{1,0:T(8,128)(2,1)S(1)}, u32[]{:S(2)}, u32[]{:S(2)}) %collective-permute-start.1) | collective-permute-done | bytes 270368 | tf_op jit(solution)/shard_map/ppermute | solution.py:451
  18.4 6.4 %collective-permute-done.2 = bf16[1056,128]{1,0:T(8,128)(2,1)S(1)} collective-permute-done((bf16[1056,128]{1,0:T(8,128)(2,1)}, bf16[1056,128]{1,0:T(8,128)(2,1)S(1)}, u32[]{:S(2)}, u32[]{:S(2)}) %collective-permute-start.2) | collective-permute-done | bytes 270368 | tf_op jit(solution)/shard_map/ppermute | solution.py:451
  25.8 3.8 %collective-permute-start.5 = (bf16[1056,128]{1,0:T(8,128)(2,1)}, bf16[1056,128]{1,0:T(8,128)(2,1)}, u32[]{:S(2)}, u32[]{:S(2)}) collective-permute-start(bf16[1056,128]{1,0:T(8,128)(2,1)} %get-tuple-element.160), channel_id=1, source_target_pairs={{0,24},{4,28},{8,0},{12,4},{16,8},{20,12},{24,16},{28,20},{1,25},{... | collective-permute-start | bytes 811016 | tf_op jit(solution)/shard_map/ppermute | solution.py:454
  29.6 3.4 %collective-permute-done.8.refs_2_.refs_6_ = bf16[192,1536]{1,0:T(8,128)(2,1)} collective-permute-done((bf16[192,1536]{1,0:T(8,128)(2,1)}, bf16[192,1536]{1,0:T(8,128)(2,1)}, u32[]{:S(2)}, u32[]{:S(2)}) %collective-permute-start.8) | collective-permute-done | bytes 589856 | tf_op jit(solution)/shard_map/ppermute | solution.py:454
  33.1 4.4 %grad_pieces.2 = (bf16[864,128]{1,0:T(8,128)(2,1)S(1)}, bf16[864,128]{1,0:T(8,128)(2,1)}, bf16[864,128]{1,0:T(8,128)(2,1)}, bf16[864,128]{1,0:T(8,128)(2,1)}) custom-call(bf16[192,1536]{1,0:T(8,128)(2,1)S(1)} %copy-done.1, bf16[192,1536]{1,0:T(8,128)(2,1)S(1)} %collective-permute-done.7.refs_1_.refs_5_, ...), custom_call_target="tpu_custom_call" | custom-call | flops 40000000000 | tf_op jit(solution)/shard_map/grad_pieces/pallas_call | solution.py:314
  38.7 1.8 %collective-permute-start.10 = (bf16[864,128]{1,0:T(8,128)(2,1)}, bf16[864,128]{1,0:T(8,128)(2,1)}, u32[]{:S(2)}, u32[]{:S(2)}) collective-permute-start(bf16[864,128]{1,0:T(8,128)(2,1)} %get-tuple-element.100), channel_id=1, source_target_pairs={{0,2},{1,3},{2,0},{3,1},{4,6},{5,7},{6,4},{7,5},{8,10},{9,11},{10,... | collective-permute-start | bytes 663560 | tf_op jit(solution)/shard_map/ppermute | solution.py:451
  43.0 12.1 %collective-permute-done.6.refs_3_ = bf16[1056,128]{1,0:T(8,128)(2,1)} collective-permute-done((bf16[1056,128]{1,0:T(8,128)(2,1)}, bf16[1056,128]{1,0:T(8,128)(2,1)}, u32[]{:S(2)}, u32[]{:S(2)}) %collective-permute-start.6) | collective-permute-done | bytes 270368 | tf_op jit(solution)/shard_map/ppermute | solution.py:454
  57.9 7.0 %attention_forward.1 = (bf16[3,1536,384]{2,1,0:T(8,128)(2,1)}, bf16[1152,128]{1,0:T(8,128)(2,1)S(1)}, bf16[1152,128]{1,0:T(8,128)(2,1)S(1)}, bf16[2,1536,128]{2,1,0:T(8,128)(2,1)S(1)}, bf16[2,1536,128]{2,1,0:T(8,128)(2,1)S(1)}) custom-call(bf16[1056,128]{1,0:T(8,128)(2,1)S(1)} %get-tuple-element.102.refs_0_, ...), custom_call_target="tpu_custom_call" | custom-call | flops 40000000000 | tf_op jit(solution)/shard_map/attention_forward/pallas_call | solution.py:167
  64.8 1.6 %collective-permute-start.18 = (bf16[288,128]{1,0:T(8,128)(2,1)S(1)}, bf16[288,128]{1,0:T(8,128)(2,1)S(1)}, u32[]{:S(2)}, u32[]{:S(2)}) collective-permute-start(bf16[288,128]{1,0:T(8,128)(2,1)S(1)} %get-tuple-element.213), channel_id=1, source_target_pairs={{0,1},{1,0},{2,3},{3,2},{4,5},{5,4},{6,7},{7,6},{8,9},{9,8},{10,11... | collective-permute-start | bytes 221192 | tf_op jit(solution)/shard_map/ppermute | solution.py:451
  68.5 1.6 %collective-permute-start.16 = (bf16[864,128]{1,0:T(8,128)(2,1)S(1)}, bf16[864,128]{1,0:T(8,128)(2,1)S(1)}, u32[]{:S(2)}, u32[]{:S(2)}) collective-permute-start(bf16[864,128]{1,0:T(8,128)(2,1)S(1)} %get-tuple-element.211), channel_id=1, source_target_pairs={{0,1},{1,0},{2,3},{3,2},{4,5},{5,4},{6,7},{7,6},{8,9},{9,8},{10,11... | collective-permute-start | bytes 663560 | tf_op jit(solution)/shard_map/ppermute | solution.py:451
  72.3 2.0 %grad_pieces.3 = (bf16[288,128]{1,0:T(8,128)(2,1)S(1)}, bf16[288,128]{1,0:T(8,128)(2,1)S(1)}, bf16[288,128]{1,0:T(8,128)(2,1)S(1)}, bf16[288,128]{1,0:T(8,128)(2,1)S(1)}) custom-call(bf16[192,1536]{1,0:T(8,128)(2,1)} %collective-permute-done.21.refs_0_.refs_7_, bf16[384,1536]{1,0:T(8,128)(2,1)S(1)} %copy-done, ...), custom_call_target="tpu_custom_call" | custom-call | flops 40000000000 | tf_op jit(solution)/shard_map/grad_pieces/pallas_call | solution.py:314
  74.4 1.6 %collective-permute-start.23 = (bf16[288,128]{1,0:T(8,128)(2,1)S(1)}, bf16[288,128]{1,0:T(8,128)(2,1)S(1)}, u32[]{:S(2)}, u32[]{:S(2)}) collective-permute-start(bf16[288,128]{1,0:T(8,128)(2,1)S(1)} %get-tuple-element.115), channel_id=1, source_target_pairs={{0,1},{1,0},{2,3},{3,2},{4,5},{5,4},{6,7},{7,6},{8,9},{9,8},{10,11... | collective-permute-start | bytes 221192 | tf_op jit(solution)/shard_map/ppermute | solution.py:451
  79.1 2.0 %collective-permute-done.24.refs_3_ = bf16[288,128]{1,0:T(8,128)(2,1)S(1)} collective-permute-done((bf16[288,128]{1,0:T(8,128)(2,1)S(1)}, bf16[288,128]{1,0:T(8,128)(2,1)S(1)}, u32[]{:S(2)}, u32[]{:S(2)}) %collective-permute-start.24) | collective-permute-done | bytes 73760 | tf_op jit(solution)/shard_map/ppermute | solution.py:451
  81.1 1.6 %collective-permute-done.25.refs_4_ = bf16[288,128]{1,0:T(8,128)(2,1)S(1)} collective-permute-done((bf16[288,128]{1,0:T(8,128)(2,1)S(1)}, bf16[288,128]{1,0:T(8,128)(2,1)S(1)}, u32[]{:S(2)}, u32[]{:S(2)}) %collective-permute-start.25) | collective-permute-done | bytes 73760 | tf_op jit(solution)/shard_map/ppermute | solution.py:451
  82.7 5.2 %attention_backward.1 = (bf16[1152,128]{1,0:T(8,128)(2,1)S(1)}, f32[2,2,768,128]{3,2,1,0:T(8,128)S(1)}, bf16[2,2,768,128]{3,2,1,0:T(8,128)(2,1)S(1)}) custom-call(bf16[1152,128]{1,0:T(8,128)(2,1)S(1)} %get-tuple-element.121.q_ref, bf16[2,1536,128]{2,1,0:T(8,128)(2,1)S(1)} %get-tuple-element.122.k_ref, bf16[2,1536,128]{2,1,0:T(8,128)(2,1)S(1)} %get-tuple-element.123.v_ref, ...), custom_call_target="tpu_custom_call" | custom-call | flops 40000000000 | tf_op jit(solution)/shard_map/attention_backward/pallas_call | solution.py:239
  90.7 1.9 %collective-permute-start.30 = (bf16[1056,128]{1,0:T(8,128)(2,1)S(1)}, bf16[1056,128]{1,0:T(8,128)(2,1)S(1)}, u32[]{:S(2)}, u32[]{:S(2)}) collective-permute-start(bf16[1056,128]{1,0:T(8,128)(2,1)S(1)} %get-tuple-element.172), channel_id=1, source_target_pairs={{0,24},{4,28},{8,0},{12,4},{16,8},{20,12},{24,16},{28,20},{1,25},{... | collective-permute-start | bytes 811016 | tf_op jit(solution)/shard_map/ppermute | solution.py:454
  93.7 8.0 %collective-permute-done.17 = bf16[2,864,128]{2,1,0:T(8,128)(2,1)S(1)} collective-permute-done((bf16[2,864,128]{2,1,0:T(8,128)(2,1)S(1)}, bf16[2,864,128]{2,1,0:T(8,128)(2,1)S(1)}, u32[]{:S(2)}, u32[]{:S(2)}) %collective-permute-start.17) | collective-permute-done | bytes 442400 | tf_op jit(solution)/shard_map/ppermute | solution.py:451
  103.3 3.1 %weight_grad.2 = bf16[384,1536]{1,0:T(8,128)(2,1)S(1)} custom-call(bf16[192,384]{1,0:T(8,128)(2,1)S(1)} %get-tuple-element.134.refs_0_, bf16[192,384]{1,0:T(8,128)(2,1)S(1)} %get-tuple-element.135.refs_1_, bf16[192,384]{1,0:T(8,128)(2,1)S(1)} %get-tuple-element.136.refs_2_, bf16[192,384]{1,0:T(8,128)(2,1)S(1)} %get-tuple-element.137.refs_3_, ...), custom_call_target="tpu_custom_call" | custom-call | flops 40000000000 | tf_op jit(solution)/shard_map/weight_grad/pallas_call | solution.py:358
  106.5 1.6 %mixed_term.5 = bf16[192,1536]{1,0:T(8,128)(2,1)} custom-call(bf16[192,768]{1,0:T(8,128)(2,1)S(1)} %get-tuple-element.139.block_ref, bf16[384,1536]{1,0:T(8,128)(2,1)S(1)} %copy-done, bf16[384,1536]{1,0:T(8,128)(2,1)S(1)} %collective-permute-done.refs_4_.refs_2_.other_ref), custom_call_target="tpu_custom_call" | custom-call | flops 40000000000 | tf_op jit(solution)/shard_map/mixed_term/pallas_call | solution.py:337
  109.8 4.1 %weight_grad.3 = bf16[384,1536]{1,0:T(8,128)(2,1)} custom-call(bf16[192,384]{1,0:T(8,128)(2,1)S(1)} %get-tuple-element.196.refs_0_, bf16[192,384]{1,0:T(8,128)(2,1)S(1)} %get-tuple-element.215.refs_1_, bf16[192,384]{1,0:T(8,128)(2,1)S(1)} %get-tuple-element.192.refs_2_, bf16[192,384]{1,0:T(8,128)(2,1)S(1)} %get-tuple-element.190.refs_3_, ...), custom_call_target="tpu_custom_call" | custom-call | flops 40000000000 | tf_op jit(solution)/shard_map/weight_grad/pallas_call | solution.py:358
  114.0 3.6 %collective-permute-done.31 = bf16[1056,128]{1,0:T(8,128)(2,1)S(1)} collective-permute-done((bf16[1056,128]{1,0:T(8,128)(2,1)S(1)}, bf16[1056,128]{1,0:T(8,128)(2,1)S(1)}, u32[]{:S(2)}, u32[]{:S(2)}) %collective-permute-start.31) | collective-permute-done | bytes 270368 | tf_op jit(solution)/shard_map/ppermute | solution.py:454
  117.5 3.8 %collective-permute-start.34 = (bf16[192,1536]{1,0:T(8,128)(2,1)}, bf16[192,1536]{1,0:T(8,128)(2,1)}, u32[]{:S(2)}, u32[]{:S(2)}) collective-permute-start(bf16[192,1536]{1,0:T(8,128)(2,1)} %mixed_term.5), channel_id=1, source_target_pairs={{0,24},{4,28},{8,0},{12,4},{16,8},{20,12},{24,16},{28,20},{1,25},{... | collective-permute-start | bytes 1769480 | tf_op jit(solution)/shard_map/ppermute | solution.py:454
  124.6 1.5 %collective-permute-start.37 = (bf16[1056,128]{1,0:T(8,128)(2,1)S(1)}, bf16[1056,128]{1,0:T(8,128)(2,1)S(1)}, u32[]{:S(2)}, u32[]{:S(2)}) collective-permute-start(bf16[1056,128]{1,0:T(8,128)(2,1)S(1)} %get-tuple-element.156), channel_id=1, source_target_pairs={{0,2},{1,3},{2,0},{3,1},{4,6},{5,7},{6,4},{7,5},{8,10},{9,11},{10,... | collective-permute-start | bytes 811016 | tf_op jit(solution)/shard_map/ppermute | solution.py:451
  126.6 5.9 %collective-permute-done.36.refs_1_ = bf16[1056,128]{1,0:T(8,128)(2,1)S(1)} collective-permute-done((bf16[1056,128]{1,0:T(8,128)(2,1)S(1)}, bf16[1056,128]{1,0:T(8,128)(2,1)S(1)}, u32[]{:S(2)}, u32[]{:S(2)}) %collective-permute-start.36) | collective-permute-done | bytes 270368 | tf_op jit(solution)/shard_map/ppermute | solution.py:451
  132.5 5.5 %collective-permute-done.37.refs_2_ = bf16[1056,128]{1,0:T(8,128)(2,1)S(1)} collective-permute-done((bf16[1056,128]{1,0:T(8,128)(2,1)S(1)}, bf16[1056,128]{1,0:T(8,128)(2,1)S(1)}, u32[]{:S(2)}, u32[]{:S(2)}) %collective-permute-start.37) | collective-permute-done | bytes 270368 | tf_op jit(solution)/shard_map/ppermute | solution.py:451
  138.8 2.3 %unpack_outputs.1 = (bf16[192,768]{1,0:T(8,128)(2,1)}, bf16[192,768]{1,0:T(8,128)(2,1)}, bf16[192,768]{1,0:T(8,128)(2,1)}) custom-call(bf16[1056,128]{1,0:T(8,128)(2,1)} %get-tuple-element.158.refs_0_, bf16[1056,128]{1,0:T(8,128)(2,1)} %copy-done.7, bf16[1056,128]{1,0:T(8,128)(2,1)} %copy-done.8, bf16[1056,128]{1,0:T(8,128)(2,1)} %copy-done.9), custom_call_target="tpu_custom_call" | custom-call | flops 1000000 | bytes 1000 | tf_op jit(solution)/shard_map/unpack_outputs/pallas_call | solution.py:398
  141.1 4.7 %collective-permute-done.34 = bf16[192,1536]{1,0:T(8,128)(2,1)} collective-permute-done((bf16[192,1536]{1,0:T(8,128)(2,1)}, bf16[192,1536]{1,0:T(8,128)(2,1)}, u32[]{:S(2)}, u32[]{:S(2)}) %collective-permute-start.34) | collective-permute-done | bytes 589856 | tf_op jit(solution)/shard_map/ppermute | solution.py:454
  145.8 2.2 %add_convert_fusion.1 = bf16[192,1536]{1,0:T(8,128)(2,1)} fusion(bf16[192,1536]{1,0:T(8,128)(2,1)} %collective-permute-done.35, f32[192,1536]{1,0:T(8,128)S(1)} %mixed_term.7, bf16[192,1536]{1,0:T(8,128)(2,1)} %collective-permute-done.34), kind=kLoop, calls=%fused_computation.1 | loop fusion | flops 1474560 | bytes 2949120 | tf_op jit(solution)/shard_map/convert_element_type | solution.py:548
  (129 shorter events, 29.7 us)
Async XLA Ops:
  0.6 29.0 %collective-permute-start.7 = (bf16[192,1536]{1,0:T(8,128)(2,1)}, bf16[192,1536]{1,0:T(8,128)(2,1)S(1)}, u32[]{:S(2)}, u32[]{:S(2)}) collective-permute-start(bf16[192,1536]{1,0:T(8,128)(2,1)} %refs_4_.3), channel_id=1, source_target_pairs={{0,8},{4,12},{8,16},{12,20},{16,24},{20,28},{24,0},{28,4},{1,9},{5... | collective-permute-start | bytes 1769480 | tf_op jit(solution)/shard_map/ppermute | solution.py:454
  3.7 29.3 %collective-permute-start.8 = (bf16[192,1536]{1,0:T(8,128)(2,1)}, bf16[192,1536]{1,0:T(8,128)(2,1)}, u32[]{:S(2)}, u32[]{:S(2)}) collective-permute-start(bf16[192,1536]{1,0:T(8,128)(2,1)} %refs_4_.3), channel_id=1, source_target_pairs={{0,24},{4,28},{8,0},{12,4},{16,8},{20,12},{24,16},{28,20},{1,25},{... | collective-permute-start | bytes 1769480 | tf_op jit(solution)/shard_map/ppermute | solution.py:454
  5.8 3.1 %collective-permute-start = (bf16[384,1536]{1,0:T(8,128)(2,1)}, bf16[384,1536]{1,0:T(8,128)(2,1)S(1)}, u32[]{:S(2)}, u32[]{:S(2)}) collective-permute-start(bf16[384,1536]{1,0:T(8,128)(2,1)} %own_ref.7), channel_id=1, source_target_pairs={{0,4},{4,0},{8,12},{12,8},{16,20},{20,16},{24,28},{28,24},{1,5},{5... | collective-permute-start | bytes 3538952 | tf_op jit(solution)/shard_map/ppermute | solution.py:457
  8.9 9.5 %collective-permute-start.1 = (bf16[1056,128]{1,0:T(8,128)(2,1)}, bf16[1056,128]{1,0:T(8,128)(2,1)S(1)}, u32[]{:S(2)}, u32[]{:S(2)}) collective-permute-start(bf16[1056,128]{1,0:T(8,128)(2,1)} %get-tuple-element.88), channel_id=1, source_target_pairs={{0,1},{1,0},{2,3},{3,2},{4,5},{5,4},{6,7},{7,6},{8,9},{9,8},{10,11... | collective-permute-start | bytes 811016 | tf_op jit(solution)/shard_map/ppermute | solution.py:451
  10.5 14.2 %collective-permute-start.2 = (bf16[1056,128]{1,0:T(8,128)(2,1)}, bf16[1056,128]{1,0:T(8,128)(2,1)S(1)}, u32[]{:S(2)}, u32[]{:S(2)}) collective-permute-start(bf16[1056,128]{1,0:T(8,128)(2,1)} %get-tuple-element.89), channel_id=1, source_target_pairs={{0,2},{1,3},{2,0},{3,1},{4,6},{5,7},{6,4},{7,5},{8,10},{9,11},{10,... | collective-permute-start | bytes 811016 | tf_op jit(solution)/shard_map/ppermute | solution.py:451
  12.0 12.7 %collective-permute-start.3 = (bf16[1056,128]{1,0:T(8,128)(2,1)}, bf16[1056,128]{1,0:T(8,128)(2,1)S(1)}, u32[]{:S(2)}, u32[]{:S(2)}) collective-permute-start(bf16[1056,128]{1,0:T(8,128)(2,1)} %get-tuple-element.90), channel_id=1, source_target_pairs={{0,3},{1,2},{2,1},{3,0},{4,7},{5,6},{6,5},{7,4},{8,11},{9,10},{10,... | collective-permute-start | bytes 811016 | tf_op jit(solution)/shard_map/ppermute | solution.py:451
  25.8 12.9 %collective-permute-start.4 = (bf16[1056,128]{1,0:T(8,128)(2,1)S(1)}, bf16[1056,128]{1,0:T(8,128)(2,1)}, u32[]{:S(2)}, u32[]{:S(2)}) collective-permute-start(bf16[1056,128]{1,0:T(8,128)(2,1)S(1)} %get-tuple-element.161), channel_id=1, source_target_pairs={{0,8},{4,12},{8,16},{12,20},{16,24},{20,28},{24,0},{28,4},{1,9},{5... | collective-permute-start | bytes 811016 | tf_op jit(solution)/shard_map/ppermute | solution.py:454
  25.8 17.2 %collective-permute-start.5 = (bf16[1056,128]{1,0:T(8,128)(2,1)}, bf16[1056,128]{1,0:T(8,128)(2,1)}, u32[]{:S(2)}, u32[]{:S(2)}) collective-permute-start(bf16[1056,128]{1,0:T(8,128)(2,1)} %get-tuple-element.160), channel_id=1, source_target_pairs={{0,24},{4,28},{8,0},{12,4},{16,8},{20,12},{24,16},{28,20},{1,25},{... | collective-permute-start | bytes 811016 | tf_op jit(solution)/shard_map/ppermute | solution.py:454
  29.6 25.6 %collective-permute-start.6 = (bf16[1056,128]{1,0:T(8,128)(2,1)}, bf16[1056,128]{1,0:T(8,128)(2,1)}, u32[]{:S(2)}, u32[]{:S(2)}) collective-permute-start(bf16[1056,128]{1,0:T(8,128)(2,1)} %get-tuple-element.159), channel_id=1, source_target_pairs={{0,16},{4,20},{8,24},{12,28},{16,0},{20,4},{24,8},{28,12},{1,17},{... | collective-permute-start | bytes 811016 | tf_op jit(solution)/shard_map/ppermute | solution.py:454
  38.7 16.5 %collective-permute-start.10 = (bf16[864,128]{1,0:T(8,128)(2,1)}, bf16[864,128]{1,0:T(8,128)(2,1)}, u32[]{:S(2)}, u32[]{:S(2)}) collective-permute-start(bf16[864,128]{1,0:T(8,128)(2,1)} %get-tuple-element.100), channel_id=1, source_target_pairs={{0,2},{1,3},{2,0},{3,1},{4,6},{5,7},{6,4},{7,5},{8,10},{9,11},{10,... | collective-permute-start | bytes 663560 | tf_op jit(solution)/shard_map/ppermute | solution.py:451
  40.5 14.7 %collective-permute-start.11 = (bf16[864,128]{1,0:T(8,128)(2,1)}, bf16[864,128]{1,0:T(8,128)(2,1)}, u32[]{:S(2)}, u32[]{:S(2)}) collective-permute-start(bf16[864,128]{1,0:T(8,128)(2,1)} %get-tuple-element.101), channel_id=1, source_target_pairs={{0,3},{1,2},{2,1},{3,0},{4,7},{5,6},{6,5},{7,4},{8,11},{9,10},{10,... | collective-permute-start | bytes 663560 | tf_op jit(solution)/shard_map/ppermute | solution.py:451
  41.9 13.8 %collective-permute-start.9 = (bf16[864,128]{1,0:T(8,128)(2,1)}, bf16[864,128]{1,0:T(8,128)(2,1)}, u32[]{:S(2)}, u32[]{:S(2)}) collective-permute-start(bf16[864,128]{1,0:T(8,128)(2,1)} %get-tuple-element.99), channel_id=1, source_target_pairs={{0,1},{1,0},{2,3},{3,2},{4,5},{5,4},{6,7},{7,6},{8,9},{9,8},{10,11... | collective-permute-start | bytes 663560 | tf_op jit(solution)/shard_map/ppermute | solution.py:451
  43.0 12.8 %collective-permute-start.12 = (bf16[1056,128]{1,0:T(8,128)(2,1)S(1)}, bf16[1056,128]{1,0:T(8,128)(2,1)}, u32[]{:S(2)}, u32[]{:S(2)}) collective-permute-start(bf16[1056,128]{1,0:T(8,128)(2,1)S(1)} %get-tuple-element.102.refs_0_), channel_id=1, source_target_pairs={{0,4},{4,0},{8,12},{12,8},{16,20},{20,16},{24,28},{28,24},{1,5},{5... | collective-permute-start | bytes 811016 | tf_op jit(solution)/shard_map/ppermute | solution.py:457
  55.2 17.2 %collective-permute-start.21 = (bf16[192,1536]{1,0:T(8,128)(2,1)S(1)}, bf16[192,1536]{1,0:T(8,128)(2,1)}, u32[]{:S(2)}, u32[]{:S(2)}) collective-permute-start(bf16[192,1536]{1,0:T(8,128)(2,1)S(1)} %collective-permute-done.7.refs_1_.refs_5_), channel_id=1, source_target_pairs={{0,8},{4,12},{8,16},{12,20},{16,24},{20,28},{24,0},{28,4},{1,9},{5... | collective-permute-start | bytes 1769480 | tf_op jit(solution)/shard_map/ppermute | solution.py:454
  64.8 11.1 %collective-permute-start.18 = (bf16[288,128]{1,0:T(8,128)(2,1)S(1)}, bf16[288,128]{1,0:T(8,128)(2,1)S(1)}, u32[]{:S(2)}, u32[]{:S(2)}) collective-permute-start(bf16[288,128]{1,0:T(8,128)(2,1)S(1)} %get-tuple-element.213), channel_id=1, source_target_pairs={{0,1},{1,0},{2,3},{3,2},{4,5},{5,4},{6,7},{7,6},{8,9},{9,8},{10,11... | collective-permute-start | bytes 221192 | tf_op jit(solution)/shard_map/ppermute | solution.py:451
  66.4 11.0 %collective-permute-start.19 = (bf16[288,128]{1,0:T(8,128)(2,1)S(1)}, bf16[288,128]{1,0:T(8,128)(2,1)S(1)}, u32[]{:S(2)}, u32[]{:S(2)}) collective-permute-start(bf16[288,128]{1,0:T(8,128)(2,1)S(1)} %get-tuple-element.213), channel_id=1, source_target_pairs={{0,2},{1,3},{2,0},{3,1},{4,6},{5,7},{6,4},{7,5},{8,10},{9,11},{10,... | collective-permute-start | bytes 221192 | tf_op jit(solution)/shard_map/ppermute | solution.py:451
  67.9 10.0 %collective-permute-start.20 = (bf16[288,128]{1,0:T(8,128)(2,1)S(1)}, bf16[288,128]{1,0:T(8,128)(2,1)S(1)}, u32[]{:S(2)}, u32[]{:S(2)}) collective-permute-start(bf16[288,128]{1,0:T(8,128)(2,1)S(1)} %get-tuple-element.213), channel_id=1, source_target_pairs={{0,3},{1,2},{2,1},{3,0},{4,7},{5,6},{6,5},{7,4},{8,11},{9,10},{10,... | collective-permute-start | bytes 221192 | tf_op jit(solution)/shard_map/ppermute | solution.py:451
  68.5 20.2 %collective-permute-start.16 = (bf16[864,128]{1,0:T(8,128)(2,1)S(1)}, bf16[864,128]{1,0:T(8,128)(2,1)S(1)}, u32[]{:S(2)}, u32[]{:S(2)}) collective-permute-start(bf16[864,128]{1,0:T(8,128)(2,1)S(1)} %get-tuple-element.211), channel_id=1, source_target_pairs={{0,1},{1,0},{2,3},{3,2},{4,5},{5,4},{6,7},{7,6},{8,9},{9,8},{10,11... | collective-permute-start | bytes 663560 | tf_op jit(solution)/shard_map/ppermute | solution.py:451
  74.4 4.7 %collective-permute-start.23 = (bf16[288,128]{1,0:T(8,128)(2,1)S(1)}, bf16[288,128]{1,0:T(8,128)(2,1)S(1)}, u32[]{:S(2)}, u32[]{:S(2)}) collective-permute-start(bf16[288,128]{1,0:T(8,128)(2,1)S(1)} %get-tuple-element.115), channel_id=1, source_target_pairs={{0,1},{1,0},{2,3},{3,2},{4,5},{5,4},{6,7},{7,6},{8,9},{9,8},{10,11... | collective-permute-start | bytes 221192 | tf_op jit(solution)/shard_map/ppermute | solution.py:451
  75.9 5.1 %collective-permute-start.24 = (bf16[288,128]{1,0:T(8,128)(2,1)S(1)}, bf16[288,128]{1,0:T(8,128)(2,1)S(1)}, u32[]{:S(2)}, u32[]{:S(2)}) collective-permute-start(bf16[288,128]{1,0:T(8,128)(2,1)S(1)} %get-tuple-element.116), channel_id=1, source_target_pairs={{0,2},{1,3},{2,0},{3,1},{4,6},{5,7},{6,4},{7,5},{8,10},{9,11},{10,... | collective-permute-start | bytes 221192 | tf_op jit(solution)/shard_map/ppermute | solution.py:451
  77.4 5.3 %collective-permute-start.25 = (bf16[288,128]{1,0:T(8,128)(2,1)S(1)}, bf16[288,128]{1,0:T(8,128)(2,1)S(1)}, u32[]{:S(2)}, u32[]{:S(2)}) collective-permute-start(bf16[288,128]{1,0:T(8,128)(2,1)S(1)} %get-tuple-element.117), channel_id=1, source_target_pairs={{0,3},{1,2},{2,1},{3,0},{4,7},{5,6},{6,5},{7,4},{8,11},{9,10},{10,... | collective-permute-start | bytes 221192 | tf_op jit(solution)/shard_map/ppermute | solution.py:451
  78.9 22.8 %collective-permute-start.22 = (bf16[192,1536]{1,0:T(8,128)(2,1)S(1)}, bf16[192,1536]{1,0:T(8,128)(2,1)S(1)}, u32[]{:S(2)}, u32[]{:S(2)}) collective-permute-start(bf16[192,1536]{1,0:T(8,128)(2,1)S(1)} %mixed_term.4), channel_id=1, source_target_pairs={{0,8},{4,12},{8,16},{12,20},{16,24},{20,28},{24,0},{28,4},{1,9},{5... | collective-permute-start | bytes 1769480 | tf_op jit(solution)/shard_map/ppermute | solution.py:454
  89.5 12.2 %collective-permute-start.17 = (bf16[2,864,128]{2,1,0:T(8,128)(2,1)S(1)}, bf16[2,864,128]{2,1,0:T(8,128)(2,1)S(1)}, u32[]{:S(2)}, u32[]{:S(2)}) collective-permute-start(bf16[2,864,128]{2,1,0:T(8,128)(2,1)S(1)} %pad_maximum_fusion.2), channel_id=1, source_target_pairs={{0,2},{1,3},{2,0},{3,1},{4,6},{5,7},{6,4},{7,5},{8,10},{9,11},{10,... | collective-permute-start | bytes 1327112 | tf_op jit(solution)/shard_map/ppermute | solution.py:451
  90.7 23.2 %collective-permute-start.30 = (bf16[1056,128]{1,0:T(8,128)(2,1)S(1)}, bf16[1056,128]{1,0:T(8,128)(2,1)S(1)}, u32[]{:S(2)}, u32[]{:S(2)}) collective-permute-start(bf16[1056,128]{1,0:T(8,128)(2,1)S(1)} %get-tuple-element.172), channel_id=1, source_target_pairs={{0,24},{4,28},{8,0},{12,4},{16,8},{20,12},{24,16},{28,20},{1,25},{... | collective-permute-start | bytes 811016 | tf_op jit(solution)/shard_map/ppermute | solution.py:454
  92.6 24.9 %collective-permute-start.31 = (bf16[1056,128]{1,0:T(8,128)(2,1)S(1)}, bf16[1056,128]{1,0:T(8,128)(2,1)S(1)}, u32[]{:S(2)}, u32[]{:S(2)}) collective-permute-start(bf16[1056,128]{1,0:T(8,128)(2,1)S(1)} %get-tuple-element.171), channel_id=1, source_target_pairs={{0,16},{4,20},{8,24},{12,28},{16,0},{20,4},{24,8},{28,12},{1,17},{... | collective-permute-start | bytes 811016 | tf_op jit(solution)/shard_map/ppermute | solution.py:454
  92.6 24.9 %collective-permute-start.32 = (bf16[1056,128]{1,0:T(8,128)(2,1)S(1)}, bf16[1056,128]{1,0:T(8,128)(2,1)S(1)}, u32[]{:S(2)}, u32[]{:S(2)}) collective-permute-start(bf16[1056,128]{1,0:T(8,128)(2,1)S(1)} %get-tuple-element.170), channel_id=1, source_target_pairs={{0,8},{4,12},{8,16},{12,20},{16,24},{20,28},{24,0},{28,4},{1,9},{5... | collective-permute-start | bytes 811016 | tf_op jit(solution)/shard_map/ppermute | solution.py:454
  106.4 3.4 %collective-permute-start.33 = (bf16[384,1536]{1,0:T(8,128)(2,1)S(1)}, bf16[384,1536]{1,0:T(8,128)(2,1)S(1)}, u32[]{:S(2)}, u32[]{:S(2)}) collective-permute-start(bf16[384,1536]{1,0:T(8,128)(2,1)S(1)} %weight_grad.2), channel_id=1, source_target_pairs={{0,4},{4,0},{8,12},{12,8},{16,20},{20,16},{24,28},{28,24},{1,5},{5... | collective-permute-start | bytes 3538952 | tf_op jit(solution)/shard_map/ppermute | solution.py:457
  117.5 23.5 %collective-permute-start.35 = (bf16[192,1536]{1,0:T(8,128)(2,1)}, bf16[192,1536]{1,0:T(8,128)(2,1)}, u32[]{:S(2)}, u32[]{:S(2)}) collective-permute-start(bf16[192,1536]{1,0:T(8,128)(2,1)} %add_convert_fusion.2), channel_id=1, source_target_pairs={{0,8},{4,12},{8,16},{12,20},{16,24},{20,28},{24,0},{28,4},{1,9},{5... | collective-permute-start | bytes 1769480 | tf_op jit(solution)/shard_map/ppermute | solution.py:454
  117.5 28.3 %collective-permute-start.34 = (bf16[192,1536]{1,0:T(8,128)(2,1)}, bf16[192,1536]{1,0:T(8,128)(2,1)}, u32[]{:S(2)}, u32[]{:S(2)}) collective-permute-start(bf16[192,1536]{1,0:T(8,128)(2,1)} %mixed_term.5), channel_id=1, source_target_pairs={{0,24},{4,28},{8,0},{12,4},{16,8},{20,12},{24,16},{28,20},{1,25},{... | collective-permute-start | bytes 1769480 | tf_op jit(solution)/shard_map/ppermute | solution.py:454
  123.1 9.4 %collective-permute-start.36 = (bf16[1056,128]{1,0:T(8,128)(2,1)S(1)}, bf16[1056,128]{1,0:T(8,128)(2,1)S(1)}, u32[]{:S(2)}, u32[]{:S(2)}) collective-permute-start(bf16[1056,128]{1,0:T(8,128)(2,1)S(1)} %get-tuple-element.157), channel_id=1, source_target_pairs={{0,1},{1,0},{2,3},{3,2},{4,5},{5,4},{6,7},{7,6},{8,9},{9,8},{10,11... | collective-permute-start | bytes 811016 | tf_op jit(solution)/shard_map/ppermute | solution.py:451
  124.6 13.4 %collective-permute-start.37 = (bf16[1056,128]{1,0:T(8,128)(2,1)S(1)}, bf16[1056,128]{1,0:T(8,128)(2,1)S(1)}, u32[]{:S(2)}, u32[]{:S(2)}) collective-permute-start(bf16[1056,128]{1,0:T(8,128)(2,1)S(1)} %get-tuple-element.156), channel_id=1, source_target_pairs={{0,2},{1,3},{2,0},{3,1},{4,6},{5,7},{6,4},{7,5},{8,10},{9,11},{10,... | collective-permute-start | bytes 811016 | tf_op jit(solution)/shard_map/ppermute | solution.py:451
  126.1 11.9 %collective-permute-start.38 = (bf16[1056,128]{1,0:T(8,128)(2,1)S(1)}, bf16[1056,128]{1,0:T(8,128)(2,1)S(1)}, u32[]{:S(2)}, u32[]{:S(2)}) collective-permute-start(bf16[1056,128]{1,0:T(8,128)(2,1)S(1)} %get-tuple-element.155), channel_id=1, source_target_pairs={{0,3},{1,2},{2,1},{3,0},{4,7},{5,6},{6,5},{7,4},{8,11},{9,10},{10,... | collective-permute-start | bytes 811016 | tf_op jit(solution)/shard_map/ppermute | solution.py:451
  (17 other events, 72.8 us)

commit v8 on v6

--- a/solution.py
+++ b/solution.py
@@ -130,7 +130,8 @@
 
 
 def forward_kernel(*refs):
-    own_refs, other_refs, (p_ref, attn_ref, q_ref, k_ref, v_ref) = refs[:PLANES], refs[PLANES:-5], refs[-5:]
+    own_refs, other_refs, refs = refs[:PLANES], refs[PLANES : 2 * PLANES], refs[2 * PLANES :]
+    p_ref, attn_ref, q_ref, k_ref, v_ref, sems = refs
     step = pl.program_id(0)
     rows = attn_ref.shape[0]
 
@@ -138,15 +139,24 @@
     def _():
         tokens = k_ref.shape[1] // (2 * PLANES)
         half = tokens // 2
+        moves = []
         for p, own_ref in enumerate(own_refs):
-            q_ref[p * tokens : (p + 1) * tokens] = own_ref[:tokens]
-            at = PLANES * tokens + p * half
-            q_ref[at : at + half] = own_ref[tokens : tokens + half]
+            moves.append((own_ref, 0, tokens, q_ref, p * tokens))
+            moves.append((own_ref, tokens, half, q_ref, PLANES * tokens + p * half))
         for p, in_ref in enumerate(own_refs + other_refs):
             for i in range(4):
-                at = tokens + half + i * tokens
-                out_ref = (k_ref, v_ref)[i // 2]
-                out_ref[i % 2, p * tokens : (p + 1) * tokens] = in_ref[at : at + tokens]
+                out_ref = (k_ref, v_ref)[i // 2].at[i % 2]
+                moves.append((in_ref, tokens + half + i * tokens, tokens, out_ref, p * tokens))
+        copies = [
+            pltpu.make_async_copy(
+                in_ref.at[pl.ds(at, n)], out_ref.at[pl.ds(to, n)], sems.at[i]
+            )
+            for i, (in_ref, at, n, out_ref, to) in enumerate(moves)
+        ]
+        for copy in copies:
+            copy.start()
+        for copy in copies:
+            copy.wait()
 
     head = lax.div(step, 2)
     raw = nt(k_ref[head], q_ref[pl.ds(pl.multiple_of(step * rows, rows), rows)])
@@ -167,7 +177,8 @@
     return pl.pallas_call(
         forward_kernel,
         grid=(3,),
-        in_specs=[whole(*own[0].shape)] * (2 * PLANES),
+        in_specs=[pl.BlockSpec(memory_space=pl.ANY)] * (2 * PLANES),
+        scratch_shapes=[pltpu.SemaphoreType.DMA((10 * PLANES,))],
         out_specs=[
             pl.BlockSpec((1, keys, rows), lambda i: (i, 0, 0)),
             pl.BlockSpec((rows, HD), lambda i: (i, 0)),
@@ -403,6 +414,21 @@
     )(*blocks)
 
 
+def hold_kernel(*refs):
+    n = len(refs) // 2
+    for in_ref, out_ref in zip(refs[:n], refs[n:]):
+        out_ref[...] = in_ref[...]
+
+
+def hold(blocks):
+    return pl.pallas_call(
+        hold_kernel,
+        out_shape=[pltpu.VMEM(block.shape, block.dtype) for block in blocks],
+        cost_estimate=SMALL,
+        name="hold",
+    )(*blocks)
+
+
 def fence_kernel(in_ref, out_ref):
     del in_ref, out_ref
 
@@ -463,7 +489,8 @@
     pieces = pack(*after((queries, keys_tile, values_tile), fence0(queries)))
     pieces = after(pieces, weights[1])
     moved = after([to_col(pieces[j], j) for j in (1, 2, 3)], fence(pieces))
-    over_col = jnp.stack([pieces[0], *moved])
+    weights = hold(weights)
+    over_col = jnp.stack([pieces[0], *after(moved, weights)])
 
     arrived = [pick(over_col, col ^ plane)]
     for s in ORDER[1:]:

time: 147 us -> 147 us (level)
  waiting for transfers between devices: 64.7 us -> 60.9 us
  Pallas kernels: 34.3 us -> 36.5 us
    pallas_call x1 -> x2, Pallas kernels: 6.95 us -> 9.18 us  [the longest x1 7.36 us: attention_forward(): pl.pallas_call(forward_kernel, grid=(3,), in_specs=[pl.BlockSpec(memory_s...]
    ppermute x17, waiting for transfers between devices: 34.9 us -> 32.8 us  [to_col(): return lax.ppermute(block, 'col', col_xor(j))]
    ppermute x12, waiting for transfers between devices: 26.4 us -> 24.7 us  [to_plane(): return lax.ppermute(block, 'row', row_shift(s))]
  transfers between devices with their start and end apart: 39 -> 39, of which waited for: 20 -> 20; matrix products, arithmetic and copies ran while one was open for 4% -> 5% of each run, Pallas kernels for 23% -> 25%
where the time goes in v8:
time: 147 us
  waiting for transfers between devices  60.9 us (41%)
  starting transfers between devices  37.7 us (26%)
  Pallas kernels  36.5 us (25%)
  local copies, waits for them, and re-layouts  5.56 us (4%)
  other arithmetic  5.01 us (3%)
    ppermute x17, waiting for transfers between devices, to_col(): return lax.ppermute(block, 'col', col_xor(j))  32.8 us
    ppermute x12, waiting for transfers between devices, to_plane(): return lax.ppermute(block, 'row', row_shift(s))  24.7 us
    ppermute x17, starting transfers between devices, to_col(): return lax.ppermute(block, 'col', col_xor(j))  19.6 us
    ppermute x12, starting transfers between devices, to_plane(): return lax.ppermute(block, 'row', row_shift(s))  16.3 us
    pallas_call x1, Pallas kernels, attention_forward(): pl.pallas_call(forward_kernel, grid=(3,), in_specs=[pl.BlockSpec(memory_s...  7.36 us
    pallas_call x2, Pallas kernels, weight_grad_part(): pl.pallas_call(functools.partial(weight_grad_kernel, len(heads)), out_sha...  7.2 us
    pallas_call x2, Pallas kernels, grad_pieces(): pl.pallas_call(grad_kernel, out_shape=[piece] * COLS, scratch_shapes=[plt...  6.37 us
    pallas_call x1, Pallas kernels, attention_backward(): pl.pallas_call(backward_kernel, grid=(3,), in_specs=[by_query, by_head, b...  5.23 us
  transfers between devices with their start and end apart: 39, of which 20 were waited for; matrix products, arithmetic and copies ran while one was open for 5% of the time, Pallas kernels for 25%

profile of v8, /device:TPU:0, one launch (start us, length us, event | category | flops | bytes accessed | tf_op | source)
XLA Modules:
  0.0 146.8 jit_solution(1103298457107049930)
XLA Ops:
  0.6 3.1 %collective-permute-start.7 = (bf16[192,1536]{1,0:T(8,128)(2,1)}, bf16[192,1536]{1,0:T(8,128)(2,1)S(1)}, u32[]{:S(2)}, u32[]{:S(2)}) collective-permute-start(bf16[192,1536]{1,0:T(8,128)(2,1)} %refs_4_.3), channel_id=1, source_target_pairs={{0,8},{4,12},{8,16},{12,20},{16,24},{20,28},{24,0},{28,4},{1,9},{5... | collective-permute-start | bytes 1769480 | tf_op jit(solution)/shard_map/ppermute | solution.py:480
  3.7 2.1 %collective-permute-start.8 = (bf16[192,1536]{1,0:T(8,128)(2,1)}, bf16[192,1536]{1,0:T(8,128)(2,1)}, u32[]{:S(2)}, u32[]{:S(2)}) collective-permute-start(bf16[192,1536]{1,0:T(8,128)(2,1)} %refs_4_.3), channel_id=1, source_target_pairs={{0,24},{4,28},{8,0},{12,4},{16,8},{20,12},{24,16},{28,20},{1,25},{... | collective-permute-start | bytes 1769480 | tf_op jit(solution)/shard_map/ppermute | solution.py:480
  5.8 2.3 %pack_inputs.1 = (bf16[1056,128]{1,0:T(8,128)(2,1)}, bf16[1056,128]{1,0:T(8,128)(2,1)}, bf16[1056,128]{1,0:T(8,128)(2,1)}, bf16[1056,128]{1,0:T(8,128)(2,1)}) custom-call(bf16[192,768]{1,0:T(8,128)(2,1)} %q_ref, bf16[192,768]{1,0:T(8,128)(2,1)} %k_ref, bf16[192,768]{1,0:T(8,128)(2,1)} %v_ref), custom_call_target="tpu_custom_call" | custom-call | flops 40000000000 | tf_op jit(solution)/shard_map/pack_inputs/pallas_call | solution.py:293
  8.9 1.6 %collective-permute-start.1 = (bf16[1056,128]{1,0:T(8,128)(2,1)}, bf16[1056,128]{1,0:T(8,128)(2,1)}, u32[]{:S(2)}, u32[]{:S(2)}) collective-permute-start(bf16[1056,128]{1,0:T(8,128)(2,1)} %get-tuple-element.97), channel_id=1, source_target_pairs={{0,1},{1,0},{2,3},{3,2},{4,5},{5,4},{6,7},{7,6},{8,9},{9,8},{10,11... | collective-permute-start | bytes 811016 | tf_op jit(solution)/shard_map/ppermute | solution.py:477
  10.5 1.5 %collective-permute-start.2 = (bf16[1056,128]{1,0:T(8,128)(2,1)}, bf16[1056,128]{1,0:T(8,128)(2,1)}, u32[]{:S(2)}, u32[]{:S(2)}) collective-permute-start(bf16[1056,128]{1,0:T(8,128)(2,1)} %get-tuple-element.98), channel_id=1, source_target_pairs={{0,2},{1,3},{2,0},{3,1},{4,6},{5,7},{6,4},{7,5},{8,10},{9,11},{10,... | collective-permute-start | bytes 811016 | tf_op jit(solution)/shard_map/ppermute | solution.py:477
  12.9 1.8 %hold.1 = (bf16[384,1536]{1,0:T(8,128)(2,1)S(1)}, bf16[384,1536]{1,0:T(8,128)(2,1)S(1)}) custom-call(bf16[384,1536]{1,0:T(8,128)(2,1)} %refs_0_.2, bf16[384,1536]{1,0:T(8,128)(2,1)} %copy-done.5), custom_call_target="tpu_custom_call" | custom-call | flops 1000000 | bytes 1000 | tf_op jit(solution)/shard_map/hold/pallas_call | solution.py:424
  14.8 3.7 %collective-permute-done.1 = bf16[1056,128]{1,0:T(8,128)(2,1)} collective-permute-done((bf16[1056,128]{1,0:T(8,128)(2,1)}, bf16[1056,128]{1,0:T(8,128)(2,1)}, u32[]{:S(2)}, u32[]{:S(2)}) %collective-permute-start.1) | collective-permute-done | bytes 270368 | tf_op jit(solution)/shard_map/ppermute | solution.py:477
  18.5 6.4 %collective-permute-done.2 = bf16[1056,128]{1,0:T(8,128)(2,1)} collective-permute-done((bf16[1056,128]{1,0:T(8,128)(2,1)}, bf16[1056,128]{1,0:T(8,128)(2,1)}, u32[]{:S(2)}, u32[]{:S(2)}) %collective-permute-start.2) | collective-permute-done | bytes 270368 | tf_op jit(solution)/shard_map/ppermute | solution.py:477
  27.0 3.8 %collective-permute-start.5 = (bf16[1056,128]{1,0:T(8,128)(2,1)}, bf16[1056,128]{1,0:T(8,128)(2,1)}, u32[]{:S(2)}, u32[]{:S(2)}) collective-permute-start(bf16[1056,128]{1,0:T(8,128)(2,1)} %get-tuple-element.178), channel_id=1, source_target_pairs={{0,24},{4,28},{8,0},{12,4},{16,8},{20,12},{24,16},{28,20},{1,25},{... | collective-permute-start | bytes 811016 | tf_op jit(solution)/shard_map/ppermute | solution.py:480
  30.8 2.2 %collective-permute-done.8.refs_2_.refs_6_ = bf16[192,1536]{1,0:T(8,128)(2,1)} collective-permute-done((bf16[192,1536]{1,0:T(8,128)(2,1)}, bf16[192,1536]{1,0:T(8,128)(2,1)}, u32[]{:S(2)}, u32[]{:S(2)}) %collective-permute-start.8) | collective-permute-done | bytes 589856 | tf_op jit(solution)/shard_map/ppermute | solution.py:480
  33.1 4.4 %grad_pieces.2 = (bf16[864,128]{1,0:T(8,128)(2,1)S(1)}, bf16[864,128]{1,0:T(8,128)(2,1)}, bf16[864,128]{1,0:T(8,128)(2,1)}, bf16[864,128]{1,0:T(8,128)(2,1)}) custom-call(bf16[192,1536]{1,0:T(8,128)(2,1)S(1)} %copy-done, bf16[192,1536]{1,0:T(8,128)(2,1)S(1)} %collective-permute-done.7.refs_1_.refs_5_, ...), custom_call_target="tpu_custom_call" | custom-call | flops 40000000000 | tf_op jit(solution)/shard_map/grad_pieces/pallas_call | solution.py:325
  38.7 1.8 %collective-permute-start.10 = (bf16[864,128]{1,0:T(8,128)(2,1)}, bf16[864,128]{1,0:T(8,128)(2,1)}, u32[]{:S(2)}, u32[]{:S(2)}) collective-permute-start(bf16[864,128]{1,0:T(8,128)(2,1)} %get-tuple-element.114), channel_id=1, source_target_pairs={{0,2},{1,3},{2,0},{3,1},{4,6},{5,7},{6,4},{7,5},{8,10},{9,11},{10,... | collective-permute-start | bytes 663560 | tf_op jit(solution)/shard_map/ppermute | solution.py:477
  43.0 12.1 %collective-permute-done.6.refs_3_ = bf16[1056,128]{1,0:T(8,128)(2,1)} collective-permute-done((bf16[1056,128]{1,0:T(8,128)(2,1)}, bf16[1056,128]{1,0:T(8,128)(2,1)}, u32[]{:S(2)}, u32[]{:S(2)}) %collective-permute-start.6) | collective-permute-done | bytes 270368 | tf_op jit(solution)/shard_map/ppermute | solution.py:480
  57.9 7.4 %attention_forward.1 = (bf16[3,1536,384]{2,1,0:T(8,128)(2,1)}, bf16[1152,128]{1,0:T(8,128)(2,1)S(1)}, bf16[1152,128]{1,0:T(8,128)(2,1)S(1)}, bf16[2,1536,128]{2,1,0:T(8,128)(2,1)S(1)}, bf16[2,1536,128]{2,1,0:T(8,128)(2,1)S(1)}) custom-call(bf16[1056,128]{1,0:T(8,128)(2,1)S(1)} %get-tuple-element.116.refs_0_, ...), custom_call_target="tpu_custom_call" | custom-call | flops 40000000000 | tf_op jit(solution)/shard_map/attention_forward/pallas_call | solution.py:177
  65.3 1.6 %collective-permute-start.18 = (bf16[288,128]{1,0:T(8,128)(2,1)S(1)}, bf16[288,128]{1,0:T(8,128)(2,1)S(1)}, u32[]{:S(2)}, u32[]{:S(2)}) collective-permute-start(bf16[288,128]{1,0:T(8,128)(2,1)S(1)} %get-tuple-element.231), channel_id=1, source_target_pairs={{0,1},{1,0},{2,3},{3,2},{4,5},{5,4},{6,7},{7,6},{8,9},{9,8},{10,11... | collective-permute-start | bytes 221192 | tf_op jit(solution)/shard_map/ppermute | solution.py:477
  68.9 1.6 %collective-permute-start.16 = (bf16[864,128]{1,0:T(8,128)(2,1)S(1)}, bf16[864,128]{1,0:T(8,128)(2,1)S(1)}, u32[]{:S(2)}, u32[]{:S(2)}) collective-permute-start(bf16[864,128]{1,0:T(8,128)(2,1)S(1)} %get-tuple-element.229), channel_id=1, source_target_pairs={{0,1},{1,0},{2,3},{3,2},{4,5},{5,4},{6,7},{7,6},{8,9},{9,8},{10,11... | collective-permute-start | bytes 663560 | tf_op jit(solution)/shard_map/ppermute | solution.py:477
  72.3 2.0 %grad_pieces.3 = (bf16[288,128]{1,0:T(8,128)(2,1)S(1)}, bf16[288,128]{1,0:T(8,128)(2,1)S(1)}, bf16[288,128]{1,0:T(8,128)(2,1)S(1)}, bf16[288,128]{1,0:T(8,128)(2,1)S(1)}) custom-call(bf16[192,1536]{1,0:T(8,128)(2,1)} %collective-permute-done.21.refs_0_.refs_7_, bf16[384,1536]{1,0:T(8,128)(2,1)S(1)} %get-tuple-element.104.refs_3_.refs_1_.own_ref, ...), custom_call_target="tpu_custom_call" | custom-call | flops 40000000000 | tf_op jit(solution)/shard_map/grad_pieces/pallas_call | solution.py:325
  74.4 1.6 %collective-permute-start.23 = (bf16[288,128]{1,0:T(8,128)(2,1)S(1)}, bf16[288,128]{1,0:T(8,128)(2,1)S(1)}, u32[]{:S(2)}, u32[]{:S(2)}) collective-permute-start(bf16[288,128]{1,0:T(8,128)(2,1)S(1)} %get-tuple-element.129), channel_id=1, source_target_pairs={{0,1},{1,0},{2,3},{3,2},{4,5},{5,4},{6,7},{7,6},{8,9},{9,8},{10,11... | collective-permute-start | bytes 221192 | tf_op jit(solution)/shard_map/ppermute | solution.py:477
  75.9 1.5 %collective-permute-start.24 = (bf16[288,128]{1,0:T(8,128)(2,1)S(1)}, bf16[288,128]{1,0:T(8,128)(2,1)S(1)}, u32[]{:S(2)}, u32[]{:S(2)}) collective-permute-start(bf16[288,128]{1,0:T(8,128)(2,1)S(1)} %get-tuple-element.130), channel_id=1, source_target_pairs={{0,2},{1,3},{2,0},{3,1},{4,6},{5,7},{6,4},{7,5},{8,10},{9,11},{10,... | collective-permute-start | bytes 221192 | tf_op jit(solution)/shard_map/ppermute | solution.py:477
  79.1 2.0 %collective-permute-done.24.refs_3_ = bf16[288,128]{1,0:T(8,128)(2,1)S(1)} collective-permute-done((bf16[288,128]{1,0:T(8,128)(2,1)S(1)}, bf16[288,128]{1,0:T(8,128)(2,1)S(1)}, u32[]{:S(2)}, u32[]{:S(2)}) %collective-permute-start.24) | collective-permute-done | bytes 73760 | tf_op jit(solution)/shard_map/ppermute | solution.py:477
  81.1 1.6 %collective-permute-done.25.refs_4_ = bf16[288,128]{1,0:T(8,128)(2,1)S(1)} collective-permute-done((bf16[288,128]{1,0:T(8,128)(2,1)S(1)}, bf16[288,128]{1,0:T(8,128)(2,1)S(1)}, u32[]{:S(2)}, u32[]{:S(2)}) %collective-permute-start.25) | collective-permute-done | bytes 73760 | tf_op jit(solution)/shard_map/ppermute | solution.py:477
  82.7 5.2 %attention_backward.1 = (bf16[1152,128]{1,0:T(8,128)(2,1)S(1)}, f32[2,2,768,128]{3,2,1,0:T(8,128)S(1)}, bf16[2,2,768,128]{3,2,1,0:T(8,128)(2,1)S(1)}) custom-call(bf16[1152,128]{1,0:T(8,128)(2,1)S(1)} %get-tuple-element.135.q_ref, bf16[2,1536,128]{2,1,0:T(8,128)(2,1)S(1)} %get-tuple-element.136.k_ref, bf16[2,1536,128]{2,1,0:T(8,128)(2,1)S(1)} %get-tuple-element.137.v_ref, ...), custom_call_target="tpu_custom_call" | custom-call | flops 40000000000 | tf_op jit(solution)/shard_map/attention_backward/pallas_call | solution.py:250
  90.7 2.3 %collective-permute-start.30 = (bf16[1056,128]{1,0:T(8,128)(2,1)S(1)}, bf16[1056,128]{1,0:T(8,128)(2,1)S(1)}, u32[]{:S(2)}, u32[]{:S(2)}) collective-permute-start(bf16[1056,128]{1,0:T(8,128)(2,1)S(1)} %get-tuple-element.190), channel_id=1, source_target_pairs={{0,24},{4,28},{8,0},{12,4},{16,8},{20,12},{24,16},{28,20},{1,25},{... | collective-permute-start | bytes 811016 | tf_op jit(solution)/shard_map/ppermute | solution.py:480
  94.1 7.6 %collective-permute-done.17 = bf16[2,864,128]{2,1,0:T(8,128)(2,1)S(1)} collective-permute-done((bf16[2,864,128]{2,1,0:T(8,128)(2,1)S(1)}, bf16[2,864,128]{2,1,0:T(8,128)(2,1)S(1)}, u32[]{:S(2)}, u32[]{:S(2)}) %collective-permute-start.17) | collective-permute-done | bytes 442400 | tf_op jit(solution)/shard_map/ppermute | solution.py:477
  103.3 3.1 %weight_grad.2 = bf16[384,1536]{1,0:T(8,128)(2,1)S(1)} custom-call(bf16[192,384]{1,0:T(8,128)(2,1)S(1)} %get-tuple-element.148.refs_0_, bf16[192,384]{1,0:T(8,128)(2,1)S(1)} %get-tuple-element.149.refs_1_, bf16[192,384]{1,0:T(8,128)(2,1)S(1)} %get-tuple-element.150.refs_2_, bf16[192,384]{1,0:T(8,128)(2,1)S(1)} %get-tuple-element.151.refs_3_, ...), custom_call_target="tpu_custom_call" | custom-call | flops 40000000000 | tf_op jit(solution)/shard_map/weight_grad/pallas_call | solution.py:369
  107.3 1.6 %mixed_term.5 = bf16[192,1536]{1,0:T(8,128)(2,1)} custom-call(bf16[192,768]{1,0:T(8,128)(2,1)S(1)} %get-tuple-element.153.block_ref, bf16[384,1536]{1,0:T(8,128)(2,1)S(1)} %get-tuple-element.104.refs_3_.refs_1_.own_ref, bf16[384,1536]{1,0:T(8,128)(2,1)S(1)} %get-tuple-element.105.refs_4_.refs_2_.other_ref), custom_call_target="tpu_custom_call" | custom-call | flops 1000000 | bytes 1000 | tf_op jit(solution)/shard_map/mixed_term/pallas_call | solution.py:348
  110.6 6.9 %collective-permute-done.31 = bf16[1056,128]{1,0:T(8,128)(2,1)S(1)} collective-permute-done((bf16[1056,128]{1,0:T(8,128)(2,1)S(1)}, bf16[1056,128]{1,0:T(8,128)(2,1)S(1)}, u32[]{:S(2)}, u32[]{:S(2)}) %collective-permute-start.31) | collective-permute-done | bytes 270368 | tf_op jit(solution)/shard_map/ppermute | solution.py:480
  117.5 3.8 %collective-permute-start.34 = (bf16[192,1536]{1,0:T(8,128)(2,1)}, bf16[192,1536]{1,0:T(8,128)(2,1)S(1)}, u32[]{:S(2)}, u32[]{:S(2)}) collective-permute-start(bf16[192,1536]{1,0:T(8,128)(2,1)} %mixed_term.5), channel_id=1, source_target_pairs={{0,24},{4,28},{8,0},{12,4},{16,8},{20,12},{24,16},{28,20},{1,25},{... | collective-permute-start | bytes 1769480 | tf_op jit(solution)/shard_map/ppermute | solution.py:480
  121.4 4.1 %weight_grad.3 = bf16[384,1536]{1,0:T(8,128)(2,1)} custom-call(bf16[192,384]{1,0:T(8,128)(2,1)S(1)} %get-tuple-element.162.refs_0_, bf16[192,384]{1,0:T(8,128)(2,1)S(1)} %get-tuple-element.163.refs_1_, bf16[192,384]{1,0:T(8,128)(2,1)S(1)} %get-tuple-element.164.refs_2_, bf16[192,384]{1,0:T(8,128)(2,1)S(1)} %get-tuple-element.165.refs_3_, ...), custom_call_target="tpu_custom_call" | custom-call | flops 40000000000 | tf_op jit(solution)/shard_map/weight_grad/pallas_call | solution.py:369
  129.9 5.9 %collective-permute-done.36.refs_1_ = bf16[1056,128]{1,0:T(8,128)(2,1)S(1)} collective-permute-done((bf16[1056,128]{1,0:T(8,128)(2,1)S(1)}, bf16[1056,128]{1,0:T(8,128)(2,1)S(1)}, u32[]{:S(2)}, u32[]{:S(2)}) %collective-permute-start.36) | collective-permute-done | bytes 270368 | tf_op jit(solution)/shard_map/ppermute | solution.py:477
  135.8 5.5 %collective-permute-done.37.refs_2_ = bf16[1056,128]{1,0:T(8,128)(2,1)S(1)} collective-permute-done((bf16[1056,128]{1,0:T(8,128)(2,1)S(1)}, bf16[1056,128]{1,0:T(8,128)(2,1)S(1)}, u32[]{:S(2)}, u32[]{:S(2)}) %collective-permute-start.37) | collective-permute-done | bytes 270368 | tf_op jit(solution)/shard_map/ppermute | solution.py:477
  142.8 2.3 %unpack_outputs.1 = (bf16[192,768]{1,0:T(8,128)(2,1)}, bf16[192,768]{1,0:T(8,128)(2,1)}, bf16[192,768]{1,0:T(8,128)(2,1)}) custom-call(bf16[1056,128]{1,0:T(8,128)(2,1)} %get-tuple-element.176.refs_0_, bf16[1056,128]{1,0:T(8,128)(2,1)} %copy-done.7, bf16[1056,128]{1,0:T(8,128)(2,1)} %copy-done.8, bf16[1056,128]{1,0:T(8,128)(2,1)} %copy-done.9), custom_call_target="tpu_custom_call" | custom-call | flops 1000000 | bytes 1000 | tf_op jit(solution)/shard_map/unpack_outputs/pallas_call | solution.py:409
  (130 shorter events, 31.2 us)
Async XLA Ops:
  0.6 30.2 %collective-permute-start.7 = (bf16[192,1536]{1,0:T(8,128)(2,1)}, bf16[192,1536]{1,0:T(8,128)(2,1)S(1)}, u32[]{:S(2)}, u32[]{:S(2)}) collective-permute-start(bf16[192,1536]{1,0:T(8,128)(2,1)} %refs_4_.3), channel_id=1, source_target_pairs={{0,8},{4,12},{8,16},{12,20},{16,24},{20,28},{24,0},{28,4},{1,9},{5... | collective-permute-start | bytes 1769480 | tf_op jit(solution)/shard_map/ppermute | solution.py:480
  3.7 29.3 %collective-permute-start.8 = (bf16[192,1536]{1,0:T(8,128)(2,1)}, bf16[192,1536]{1,0:T(8,128)(2,1)}, u32[]{:S(2)}, u32[]{:S(2)}) collective-permute-start(bf16[192,1536]{1,0:T(8,128)(2,1)} %refs_4_.3), channel_id=1, source_target_pairs={{0,24},{4,28},{8,0},{12,4},{16,8},{20,12},{24,16},{28,20},{1,25},{... | collective-permute-start | bytes 1769480 | tf_op jit(solution)/shard_map/ppermute | solution.py:480
  5.8 3.1 %collective-permute-start = (bf16[384,1536]{1,0:T(8,128)(2,1)}, bf16[384,1536]{1,0:T(8,128)(2,1)S(1)}, u32[]{:S(2)}, u32[]{:S(2)}) collective-permute-start(bf16[384,1536]{1,0:T(8,128)(2,1)} %refs_0_.2), channel_id=1, source_target_pairs={{0,4},{4,0},{8,12},{12,8},{16,20},{20,16},{24,28},{28,24},{1,5},{5... | collective-permute-start | bytes 3538952 | tf_op jit(solution)/shard_map/ppermute | solution.py:483
  8.9 9.6 %collective-permute-start.1 = (bf16[1056,128]{1,0:T(8,128)(2,1)}, bf16[1056,128]{1,0:T(8,128)(2,1)}, u32[]{:S(2)}, u32[]{:S(2)}) collective-permute-start(bf16[1056,128]{1,0:T(8,128)(2,1)} %get-tuple-element.97), channel_id=1, source_target_pairs={{0,1},{1,0},{2,3},{3,2},{4,5},{5,4},{6,7},{7,6},{8,9},{9,8},{10,11... | collective-permute-start | bytes 811016 | tf_op jit(solution)/shard_map/ppermute | solution.py:477
  10.5 14.4 %collective-permute-start.2 = (bf16[1056,128]{1,0:T(8,128)(2,1)}, bf16[1056,128]{1,0:T(8,128)(2,1)}, u32[]{:S(2)}, u32[]{:S(2)}) collective-permute-start(bf16[1056,128]{1,0:T(8,128)(2,1)} %get-tuple-element.98), channel_id=1, source_target_pairs={{0,2},{1,3},{2,0},{3,1},{4,6},{5,7},{6,4},{7,5},{8,10},{9,11},{10,... | collective-permute-start | bytes 811016 | tf_op jit(solution)/shard_map/ppermute | solution.py:477
  12.0 12.8 %collective-permute-start.3 = (bf16[1056,128]{1,0:T(8,128)(2,1)}, bf16[1056,128]{1,0:T(8,128)(2,1)}, u32[]{:S(2)}, u32[]{:S(2)}) collective-permute-start(bf16[1056,128]{1,0:T(8,128)(2,1)} %get-tuple-element.99), channel_id=1, source_target_pairs={{0,3},{1,2},{2,1},{3,0},{4,7},{5,6},{6,5},{7,4},{8,11},{9,10},{10,... | collective-permute-start | bytes 811016 | tf_op jit(solution)/shard_map/ppermute | solution.py:477
  27.0 11.7 %collective-permute-start.4 = (bf16[1056,128]{1,0:T(8,128)(2,1)S(1)}, bf16[1056,128]{1,0:T(8,128)(2,1)}, u32[]{:S(2)}, u32[]{:S(2)}) collective-permute-start(bf16[1056,128]{1,0:T(8,128)(2,1)S(1)} %get-tuple-element.179), channel_id=1, source_target_pairs={{0,8},{4,12},{8,16},{12,20},{16,24},{20,28},{24,0},{28,4},{1,9},{5... | collective-permute-start | bytes 811016 | tf_op jit(solution)/shard_map/ppermute | solution.py:480
  27.0 16.0 %collective-permute-start.5 = (bf16[1056,128]{1,0:T(8,128)(2,1)}, bf16[1056,128]{1,0:T(8,128)(2,1)}, u32[]{:S(2)}, u32[]{:S(2)}) collective-permute-start(bf16[1056,128]{1,0:T(8,128)(2,1)} %get-tuple-element.178), channel_id=1, source_target_pairs={{0,24},{4,28},{8,0},{12,4},{16,8},{20,12},{24,16},{28,20},{1,25},{... | collective-permute-start | bytes 811016 | tf_op jit(solution)/shard_map/ppermute | solution.py:480
  30.8 24.4 %collective-permute-start.6 = (bf16[1056,128]{1,0:T(8,128)(2,1)}, bf16[1056,128]{1,0:T(8,128)(2,1)}, u32[]{:S(2)}, u32[]{:S(2)}) collective-permute-start(bf16[1056,128]{1,0:T(8,128)(2,1)} %get-tuple-element.177), channel_id=1, source_target_pairs={{0,16},{4,20},{8,24},{12,28},{16,0},{20,4},{24,8},{28,12},{1,17},{... | collective-permute-start | bytes 811016 | tf_op jit(solution)/shard_map/ppermute | solution.py:480
  38.7 16.5 %collective-permute-start.10 = (bf16[864,128]{1,0:T(8,128)(2,1)}, bf16[864,128]{1,0:T(8,128)(2,1)}, u32[]{:S(2)}, u32[]{:S(2)}) collective-permute-start(bf16[864,128]{1,0:T(8,128)(2,1)} %get-tuple-element.114), channel_id=1, source_target_pairs={{0,2},{1,3},{2,0},{3,1},{4,6},{5,7},{6,4},{7,5},{8,10},{9,11},{10,... | collective-permute-start | bytes 663560 | tf_op jit(solution)/shard_map/ppermute | solution.py:477
  40.5 14.7 %collective-permute-start.11 = (bf16[864,128]{1,0:T(8,128)(2,1)}, bf16[864,128]{1,0:T(8,128)(2,1)}, u32[]{:S(2)}, u32[]{:S(2)}) collective-permute-start(bf16[864,128]{1,0:T(8,128)(2,1)} %get-tuple-element.115), channel_id=1, source_target_pairs={{0,3},{1,2},{2,1},{3,0},{4,7},{5,6},{6,5},{7,4},{8,11},{9,10},{10,... | collective-permute-start | bytes 663560 | tf_op jit(solution)/shard_map/ppermute | solution.py:477
  41.9 13.8 %collective-permute-start.9 = (bf16[864,128]{1,0:T(8,128)(2,1)}, bf16[864,128]{1,0:T(8,128)(2,1)}, u32[]{:S(2)}, u32[]{:S(2)}) collective-permute-start(bf16[864,128]{1,0:T(8,128)(2,1)} %get-tuple-element.113), channel_id=1, source_target_pairs={{0,1},{1,0},{2,3},{3,2},{4,5},{5,4},{6,7},{7,6},{8,9},{9,8},{10,11... | collective-permute-start | bytes 663560 | tf_op jit(solution)/shard_map/ppermute | solution.py:477
  43.0 12.8 %collective-permute-start.12 = (bf16[1056,128]{1,0:T(8,128)(2,1)S(1)}, bf16[1056,128]{1,0:T(8,128)(2,1)}, u32[]{:S(2)}, u32[]{:S(2)}) collective-permute-start(bf16[1056,128]{1,0:T(8,128)(2,1)S(1)} %get-tuple-element.116.refs_0_), channel_id=1, source_target_pairs={{0,4},{4,0},{8,12},{12,8},{16,20},{20,16},{24,28},{28,24},{1,5},{5... | collective-permute-start | bytes 811016 | tf_op jit(solution)/shard_map/ppermute | solution.py:483
  55.2 17.2 %collective-permute-start.21 = (bf16[192,1536]{1,0:T(8,128)(2,1)S(1)}, bf16[192,1536]{1,0:T(8,128)(2,1)}, u32[]{:S(2)}, u32[]{:S(2)}) collective-permute-start(bf16[192,1536]{1,0:T(8,128)(2,1)S(1)} %collective-permute-done.7.refs_1_.refs_5_), channel_id=1, source_target_pairs={{0,8},{4,12},{8,16},{12,20},{16,24},{20,28},{24,0},{28,4},{1,9},{5... | collective-permute-start | bytes 1769480 | tf_op jit(solution)/shard_map/ppermute | solution.py:480
  65.3 10.6 %collective-permute-start.18 = (bf16[288,128]{1,0:T(8,128)(2,1)S(1)}, bf16[288,128]{1,0:T(8,128)(2,1)S(1)}, u32[]{:S(2)}, u32[]{:S(2)}) collective-permute-start(bf16[288,128]{1,0:T(8,128)(2,1)S(1)} %get-tuple-element.231), channel_id=1, source_target_pairs={{0,1},{1,0},{2,3},{3,2},{4,5},{5,4},{6,7},{7,6},{8,9},{9,8},{10,11... | collective-permute-start | bytes 221192 | tf_op jit(solution)/shard_map/ppermute | solution.py:477
  66.8 10.6 %collective-permute-start.19 = (bf16[288,128]{1,0:T(8,128)(2,1)S(1)}, bf16[288,128]{1,0:T(8,128)(2,1)S(1)}, u32[]{:S(2)}, u32[]{:S(2)}) collective-permute-start(bf16[288,128]{1,0:T(8,128)(2,1)S(1)} %get-tuple-element.231), channel_id=1, source_target_pairs={{0,2},{1,3},{2,0},{3,1},{4,6},{5,7},{6,4},{7,5},{8,10},{9,11},{10,... | collective-permute-start | bytes 221192 | tf_op jit(solution)/shard_map/ppermute | solution.py:477
  68.3 9.6 %collective-permute-start.20 = (bf16[288,128]{1,0:T(8,128)(2,1)S(1)}, bf16[288,128]{1,0:T(8,128)(2,1)S(1)}, u32[]{:S(2)}, u32[]{:S(2)}) collective-permute-start(bf16[288,128]{1,0:T(8,128)(2,1)S(1)} %get-tuple-element.231), channel_id=1, source_target_pairs={{0,3},{1,2},{2,1},{3,0},{4,7},{5,6},{6,5},{7,4},{8,11},{9,10},{10,... | collective-permute-start | bytes 221192 | tf_op jit(solution)/shard_map/ppermute | solution.py:477
  68.9 19.8 %collective-permute-start.16 = (bf16[864,128]{1,0:T(8,128)(2,1)S(1)}, bf16[864,128]{1,0:T(8,128)(2,1)S(1)}, u32[]{:S(2)}, u32[]{:S(2)}) collective-permute-start(bf16[864,128]{1,0:T(8,128)(2,1)S(1)} %get-tuple-element.229), channel_id=1, source_target_pairs={{0,1},{1,0},{2,3},{3,2},{4,5},{5,4},{6,7},{7,6},{8,9},{9,8},{10,11... | collective-permute-start | bytes 663560 | tf_op jit(solution)/shard_map/ppermute | solution.py:477
  74.4 4.7 %collective-permute-start.23 = (bf16[288,128]{1,0:T(8,128)(2,1)S(1)}, bf16[288,128]{1,0:T(8,128)(2,1)S(1)}, u32[]{:S(2)}, u32[]{:S(2)}) collective-permute-start(bf16[288,128]{1,0:T(8,128)(2,1)S(1)} %get-tuple-element.129), channel_id=1, source_target_pairs={{0,1},{1,0},{2,3},{3,2},{4,5},{5,4},{6,7},{7,6},{8,9},{9,8},{10,11... | collective-permute-start | bytes 221192 | tf_op jit(solution)/shard_map/ppermute | solution.py:477
  75.9 5.1 %collective-permute-start.24 = (bf16[288,128]{1,0:T(8,128)(2,1)S(1)}, bf16[288,128]{1,0:T(8,128)(2,1)S(1)}, u32[]{:S(2)}, u32[]{:S(2)}) collective-permute-start(bf16[288,128]{1,0:T(8,128)(2,1)S(1)} %get-tuple-element.130), channel_id=1, source_target_pairs={{0,2},{1,3},{2,0},{3,1},{4,6},{5,7},{6,4},{7,5},{8,10},{9,11},{10,... | collective-permute-start | bytes 221192 | tf_op jit(solution)/shard_map/ppermute | solution.py:477
  77.4 5.3 %collective-permute-start.25 = (bf16[288,128]{1,0:T(8,128)(2,1)S(1)}, bf16[288,128]{1,0:T(8,128)(2,1)S(1)}, u32[]{:S(2)}, u32[]{:S(2)}) collective-permute-start(bf16[288,128]{1,0:T(8,128)(2,1)S(1)} %get-tuple-element.131), channel_id=1, source_target_pairs={{0,3},{1,2},{2,1},{3,0},{4,7},{5,6},{6,5},{7,4},{8,11},{9,10},{10,... | collective-permute-start | bytes 221192 | tf_op jit(solution)/shard_map/ppermute | solution.py:477
  78.9 22.8 %collective-permute-start.22 = (bf16[192,1536]{1,0:T(8,128)(2,1)S(1)}, bf16[192,1536]{1,0:T(8,128)(2,1)S(1)}, u32[]{:S(2)}, u32[]{:S(2)}) collective-permute-start(bf16[192,1536]{1,0:T(8,128)(2,1)S(1)} %mixed_term.4), channel_id=1, source_target_pairs={{0,8},{4,12},{8,16},{12,20},{16,24},{20,28},{24,0},{28,4},{1,9},{5... | collective-permute-start | bytes 1769480 | tf_op jit(solution)/shard_map/ppermute | solution.py:480
  89.5 12.2 %collective-permute-start.17 = (bf16[2,864,128]{2,1,0:T(8,128)(2,1)S(1)}, bf16[2,864,128]{2,1,0:T(8,128)(2,1)S(1)}, u32[]{:S(2)}, u32[]{:S(2)}) collective-permute-start(bf16[2,864,128]{2,1,0:T(8,128)(2,1)S(1)} %pad_maximum_fusion.2), channel_id=1, source_target_pairs={{0,2},{1,3},{2,0},{3,1},{4,6},{5,7},{6,4},{7,5},{8,10},{9,11},{10,... | collective-permute-start | bytes 1327112 | tf_op jit(solution)/shard_map/ppermute | solution.py:477
  90.7 19.9 %collective-permute-start.30 = (bf16[1056,128]{1,0:T(8,128)(2,1)S(1)}, bf16[1056,128]{1,0:T(8,128)(2,1)S(1)}, u32[]{:S(2)}, u32[]{:S(2)}) collective-permute-start(bf16[1056,128]{1,0:T(8,128)(2,1)S(1)} %get-tuple-element.190), channel_id=1, source_target_pairs={{0,24},{4,28},{8,0},{12,4},{16,8},{20,12},{24,16},{28,20},{1,25},{... | collective-permute-start | bytes 811016 | tf_op jit(solution)/shard_map/ppermute | solution.py:480
  93.0 24.5 %collective-permute-start.31 = (bf16[1056,128]{1,0:T(8,128)(2,1)S(1)}, bf16[1056,128]{1,0:T(8,128)(2,1)S(1)}, u32[]{:S(2)}, u32[]{:S(2)}) collective-permute-start(bf16[1056,128]{1,0:T(8,128)(2,1)S(1)} %get-tuple-element.189), channel_id=1, source_target_pairs={{0,16},{4,20},{8,24},{12,28},{16,0},{20,4},{24,8},{28,12},{1,17},{... | collective-permute-start | bytes 811016 | tf_op jit(solution)/shard_map/ppermute | solution.py:480
  93.0 24.5 %collective-permute-start.32 = (bf16[1056,128]{1,0:T(8,128)(2,1)S(1)}, bf16[1056,128]{1,0:T(8,128)(2,1)S(1)}, u32[]{:S(2)}, u32[]{:S(2)}) collective-permute-start(bf16[1056,128]{1,0:T(8,128)(2,1)S(1)} %get-tuple-element.188), channel_id=1, source_target_pairs={{0,8},{4,12},{8,16},{12,20},{16,24},{20,28},{24,0},{28,4},{1,9},{5... | collective-permute-start | bytes 811016 | tf_op jit(solution)/shard_map/ppermute | solution.py:480
  106.4 11.1 %collective-permute-start.33 = (bf16[384,1536]{1,0:T(8,128)(2,1)S(1)}, bf16[384,1536]{1,0:T(8,128)(2,1)S(1)}, u32[]{:S(2)}, u32[]{:S(2)}) collective-permute-start(bf16[384,1536]{1,0:T(8,128)(2,1)S(1)} %weight_grad.2), channel_id=1, source_target_pairs={{0,4},{4,0},{8,12},{12,8},{16,20},{20,16},{24,28},{28,24},{1,5},{5... | collective-permute-start | bytes 3538952 | tf_op jit(solution)/shard_map/ppermute | solution.py:483
  117.5 27.5 %collective-permute-start.35 = (bf16[192,1536]{1,0:T(8,128)(2,1)}, bf16[192,1536]{1,0:T(8,128)(2,1)S(1)}, u32[]{:S(2)}, u32[]{:S(2)}) collective-permute-start(bf16[192,1536]{1,0:T(8,128)(2,1)} %add_convert_fusion.2), channel_id=1, source_target_pairs={{0,8},{4,12},{8,16},{12,20},{16,24},{20,28},{24,0},{28,4},{1,9},{5... | collective-permute-start | bytes 1769480 | tf_op jit(solution)/shard_map/ppermute | solution.py:480
  117.5 28.2 %collective-permute-start.34 = (bf16[192,1536]{1,0:T(8,128)(2,1)}, bf16[192,1536]{1,0:T(8,128)(2,1)S(1)}, u32[]{:S(2)}, u32[]{:S(2)}) collective-permute-start(bf16[192,1536]{1,0:T(8,128)(2,1)} %mixed_term.5), channel_id=1, source_target_pairs={{0,24},{4,28},{8,0},{12,4},{16,8},{20,12},{24,16},{28,20},{1,25},{... | collective-permute-start | bytes 1769480 | tf_op jit(solution)/shard_map/ppermute | solution.py:480
  126.4 9.4 %collective-permute-start.36 = (bf16[1056,128]{1,0:T(8,128)(2,1)S(1)}, bf16[1056,128]{1,0:T(8,128)(2,1)S(1)}, u32[]{:S(2)}, u32[]{:S(2)}) collective-permute-start(bf16[1056,128]{1,0:T(8,128)(2,1)S(1)} %get-tuple-element.175), channel_id=1, source_target_pairs={{0,1},{1,0},{2,3},{3,2},{4,5},{5,4},{6,7},{7,6},{8,9},{9,8},{10,11... | collective-permute-start | bytes 811016 | tf_op jit(solution)/shard_map/ppermute | solution.py:477
  127.9 13.4 %collective-permute-start.37 = (bf16[1056,128]{1,0:T(8,128)(2,1)S(1)}, bf16[1056,128]{1,0:T(8,128)(2,1)S(1)}, u32[]{:S(2)}, u32[]{:S(2)}) collective-permute-start(bf16[1056,128]{1,0:T(8,128)(2,1)S(1)} %get-tuple-element.174), channel_id=1, source_target_pairs={{0,2},{1,3},{2,0},{3,1},{4,6},{5,7},{6,4},{7,5},{8,10},{9,11},{10,... | collective-permute-start | bytes 811016 | tf_op jit(solution)/shard_map/ppermute | solution.py:477
  129.4 11.9 %collective-permute-start.38 = (bf16[1056,128]{1,0:T(8,128)(2,1)S(1)}, bf16[1056,128]{1,0:T(8,128)(2,1)S(1)}, u32[]{:S(2)}, u32[]{:S(2)}) collective-permute-start(bf16[1056,128]{1,0:T(8,128)(2,1)S(1)} %get-tuple-element.173), channel_id=1, source_target_pairs={{0,3},{1,2},{2,1},{3,0},{4,7},{5,6},{6,5},{7,4},{8,11},{9,10},{10,... | collective-permute-start | bytes 811016 | tf_op jit(solution)/shard_map/ppermute | solution.py:477
  (17 other events, 132.9 us)
